TPU v7x, 32 devices: a whole 2x2x4 slice. The times are simulated.
32 devices in a mesh: narrow: 4 (over y, x), wide: 4 (over z), seq: 2 (over core).
Axes of the slice: x: 2, y: 2, z: 4, core: 2. Of those that a mesh axis runs over, the one named last changes fastest.
Arguments:
- inputs: bfloat16 [8192, 1536], P(('narrow', 'wide', 'seq')), may hold values from -6 to 6
- doc_start: int32 [8192], P(('narrow', 'wide', 'seq')), may hold values from 0 to 8191, as said below
- norm_gain: float32 [1536], replicated, may hold values from 0.5 to 1.5
- qkv_weight: bfloat16 [1536, 4608], P('wide'), may hold values from -0.15625 to 0.15625
- logit_kernel: float32 [16, 6, 11], replicated, may hold values from -1 to 1
- head_mix: float32 [16, 2], replicated, may hold values from 0.2 to 1
- group_gain: float32 [1536], replicated, may hold values from 0.5 to 1.5
- out_weight: bfloat16 [1536, 1536], P('wide'), may hold values from -0.15625 to 0.15625
- feed_gain: float32 [1536], replicated, may hold values from 0.5 to 1.5
- gate_up: bfloat16 [1536, 8192], P('wide'), may hold values from -0.15625 to 0.15625
- down_weight: bfloat16 [4096, 1536], P('wide'), may hold values from -0.09375 to 0.09375
- cotangent: bfloat16 [8192, 1536], P(('narrow', 'wide', 'seq')), may hold values from -6 to 6
Outputs:
- block_out: bfloat16 [8192, 1536], P(('narrow', 'wide', 'seq'))
- grad_input: float32 [8192, 1536], P(('narrow', 'wide', 'seq'))
- grad_norm: float32 [1536], replicated
- grad_qkv: float32 [1536, 4608], P('wide')
- grad_kernel: float32 [16, 6, 11], replicated
- grad_mix: float32 [16, 2], replicated
- grad_group: float32 [1536], replicated
- grad_out: float32 [1536, 1536], P('wide')
- grad_feed: float32 [1536], replicated
- grad_gate: float32 [1536, 8192], P('wide')
- grad_down: float32 [4096, 1536], P('wide')
Inputs may be any that keep to these rules, and one draw needn't show every extreme that they name: `doc_start`: each token holds the global index of the first token of its document; documents lie inside aligned rows of 512 tokens, the first starting at the row's first token and the last being the row's last token alone, and in every row one document covers the 17 positions around the row's middle.
All inputs are finite; a program needn't handle non-finite values.
Results may differ from a plain program's by a relative error of at most 0.02.
Values may be sent and summed in bfloat16 or wider, within the bound.
No kernel may reach another device: no remote copies, remote signals or barrier semaphores. Data moves between devices by JAX's collectives and lax.ppermute only.
A program may use at most 320 MiB of HBM per device.

v0:
```python
import jax
import jax.numpy as jnp
from jax import lax
from jax.sharding import PartitionSpec as P


def shifted_2(array, axis, by):
    count = lax.axis_size(axis)
    pairs = [(i, i + by) for i in range(count) if 0 <= i + by < count]
    return lax.ppermute(array, axis, pairs)


def rms_norm(values, scale_row):
    return values * lax.rsqrt(jnp.mean(values * values, axis=-1, keepdims=True) + 1e-06) * scale_row


def group_norm(values, scale_row):
    centered = values - jnp.mean(values, axis=-1, keepdims=True)
    spread = jnp.mean(centered * centered, axis=-1, keepdims=True)
    normal = centered * lax.rsqrt(spread + 1e-05)
    return normal.reshape(values.shape[0], -1) * scale_row


def swiglu(joined):
    half_cols = joined.shape[1] // 2
    gating = joined[:, :half_cols]
    upward = joined[:, half_cols:]
    return gating / (1.0 + jnp.exp(-gating)) * upward


def shift_keys(slab_in, offset):
    length = slab_in.shape[-1]
    if offset > 0:
        return jnp.pad(slab_in[..., : length - offset], ((0, 0), (0, 0), (offset, 0)))
    if offset < 0:
        return jnp.pad(slab_in[..., -offset:], ((0, 0), (0, 0), (0, -offset)))
    return slab_in


def convolve(scores, kernel, out_pos, out_start, key_pos):
    query_taps = kernel.shape[1]
    key_taps = kernel.shape[2]
    margin = query_taps - 1
    half_taps = (key_taps - 1) // 2
    out_count = out_pos.shape[0]
    summed = jnp.zeros((scores.shape[0], out_count, scores.shape[2]), jnp.float32)
    for tap_q in range(query_taps):
        rows_at = scores[:, margin - tap_q : margin - tap_q + out_count, :]
        source = out_pos - tap_q
        inside = (
            (source >= out_start)[:, None]
            & (key_pos[None, :] >= out_start[:, None])
            & (key_pos[None, :] <= source[:, None])
        )
        masked = jnp.where(inside[None], rows_at, 0.0)
        for tap_k in range(key_taps):
            shifted = shift_keys(masked, tap_k - half_taps)
            summed = summed + kernel[:, tap_q, tap_k][:, None, None] * shifted
    return summed


def combine_heads(mix_group, weights):
    return jnp.stack(
        [
            mix_group[0, 0] * weights[0] + mix_group[0, 1] * weights[1],
            mix_group[1, 0] * weights[0] + mix_group[1, 1] * weights[1],
        ]
    )


def allowed_keys(out_pos, out_start, key_pos):
    return (key_pos[None, :] >= out_start[:, None]) & (key_pos[None, :] <= out_pos[:, None])


def attend(q_group, k_group, v_group, kernel, mix_group, out_pos, out_start, key_pos, scaling):
    scores = (
        jnp.einsum("qhd,khd->hqk", q_group, k_group, preferred_element_type=jnp.float32) * scaling
    )
    convolved = convolve(scores, kernel, out_pos, out_start, key_pos)
    allowed = allowed_keys(out_pos, out_start, key_pos)
    logits = jnp.where(allowed[None], convolved, -1e30)
    highest = jnp.max(logits, axis=-1, keepdims=True)
    raised = jnp.exp(logits - highest)
    summed = jnp.sum(raised, axis=-1, keepdims=True)
    weights = raised / summed
    mixed_low = combine_heads(mix_group, weights).astype(jnp.bfloat16)
    attended = jnp.einsum("hqk,khd->qhd", mixed_low, v_group, preferred_element_type=jnp.float32)
    return (attended, highest[..., 0] + jnp.log(summed[..., 0]))


def attend_back(
    q_group,
    k_group,
    v_group,
    kernel,
    mix_group,
    grad_att,
    log_total,
    out_pos,
    out_start,
    key_pos,
    scaling,
):
    scores = (
        jnp.einsum("qhd,khd->hqk", q_group, k_group, preferred_element_type=jnp.float32) * scaling
    )

    def conv_only(scores_in, kernel_in):
        return convolve(scores_in, kernel_in, out_pos, out_start, key_pos)

    convolved, conv_back = jax.vjp(conv_only, scores, kernel)
    allowed = allowed_keys(out_pos, out_start, key_pos)
    weights = jnp.where(allowed[None], jnp.exp(convolved - log_total[..., None]), 0.0)
    mixed_low = combine_heads(mix_group, weights).astype(jnp.bfloat16)
    grad_mixed = jnp.einsum("qhd,khd->hqk", grad_att, v_group, preferred_element_type=jnp.float32)
    grad_values = jnp.einsum(
        "hqk,qhd->khd", mixed_low, grad_att, preferred_element_type=jnp.float32
    )
    grad_mixes = jnp.stack(
        [
            jnp.sum(grad_mixed * weights[0], axis=(1, 2)),
            jnp.sum(grad_mixed * weights[1], axis=(1, 2)),
        ],
        1,
    )
    grad_weights = jnp.stack(
        [
            mix_group[0, 0] * grad_mixed[0] + mix_group[1, 0] * grad_mixed[1],
            mix_group[0, 1] * grad_mixed[0] + mix_group[1, 1] * grad_mixed[1],
        ]
    )
    grad_conv = weights * (grad_weights - jnp.sum(grad_weights * weights, axis=-1, keepdims=True))
    grad_scores, grad_kernel = conv_back(grad_conv)
    grad_scores_low = grad_scores.astype(jnp.bfloat16)
    grad_queries = (
        jnp.einsum("hqk,khd->qhd", grad_scores_low, k_group, preferred_element_type=jnp.float32)
        * scaling
    )
    grad_keys = (
        jnp.einsum("hqk,qhd->khd", grad_scores_low, q_group, preferred_element_type=jnp.float32)
        * scaling
    )
    return (grad_queries, grad_keys, grad_values, grad_kernel, grad_mixes)


def project(acts, weight):
    return jnp.dot(
        acts, lax.all_gather(weight, "wide", axis=0, tiled=True), preferred_element_type=jnp.float32
    )


def back_project(grads_in, weight):
    return lax.dot_general(
        grads_in,
        lax.all_gather(weight, "wide", axis=0, tiled=True),
        (((1,), (1,)), ((), ())),
        preferred_element_type=jnp.float32,
    )


def row_product(left, right):
    return lax.dot_general(
        left, right, (((0,), (0,)), ((), ())), preferred_element_type=jnp.float32
    )


def scatter_rows(left, right):
    return lax.psum_scatter(
        row_product(left, right).astype(jnp.bfloat16), "wide", scatter_dimension=0, tiled=True
    ).astype(jnp.float32)


def on_device(
    inputs,
    doc_start,
    norm_gain,
    qkv_weight,
    logit_kernel,
    head_mix,
    group_gain,
    out_weight,
    feed_gain,
    gate_up,
    down_weight,
    cotangent,
):
    tokens_dev = inputs.shape[0]
    model_width = inputs.shape[1]
    head_count = logit_kernel.shape[0]
    query_taps = logit_kernel.shape[1]
    key_taps = logit_kernel.shape[2]
    head_size = model_width // head_count
    groups = head_count // 2
    margin = query_taps - 1
    seq_parts = lax.axis_size("seq")
    scaling = head_size ** (-0.5)
    first_pos = lax.axis_index(("narrow", "wide", "seq")) * tokens_dev
    own_pos = first_pos + jnp.arange(tokens_dev, dtype=jnp.int32)
    row_first = first_pos - lax.axis_index("seq") * tokens_dev
    key_pos = row_first + jnp.arange(seq_parts * tokens_dev, dtype=jnp.int32)
    inputs_f = inputs.astype(jnp.float32)
    normed = rms_norm(inputs_f, norm_gain).astype(jnp.bfloat16)
    projected = project(normed, qkv_weight).astype(jnp.bfloat16)
    queries = projected[:, :model_width]
    keys_own = projected[:, model_width : 2 * model_width]
    values_own = projected[:, 2 * model_width :]
    rim_rows = shifted_2(queries[tokens_dev - margin :], "seq", 1)
    queries_ext = jnp.concatenate([rim_rows, queries], 0)
    keys_row, values_row = (
        lax.all_gather(keys_own, "seq", axis=0, tiled=True),
        lax.all_gather(values_own, "seq", axis=0, tiled=True),
    )

    def by_group(matrix):
        return jnp.moveaxis(matrix.reshape(matrix.shape[0], groups, 2, head_size), 1, 0)

    def ungroup(grouped_arr):
        return jnp.moveaxis(grouped_arr, 0, 1).reshape(grouped_arr.shape[1], model_width)

    q_groups = by_group(queries_ext)
    k_groups = by_group(keys_row)
    v_groups = by_group(values_row)
    kernels = logit_kernel.reshape(groups, 2, query_taps, key_taps)
    mix_groups = head_mix.reshape(groups, 2, 2)

    def forward_group(group_items):
        q_group, k_group, v_group, kernel, mix_group = group_items
        return attend(
            q_group, k_group, v_group, kernel, mix_group, own_pos, doc_start, key_pos, scaling
        )

    attended_g, log_totals = lax.map(
        forward_group, (q_groups, k_groups, v_groups, kernels, mix_groups)
    )
    attended = jnp.moveaxis(attended_g, 0, 1).reshape(tokens_dev, head_count, head_size)
    grouped = group_norm(attended, group_gain).astype(jnp.bfloat16)
    branch = project(grouped, out_weight)
    residual = inputs_f + branch
    normed_ffn = rms_norm(residual, feed_gain).astype(jnp.bfloat16)
    gate_vals = project(normed_ffn, gate_up)
    hidden = swiglu(gate_vals).astype(jnp.bfloat16)
    branch_ffn = project(hidden, down_weight)
    block_out = (residual + branch_ffn).astype(jnp.bfloat16)
    grad_hidden = back_project(cotangent, down_weight)
    swiglu_back = jax.vjp(swiglu, gate_vals)[1]
    grad_gates = swiglu_back(grad_hidden)[0].astype(jnp.bfloat16)
    grad_normed_ffn = back_project(grad_gates, gate_up)
    second_back = jax.vjp(rms_norm, residual, feed_gain)[1]
    grad_residual_norm, grad_feed = second_back(grad_normed_ffn)
    grad_residual = grad_residual_norm + cotangent.astype(jnp.float32)
    grad_branch = grad_residual.astype(jnp.bfloat16)
    grad_grouped = back_project(grad_branch, out_weight)
    group_back = jax.vjp(group_norm, attended, group_gain)[1]
    grad_attended, grad_group = group_back(grad_grouped)
    grad_att_groups = by_group(grad_attended.reshape(tokens_dev, model_width).astype(jnp.bfloat16))

    def backward_group(group_items):
        q_group, k_group, v_group, kernel, mix_group, grad_att, log_total = group_items
        return attend_back(
            q_group,
            k_group,
            v_group,
            kernel,
            mix_group,
            grad_att,
            log_total,
            own_pos,
            doc_start,
            key_pos,
            scaling,
        )

    grad_q_g, grad_k_g, grad_v_g, grad_kernels, grad_mixes = lax.map(
        backward_group,
        (q_groups, k_groups, v_groups, kernels, mix_groups, grad_att_groups, log_totals),
    )
    grad_keys, grad_values = (
        lax.psum_scatter(
            ungroup(grad_k_g).astype(jnp.bfloat16), "seq", scatter_dimension=0, tiled=True
        ).astype(jnp.float32),
        lax.psum_scatter(
            ungroup(grad_v_g).astype(jnp.bfloat16), "seq", scatter_dimension=0, tiled=True
        ).astype(jnp.float32),
    )
    grad_q_ext = ungroup(grad_q_g)
    rim_back = shifted_2(grad_q_ext[:margin], "seq", -1)
    grad_queries = grad_q_ext[margin:]
    grad_queries = jnp.concatenate(
        [grad_queries[: tokens_dev - margin], grad_queries[tokens_dev - margin :] + rim_back], 0
    )
    grad_projected = jnp.concatenate([grad_queries, grad_keys, grad_values], 1).astype(jnp.bfloat16)
    grad_normed = back_project(grad_projected, qkv_weight)
    first_back = jax.vjp(rms_norm, inputs_f, norm_gain)[1]
    grad_input_norm, grad_norm = first_back(grad_normed)
    grad_input = grad_input_norm + grad_residual
    grad_norm, grad_kernel, grad_mix, grad_group, grad_feed = lax.psum(
        (
            grad_norm,
            grad_kernels.reshape(head_count, query_taps, key_taps),
            grad_mixes.reshape(head_count, 2),
            grad_group,
            grad_feed,
        ),
        ("narrow", "wide", "seq"),
    )
    shard_qkv = scatter_rows(normed, grad_projected)
    shard_out = scatter_rows(grouped, grad_branch)
    shard_gate = scatter_rows(normed_ffn, grad_gates)
    shard_down = scatter_rows(hidden, cotangent)
    grad_qkv, grad_out, grad_gate, grad_down = (
        lax.psum(shard_qkv.astype(jnp.bfloat16), ("narrow", "seq")).astype(jnp.float32),
        lax.psum(shard_out.astype(jnp.bfloat16), ("narrow", "seq")).astype(jnp.float32),
        lax.psum(shard_gate.astype(jnp.bfloat16), ("narrow", "seq")).astype(jnp.float32),
        lax.psum(shard_down.astype(jnp.bfloat16), ("narrow", "seq")).astype(jnp.float32),
    )
    return (
        block_out,
        grad_input,
        grad_norm,
        grad_qkv,
        grad_kernel,
        grad_mix,
        grad_group,
        grad_out,
        grad_feed,
        grad_gate,
        grad_down,
    )


def solution(mesh):
    return jax.shard_map(
        on_device,
        mesh=mesh,
        in_specs=(
            P(("narrow", "wide", "seq"), None),
            P(("narrow", "wide", "seq")),
            P(),
            P("wide", None),
            P(),
            P(),
            P(),
            P("wide", None),
            P(),
            P("wide", None),
            P("wide", None),
            P(("narrow", "wide", "seq"), None),
        ),
        out_specs=(
            P(("narrow", "wide", "seq"), None),
            P(("narrow", "wide", "seq"), None),
            P(),
            P("wide", None),
            P(),
            P(),
            P(),
            P("wide", None),
            P(),
            P("wide", None),
            P("wide", None),
        ),
        check_vma=False,
    )
```

profile of v0, /device:TPU:0, one launch (start us, length us, event | category | flops | bytes accessed | tf_op | source)
XLA Modules:
  0.0 3662.6 jit_solution(9556231409914986525)
XLA Ops:
  9.1 247.1 %all-gather.7.cloned.1.call-done = bf16[1536,4608]{1,0:T(8,128)(2,1)} async-done(((bf16[384,4608]{1,0:T(8,128)(2,1)}), bf16[1536,4608]{1,0:T(8,128)(2,1)}) %all-gather.7.cloned.1.call-update) | async-done | bytes 14155792 | tf_op jit(solution)/shard_map/all_gather | solution.py:148
  256.3 9.2 convolution_convert_fusion.4
  277.9 10.3 all-gather.11.cloned.1.call-done
  290.8 615.4 %while.36 = (s32[]{:T(128)}, f32[8,256,2,96]{1,3,2,0:T(8,128)}, f32[8,2,256]{2,1,0:T(2,128)S(1)}, bf16[8,512,2,96]{1,3,2,0:T(8,128)(2,1)}, f32[8,2,2]{2,1,0:T(2,...) while((s32[]{:T(128)}, f32[8,256,2,96]{1,3,2,0:T(8,128)}, ...), condition=%wide.region_4.5_spmd.clone, body=%wide.region_1.4_spmd.clone.sunk | while | flops 143337216 | bytes 216475712 | solution.py:232
  340.8 20.9 fusion.324
  417.5 20.8 fusion.324
  494.2 20.9 fusion.324
  570.8 20.9 fusion.324
  647.5 20.8 fusion.324
  723.9 20.7 fusion.324
  800.2 23.2 fusion.324
  879.2 20.9 fusion.324
  917.4 5.7 multiply_reduce_fusion.73
  923.2 14.3 fusion.113
  937.5 85.7 %all-gather.17.cloned.1.call-done = bf16[4096,1536]{1,0:T(8,128)(2,1)} async-done(((bf16[1024,1536]{1,0:T(8,128)(2,1)}), bf16[4096,1536]{1,0:T(8,128)(2,1)}) %all-gather.17.cloned.1.call-update) | async-done | bytes 12582928 | tf_op jit(solution)/shard_map/all_gather | solution.py:148
  1023.2 12.5 fusion.99
  1035.7 16.3 multiply_reduce_fusion.69
  1054.6 6.1 multiply_reduce_fusion.70
  1076.0 1380.0 %while.37 = (s32[]{:T(128)}, f32[8,261,2,96]{3,1,2,0:T(8,128)}, bf16[8,512,2,96]{1,3,2,0:T(8,128)(2,1)}, bf16[8,512,2,96]{1,3,2,0:T(8,128)(2,1)}, f32[8,2,6,11]{...) while((s32[]{:T(128)}, f32[8,261,2,96]{3,1,2,0:T(8,128)}, ...), condition=%wide.region_81.82_spmd.clone, body=%wide.region_11.81_spmd.clone.sunk | while | flops 369531840 | bytes 730533504 | solution.py:273
  1140.0 22.6 multiply_reduce_fusion.80
  1168.7 9.0 multiply_reduce_fusion.81
  1179.7 5.7 multiply_reduce_fusion.84
  1223.3 5.3 add_select_fusion.18
  1311.4 22.8 multiply_reduce_fusion.80
  1340.3 9.0 multiply_reduce_fusion.81
  1351.3 5.7 multiply_reduce_fusion.84
  1358.0 4.9 multiply_reduce_fusion.83
  1394.7 5.3 add_select_fusion.18
  1483.0 22.6 multiply_reduce_fusion.80
  1511.7 9.0 multiply_reduce_fusion.81
  1522.6 5.7 multiply_reduce_fusion.84
  1566.1 5.3 add_select_fusion.18
  1654.4 22.6 multiply_reduce_fusion.80
  1683.0 9.0 multiply_reduce_fusion.81
  1694.0 5.7 multiply_reduce_fusion.84
  1737.7 5.3 add_select_fusion.18
  1825.8 22.8 multiply_reduce_fusion.80
  1854.7 9.0 multiply_reduce_fusion.81
  1865.7 5.7 multiply_reduce_fusion.84
  1909.0 5.3 add_select_fusion.18
  1997.4 22.6 multiply_reduce_fusion.80
  2026.0 9.0 multiply_reduce_fusion.81
  2037.0 5.7 multiply_reduce_fusion.84
  2080.4 5.3 add_select_fusion.18
  2168.7 22.6 multiply_reduce_fusion.80
  2197.4 9.0 multiply_reduce_fusion.81
  2208.4 5.7 multiply_reduce_fusion.84
  2252.0 5.3 add_select_fusion.18
  2340.1 22.8 multiply_reduce_fusion.80
  2369.0 9.0 multiply_reduce_fusion.81
  2380.0 5.7 multiply_reduce_fusion.84
  2423.4 5.3 add_select_fusion.18
  2462.7 8.3 convolution_convert_fusion.2
  2481.1 10.9 convolution_convert_fusion.1
  2493.4 15.0 convolution_convert_fusion
  2508.7 56.8 %reduce-scatter.13.cloned.1.call-done = bf16[384,1536]{1,0:T(8,128)(2,1)} async-done(((bf16[1536,1536]{1,0:T(8,128)(2,1)}), bf16[384,1536]{1,0:T(8,128)(2,1)}) %reduce-scatter.13.cloned.1.call-update) | async-done | bytes 1179664 | tf_op jit(solution)/shard_map/reduce_scatter | solution.py:168
  2565.5 215.2 %reduce-scatter.17.cloned.1.call-done = bf16[1024,1536]{1,0:T(8,128)(2,1)} async-done(((bf16[4096,1536]{1,0:T(8,128)(2,1)}), bf16[1024,1536]{1,0:T(8,128)(2,1)}) %reduce-scatter.17.cloned.1.call-update) | async-done | bytes 3145744 | tf_op jit(solution)/shard_map/reduce_scatter | solution.py:168
  2780.7 240.7 %reduce-scatter.11.cloned.1.call-done = bf16[384,4608]{1,0:T(8,128)(2,1)} async-done(((bf16[1536,4608]{1,0:T(8,128)(2,1)}), bf16[384,4608]{1,0:T(8,128)(2,1)}) %reduce-scatter.11.cloned.1.call-update) | async-done | bytes 3538960 | tf_op jit(solution)/shard_map/reduce_scatter | solution.py:168
  3021.4 417.6 %reduce-scatter.15.cloned.1.call-done = bf16[384,8192]{1,0:T(8,128)(2,1)} async-done(((bf16[1536,8192]{1,0:T(8,128)(2,1)}), bf16[384,8192]{1,0:T(8,128)(2,1)}) %reduce-scatter.15.cloned.1.call-update) | async-done | bytes 6291472 | tf_op jit(solution)/shard_map/reduce_scatter | solution.py:168
  3439.8 9.6 fusion.85
  3449.4 12.5 fusion.89
  3462.0 44.7 %all-reduce.254 = (f32[1536]{0:T(1024)}, f32[16,6,11]{2,0,1:T(8,128)S(1)}, f32[16,2]{0,1:T(2,128)}, f32[1536]{0:T(1024)}, f32[1536]{0:T(1024)}) all-reduce(f32[1536]{0:T(1024)S(1)} %get-tuple-element.668, f32[16,6,11]{2,0,1:T(8,128)S(1)} %bitcast.780, ...), channel_id=1, replica_groups=mesh['narrow'=4,'wide'=4,'seq'=2] {'narrow','wide','seq'}, use_global_device_ids=true, to_apply=%region_86.87 | all-reduce | flops 5696 | bytes 45568 | tf_op jit(solution)/shard_map/psum | solution.py:296
  3510.4 127.1 %all-reduce.258.cloned.1.call-done = (bf16[384,4608]{1,0:T(8,128)(2,1)}, bf16[384,1536]{1,0:T(8,128)(2,1)}, bf16[384,8192]{1,0:T(8,128)(2,1)}, bf16[1024,1536]{1,0:T(8,128)(2,1)}) async-done(((bf16[384,4608]{1,0:T(8,128)(2,1)}, bf16[384,1536]{1,0:T(8,128)(2,1)}, bf16[384,8192]{1,0:T(8,128)(2,1)}, bf16[1024,1536]{1,0:T(8,128)(2,1)}), (bf16[384,4608]{1,0:T(8,128)(2,1)}, bf16[384,1536]{1,0:T(8,128)(2,1)}, ...) | async-done | bytes 14155792 | tf_op jit(solution)/shard_map/psum | solution.py:311
  3637.5 9.3 convert_element_type.266
  (3695 shorter events, 1529.9 us)
Async XLA Ops:
  7.2 249.1 %copy-start.181 = (f32[1536]{0:T(1024)S(1)}, f32[1536]{0:T(1024)}, u32[]{:S(2)}) copy-start(f32[1536]{0:T(1024)} %param.18) | copy-start | bytes 18436
  7.2 249.1 %all-gather.7.cloned.1.call-start = ((), (), s32[]{:S(2)}) async-start(), calls=%async_computation.6 | async-start | bytes 17694720 | tf_op jit(solution)/shard_map/all_gather | solution.py:148
  7.9 267.4 %all-gather.9.cloned.1.call-start = ((), (), s32[]{:S(2)}) async-start(), calls=%async_computation.7 | async-start | bytes 2359296 | tf_op jit(solution)/shard_map/all_gather | solution.py:211
  9.1 256.4 %copy-start.188 = (f32[256]{0:T(256)}, f32[256]{0:T(256)S(1)}, u32[]{:S(2)}) copy-start(f32[256]{0:T(256)S(1)} %fusion.107) | copy-start | bytes 3076
  266.9 21.3 all-gather.11.cloned.1.call-start
  267.7 649.8 %all-gather.13.cloned.1.call-start = ((), (), s32[]{:S(2)}) async-start(), calls=%async_computation.9 | async-start | bytes 5898240 | tf_op jit(solution)/shard_map/all_gather | solution.py:148
  268.2 655.0 %all-gather.15.cloned.1.call-start = ((), (), s32[]{:S(2)}) async-start(), calls=%async_computation.10 | async-start | bytes 31457280 | tf_op jit(solution)/shard_map/all_gather | solution.py:148
  268.9 754.3 %all-gather.17.cloned.1.call-start = ((), (), s32[]{:S(2)}) async-start(), calls=%async_computation.11 | async-start | bytes 15728640 | tf_op jit(solution)/shard_map/all_gather | solution.py:148
  269.4 2211.6 %reduce-scatter.7.cloned.1.call-start = ((), (), s32[]{:S(2)}) async-start(), calls=%async_computation.12 | async-start | bytes 2359296 | tf_op jit(solution)/shard_map/reduce_scatter | solution.py:278
  269.5 3.5 collective-permute-start
  917.4 137.2 %copy-start.72 = (f32[256,1536]{1,0:T(8,128)}, f32[256,1536]{1,0:T(8,128)S(1)}, u32[]{:S(2)}) copy-start(f32[256,1536]{1,0:T(8,128)S(1)} %get-tuple-element.742) | copy-start | bytes 4718596
  923.2 128.8 %copy-start.172 = (f32[256]{0:T(256)}, f32[256]{0:T(256)S(1)}, u32[]{:S(2)}) copy-start(f32[256]{0:T(256)S(1)} %fusion.108) | copy-start | bytes 3076
  1080.7 59.2 %copy-start = (f32[2,256,512]{2,1,0:T(8,128)}, f32[2,256,512]{2,1,0:T(8,128)S(1)}, u32[]{:S(2)}) copy-start(f32[2,256,512]{2,1,0:T(8,128)S(1)} %get-tuple-element.1984) | copy-start | bytes 3145732 | tf_op jit(solution)/shard_map/while
  1080.7 59.2 %copy-start.2 = (f32[2,256,512]{2,1,0:T(8,128)}, f32[2,256,512]{2,1,0:T(8,128)S(1)}, u32[]{:S(2)}) copy-start(f32[2,256,512]{2,1,0:T(8,128)S(1)} %get-tuple-element.2050) | copy-start | bytes 3145732 | tf_op jit(solution)/shard_map/while
  1080.7 59.2 %copy-start.4 = (f32[2,256,512]{2,1,0:T(8,128)}, f32[2,256,512]{2,1,0:T(8,128)S(1)}, u32[]{:S(2)}) copy-start(f32[2,256,512]{2,1,0:T(8,128)S(1)} %get-tuple-element.1934) | copy-start | bytes 3145732 | tf_op jit(solution)/shard_map/while
  1080.7 59.2 %copy-start.5 = (f32[2,256,512]{2,1,0:T(8,128)}, f32[2,256,512]{2,1,0:T(8,128)S(1)}, u32[]{:S(2)}) copy-start(f32[2,256,512]{2,1,0:T(8,128)S(1)} %get-tuple-element.1936) | copy-start | bytes 3145732 | tf_op jit(solution)/shard_map/while
  1085.8 54.1 %copy-start.6 = (f32[2,256,510]{2,1,0:T(8,128)}, f32[2,256,510]{2,1,0:T(8,128)S(1)}, u32[]{:S(2)}) copy-start(f32[2,256,510]{2,1,0:T(8,128)S(1)} %get-tuple-element.1976) | copy-start | bytes 3133444 | tf_op jit(solution)/shard_map/while
  1252.1 59.2 %copy-start = (f32[2,256,512]{2,1,0:T(8,128)}, f32[2,256,512]{2,1,0:T(8,128)S(1)}, u32[]{:S(2)}) copy-start(f32[2,256,512]{2,1,0:T(8,128)S(1)} %get-tuple-element.1984) | copy-start | bytes 3145732 | tf_op jit(solution)/shard_map/while
  1252.1 59.2 %copy-start.2 = (f32[2,256,512]{2,1,0:T(8,128)}, f32[2,256,512]{2,1,0:T(8,128)S(1)}, u32[]{:S(2)}) copy-start(f32[2,256,512]{2,1,0:T(8,128)S(1)} %get-tuple-element.2050) | copy-start | bytes 3145732 | tf_op jit(solution)/shard_map/while
  1252.1 59.2 %copy-start.4 = (f32[2,256,512]{2,1,0:T(8,128)}, f32[2,256,512]{2,1,0:T(8,128)S(1)}, u32[]{:S(2)}) copy-start(f32[2,256,512]{2,1,0:T(8,128)S(1)} %get-tuple-element.1934) | copy-start | bytes 3145732 | tf_op jit(solution)/shard_map/while
  1252.1 59.2 %copy-start.5 = (f32[2,256,512]{2,1,0:T(8,128)}, f32[2,256,512]{2,1,0:T(8,128)S(1)}, u32[]{:S(2)}) copy-start(f32[2,256,512]{2,1,0:T(8,128)S(1)} %get-tuple-element.1936) | copy-start | bytes 3145732 | tf_op jit(solution)/shard_map/while
  1257.2 54.1 %copy-start.6 = (f32[2,256,510]{2,1,0:T(8,128)}, f32[2,256,510]{2,1,0:T(8,128)S(1)}, u32[]{:S(2)}) copy-start(f32[2,256,510]{2,1,0:T(8,128)S(1)} %get-tuple-element.1976) | copy-start | bytes 3133444 | tf_op jit(solution)/shard_map/while
  1258.5 52.8 %copy-start.8 = (f32[2,256,509]{2,1,0:T(8,128)}, f32[2,256,509]{2,1,0:T(8,128)S(1)}, u32[]{:S(2)}) copy-start(f32[2,256,509]{2,1,0:T(8,128)S(1)} %get-tuple-element.1978) | copy-start | bytes 3127300 | tf_op jit(solution)/shard_map/while
  1423.7 59.2 %copy-start = (f32[2,256,512]{2,1,0:T(8,128)}, f32[2,256,512]{2,1,0:T(8,128)S(1)}, u32[]{:S(2)}) copy-start(f32[2,256,512]{2,1,0:T(8,128)S(1)} %get-tuple-element.1984) | copy-start | bytes 3145732 | tf_op jit(solution)/shard_map/while
  1423.7 59.2 %copy-start.2 = (f32[2,256,512]{2,1,0:T(8,128)}, f32[2,256,512]{2,1,0:T(8,128)S(1)}, u32[]{:S(2)}) copy-start(f32[2,256,512]{2,1,0:T(8,128)S(1)} %get-tuple-element.2050) | copy-start | bytes 3145732 | tf_op jit(solution)/shard_map/while
  1423.7 59.2 %copy-start.4 = (f32[2,256,512]{2,1,0:T(8,128)}, f32[2,256,512]{2,1,0:T(8,128)S(1)}, u32[]{:S(2)}) copy-start(f32[2,256,512]{2,1,0:T(8,128)S(1)} %get-tuple-element.1934) | copy-start | bytes 3145732 | tf_op jit(solution)/shard_map/while
  1423.7 59.2 %copy-start.5 = (f32[2,256,512]{2,1,0:T(8,128)}, f32[2,256,512]{2,1,0:T(8,128)S(1)}, u32[]{:S(2)}) copy-start(f32[2,256,512]{2,1,0:T(8,128)S(1)} %get-tuple-element.1936) | copy-start | bytes 3145732 | tf_op jit(solution)/shard_map/while
  1428.8 54.1 %copy-start.6 = (f32[2,256,510]{2,1,0:T(8,128)}, f32[2,256,510]{2,1,0:T(8,128)S(1)}, u32[]{:S(2)}) copy-start(f32[2,256,510]{2,1,0:T(8,128)S(1)} %get-tuple-element.1976) | copy-start | bytes 3133444 | tf_op jit(solution)/shard_map/while
  1595.1 59.2 %copy-start = (f32[2,256,512]{2,1,0:T(8,128)}, f32[2,256,512]{2,1,0:T(8,128)S(1)}, u32[]{:S(2)}) copy-start(f32[2,256,512]{2,1,0:T(8,128)S(1)} %get-tuple-element.1984) | copy-start | bytes 3145732 | tf_op jit(solution)/shard_map/while
  1595.1 59.2 %copy-start.2 = (f32[2,256,512]{2,1,0:T(8,128)}, f32[2,256,512]{2,1,0:T(8,128)S(1)}, u32[]{:S(2)}) copy-start(f32[2,256,512]{2,1,0:T(8,128)S(1)} %get-tuple-element.2050) | copy-start | bytes 3145732 | tf_op jit(solution)/shard_map/while
  1595.1 59.2 %copy-start.4 = (f32[2,256,512]{2,1,0:T(8,128)}, f32[2,256,512]{2,1,0:T(8,128)S(1)}, u32[]{:S(2)}) copy-start(f32[2,256,512]{2,1,0:T(8,128)S(1)} %get-tuple-element.1934) | copy-start | bytes 3145732 | tf_op jit(solution)/shard_map/while
  1595.1 59.2 %copy-start.5 = (f32[2,256,512]{2,1,0:T(8,128)}, f32[2,256,512]{2,1,0:T(8,128)S(1)}, u32[]{:S(2)}) copy-start(f32[2,256,512]{2,1,0:T(8,128)S(1)} %get-tuple-element.1936) | copy-start | bytes 3145732 | tf_op jit(solution)/shard_map/while
  1600.2 54.1 %copy-start.6 = (f32[2,256,510]{2,1,0:T(8,128)}, f32[2,256,510]{2,1,0:T(8,128)S(1)}, u32[]{:S(2)}) copy-start(f32[2,256,510]{2,1,0:T(8,128)S(1)} %get-tuple-element.1976) | copy-start | bytes 3133444 | tf_op jit(solution)/shard_map/while
  1766.5 59.2 %copy-start = (f32[2,256,512]{2,1,0:T(8,128)}, f32[2,256,512]{2,1,0:T(8,128)S(1)}, u32[]{:S(2)}) copy-start(f32[2,256,512]{2,1,0:T(8,128)S(1)} %get-tuple-element.1984) | copy-start | bytes 3145732 | tf_op jit(solution)/shard_map/while
  1766.5 59.2 %copy-start.2 = (f32[2,256,512]{2,1,0:T(8,128)}, f32[2,256,512]{2,1,0:T(8,128)S(1)}, u32[]{:S(2)}) copy-start(f32[2,256,512]{2,1,0:T(8,128)S(1)} %get-tuple-element.2050) | copy-start | bytes 3145732 | tf_op jit(solution)/shard_map/while
  1766.5 59.2 %copy-start.4 = (f32[2,256,512]{2,1,0:T(8,128)}, f32[2,256,512]{2,1,0:T(8,128)S(1)}, u32[]{:S(2)}) copy-start(f32[2,256,512]{2,1,0:T(8,128)S(1)} %get-tuple-element.1934) | copy-start | bytes 3145732 | tf_op jit(solution)/shard_map/while
  1766.5 59.2 %copy-start.5 = (f32[2,256,512]{2,1,0:T(8,128)}, f32[2,256,512]{2,1,0:T(8,128)S(1)}, u32[]{:S(2)}) copy-start(f32[2,256,512]{2,1,0:T(8,128)S(1)} %get-tuple-element.1936) | copy-start | bytes 3145732 | tf_op jit(solution)/shard_map/while
  1771.6 54.1 %copy-start.6 = (f32[2,256,510]{2,1,0:T(8,128)}, f32[2,256,510]{2,1,0:T(8,128)S(1)}, u32[]{:S(2)}) copy-start(f32[2,256,510]{2,1,0:T(8,128)S(1)} %get-tuple-element.1976) | copy-start | bytes 3133444 | tf_op jit(solution)/shard_map/while
  1772.9 52.8 %copy-start.8 = (f32[2,256,509]{2,1,0:T(8,128)}, f32[2,256,509]{2,1,0:T(8,128)S(1)}, u32[]{:S(2)}) copy-start(f32[2,256,509]{2,1,0:T(8,128)S(1)} %get-tuple-element.1978) | copy-start | bytes 3127300 | tf_op jit(solution)/shard_map/while
  1938.0 59.2 %copy-start = (f32[2,256,512]{2,1,0:T(8,128)}, f32[2,256,512]{2,1,0:T(8,128)S(1)}, u32[]{:S(2)}) copy-start(f32[2,256,512]{2,1,0:T(8,128)S(1)} %get-tuple-element.1984) | copy-start | bytes 3145732 | tf_op jit(solution)/shard_map/while
  1938.1 59.2 %copy-start.2 = (f32[2,256,512]{2,1,0:T(8,128)}, f32[2,256,512]{2,1,0:T(8,128)S(1)}, u32[]{:S(2)}) copy-start(f32[2,256,512]{2,1,0:T(8,128)S(1)} %get-tuple-element.2050) | copy-start | bytes 3145732 | tf_op jit(solution)/shard_map/while
  1938.1 59.2 %copy-start.4 = (f32[2,256,512]{2,1,0:T(8,128)}, f32[2,256,512]{2,1,0:T(8,128)S(1)}, u32[]{:S(2)}) copy-start(f32[2,256,512]{2,1,0:T(8,128)S(1)} %get-tuple-element.1934) | copy-start | bytes 3145732 | tf_op jit(solution)/shard_map/while
  1938.1 59.2 %copy-start.5 = (f32[2,256,512]{2,1,0:T(8,128)}, f32[2,256,512]{2,1,0:T(8,128)S(1)}, u32[]{:S(2)}) copy-start(f32[2,256,512]{2,1,0:T(8,128)S(1)} %get-tuple-element.1936) | copy-start | bytes 3145732 | tf_op jit(solution)/shard_map/while
  1943.2 54.1 %copy-start.6 = (f32[2,256,510]{2,1,0:T(8,128)}, f32[2,256,510]{2,1,0:T(8,128)S(1)}, u32[]{:S(2)}) copy-start(f32[2,256,510]{2,1,0:T(8,128)S(1)} %get-tuple-element.1976) | copy-start | bytes 3133444 | tf_op jit(solution)/shard_map/while
  2109.4 59.2 %copy-start = (f32[2,256,512]{2,1,0:T(8,128)}, f32[2,256,512]{2,1,0:T(8,128)S(1)}, u32[]{:S(2)}) copy-start(f32[2,256,512]{2,1,0:T(8,128)S(1)} %get-tuple-element.1984) | copy-start | bytes 3145732 | tf_op jit(solution)/shard_map/while
  2109.4 59.2 %copy-start.2 = (f32[2,256,512]{2,1,0:T(8,128)}, f32[2,256,512]{2,1,0:T(8,128)S(1)}, u32[]{:S(2)}) copy-start(f32[2,256,512]{2,1,0:T(8,128)S(1)} %get-tuple-element.2050) | copy-start | bytes 3145732 | tf_op jit(solution)/shard_map/while
  2109.4 59.2 %copy-start.4 = (f32[2,256,512]{2,1,0:T(8,128)}, f32[2,256,512]{2,1,0:T(8,128)S(1)}, u32[]{:S(2)}) copy-start(f32[2,256,512]{2,1,0:T(8,128)S(1)} %get-tuple-element.1934) | copy-start | bytes 3145732 | tf_op jit(solution)/shard_map/while
  2109.5 59.2 %copy-start.5 = (f32[2,256,512]{2,1,0:T(8,128)}, f32[2,256,512]{2,1,0:T(8,128)S(1)}, u32[]{:S(2)}) copy-start(f32[2,256,512]{2,1,0:T(8,128)S(1)} %get-tuple-element.1936) | copy-start | bytes 3145732 | tf_op jit(solution)/shard_map/while
  2114.5 54.1 %copy-start.6 = (f32[2,256,510]{2,1,0:T(8,128)}, f32[2,256,510]{2,1,0:T(8,128)S(1)}, u32[]{:S(2)}) copy-start(f32[2,256,510]{2,1,0:T(8,128)S(1)} %get-tuple-element.1976) | copy-start | bytes 3133444 | tf_op jit(solution)/shard_map/while
  2280.8 59.2 %copy-start = (f32[2,256,512]{2,1,0:T(8,128)}, f32[2,256,512]{2,1,0:T(8,128)S(1)}, u32[]{:S(2)}) copy-start(f32[2,256,512]{2,1,0:T(8,128)S(1)} %get-tuple-element.1984) | copy-start | bytes 3145732 | tf_op jit(solution)/shard_map/while
  2280.8 59.2 %copy-start.2 = (f32[2,256,512]{2,1,0:T(8,128)}, f32[2,256,512]{2,1,0:T(8,128)S(1)}, u32[]{:S(2)}) copy-start(f32[2,256,512]{2,1,0:T(8,128)S(1)} %get-tuple-element.2050) | copy-start | bytes 3145732 | tf_op jit(solution)/shard_map/while
  2280.8 59.2 %copy-start.4 = (f32[2,256,512]{2,1,0:T(8,128)}, f32[2,256,512]{2,1,0:T(8,128)S(1)}, u32[]{:S(2)}) copy-start(f32[2,256,512]{2,1,0:T(8,128)S(1)} %get-tuple-element.1934) | copy-start | bytes 3145732 | tf_op jit(solution)/shard_map/while
  2280.8 59.2 %copy-start.5 = (f32[2,256,512]{2,1,0:T(8,128)}, f32[2,256,512]{2,1,0:T(8,128)S(1)}, u32[]{:S(2)}) copy-start(f32[2,256,512]{2,1,0:T(8,128)S(1)} %get-tuple-element.1936) | copy-start | bytes 3145732 | tf_op jit(solution)/shard_map/while
  2285.9 54.1 %copy-start.6 = (f32[2,256,510]{2,1,0:T(8,128)}, f32[2,256,510]{2,1,0:T(8,128)S(1)}, u32[]{:S(2)}) copy-start(f32[2,256,510]{2,1,0:T(8,128)S(1)} %get-tuple-element.1976) | copy-start | bytes 3133444 | tf_op jit(solution)/shard_map/while
  2287.3 52.8 %copy-start.8 = (f32[2,256,509]{2,1,0:T(8,128)}, f32[2,256,509]{2,1,0:T(8,128)S(1)}, u32[]{:S(2)}) copy-start(f32[2,256,509]{2,1,0:T(8,128)S(1)} %get-tuple-element.1978) | copy-start | bytes 3127300 | tf_op jit(solution)/shard_map/while
  2456.1 25.0 reduce-scatter.9.cloned.1.call-start
  2456.8 108.6 %reduce-scatter.13.cloned.1.call-start = ((), (), s32[]{:S(2)}) async-start(), calls=%async_computation.15 | async-start | bytes 5898240 | tf_op jit(solution)/shard_map/reduce_scatter | solution.py:168
  2461.6 319.1 %reduce-scatter.17.cloned.1.call-start = ((), (), s32[]{:S(2)}) async-start(), calls=%async_computation.17 | async-start | bytes 15728640 | tf_op jit(solution)/shard_map/reduce_scatter | solution.py:168
  2471.1 550.3 %reduce-scatter.11.cloned.1.call-start = ((), (), s32[]{:S(2)}) async-start(), calls=%async_computation.14 | async-start | bytes 17694720 | tf_op jit(solution)/shard_map/reduce_scatter | solution.py:168
  2476.2 4.6 collective-permute-start.1
  2492.0 947.0 %reduce-scatter.15.cloned.1.call-start = ((), (), s32[]{:S(2)}) async-start(), calls=%async_computation.16 | async-start | bytes 31457280 | tf_op jit(solution)/shard_map/reduce_scatter | solution.py:168
  2508.4 1129.0 %all-reduce.258.cloned.1.call-start = ((), (), s32[]{:S(2)}) async-start(), calls=%async_computation.18 | async-start | bytes 28311552 | tf_op jit(solution)/shard_map/psum | solution.py:311
  3449.4 58.0 %copy-start.180 = (f32[256]{0:T(256)S(1)}, f32[256]{0:T(256)}, u32[]{:S(2)}) copy-start(f32[256]{0:T(256)} %copy-done.179) | copy-start | bytes 3076
  3449.4 58.0 %copy-start.83 = (bf16[256,1536]{1,0:T(8,128)(2,1)S(1)}, bf16[256,1536]{1,0:T(8,128)(2,1)}, u32[]{:S(2)}) copy-start(bf16[256,1536]{1,0:T(8,128)(2,1)} %param.16) | copy-start | bytes 2359300
  (1234 other events, 9965.2 us)
Sparse Core Ops, SparseCore 0:
  9.6 246.6 all-gather.6
  267.0 7.9 all-gather.8
  277.2 10.9 all-gather.10
  289.6 90.5 all-gather.12
  381.7 423.6 all-gather.14
  806.8 216.3 all-gather.16
  2456.2 7.2 reduce-scatter.6
  2465.8 10.2 reduce-scatter.8
  2479.0 86.4 reduce-scatter.12
  2568.3 212.3 reduce-scatter.16
  2783.0 238.2 reduce-scatter.10
  3023.6 415.3 reduce-scatter.14
  3443.6 193.8 all-reduce.257
where the time goes:
time: 3670 us; the launch traced here: 3660 us
  waiting for transfers between devices  1400 us (38%)
  other arithmetic  1050 us (29%)
  local copies, waits for them, and re-layouts  900 us (25%)
  matrix products  217 us (6%)
  blocking collectives  44.7 us (1%)
    reduce_scatter x4, waiting for transfers between devices, scatter_rows(): lax.psum_scatter(row_product(left, right).astype(jnp.bfloat16), 'wide', s...  930 us
    slice x448, local copies, waits for them, and re-layouts, shift_keys(): return jnp.pad(slab_in[..., -offset:], ((0, 0), (0, 0), (0, -offset)))  693 us
    all_gather x4, waiting for transfers between devices, project(): lax.all_gather(weight, 'wide', axis=0, tiled=True)  333 us
    select_n x64, other arithmetic, convolve(): masked = jnp.where(inside[None], rows_at, 0.0)  201 us
    reduce_sum x8, other arithmetic, attend_back(): jnp.sum(grad_weights * weights, axis=-1, keepdims=True)  182 us
    reduce_sum x32, other arithmetic, convolve(): summed = summed + kernel[:, tap_q, tap_k][:, None, None] * shifted  177 us
    reduce_max x8, other arithmetic, attend(): highest = jnp.max(logits, axis=-1, keepdims=True)  169 us
    mul x80, other arithmetic, convolve(): summed = summed + kernel[:, tap_q, tap_k][:, None, None] * shifted  163 us
  transfers between devices with their start and end apart: 15, of which 8 were waited for; matrix products, arithmetic and copies ran while one was open for 20% of the time, Pallas kernels for 0%

commit v1 on v0

v1 whole, which is shorter than its diff:
```python
import functools
import jax
import jax.numpy as jnp
from jax import lax
from jax.experimental import pallas as pl
from jax.experimental.pallas import tpu as pltpu

LANES = 128
EDGE = 64
TOP = 16


def tap_bands(kernel, scaling):
    heads, taps_q, taps_k = kernel.shape
    half = (taps_k - 1) // 2
    row = jnp.arange(2 * LANES)[:, None]
    col = jnp.arange(LANES)[None, :]
    forth = col - row + EDGE + half
    back = row - col - EDGE + half
    spread = jnp.zeros((heads, 2 * LANES, taps_q, LANES), jnp.float32)
    spread_back = jnp.zeros((heads, taps_q, 2 * LANES, LANES), jnp.float32)
    for tap in range(taps_k):
        spread = spread + jnp.where((forth == tap)[None, :, None, :], kernel[:, None, :, tap, None], 0.0)
        spread_back = spread_back + jnp.where(
            (back == tap)[None, None, :, :], kernel[:, :, tap, None, None], 0.0
        )
    spread = spread.reshape(heads, 2 * LANES, taps_q * LANES) * scaling
    high = spread.astype(jnp.bfloat16)
    low = (spread - high.astype(jnp.float32)).astype(jnp.bfloat16)
    forward = jnp.concatenate([high, high, low], 1)
    backward = spread_back.reshape(heads, taps_q * 2 * LANES, LANES).astype(jnp.bfloat16)
    return forward, backward


def masked_scores(q_blk, keys, since, first_row):
    scores = lax.dot_general(q_blk, keys, (((1,), (1,)), ((), ())), preferred_element_type=jnp.float32)
    rows = first_row + lax.broadcasted_iota(jnp.int32, scores.shape, 0)
    back = rows + EDGE - lax.broadcasted_iota(jnp.int32, scores.shape, 1)
    limit = jnp.concatenate([since] * (scores.shape[1] // LANES), 1)
    return jnp.where((back >= 0) & (back <= limit), scores, 0.0)


def forward_kernel(
    taps_q, head_size, mix_ref, proj_ref, since_ref, taps_ref, gain_ref,
    att_ref, grouped_ref, weights_ref, keys_pad, s_high, s_low, spread,
):
    seq_len = proj_ref.shape[0]
    blocks = seq_len // LANES
    keys_pad[...] = jnp.zeros_like(keys_pad)
    s_high[...] = jnp.zeros_like(s_high)
    s_low[...] = jnp.zeros_like(s_low)

    def one_head(head, carry):
        lane = pl.multiple_of(head * LANES, LANES)
        lane_k = pl.multiple_of((head + 2) * LANES, LANES)
        keys_pad[EDGE : EDGE + seq_len, :] = proj_ref[:, pl.ds(lane_k, LANES)]
        for qi in range(blocks):
            first = qi * LANES
            width = (qi + 2) * LANES
            scores = masked_scores(
                proj_ref[first : first + LANES, pl.ds(lane, LANES)],
                keys_pad[:width, :],
                since_ref[first : first + LANES, :],
                first,
            )
            high = scores.astype(jnp.bfloat16)
            s_high[TOP + first : TOP + first + LANES, :width] = high
            s_low[TOP + first : TOP + first + LANES, :width] = (scores - high.astype(jnp.float32)).astype(jnp.bfloat16)
        for m in range(blocks):
            first = m * LANES
            count = seq_len - first
            high = s_high[first:, first : first + 2 * LANES]
            left = jnp.concatenate([high, s_low[first:, first : first + 2 * LANES], high], 1)
            spread[first:, :] = jnp.dot(left, taps_ref[head], preferred_element_type=jnp.float32)
            since = since_ref[first:, :]
            logits = spread[TOP + first :, :LANES]
            for tap in range(1, taps_q):
                moved = spread[TOP + first - tap : TOP + seq_len - tap, tap * LANES : (tap + 1) * LANES]
                logits = logits + jnp.where(since >= tap, moved, 0.0)
            weights_ref[head, first:, first : first + LANES] = logits
        for qi in range(blocks):
            first = qi * LANES
            width = (qi + 1) * LANES
            logits = weights_ref[head, first : first + LANES, :width]
            rows = first + lax.broadcasted_iota(jnp.int32, logits.shape, 0)
            back = rows - lax.broadcasted_iota(jnp.int32, logits.shape, 1)
            limit = jnp.concatenate([since_ref[first : first + LANES, :]] * (qi + 1), 1)
            logits = jnp.where((back >= 0) & (back <= limit), logits, -1e30)
            raised = jnp.exp(logits - jnp.max(logits, axis=1, keepdims=True))
            weights_ref[head, first : first + LANES, :width] = raised / jnp.sum(raised, axis=1, keepdims=True)
        return carry

    lax.fori_loop(0, 2, one_head, 0)
    real = lax.broadcasted_iota(jnp.int32, (LANES, LANES), 1) < head_size
    for qi in range(blocks):
        first = qi * LANES
        width = (qi + 1) * LANES
        low = weights_ref[0, first : first + LANES, :width]
        upp = weights_ref[1, first : first + LANES, :width]
        for head in range(2):
            mixed = (mix_ref[head, 0] * low + mix_ref[head, 1] * upp).astype(jnp.bfloat16)
            cols = slice(head * LANES, (head + 1) * LANES)
            att = jnp.dot(
                mixed, proj_ref[:width, (4 + head) * LANES : (5 + head) * LANES], preferred_element_type=jnp.float32
            )
            att_ref[first : first + LANES, cols] = att
            normal, _ = normalize(att, real, head_size)
            grouped_ref[first : first + LANES, cols] = (normal * gain_ref[:, cols]).astype(jnp.bfloat16)


def normalize(att, real, head_size):
    mean = jnp.sum(att, axis=1, keepdims=True) * (1.0 / head_size)
    centered = jnp.where(real, att - mean, 0.0)
    spread = jnp.sum(centered * centered, axis=1, keepdims=True) * (1.0 / head_size)
    scale = lax.rsqrt(spread + 1e-05)
    return centered * scale, scale


def attend_row(proj, since, mix, taps_forward, gain_pad, taps_q, head_size):
    seq_len = proj.shape[0]
    full = seq_len + 2 * EDGE
    return pl.pallas_call(
        functools.partial(forward_kernel, taps_q, head_size),
        out_shape=(
            jax.ShapeDtypeStruct((seq_len, 2 * LANES), jnp.float32),
            jax.ShapeDtypeStruct((seq_len, 2 * LANES), jnp.bfloat16),
            jax.ShapeDtypeStruct((2, seq_len, seq_len), jnp.float32),
        ),
        in_specs=[pl.BlockSpec(memory_space=pltpu.SMEM)] + [pl.BlockSpec(memory_space=pltpu.VMEM)] * 4,
        out_specs=(pl.BlockSpec(memory_space=pltpu.VMEM),) * 3,
        scratch_shapes=[
            pltpu.VMEM((full, LANES), jnp.bfloat16),
            pltpu.VMEM((TOP + seq_len, full), jnp.bfloat16),
            pltpu.VMEM((TOP + seq_len, full), jnp.bfloat16),
            pltpu.VMEM((TOP + seq_len, taps_q * LANES), jnp.float32),
        ],
        compiler_params=pltpu.CompilerParams(vmem_limit_bytes=40 * 1024 * 1024),
        cost_estimate=pl.CostEstimate(flops=10_000_000_000, bytes_accessed=8_000_000, transcendentals=600_000),
        name="attend_row",
    )(mix, proj, since, taps_forward, gain_pad)


def backward_kernel(
    taps_q, taps_k, head_size, scaling, mix_ref, proj_ref, since_ref, taps_ref, gain_ref, att_ref, weights_ref, grad_ref,
    out_ref, small_ref, tap_ref,
    keys_pad, grad_att, conv_grad, shifted, s_low, s_grad, since_pad,
):
    seq_len = proj_ref.shape[0]
    blocks = seq_len // LANES
    half = (taps_k - 1) // 2
    full = seq_len + 2 * EDGE
    keys_pad[...] = jnp.zeros_like(keys_pad)
    s_low[...] = jnp.zeros_like(s_low)
    s_grad[...] = jnp.zeros_like(s_grad)
    shifted[...] = jnp.zeros_like(shifted)
    conv_grad[...] = jnp.zeros_like(conv_grad)
    since_pad[:seq_len, :] = since_ref[...]
    since_pad[seq_len:, :] = jnp.zeros((8, LANES), jnp.int32)
    small_ref[...] = jnp.zeros_like(small_ref)

    real = lax.broadcasted_iota(jnp.int32, (LANES, LANES), 1) < head_size
    for head in range(2):
        cols = slice(head * LANES, (head + 1) * LANES)
        group_sum = jnp.zeros((1, LANES), jnp.float32)
        for qi in range(blocks):
            rows = slice(qi * LANES, (qi + 1) * LANES)
            normal, scale = normalize(att_ref[rows, cols], real, head_size)
            grad = grad_ref[rows, cols]
            group_sum = group_sum + jnp.sum(grad * normal, axis=0, keepdims=True)
            lift = grad * gain_ref[:, cols]
            mean = jnp.sum(lift, axis=1, keepdims=True) * (1.0 / head_size)
            along = jnp.sum(lift * normal, axis=1, keepdims=True) * (1.0 / head_size)
            grad_att[rows, cols] = jnp.where(real, scale * (lift - mean - normal * along), 0.0).astype(jnp.bfloat16)
        small_ref[head : head + 1, :] = group_sum

    sums = [[jnp.zeros((1, LANES), jnp.float32) for _ in range(2)] for _ in range(2)]
    grad_v = [[], []]
    for qi in range(blocks):
        first = qi * LANES
        width = (qi + 1) * LANES
        rows = slice(first, first + LANES)
        maps = [weights_ref[k, rows, :width] for k in range(2)]
        grad_mixed = []
        for head in range(2):
            cols = slice(head * LANES, (head + 1) * LANES)
            values = proj_ref[:width, (4 + head) * LANES : (5 + head) * LANES]
            gm = lax.dot_general(
                grad_att[rows, cols], values, (((1,), (1,)), ((), ())), preferred_element_type=jnp.float32
            )
            grad_mixed.append(gm)
        for head in range(2):
            for k in range(2):
                part = jnp.sum(grad_mixed[head] * maps[k], axis=0, keepdims=True)
                for b in range(qi + 1):
                    sums[head][k] = sums[head][k] + part[:, b * LANES : (b + 1) * LANES]
        for k in range(2):
            grad_w = mix_ref[0, k] * grad_mixed[0] + mix_ref[1, k] * grad_mixed[1]
            inner = jnp.sum(grad_w * maps[k], axis=1, keepdims=True)
            conv_grad[k, rows, :width] = maps[k] * (grad_w - inner)
    for head in range(2):
        for k in range(2):
            small_ref[2 + 2 * head + k : 3 + 2 * head + k, :] = sums[head][k]
        cols = slice(head * LANES, (head + 1) * LANES)
        for kb in range(blocks):
            first = kb * LANES
            mixed = (
                mix_ref[head, 0] * weights_ref[0, first:, first : first + LANES]
                + mix_ref[head, 1] * weights_ref[1, first:, first : first + LANES]
            ).astype(jnp.bfloat16)
            out_ref[first : first + LANES, (4 + head) * LANES : (5 + head) * LANES] = lax.dot_general(
                mixed, grad_att[first:, cols], (((0,), (0,)), ((), ())), preferred_element_type=jnp.float32
            ).astype(jnp.bfloat16)

    def one_head(head, carry):
        lane = pl.multiple_of(head * LANES, LANES)
        lane_k = pl.multiple_of((head + 2) * LANES, LANES)
        keys_pad[EDGE : EDGE + seq_len, :] = proj_ref[:, pl.ds(lane_k, LANES)]
        for qi in range(blocks):
            first = qi * LANES
            width = (qi + 2) * LANES
            scores = masked_scores(
                proj_ref[first : first + LANES, pl.ds(lane, LANES)],
                keys_pad[:width, :],
                since_ref[first : first + LANES, :],
                first,
            )
            s_low[TOP + first : TOP + first + LANES, :width] = scores.astype(jnp.bfloat16)
            reach = min(width, seq_len)
            for tap in range(taps_q):
                moved = conv_grad[head, first + tap : first + tap + LANES, :reach]
                if tap > 0:
                    limit = since_pad[first + tap : first + tap + LANES, :]
                    limit = jnp.concatenate([limit] * (reach // LANES), 1)
                    moved = jnp.where(limit >= tap, moved, 0.0)
                shifted[tap, TOP + first : TOP + first + LANES, LANES : LANES + reach] = moved.astype(jnp.bfloat16)
        for m in range(blocks + 1):
            first = max(m - 1, 0) * LANES
            left = jnp.concatenate(
                [shifted[tap, TOP + first :, m * LANES : (m + 2) * LANES] for tap in range(taps_q)], 1
            )
            grad = jnp.dot(left, taps_ref[head], preferred_element_type=jnp.float32)
            rows = first + lax.broadcasted_iota(jnp.int32, grad.shape, 0)
            back = rows + EDGE - m * LANES - lax.broadcasted_iota(jnp.int32, grad.shape, 1)
            keep = (back >= 0) & (back <= since_ref[first:, :])
            s_grad[first:, m * LANES : (m + 1) * LANES] = jnp.where(keep, grad, 0.0).astype(jnp.bfloat16)
        total = jnp.zeros((2 * LANES, taps_q * LANES), jnp.float32)
        for m in range(blocks):
            first = m * LANES
            right = jnp.concatenate(
                [shifted[tap, first:, (m + 1) * LANES : (m + 2) * LANES] for tap in range(taps_q)], 1
            )
            total = total + lax.dot_general(
                s_low[first:, first : first + 2 * LANES], right, (((0,), (0,)), ((), ())),
                preferred_element_type=jnp.float32,
            )
        ridge = lax.broadcasted_iota(jnp.int32, (2 * LANES, LANES), 1) - lax.broadcasted_iota(
            jnp.int32, (2 * LANES, LANES), 0
        )
        for tap_k in range(taps_k):
            on = ridge == tap_k - EDGE - half
            for tap in range(taps_q):
                line = jnp.where(on, total[:, tap * LANES : (tap + 1) * LANES], 0.0)
                tap_ref[head, tap * taps_k + tap_k : tap * taps_k + tap_k + 1, :] = jnp.sum(line, axis=0, keepdims=True)
        for qi in range(blocks):
            first = qi * LANES
            width = (qi + 2) * LANES
            grad_q = jnp.dot(
                s_grad[first : first + LANES, :width], keys_pad[:width, :], preferred_element_type=jnp.float32
            )
            out_ref[first : first + LANES, pl.ds(lane, LANES)] = (grad_q * scaling).astype(jnp.bfloat16)
        for kb in range(blocks):
            first = kb * LANES
            grad_k = lax.dot_general(
                s_grad[first:, first + EDGE : first + EDGE + LANES],
                proj_ref[first:, pl.ds(lane, LANES)],
                (((0,), (0,)), ((), ())),
                preferred_element_type=jnp.float32,
            )
            out_ref[first : first + LANES, pl.ds(lane_k, LANES)] = (grad_k * scaling).astype(jnp.bfloat16)
        return carry

    lax.fori_loop(0, 2, one_head, 0)


def attend_row_back(proj, since, mix, taps_backward, gain_pad, att, weights, grad_grouped, taps_q, taps_k, head_size):
    seq_len = proj.shape[0]
    full = seq_len + 2 * EDGE
    return pl.pallas_call(
        functools.partial(backward_kernel, taps_q, taps_k, head_size, head_size ** (-0.5)),
        out_shape=(
            jax.ShapeDtypeStruct((seq_len, 6 * LANES), jnp.bfloat16),
            jax.ShapeDtypeStruct((8, LANES), jnp.float32),
            jax.ShapeDtypeStruct((2, taps_q * taps_k, LANES), jnp.float32),
        ),
        in_specs=[pl.BlockSpec(memory_space=pltpu.SMEM)] + [pl.BlockSpec(memory_space=pltpu.VMEM)] * 7,
        out_specs=(pl.BlockSpec(memory_space=pltpu.VMEM),) * 3,
        scratch_shapes=[
            pltpu.VMEM((full, LANES), jnp.bfloat16),
            pltpu.VMEM((seq_len, 2 * LANES), jnp.bfloat16),
            pltpu.VMEM((2, seq_len + 8, seq_len), jnp.float32),
            pltpu.VMEM((taps_q, TOP + seq_len, seq_len + 2 * LANES), jnp.bfloat16),
            pltpu.VMEM((TOP + seq_len, full), jnp.bfloat16),
            pltpu.VMEM((seq_len, full), jnp.bfloat16),
            pltpu.VMEM((seq_len + 8, LANES), jnp.int32),
        ],
        compiler_params=pltpu.CompilerParams(vmem_limit_bytes=48 * 1024 * 1024),
        cost_estimate=pl.CostEstimate(flops=15_000_000_000, bytes_accessed=8_000_000, transcendentals=0),
        name="attend_row_back",
    )(mix, proj, since, taps_backward, gain_pad, att, weights, grad_grouped)


from jax.sharding import PartitionSpec as P

PLANE = ("narrow", "seq")
SWAP = [(0, 1), (1, 0)]


def seq_swap(array):
    return lax.ppermute(array, "seq", SWAP)


def x_swap(array):
    return lax.ppermute(array, "narrow", [(0, 1), (1, 0), (2, 3), (3, 2)])


def y_swap(array):
    return lax.ppermute(array, "narrow", [(0, 2), (2, 0), (1, 3), (3, 1)])


def joint_move(array, pairs):
    wide = lax.axis_size("wide")
    return lax.ppermute(array, ("narrow", "wide"), [(a * wide + b, c * wide + d) for (a, b), (c, d) in pairs])


def ordered(own, other):
    first = lax.axis_index("seq") == 0
    return jnp.concatenate([jnp.where(first, own, other), jnp.where(first, other, own)], 0)


def gather_plane(own):
    half = own.shape[0] // 2
    from_x = x_swap(own)
    from_y = y_swap(own)
    own_pair = ordered(own, seq_swap(own))
    corner = jnp.concatenate([y_swap(from_x[:half]), x_swap(from_y[half:])], 0)
    x_pair = ordered(from_x, seq_swap(from_x))
    y_pair = ordered(from_y, seq_swap(from_y))
    return [own_pair, x_pair, y_pair, ordered(corner, seq_swap(corner))]


def scatter_plane(parts):
    count = parts[0].shape[0] // 2
    core = lax.axis_index("seq")

    def pair(part):
        mine = lax.dynamic_slice_in_dim(part, core * count, count, 0)
        theirs = lax.dynamic_slice_in_dim(part, (1 - core) * count, count, 0)
        return mine.astype(jnp.float32) + seq_swap(theirs.astype(jnp.bfloat16)).astype(jnp.float32)

    cut = count // 2
    corner = pair(parts[3])
    to_y = x_swap(corner[:cut].astype(jnp.bfloat16)).astype(jnp.float32)
    to_x = y_swap(corner[cut:].astype(jnp.bfloat16)).astype(jnp.float32)
    at_x = pair(parts[1])
    at_y = pair(parts[2])
    at_x = jnp.concatenate([at_x[:cut], at_x[cut:] + to_x], 0).astype(jnp.bfloat16)
    at_y = jnp.concatenate([at_y[:cut] + to_y, at_y[cut:]], 0).astype(jnp.bfloat16)
    return pair(parts[0]) + x_swap(at_x).astype(jnp.float32) + y_swap(at_y).astype(jnp.float32)


def ring_next(array):
    count = lax.axis_size("wide")
    return lax.ppermute(array, "wide", [(i, (i + 1) % count) for i in range(count)])


def gather_wide(piece, shape_piece=lambda a: a):
    count = lax.axis_size("wide")
    place = lax.axis_index("wide")
    if count > 4:
        return shape_piece(lax.all_gather(piece, "wide", axis=0, tiled=True))
    rows = piece.shape[0]
    current = piece
    whole = None
    for step in range(count):
        shaped = shape_piece(current)
        if whole is None:
            whole = jnp.zeros((count * rows,) + shaped.shape[1:], shaped.dtype)
        whole = lax.dynamic_update_slice_in_dim(whole, shaped, ((place - step) % count) * rows, 0)
        if step < count - 1:
            current = ring_next(current)
    return whole


def scatter_wide(whole):
    count = lax.axis_size("wide")
    place = lax.axis_index("wide")
    if count > 4:
        return lax.psum_scatter(whole.astype(jnp.bfloat16), "wide", scatter_dimension=0, tiled=True).astype(jnp.float32)
    rows = whole.shape[0] // count

    def block(step):
        return lax.dynamic_slice_in_dim(whole, ((place - step) % count) * rows, rows, 0)

    total = block(1)
    for step in range(2, count + 1):
        total = ring_next(total.astype(jnp.bfloat16)).astype(jnp.float32) + block(step)
    return total


def gather_out(out_weight, group_rows):
    wide = lax.axis_size("wide")
    core = lax.axis_index("seq")
    line = lax.axis_index("narrow")
    place = lax.axis_index("wide")
    if wide != 4:
        whole = lax.all_gather(out_weight, "wide", axis=0, tiled=True)
        return lax.dynamic_slice_in_dim(whole, (2 * line + core) * group_rows, group_rows, 0)
    held = lax.dynamic_slice_in_dim(out_weight, core * group_rows, group_rows, 0)
    came = joint_move(held, [((n, n), (n, n ^ 2)) for n in range(4)])
    held = jnp.where(place == line, held, came)
    came = joint_move(held, [((n, n ^ k), (n, n ^ k ^ 1)) for n in range(4) for k in (0, 2)])
    return jnp.where((place ^ line) & 1 == 0, held, came)


def scatter_out(term):
    wide = lax.axis_size("wide")
    place = lax.axis_index("wide")
    line = lax.axis_index("narrow")
    if wide != 4:
        whole = lax.all_gather(term.astype(jnp.bfloat16), PLANE, axis=0, tiled=True)
        return lax.psum_scatter(whole, "wide", scatter_dimension=0, tiled=True).astype(jnp.float32)
    low = term.astype(jnp.bfloat16)
    came = joint_move(low, [((n, n ^ k ^ 1), (n, n ^ k)) for n in range(4) for k in (0, 2)])
    term = term + came.astype(jnp.float32)
    came = joint_move(term.astype(jnp.bfloat16), [((n, n ^ 2), (n, n)) for n in range(4)])
    held = (term + came.astype(jnp.float32)).astype(jnp.bfloat16)
    came = joint_move(held, [((z, z), (z ^ 1, z)) for z in range(4)])
    held = jnp.where(place == line, held, came)
    came = joint_move(held, [((z ^ k, z), (z ^ k ^ 2, z)) for z in range(4) for k in (0, 1)])
    held = jnp.where((place ^ line) & 2 == 0, held, came)
    return ordered(held, seq_swap(held)).astype(jnp.float32)


def pad_heads(array, head_size):
    heads = array.shape[1] // head_size
    split = array.reshape(array.shape[0], heads, head_size)
    return jnp.pad(split, ((0, 0), (0, 0), (0, LANES - head_size))).reshape(array.shape[0], heads * LANES)


def unpad_heads(array, head_size):
    heads = array.shape[1] // LANES
    return array.reshape(array.shape[0], heads, LANES)[:, :, :head_size].reshape(array.shape[0], heads * head_size)


def times(left, right):
    return jnp.dot(left, right, preferred_element_type=jnp.float32)


def times_back(left, right):
    return lax.dot_general(left, right, (((1,), (1,)), ((), ())), preferred_element_type=jnp.float32)


def row_product(left, right):
    return lax.dot_general(left, right, (((0,), (0,)), ((), ())), preferred_element_type=jnp.float32)


def norm_scale(values):
    return lax.rsqrt(jnp.mean(values * values, axis=-1, keepdims=True) + 1e-06)


def norm_back(values, scale, gain, grad):
    lift = grad * gain
    along = jnp.mean(lift * values, axis=-1, keepdims=True)
    return scale * lift - values * (scale * scale * scale * along), jnp.sum(grad * values * scale, axis=0)


def on_device(
    inputs,
    doc_start,
    norm_gain,
    qkv_weight,
    logit_kernel,
    head_mix,
    group_gain,
    out_weight,
    feed_gain,
    gate_up,
    down_weight,
    cotangent,
):
    tokens_dev, width = inputs.shape
    head_count, taps_q, taps_k = logit_kernel.shape
    head_size = width // head_count
    group_cols = 2 * head_size
    cores = lax.axis_size(PLANE)
    wide = lax.axis_size("wide")
    line = lax.axis_index("narrow")
    part = lax.axis_index(PLANE)
    hidden_size = gate_up.shape[1] // 2
    chunk = hidden_size // (wide * cores)
    scaling = head_size ** (-0.5)

    first_pos = lax.axis_index(("narrow", "wide", "seq")) * tokens_dev
    since_own = first_pos + jnp.arange(tokens_dev, dtype=jnp.int32) - doc_start
    since_all = lax.all_gather(since_own, PLANE, axis=0, tiled=True).reshape(cores // 2, 2 * tokens_dev)

    inputs_f = inputs.astype(jnp.float32)
    scale_in = norm_scale(inputs_f)
    normed = (inputs_f * scale_in * norm_gain).astype(jnp.bfloat16)
    normed_rows = gather_plane(normed)

    qkv_piece = lax.dynamic_index_in_dim(
        qkv_weight.reshape(qkv_weight.shape[0], 3, cores, group_cols), part, 2, keepdims=False
    ).reshape(qkv_weight.shape[0], 3 * group_cols)
    qkv_own = gather_wide(qkv_piece, lambda a: pad_heads(a, head_size))
    out_own = gather_out(out_weight, group_cols)
    out_own = jnp.pad(
        out_own.reshape(2, head_size, width), ((0, 0), (0, LANES - head_size), (0, 0))
    ).reshape(2 * LANES, width)
    gate_piece = lax.dynamic_index_in_dim(
        gate_up.reshape(gate_up.shape[0], 2, wide, cores, chunk), part, 3, keepdims=False
    ).reshape(gate_up.shape[0], 2 * wide * chunk)
    gate_own = gather_wide(gate_piece)
    down_own = gather_wide(lax.dynamic_slice_in_dim(down_weight, part * chunk, chunk, 0))
    cotangent_rows = gather_plane(cotangent)

    kernels = lax.dynamic_slice_in_dim(logit_kernel, 2 * part, 2, 0)
    mix = lax.dynamic_slice_in_dim(head_mix, 2 * part, 2, 0)
    taps_forward, taps_backward = tap_bands(kernels, scaling)
    gain_pad = pad_heads(lax.dynamic_slice_in_dim(group_gain, part * group_cols, group_cols, 0)[None], head_size)

    rows = []
    branch_parts = []
    for k in range(4):
        since = jnp.broadcast_to(
            lax.dynamic_index_in_dim(since_all, line ^ k, 0, keepdims=False)[:, None], (2 * tokens_dev, LANES)
        )
        projected = times(normed_rows[k], qkv_own).astype(jnp.bfloat16)
        attended, grouped, weights = attend_row(projected, since, mix, taps_forward, gain_pad, taps_q, head_size)
        branch_parts.append(times(grouped, out_own))
        rows.append((projected, since, attended, grouped, weights))
    residual = inputs_f + scatter_plane(branch_parts)
    scale_mid = norm_scale(residual)
    normed_ffn = (residual * scale_mid * feed_gain).astype(jnp.bfloat16)
    ffn_rows = gather_plane(normed_ffn)

    gate_cols = wide * chunk
    gate_w, up_w = gate_own[:, :gate_cols], gate_own[:, gate_cols:]
    hidden_rows, gate_grad_rows, up_grad_rows, back_parts, ffn_parts = [], [], [], [], []
    for k in range(4):
        gating = times(ffn_rows[k], gate_w)
        upward = times(ffn_rows[k], up_w)
        grad_hidden = times_back(cotangent_rows[k], down_own)
        sig = 1.0 / (1.0 + jnp.exp(-gating))
        hidden = (gating * sig * upward).astype(jnp.bfloat16)
        grad_gate = (grad_hidden * upward * sig * (1.0 + gating * (1.0 - sig))).astype(jnp.bfloat16)
        grad_up = (grad_hidden * gating * sig).astype(jnp.bfloat16)
        back_parts.append(times_back(grad_gate, gate_w) + times_back(grad_up, up_w))
        ffn_parts.append(times(hidden, down_own))
        hidden_rows.append(hidden)
        gate_grad_rows.append(grad_gate)
        up_grad_rows.append(grad_up)
    grad_ffn = scatter_plane(back_parts)
    norm_part, grad_feed = norm_back(residual, scale_mid, feed_gain, grad_ffn)
    grad_residual = norm_part + cotangent.astype(jnp.float32)
    grad_branch = grad_residual.astype(jnp.bfloat16)
    branch_rows = gather_plane(grad_branch)

    block_out = (residual + scatter_plane(ffn_parts)).astype(jnp.bfloat16)

    ffn_all = jnp.concatenate(ffn_rows, 0)
    grad_gate_own = jnp.concatenate(
        [row_product(ffn_all, jnp.concatenate(gate_grad_rows, 0)), row_product(ffn_all, jnp.concatenate(up_grad_rows, 0))],
        1,
    )
    shard_gate = scatter_wide(grad_gate_own).astype(jnp.bfloat16)
    grad_down_own = row_product(jnp.concatenate(hidden_rows, 0), jnp.concatenate(cotangent_rows, 0))
    shard_down = scatter_wide(grad_down_own).astype(jnp.bfloat16)

    grad_proj_rows, normed_parts, smalls, tap_sums = [], [], [], []
    for k in range(4):
        projected, since, attended, grouped, weights = rows[k]
        grad_grouped = times_back(branch_rows[k], out_own)
        grad_proj, small, tap_sum = attend_row_back(
            projected, since, mix, taps_backward, gain_pad, attended, weights, grad_grouped, taps_q, taps_k, head_size
        )
        normed_parts.append(times_back(grad_proj, qkv_own))
        grad_proj_rows.append(grad_proj)
        smalls.append(small)
        tap_sums.append(tap_sum)
    grad_qkv_own = row_product(jnp.concatenate(normed_rows, 0), jnp.concatenate(grad_proj_rows, 0))
    shard_qkv = scatter_wide(unpad_heads(grad_qkv_own, head_size)).astype(jnp.bfloat16)
    grad_out_own = row_product(jnp.concatenate([r[3] for r in rows], 0), jnp.concatenate(branch_rows, 0))
    grad_out = scatter_out(
        grad_out_own.reshape(2, LANES, width)[:, :head_size].reshape(2 * head_size, width)
    )
    grad_normed = scatter_plane(normed_parts)
    norm_part, grad_norm = norm_back(inputs_f, scale_in, norm_gain, grad_normed)
    grad_input = norm_part + grad_residual

    small = smalls[0] + smalls[1] + smalls[2] + smalls[3]
    taps = jnp.sum(tap_sums[0] + tap_sums[1] + tap_sums[2] + tap_sums[3], axis=2) * scaling

    def placed(array, total):
        array = array.reshape(-1)
        return lax.dynamic_update_slice(jnp.zeros((total,), jnp.float32), array, (part * array.shape[0],))

    grad_norm, grad_feed, grad_group, grad_kernel, grad_mix = lax.psum(
        (
            grad_norm,
            grad_feed,
            placed(small[:2, :head_size], width),
            placed(taps, head_count * taps_q * taps_k),
            placed(jnp.sum(small[2:6], axis=1), 2 * head_count),
        ),
        ("narrow", "wide", "seq"),
    )

    def columns(shard, sections):
        rows_here = shard.shape[0]
        every = lax.all_gather(shard, PLANE, axis=0).reshape(cores, rows_here, sections, -1)
        return jnp.moveaxis(every, 0, 2).reshape(rows_here, -1).astype(jnp.float32)

    grad_qkv = columns(shard_qkv, 3)
    grad_gate = columns(shard_gate, 2 * wide)
    grad_down = lax.all_gather(shard_down, PLANE, axis=0, tiled=True).astype(jnp.float32)
    return (
        block_out,
        grad_input,
        grad_norm,
        grad_qkv,
        grad_kernel.reshape(head_count, taps_q, taps_k),
        grad_mix.reshape(head_count, 2),
        grad_group,
        grad_out,
        grad_feed,
        grad_gate,
        grad_down,
    )


def solution(mesh):
    tokens = P(("narrow", "wide", "seq"), None)
    rows = P("wide", None)
    return jax.shard_map(
        on_device,
        mesh=mesh,
        in_specs=(tokens, P(("narrow", "wide", "seq")), P(), rows, P(), P(), P(), rows, P(), rows, rows, tokens),
        out_specs=(tokens, tokens, P(), rows, P(), P(), P(), rows, P(), rows, rows),
        check_vma=False,
    )
```

time: 3670 us -> 871 us (0.24)
  waiting for transfers between devices: 1400 us -> 253 us
  other arithmetic: 1050 us -> 118 us
  local copies, waits for them, and re-layouts: 900 us -> 168 us
  matrix products: 217 us -> 107 us
  starting transfers between devices: 4.11 us -> 73.6 us
  Pallas kernels: 0 us -> 65.2 us
    reduce_scatter x6 -> x0, waiting for transfers between devices: 930 us -> none  [the longest x4 930 us: scatter_rows(): lax.psum_scatter(row_product(left, right).astype(jnp.bfloat16), 'wide', s...]
    slice x502 -> x35, local copies, waits for them, and re-layouts: 763 us -> 4.2 us  [the longest x8 2.2 us: gather_plane(): corner = jnp.concatenate([y_swap(from_x[:half]), x_swap(from_y[half:])], 0)]
    reduce_sum x61 -> x6, other arithmetic: 366 us -> 10.4 us  [the longest x2 7.09 us: norm_back(): jnp.sum(grad * values * scale, axis=0)]
    all_gather x6 -> x3, waiting for transfers between devices: 343 us -> 0.01 us  [the longest x2 0.01 us: columns(): lax.all_gather(shard, PLANE, axis=0).reshape(cores, rows_here, sections, -1)]
    ppermute x2 -> x89, waiting for transfers between devices: 0.01 us -> 253 us  [the longest x18 102 us: ring_next(): lax.ppermute(array, 'wide', [(i, (i + 1) % count) for i in range(count)])]
    mul x89 -> x3, other arithmetic: 205 us -> 0.02 us  [the longest x2 0.02 us: norm_back(): scale * scale * scale * along]
    select_n x64 -> x5, other arithmetic: 201 us -> 4.42 us  [the longest x1 1.96 us: scatter_out(): held = jnp.where((place ^ line) & 2 == 0, held, came)]
    reduce_max x8 -> x0, other arithmetic: 169 us -> none  [attend(): highest = jnp.max(logits, axis=-1, keepdims=True)]
  transfers between devices with their start and end apart: 15 -> 92, of which waited for: 8 -> 30; matrix products, arithmetic and copies ran while one was open for 20% -> 37% of each run, Pallas kernels for 0% -> 8%
where the time goes in v1:
time: 871 us; the launch traced here: 856 us
  waiting for transfers between devices  253 us (29%)
  local copies, waits for them, and re-layouts  168 us (19%)
  other arithmetic  118 us (14%)
  matrix products  107 us (12%)
  starting transfers between devices  73.6 us (8%)
  Pallas kernels  65.2 us (7%)
  blocking collectives  53 us (6%)
  between operations  17.7 us (2%)
    ppermute x18, waiting for transfers between devices, ring_next(): lax.ppermute(array, 'wide', [(i, (i + 1) % count) for i in range(count)])  102 us
    unnamed x387, local copies, waits for them, and re-layouts  92.9 us
    ppermute x16, waiting for transfers between devices, y_swap(): return lax.ppermute(array, 'narrow', [(0, 2), (2, 0), (1, 3), (3, 1)])  56.8 us
    ppermute x16, waiting for transfers between devices, x_swap(): return lax.ppermute(array, 'narrow', [(0, 1), (1, 0), (2, 3), (3, 2)])  54.9 us
    psum x1, blocking collectives, on_device(): lax.psum((grad_norm, grad_feed, placed(small[:2, :head_size], width), pla...  45.1 us
    dot_general x20, matrix products, times(): return jnp.dot(left, right, preferred_element_type=jnp.float32)  42 us
    dot_general x20, matrix products, times_back(): lax.dot_general(left, right, (((1,), (1,)), ((), ())), preferred_element_...  41.8 us
    pallas_call x4, Pallas kernels, attend_row_back(): pl.pallas_call(functools.partial(backward_kernel, taps_q, taps_k, head_si...  40.3 us
  transfers between devices with their start and end apart: 92, of which 30 were waited for; matrix products, arithmetic and copies ran while one was open for 37% of the time, Pallas kernels for 8%

profile of v1, /device:TPU:0, one launch (start us, length us, event | category | flops | bytes accessed | tf_op | source)
XLA Modules:
  0.0 856.0 jit_solution(17260278763768578352)
XLA Ops:
  14.4 4.4 copy.119
  23.1 5.3 collective-permute-start.4
  61.5 8.7 %copy.142 = bf16[384,8192]{0,1:T(8,128)(2,1)} copy(bf16[384,8192]{1,0:T(8,128)(2,1)} %param.21) | data formatting | bytes 12582912 | tf_op args[9]
  80.9 7.9 all-gather.2
  116.2 10.9 %collective-permute-done.11 = bf16[256,1536]{1,0:T(8,128)(2,1)S(1)} collective-permute-done((bf16[256,1536]{1,0:T(8,128)(2,1)}, bf16[256,1536]{1,0:T(8,128)(2,1)S(1)}, u32[]{:S(2)}, u32[]{:S(2)}) %collective-permute-start.11) | collective-permute-done | bytes 786464 | tf_op jit(solution)/shard_map/ppermute | solution.py:327
  129.4 13.9 %collective-permute-done.49 = bf16[256,1536]{1,0:T(8,128)(2,1)S(1)} collective-permute-done((bf16[256,1536]{1,0:T(8,128)(2,1)S(1)}, bf16[256,1536]{1,0:T(8,128)(2,1)S(1)}, u32[]{:S(2)}, u32[]{:S(2)}) %collective-permute-start.49) | collective-permute-done | bytes 786464 | tf_op jit(solution)/shard_map/ppermute | solution.py:327
  143.3 4.0 collective-permute-start.5
  161.7 4.5 collective-permute-done.48
  166.3 3.6 collective-permute-done.50
  169.9 7.3 collective-permute-done.27
  179.3 9.2 %collective-permute-done.3 = bf16[384,576]{0,1:T(8,128)(2,1)S(1)} collective-permute-done((bf16[384,576]{0,1:T(8,128)(2,1)S(1)}, bf16[384,576]{0,1:T(8,128)(2,1)S(1)}, u32[]{:S(2)}, u32[]{:S(2)}) %collective-permute-start.3) | collective-permute-done | bytes 442400 | tf_op jit(solution)/shard_map/ppermute | solution.py:373
  189.5 3.1 fusion.108.proj_ref
  192.7 6.2 attend_row.4
  207.6 3.1 fusion.99.proj_ref
  210.8 6.1 attend_row.7
  216.9 3.9 fusion.105.proj_ref
  221.0 6.5 attend_row.5
  244.5 3.1 fusion.102.proj_ref
  247.7 6.1 attend_row.6
  265.6 6.7 collective-permute-done.19
  278.3 13.8 %collective-permute-done.20 = bf16[256,1536]{1,0:T(8,128)(2,1)S(1)} collective-permute-done((bf16[256,1536]{1,0:T(8,128)(2,1)S(1)}, bf16[256,1536]{1,0:T(8,128)(2,1)S(1)}, u32[]{:S(2)}, u32[]{:S(2)}) %collective-permute-start.20) | collective-permute-done | bytes 786464 | tf_op jit(solution)/shard_map/ppermute | solution.py:327
  302.9 13.4 %collective-permute-done.29 = bf16[256,1536]{1,0:T(8,128)(2,1)S(1)} collective-permute-done((bf16[256,1536]{1,0:T(8,128)(2,1)S(1)}, bf16[256,1536]{1,0:T(8,128)(2,1)S(1)}, u32[]{:S(2)}, u32[]{:S(2)}) %collective-permute-start.29) | collective-permute-done | bytes 786464 | tf_op jit(solution)/shard_map/ppermute | solution.py:323
  324.8 2.9 fusion.142
  352.1 2.9 fusion.140
  358.3 3.6 fusion.121
  364.8 3.0 fusion.138
  371.0 3.5 fusion.24
  376.8 10.9 %collective-permute-done.86 = bf16[128,1536]{1,0:T(8,128)(2,1)S(1)} collective-permute-done((bf16[128,1536]{1,0:T(8,128)(2,1)S(1)}, bf16[128,1536]{1,0:T(8,128)(2,1)S(1)}, u32[]{:S(2)}, u32[]{:S(2)}) %collective-permute-start.86) | collective-permute-done | bytes 393248 | tf_op jit(solution)/shard_map/ppermute | solution.py:373
  392.2 8.8 %collective-permute-done.53 = bf16[128,1536]{1,0:T(8,128)(2,1)S(1)} collective-permute-done((bf16[128,1536]{1,0:T(8,128)(2,1)S(1)}, bf16[128,1536]{1,0:T(8,128)(2,1)S(1)}, u32[]{:S(2)}, u32[]{:S(2)}) %collective-permute-start.53) | collective-permute-done | bytes 393248 | tf_op jit(solution)/shard_map/ppermute | solution.py:327
  404.5 5.2 add_convert_fusion.2.taps_ref
  413.4 3.1 collective-permute-done.58
  419.2 3.5 multiply_reduce_fusion
  431.6 15.4 %collective-permute-done.61 = bf16[256,1536]{1,0:T(8,128)(2,1)} collective-permute-done((bf16[256,1536]{1,0:T(8,128)(2,1)}, bf16[256,1536]{1,0:T(8,128)(2,1)}, u32[]{:S(2)}, u32[]{:S(2)}) %collective-permute-start.61) | collective-permute-done | bytes 786464 | tf_op jit(solution)/shard_map/ppermute | solution.py:323
  456.9 10.1 %attend_row_back.4 = (bf16[512,768]{1,0:T(8,128)(2,1)S(1)}, f32[8,128]{1,0:T(8,128)S(1)}, f32[2,66,128]{2,1,0:T(8,128)S(1)}) custom-call(f32[2,2]{1,0:T(2,128)S(1)} %copy.159.mix_ref, bf16[512,768]{1,0:T(8,128)(2,1)S(1)} %fusion.108.proj_ref, s32[512,128]{1,0:T(8,128)S(1)} %broadcast_in_dim.542.since_ref, ...), custom_call_target="tpu_custom_call" | custom-call | flops 15000000512 | bytes 8000000 | tf_op jit(solution)/shard_map/attend_row_back/pallas_call | solution.py:288
  475.8 10.1 %attend_row_back.7 = (bf16[512,768]{1,0:T(8,128)(2,1)S(1)}, f32[8,128]{1,0:T(8,128)S(1)}, f32[2,66,128]{2,1,0:T(8,128)S(1)}) custom-call(f32[2,2]{1,0:T(2,128)S(1)} %copy.159.mix_ref, bf16[512,768]{1,0:T(8,128)(2,1)S(1)} %copy-done.19, s32[512,128]{1,0:T(8,128)S(1)} %copy-done.11, bf16[2,1536,128]{2,1,0:T(8,128)(2,1)S(1)} %add_convert_fusion.2.taps_ref, ...), custom_call_target="tpu_custom_call" | custom-call | flops 15000000512 | bytes 8000000 | tf_op jit(solution)/shard_map/attend_row_back/pallas_call | solution.py:288
  485.9 9.9 %attend_row_back.5 = (bf16[512,768]{1,0:T(8,128)(2,1)S(1)}, f32[8,128]{1,0:T(8,128)S(1)}, f32[2,66,128]{2,1,0:T(8,128)S(1)}) custom-call(f32[2,2]{1,0:T(2,128)S(1)} %copy.159.mix_ref, bf16[512,768]{1,0:T(8,128)(2,1)S(1)} %copy-done.21, s32[512,128]{1,0:T(8,128)S(1)} %copy-done.13, bf16[2,1536,128]{2,1,0:T(8,128)(2,1)S(1)} %add_convert_fusion.2.taps_ref, ...), custom_call_target="tpu_custom_call" | custom-call | flops 15000000512 | bytes 8000000 | tf_op jit(solution)/shard_map/attend_row_back/pallas_call | solution.py:288
  499.9 10.3 %attend_row_back.6 = (bf16[512,768]{1,0:T(8,128)(2,1)S(1)}, f32[8,128]{1,0:T(8,128)S(1)}, f32[2,66,128]{2,1,0:T(8,128)S(1)}) custom-call(f32[2,2]{1,0:T(2,128)S(1)} %copy.159.mix_ref, bf16[512,768]{1,0:T(8,128)(2,1)S(1)} %copy-done.23, s32[512,128]{1,0:T(8,128)S(1)} %broadcast_in_dim.624.since_ref, bf16[2,1536,128]{2,1,0:T(8,128)(2,1)S(1)} %add_convert_fusion.2.taps_ref, ...), custom_call_target="tpu_custom_call" | custom-call | flops 15000000512 | bytes 8000000 | tf_op jit(solution)/shard_map/attend_row_back/pallas_call | solution.py:288
  510.3 5.4 fusion
  519.2 10.8 %collective-permute-done.75 = bf16[384,576]{0,1:T(8,128)(2,1)S(1)} collective-permute-done((bf16[384,576]{0,1:T(8,128)(2,1)S(1)}, bf16[384,576]{0,1:T(8,128)(2,1)S(1)}, u32[]{:S(2)}, u32[]{:S(2)}) %collective-permute-start.75) | collective-permute-done | bytes 442400 | tf_op jit(solution)/shard_map/ppermute | solution.py:373
  531.4 11.8 %collective-permute-done.76 = bf16[384,576]{0,1:T(8,128)(2,1)S(1)} collective-permute-done((bf16[384,576]{0,1:T(8,128)(2,1)S(1)}, bf16[384,576]{0,1:T(8,128)(2,1)S(1)}, u32[]{:S(2)}, u32[]{:S(2)}) %collective-permute-start.76) | collective-permute-done | bytes 442400 | tf_op jit(solution)/shard_map/ppermute | solution.py:373
  546.3 9.2 %collective-permute-done.77 = bf16[384,576]{0,1:T(8,128)(2,1)S(1)} collective-permute-done((bf16[384,576]{0,1:T(8,128)(2,1)S(1)}, bf16[384,576]{0,1:T(8,128)(2,1)S(1)}, u32[]{:S(2)}, u32[]{:S(2)}) %collective-permute-start.77) | collective-permute-done | bytes 442400 | tf_op jit(solution)/shard_map/ppermute | solution.py:373
  556.6 7.1 fusion.8
  563.8 5.6 fusion.16
  575.3 13.1 %collective-permute-done.83 = bf16[384,1024]{0,1:T(8,128)(2,1)S(1)} collective-permute-done((bf16[384,1024]{0,1:T(8,128)(2,1)S(1)}, bf16[384,1024]{0,1:T(8,128)(2,1)S(1)}, u32[]{:S(2)}, u32[]{:S(2)}) %collective-permute-start.83) | collective-permute-done | bytes 786464 | tf_op jit(solution)/shard_map/ppermute | solution.py:373
  592.2 14.3 %collective-permute-done.84 = bf16[384,1024]{0,1:T(8,128)(2,1)S(1)} collective-permute-done((bf16[384,1024]{0,1:T(8,128)(2,1)S(1)}, bf16[384,1024]{0,1:T(8,128)(2,1)S(1)}, u32[]{:S(2)}, u32[]{:S(2)}) %collective-permute-start.84) | collective-permute-done | bytes 786464 | tf_op jit(solution)/shard_map/ppermute | solution.py:373
  608.8 14.9 %collective-permute-done.85 = bf16[384,1024]{0,1:T(8,128)(2,1)S(1)} collective-permute-done((bf16[384,1024]{0,1:T(8,128)(2,1)S(1)}, bf16[384,1024]{0,1:T(8,128)(2,1)S(1)}, u32[]{:S(2)}, u32[]{:S(2)}) %collective-permute-start.85) | collective-permute-done | bytes 786464 | tf_op jit(solution)/shard_map/ppermute | solution.py:373
  624.9 3.0 fusion.218
  630.6 3.2 fusion.221
  634.4 3.2 fusion.219
  637.9 3.2 fusion.220
  647.4 13.8 %collective-permute-done.78 = bf16[192,1536]{1,0:T(8,128)(2,1)S(1)} collective-permute-done((bf16[192,1536]{1,0:T(8,128)(2,1)S(1)}, bf16[192,1536]{1,0:T(8,128)(2,1)S(1)}, u32[]{:S(2)}, u32[]{:S(2)}) %collective-permute-start.78) | collective-permute-done | bytes 589856 | tf_op jit(solution)/shard_map/ppermute | solution.py:332
  668.7 9.9 %collective-permute-done.79 = bf16[192,1536]{1,0:T(8,128)(2,1)S(1)} collective-permute-done((bf16[192,1536]{1,0:T(8,128)(2,1)S(1)}, bf16[192,1536]{1,0:T(8,128)(2,1)S(1)}, u32[]{:S(2)}, u32[]{:S(2)}) %collective-permute-start.79) | collective-permute-done | bytes 589856 | tf_op jit(solution)/shard_map/ppermute | solution.py:332
  681.2 12.7 %collective-permute-done.80 = bf16[192,1536]{1,0:T(8,128)(2,1)S(1)} collective-permute-done((bf16[192,1536]{1,0:T(8,128)(2,1)S(1)}, bf16[192,1536]{1,0:T(8,128)(2,1)S(1)}, u32[]{:S(2)}, u32[]{:S(2)}) %collective-permute-start.80) | collective-permute-done | bytes 589856 | tf_op jit(solution)/shard_map/ppermute | solution.py:332
  700.8 10.0 %collective-permute-done.70 = bf16[256,1536]{1,0:T(8,128)(2,1)S(1)} collective-permute-done((bf16[256,1536]{1,0:T(8,128)(2,1)}, bf16[256,1536]{1,0:T(8,128)(2,1)S(1)}, u32[]{:S(2)}, u32[]{:S(2)}) %collective-permute-start.70) | collective-permute-done | bytes 786464 | tf_op jit(solution)/shard_map/ppermute | solution.py:323
  710.8 3.6 fusion.39
  714.4 45.1 %all-reduce.6 = (f32[1536]{0:T(1024)}, f32[16,6,11]{2,1,0:T(8,128)S(1)}, f32[16,2]{1,0:T(8,128)S(1)}, f32[1536]{0:T(1024)}, f32[1536]{0:T(1024)}) all-reduce(f32[1536]{0:T(1024)S(1)} %get-tuple-element.105, f32[16,6,11]{2,1,0:T(8,128)S(1)} %reshape.470, ...), channel_id=1, replica_groups=mesh['narrow'=4,'wide'=4,'seq'=2] {'narrow','wide','seq'}, use_global_device_ids=true, to_apply=%region_5.6 | all-reduce | flops 5696 | bytes 45568 | tf_op jit(solution)/shard_map/psum | solution.py:608
  763.0 5.5 fusion.37
  768.5 5.5 convert_element_type.464
  781.5 4.2 copy.154
  785.7 8.0 copy.156
  793.7 9.2 %convert_element_type.472 = f32[3072,1024]{0,1:T(8,128)} convert(bf16[3072,1024]{0,1:T(8,128)(2,1)} %all-gather.11.cloned.1.call-done) | non-fusion elementwise | flops 3145728 | bytes 18874368 | tf_op jit(solution)/shard_map/convert_element_type | solution.py:622
  802.9 12.1 %copy.183 = f32[128,8,8,384]{3,2,1,0:T(8,128)} copy(f32[128,8,8,384]{3,1,2,0:T(8,128)} %bitcast.218) | data formatting | bytes 25165824
  815.0 12.9 %copy.155 = f32[384,8,8,128]{3,2,1,0:T(8,128)} copy(f32[384,8,8,128]{0,2,3,1:T(8,128)} %bitcast.219) | data formatting | bytes 25165824 | tf_op jit(solution)/shard_map/convert_element_type | solution.py:622
  827.9 21.4 %copy.197 = f32[48,8,64,128]{3,1,2,0:T(8,128)} copy(f32[48,8,64,128]{3,2,1,0:T(8,128)} %bitcast.220) | data formatting | bytes 25165824
  (844 shorter events, 304.8 us)
Async XLA Ops:
  7.2 761.3 %all-gather.7.cloned.1.call-start = ((), (), s32[]{:S(2)}) async-start(), calls=%async_computation | async-start | bytes 3538944 | tf_op jit(solution)/shard_map/all_gather | solution.py:626
  11.5 101.6 %collective-permute-start = (bf16[256,1536]{1,0:T(8,128)(2,1)}, bf16[256,1536]{1,0:T(8,128)(2,1)}, u32[]{:S(2)}, u32[]{:S(2)}) collective-permute-start(bf16[256,1536]{1,0:T(8,128)(2,1)} %fusion.34), channel_id=1, source_target_pairs={{0,1},{1,0},{2,3},{3,2},{4,5},{5,4},{6,7},{7,6},{8,9},{9,8},{10,11... | collective-permute-start | bytes 2359304 | tf_op jit(solution)/shard_map/ppermute | solution.py:319
  11.9 101.9 %collective-permute-start.7 = (bf16[256,1536]{1,0:T(8,128)(2,1)}, bf16[256,1536]{1,0:T(8,128)(2,1)}, u32[]{:S(2)}, u32[]{:S(2)}) collective-permute-start(bf16[256,1536]{1,0:T(8,128)(2,1)} %fusion.34), channel_id=1, source_target_pairs={{0,8},{8,0},{16,24},{24,16},{1,9},{9,1},{17,25},{25,17},{2,10},{10... | collective-permute-start | bytes 2359304 | tf_op jit(solution)/shard_map/ppermute | solution.py:323
  19.6 89.4 %collective-permute-start.1 = (bf16[384,576]{0,1:T(8,128)(2,1)}, bf16[384,576]{0,1:T(8,128)(2,1)}, u32[]{:S(2)}, u32[]{:S(2)}) collective-permute-start(bf16[384,576]{0,1:T(8,128)(2,1)} %bitcast.3), channel_id=1, source_target_pairs={{0,2},{2,4},{4,6},{6,0},{1,3},{3,5},{5,7},{7,1},{8,10},{10,12},{12... | collective-permute-start | bytes 1327112 | tf_op jit(solution)/shard_map/ppermute | solution.py:373
  23.1 88.5 %collective-permute-start.4 = (bf16[192,1536]{1,0:T(8,128)(2,1)}, bf16[192,1536]{1,0:T(8,128)(2,1)}, u32[]{:S(2)}, u32[]{:S(2)}) collective-permute-start(bf16[192,1536]{1,0:T(8,128)(2,1)} %constant_dynamic-slice_fusion.15), channel_id=1, source_target_pairs={{0,4},{10,14},{20,16},{30,26},{1,5},{11,15},{21,17},{31,27}} | collective-permute-start | bytes 1769480 | tf_op jit(solution)/shard_map/ppermute | solution.py:332
  30.4 76.1 %collective-permute-start.25 = (bf16[128,1536]{1,0:T(8,128)(2,1)}, bf16[128,1536]{1,0:T(8,128)(2,1)}, u32[]{:S(2)}, u32[]{:S(2)}) collective-permute-start(bf16[128,1536]{1,0:T(8,128)(2,1)} %get-tuple-element.179), channel_id=1, source_target_pairs={{0,2},{2,4},{4,6},{6,0},{1,3},{3,5},{5,7},{7,1},{8,10},{10,12},{12... | collective-permute-start | bytes 1179656 | tf_op jit(solution)/shard_map/ppermute | solution.py:373
  106.4 20.6 %collective-permute-start.11 = (bf16[256,1536]{1,0:T(8,128)(2,1)}, bf16[256,1536]{1,0:T(8,128)(2,1)S(1)}, u32[]{:S(2)}, u32[]{:S(2)}) collective-permute-start(bf16[256,1536]{1,0:T(8,128)(2,1)} %fusion.34), channel_id=1, source_target_pairs={{0,16},{16,0},{8,24},{24,8},{1,17},{17,1},{9,25},{25,9},{2,18},{18... | collective-permute-start | bytes 2359304 | tf_op jit(solution)/shard_map/ppermute | solution.py:327
  109.1 19.9 %collective-permute-start.45 = (bf16[256,1536]{1,0:T(8,128)(2,1)S(1)}, bf16[256,1536]{1,0:T(8,128)(2,1)S(1)}, u32[]{:S(2)}, u32[]{:S(2)}) collective-permute-start(bf16[256,1536]{1,0:T(8,128)(2,1)S(1)} %copy-done.49), channel_id=1, source_target_pairs={{0,8},{8,0},{16,24},{24,16},{1,9},{9,1},{17,25},{25,17},{2,10},{10... | collective-permute-start | bytes 2359304 | tf_op jit(solution)/shard_map/ppermute | solution.py:323
  111.6 31.7 %collective-permute-start.49 = (bf16[256,1536]{1,0:T(8,128)(2,1)S(1)}, bf16[256,1536]{1,0:T(8,128)(2,1)S(1)}, u32[]{:S(2)}, u32[]{:S(2)}) collective-permute-start(bf16[256,1536]{1,0:T(8,128)(2,1)S(1)} %copy-done.49), channel_id=1, source_target_pairs={{0,16},{16,0},{8,24},{24,8},{1,17},{17,1},{9,25},{25,9},{2,18},{18... | collective-permute-start | bytes 2359304 | tf_op jit(solution)/shard_map/ppermute | solution.py:327
  113.1 34.3 %collective-permute-start.22 = (bf16[384,1024]{0,1:T(8,128)(2,1)S(1)}, bf16[384,1024]{0,1:T(8,128)(2,1)}, u32[]{:S(2)}, u32[]{:S(2)}) collective-permute-start(bf16[384,1024]{0,1:T(8,128)(2,1)S(1)} %bitcast.240), channel_id=1, source_target_pairs={{0,2},{2,4},{4,6},{6,0},{1,3},{3,5},{5,7},{7,1},{8,10},{10,12},{12... | collective-permute-start | bytes 2359304 | tf_op jit(solution)/shard_map/ppermute | solution.py:373
  113.8 38.5 %collective-permute-start.43 = (bf16[256,1536]{1,0:T(8,128)(2,1)S(1)}, bf16[256,1536]{1,0:T(8,128)(2,1)S(1)}, u32[]{:S(2)}, u32[]{:S(2)}) collective-permute-start(bf16[256,1536]{1,0:T(8,128)(2,1)S(1)} %copy-done.49), channel_id=1, source_target_pairs={{0,1},{1,0},{2,3},{3,2},{4,5},{5,4},{6,7},{7,6},{8,9},{9,8},{10,11... | collective-permute-start | bytes 2359304 | tf_op jit(solution)/shard_map/ppermute | solution.py:319
  127.1 26.3 %collective-permute-start.26 = (bf16[128,1536]{1,0:T(8,128)(2,1)}, bf16[128,1536]{1,0:T(8,128)(2,1)S(1)}, u32[]{:S(2)}, u32[]{:S(2)}) collective-permute-start(bf16[128,1536]{1,0:T(8,128)(2,1)} %collective-permute-done.25), channel_id=1, source_target_pairs={{0,2},{2,4},{4,6},{6,0},{1,3},{3,5},{5,7},{7,1},{8,10},{10,12},{12... | collective-permute-start | bytes 1179656 | tf_op jit(solution)/shard_map/ppermute | solution.py:373
  129.0 27.3 %collective-permute-start.2 = (bf16[384,576]{0,1:T(8,128)(2,1)}, bf16[384,576]{0,1:T(8,128)(2,1)S(1)}, u32[]{:S(2)}, u32[]{:S(2)}) collective-permute-start(bf16[384,576]{0,1:T(8,128)(2,1)} %collective-permute-done.1), channel_id=1, source_target_pairs={{0,2},{2,4},{4,6},{6,0},{1,3},{3,5},{5,7},{7,1},{8,10},{10,12},{12... | collective-permute-start | bytes 1327112 | tf_op jit(solution)/shard_map/ppermute | solution.py:373
  143.3 17.6 %collective-permute-start.5 = (bf16[192,1536]{1,0:T(8,128)(2,1)S(1)}, bf16[192,1536]{1,0:T(8,128)(2,1)S(1)}, u32[]{:S(2)}, u32[]{:S(2)}) collective-permute-start(bf16[192,1536]{1,0:T(8,128)(2,1)S(1)} %broadcast_select_fusion.36), channel_id=1, source_target_pairs={{0,2},{4,6},{10,8},{14,12},{20,22},{16,18},{30,28},{26,24},{1,3},{... | collective-permute-start | bytes 1769480 | tf_op jit(solution)/shard_map/ppermute | solution.py:332
  160.9 40.6 %collective-permute-start.8 = (bf16[256,1536]{1,0:T(8,128)(2,1)}, bf16[256,1536]{1,0:T(8,128)(2,1)S(1)}, u32[]{:S(2)}, u32[]{:S(2)}) collective-permute-start(bf16[256,1536]{1,0:T(8,128)(2,1)} %collective-permute-done.7), channel_id=1, source_target_pairs={{0,1},{1,0},{2,3},{3,2},{4,5},{5,4},{6,7},{7,6},{8,9},{9,8},{10,11... | collective-permute-start | bytes 2359304 | tf_op jit(solution)/shard_map/ppermute | solution.py:319
  161.1 43.8 %collective-permute-start.17 = (bf16[256,1536]{1,0:T(8,128)(2,1)S(1)}, bf16[256,1536]{1,0:T(8,128)(2,1)S(1)}, u32[]{:S(2)}, u32[]{:S(2)}) collective-permute-start(bf16[256,1536]{1,0:T(8,128)(2,1)S(1)} %collective-permute-done.11), channel_id=1, source_target_pairs={{0,1},{1,0},{2,3},{3,2},{4,5},{5,4},{6,7},{7,6},{8,9},{9,8},{10,11... | collective-permute-start | bytes 2359304 | tf_op jit(solution)/shard_map/ppermute | solution.py:319
  166.2 63.5 %collective-permute-start.46 = (bf16[256,1536]{1,0:T(8,128)(2,1)S(1)}, bf16[256,1536]{1,0:T(8,128)(2,1)}, u32[]{:S(2)}, u32[]{:S(2)}) collective-permute-start(bf16[256,1536]{1,0:T(8,128)(2,1)S(1)} %collective-permute-done.45), channel_id=1, source_target_pairs={{0,1},{1,0},{2,3},{3,2},{4,5},{5,4},{6,7},{7,6},{8,9},{9,8},{10,11... | collective-permute-start | bytes 2359304 | tf_op jit(solution)/shard_map/ppermute | solution.py:319
  169.9 64.8 %collective-permute-start.55 = (bf16[256,1536]{1,0:T(8,128)(2,1)S(1)}, bf16[256,1536]{1,0:T(8,128)(2,1)S(1)}, u32[]{:S(2)}, u32[]{:S(2)}) collective-permute-start(bf16[256,1536]{1,0:T(8,128)(2,1)S(1)} %collective-permute-done.49), channel_id=1, source_target_pairs={{0,1},{1,0},{2,3},{3,2},{4,5},{5,4},{6,7},{7,6},{8,9},{9,8},{10,11... | collective-permute-start | bytes 2359304 | tf_op jit(solution)/shard_map/ppermute | solution.py:319
  188.5 49.0 %collective-permute-start.23 = (bf16[384,1024]{0,1:T(8,128)(2,1)}, bf16[384,1024]{0,1:T(8,128)(2,1)}, u32[]{:S(2)}, u32[]{:S(2)}) collective-permute-start(bf16[384,1024]{0,1:T(8,128)(2,1)} %collective-permute-done.22), channel_id=1, source_target_pairs={{0,2},{2,4},{4,6},{6,0},{1,3},{3,5},{5,7},{7,1},{8,10},{10,12},{12... | collective-permute-start | bytes 2359304 | tf_op jit(solution)/shard_map/ppermute | solution.py:373
  201.5 39.6 %collective-permute-start.13 = (bf16[256,1536]{1,0:T(8,128)(2,1)S(1)}, bf16[256,1536]{1,0:T(8,128)(2,1)}, u32[]{:S(2)}, u32[]{:S(2)}) collective-permute-start(bf16[256,1536]{1,0:T(8,128)(2,1)S(1)} %constant_dynamic-update-slice_fusion), channel_id=1, source_target_pairs={{0,1},{1,0},{2,3},{3,2},{4,5},{5,4},{6,7},{7,6},{8,9},{9,8},{10,11... | collective-permute-start | bytes 2359304 | tf_op jit(solution)/shard_map/ppermute | solution.py:319
  204.9 72.2 %collective-permute-start.51 = (bf16[256,1536]{1,0:T(8,128)(2,1)S(1)}, bf16[256,1536]{1,0:T(8,128)(2,1)}, u32[]{:S(2)}, u32[]{:S(2)}) collective-permute-start(bf16[256,1536]{1,0:T(8,128)(2,1)S(1)} %constant_dynamic-update-slice_fusion.4), channel_id=1, source_target_pairs={{0,1},{1,0},{2,3},{3,2},{4,5},{5,4},{6,7},{7,6},{8,9},{9,8},{10,11... | collective-permute-start | bytes 2359304 | tf_op jit(solution)/shard_map/ppermute | solution.py:319
  229.7 48.6 %collective-permute-start.6 = (bf16[256,1536]{1,0:T(8,128)(2,1)}, bf16[256,1536]{1,0:T(8,128)(2,1)}, u32[]{:S(2)}, u32[]{:S(2)}) collective-permute-start(bf16[256,1536]{1,0:T(8,128)(2,1)} %dynamic-slice_convert_fusion.15), channel_id=1, source_target_pairs={{0,1},{1,0},{2,3},{3,2},{4,5},{5,4},{6,7},{7,6},{8,9},{9,8},{10,11... | collective-permute-start | bytes 2359304 | tf_op jit(solution)/shard_map/ppermute | solution.py:319
  234.7 22.6 %collective-permute-start.18 = (bf16[256,1536]{1,0:T(8,128)(2,1)}, bf16[256,1536]{1,0:T(8,128)(2,1)}, u32[]{:S(2)}, u32[]{:S(2)}) collective-permute-start(bf16[256,1536]{1,0:T(8,128)(2,1)} %dynamic-slice_convert_fusion.12), channel_id=1, source_target_pairs={{0,1},{1,0},{2,3},{3,2},{4,5},{5,4},{6,7},{7,6},{8,9},{9,8},{10,11... | collective-permute-start | bytes 2359304 | tf_op jit(solution)/shard_map/ppermute | solution.py:319
  237.5 25.1 %collective-permute-start.9 = (bf16[256,1536]{1,0:T(8,128)(2,1)}, bf16[256,1536]{1,0:T(8,128)(2,1)}, u32[]{:S(2)}, u32[]{:S(2)}) collective-permute-start(bf16[256,1536]{1,0:T(8,128)(2,1)} %dynamic-slice_convert_fusion.14), channel_id=1, source_target_pairs={{0,1},{1,0},{2,3},{3,2},{4,5},{5,4},{6,7},{7,6},{8,9},{9,8},{10,11... | collective-permute-start | bytes 2359304 | tf_op jit(solution)/shard_map/ppermute | solution.py:319
  257.3 44.6 %collective-permute-start.24 = (bf16[384,1024]{0,1:T(8,128)(2,1)}, bf16[384,1024]{0,1:T(8,128)(2,1)S(1)}, u32[]{:S(2)}, u32[]{:S(2)}) collective-permute-start(bf16[384,1024]{0,1:T(8,128)(2,1)} %collective-permute-done.23), channel_id=1, source_target_pairs={{0,2},{2,4},{4,6},{6,0},{1,3},{3,5},{5,7},{7,1},{8,10},{10,12},{12... | collective-permute-start | bytes 2359304 | tf_op jit(solution)/shard_map/ppermute | solution.py:373
  272.5 19.6 %collective-permute-start.20 = (bf16[256,1536]{1,0:T(8,128)(2,1)S(1)}, bf16[256,1536]{1,0:T(8,128)(2,1)S(1)}, u32[]{:S(2)}, u32[]{:S(2)}) collective-permute-start(bf16[256,1536]{1,0:T(8,128)(2,1)S(1)} %pad_maximum_fusion.14), channel_id=1, source_target_pairs={{0,16},{16,0},{8,24},{24,8},{1,17},{17,1},{9,25},{25,9},{2,18},{18... | collective-permute-start | bytes 2359304 | tf_op jit(solution)/shard_map/ppermute | solution.py:327
  275.5 18.8 %collective-permute-start.16 = (bf16[256,1536]{1,0:T(8,128)(2,1)S(1)}, bf16[256,1536]{1,0:T(8,128)(2,1)S(1)}, u32[]{:S(2)}, u32[]{:S(2)}) collective-permute-start(bf16[256,1536]{1,0:T(8,128)(2,1)S(1)} %pad_maximum_fusion.13), channel_id=1, source_target_pairs={{0,8},{8,0},{16,24},{24,16},{1,9},{9,1},{17,25},{25,17},{2,10},{10... | collective-permute-start | bytes 2359304 | tf_op jit(solution)/shard_map/ppermute | solution.py:323
  296.3 22.5 %collective-permute-start.21 = (bf16[256,1536]{1,0:T(8,128)(2,1)S(1)}, bf16[256,1536]{1,0:T(8,128)(2,1)S(1)}, u32[]{:S(2)}, u32[]{:S(2)}) collective-permute-start(bf16[256,1536]{1,0:T(8,128)(2,1)S(1)} %multiply_convert_fusion), channel_id=1, source_target_pairs={{0,1},{1,0},{2,3},{3,2},{4,5},{5,4},{6,7},{7,6},{8,9},{9,8},{10,11... | collective-permute-start | bytes 2359304 | tf_op jit(solution)/shard_map/ppermute | solution.py:319
  296.3 20.0 %collective-permute-start.29 = (bf16[256,1536]{1,0:T(8,128)(2,1)S(1)}, bf16[256,1536]{1,0:T(8,128)(2,1)S(1)}, u32[]{:S(2)}, u32[]{:S(2)}) collective-permute-start(bf16[256,1536]{1,0:T(8,128)(2,1)S(1)} %multiply_convert_fusion), channel_id=1, source_target_pairs={{0,8},{8,0},{16,24},{24,16},{1,9},{9,1},{17,25},{25,17},{2,10},{10... | collective-permute-start | bytes 2359304 | tf_op jit(solution)/shard_map/ppermute | solution.py:323
  297.1 20.9 %collective-permute-start.33 = (bf16[256,1536]{1,0:T(8,128)(2,1)S(1)}, bf16[256,1536]{1,0:T(8,128)(2,1)S(1)}, u32[]{:S(2)}, u32[]{:S(2)}) collective-permute-start(bf16[256,1536]{1,0:T(8,128)(2,1)S(1)} %multiply_convert_fusion), channel_id=1, source_target_pairs={{0,16},{16,0},{8,24},{24,8},{1,17},{17,1},{9,25},{25,9},{2,18},{18... | collective-permute-start | bytes 2359304 | tf_op jit(solution)/shard_map/ppermute | solution.py:327
  331.4 82.1 %collective-permute-start.44 = (bf16[256,1536]{1,0:T(8,128)(2,1)}, bf16[256,1536]{1,0:T(8,128)(2,1)}, u32[]{:S(2)}, u32[]{:S(2)}) collective-permute-start(bf16[256,1536]{1,0:T(8,128)(2,1)} %dynamic-slice_convert_fusion.7), channel_id=1, source_target_pairs={{0,1},{1,0},{2,3},{3,2},{4,5},{5,4},{6,7},{7,6},{8,9},{9,8},{10,11... | collective-permute-start | bytes 2359304 | tf_op jit(solution)/shard_map/ppermute | solution.py:319
  332.0 25.9 %collective-permute-start.35 = (bf16[256,1536]{1,0:T(8,128)(2,1)S(1)}, bf16[256,1536]{1,0:T(8,128)(2,1)S(1)}, u32[]{:S(2)}, u32[]{:S(2)}) collective-permute-start(bf16[256,1536]{1,0:T(8,128)(2,1)S(1)} %constant_dynamic-update-slice_fusion.2), channel_id=1, source_target_pairs={{0,1},{1,0},{2,3},{3,2},{4,5},{5,4},{6,7},{7,6},{8,9},{9,8},{10,11... | collective-permute-start | bytes 2359304 | tf_op jit(solution)/shard_map/ppermute | solution.py:319
  346.2 28.4 %collective-permute-start.56 = (bf16[256,1536]{1,0:T(8,128)(2,1)S(1)}, bf16[256,1536]{1,0:T(8,128)(2,1)S(1)}, u32[]{:S(2)}, u32[]{:S(2)}) collective-permute-start(bf16[256,1536]{1,0:T(8,128)(2,1)S(1)} %dynamic-slice_convert_fusion.4), channel_id=1, source_target_pairs={{0,1},{1,0},{2,3},{3,2},{4,5},{5,4},{6,7},{7,6},{8,9},{9,8},{10,11... | collective-permute-start | bytes 2359304 | tf_op jit(solution)/shard_map/ppermute | solution.py:319
  357.6 17.2 %collective-permute-start.47 = (bf16[256,1536]{1,0:T(8,128)(2,1)S(1)}, bf16[256,1536]{1,0:T(8,128)(2,1)S(1)}, u32[]{:S(2)}, u32[]{:S(2)}) collective-permute-start(bf16[256,1536]{1,0:T(8,128)(2,1)S(1)} %dynamic-slice_convert_fusion.6), channel_id=1, source_target_pairs={{0,1},{1,0},{2,3},{3,2},{4,5},{5,4},{6,7},{7,6},{8,9},{9,8},{10,11... | collective-permute-start | bytes 2359304 | tf_op jit(solution)/shard_map/ppermute | solution.py:319
  388.5 21.2 %collective-permute-start.87 = (bf16[128,1536]{1,0:T(8,128)(2,1)}, bf16[128,1536]{1,0:T(8,128)(2,1)}, u32[]{:S(2)}, u32[]{:S(2)}) collective-permute-start(bf16[128,1536]{1,0:T(8,128)(2,1)} %add_convert_fusion.12), channel_id=1, source_target_pairs={{0,2},{2,4},{4,6},{6,0},{1,3},{3,5},{5,7},{7,1},{8,10},{10,12},{12... | collective-permute-start | bytes 1179656 | tf_op jit(solution)/shard_map/ppermute | solution.py:373
  391.1 25.4 %collective-permute-start.58 = (bf16[256,1536]{1,0:T(8,128)(2,1)}, bf16[256,1536]{1,0:T(8,128)(2,1)}, u32[]{:S(2)}, u32[]{:S(2)}) collective-permute-start(bf16[256,1536]{1,0:T(8,128)(2,1)} %pad_maximum_fusion.18), channel_id=1, source_target_pairs={{0,16},{16,0},{8,24},{24,8},{1,17},{17,1},{9,25},{25,9},{2,18},{18... | collective-permute-start | bytes 2359304 | tf_op jit(solution)/shard_map/ppermute | solution.py:327
  402.2 17.0 %collective-permute-start.54 = (bf16[256,1536]{1,0:T(8,128)(2,1)}, bf16[256,1536]{1,0:T(8,128)(2,1)}, u32[]{:S(2)}, u32[]{:S(2)}) collective-permute-start(bf16[256,1536]{1,0:T(8,128)(2,1)} %pad_maximum_fusion.17), channel_id=1, source_target_pairs={{0,8},{8,0},{16,24},{24,16},{1,9},{9,1},{17,25},{25,17},{2,10},{10... | collective-permute-start | bytes 2359304 | tf_op jit(solution)/shard_map/ppermute | solution.py:323
  411.2 18.4 %collective-permute-start.88 = (bf16[128,1536]{1,0:T(8,128)(2,1)S(1)}, bf16[128,1536]{1,0:T(8,128)(2,1)S(1)}, u32[]{:S(2)}, u32[]{:S(2)}) collective-permute-start(bf16[128,1536]{1,0:T(8,128)(2,1)S(1)} %add_convert_fusion.11), channel_id=1, source_target_pairs={{0,2},{2,4},{4,6},{6,0},{1,3},{3,5},{5,7},{7,1},{8,10},{10,12},{12... | collective-permute-start | bytes 1179656 | tf_op jit(solution)/shard_map/ppermute | solution.py:373
  424.2 26.5 %collective-permute-start.59 = (bf16[256,1536]{1,0:T(8,128)(2,1)}, bf16[256,1536]{1,0:T(8,128)(2,1)}, u32[]{:S(2)}, u32[]{:S(2)}) collective-permute-start(bf16[256,1536]{1,0:T(8,128)(2,1)} %fusion.205), channel_id=1, source_target_pairs={{0,1},{1,0},{2,3},{3,2},{4,5},{5,4},{6,7},{7,6},{8,9},{9,8},{10,11... | collective-permute-start | bytes 2359304 | tf_op jit(solution)/shard_map/ppermute | solution.py:319
  424.2 22.8 %collective-permute-start.61 = (bf16[256,1536]{1,0:T(8,128)(2,1)}, bf16[256,1536]{1,0:T(8,128)(2,1)}, u32[]{:S(2)}, u32[]{:S(2)}) collective-permute-start(bf16[256,1536]{1,0:T(8,128)(2,1)} %fusion.205), channel_id=1, source_target_pairs={{0,8},{8,0},{16,24},{24,16},{1,9},{9,1},{17,25},{25,17},{2,10},{10... | collective-permute-start | bytes 2359304 | tf_op jit(solution)/shard_map/ppermute | solution.py:323
  425.6 23.6 %collective-permute-start.65 = (bf16[256,1536]{1,0:T(8,128)(2,1)}, bf16[256,1536]{1,0:T(8,128)(2,1)S(1)}, u32[]{:S(2)}, u32[]{:S(2)}) collective-permute-start(bf16[256,1536]{1,0:T(8,128)(2,1)} %fusion.205), channel_id=1, source_target_pairs={{0,16},{16,0},{8,24},{24,8},{1,17},{17,1},{9,25},{25,9},{2,18},{18... | collective-permute-start | bytes 2359304 | tf_op jit(solution)/shard_map/ppermute | solution.py:327
  429.5 333.4 %collective-permute-start.28 = (bf16[256,1536]{1,0:T(8,128)(2,1)}, bf16[256,1536]{1,0:T(8,128)(2,1)}, u32[]{:S(2)}, u32[]{:S(2)}) collective-permute-start(bf16[256,1536]{1,0:T(8,128)(2,1)} %dynamic-slice_convert_fusion.11), channel_id=1, source_target_pairs={{0,1},{1,0},{2,3},{3,2},{4,5},{5,4},{6,7},{7,6},{8,9},{9,8},{10,11... | collective-permute-start | bytes 2359304 | tf_op jit(solution)/shard_map/ppermute | solution.py:319
  431.5 345.5 %all-gather.9.cloned.1.call-start = ((), (), s32[]{:S(2)}) async-start(), calls=%async_computation.1 | async-start | bytes 3981312 | tf_op jit(solution)/shard_map/all_gather | solution.py:621
  448.0 19.0 %collective-permute-start.64 = (bf16[128,1536]{1,0:T(8,128)(2,1)S(1)}, bf16[128,1536]{1,0:T(8,128)(2,1)S(1)}, u32[]{:S(2)}, u32[]{:S(2)}) collective-permute-start(bf16[128,1536]{1,0:T(8,128)(2,1)S(1)} %slice.251), channel_id=1, source_target_pairs={{0,16},{16,0},{8,24},{24,8},{1,17},{17,1},{9,25},{25,9},{2,18},{18... | collective-permute-start | bytes 1179656 | tf_op jit(solution)/shard_map/ppermute | solution.py:327
  449.3 17.9 %collective-permute-start.66 = (bf16[128,1536]{1,0:T(8,128)(2,1)S(1)}, bf16[128,1536]{1,0:T(8,128)(2,1)S(1)}, u32[]{:S(2)}, u32[]{:S(2)}) collective-permute-start(bf16[128,1536]{1,0:T(8,128)(2,1)S(1)} %slice.252), channel_id=1, source_target_pairs={{0,8},{8,0},{16,24},{24,16},{1,9},{9,1},{17,25},{25,17},{2,10},{10... | collective-permute-start | bytes 1179656 | tf_op jit(solution)/shard_map/ppermute | solution.py:323
  467.1 28.7 %collective-permute-start.67 = (bf16[256,1536]{1,0:T(8,128)(2,1)S(1)}, bf16[256,1536]{1,0:T(8,128)(2,1)S(1)}, u32[]{:S(2)}, u32[]{:S(2)}) collective-permute-start(bf16[256,1536]{1,0:T(8,128)(2,1)S(1)} %constant_dynamic-update-slice_fusion.6), channel_id=1, source_target_pairs={{0,1},{1,0},{2,3},{3,2},{4,5},{5,4},{6,7},{7,6},{8,9},{9,8},{10,11... | collective-permute-start | bytes 2359304 | tf_op jit(solution)/shard_map/ppermute | solution.py:319
  519.2 50.5 %collective-permute-start.40 = (bf16[256,1536]{1,0:T(8,128)(2,1)}, bf16[256,1536]{1,0:T(8,128)(2,1)}, u32[]{:S(2)}, u32[]{:S(2)}) collective-permute-start(bf16[256,1536]{1,0:T(8,128)(2,1)} %dynamic-slice_convert_fusion.8), channel_id=1, source_target_pairs={{0,1},{1,0},{2,3},{3,2},{4,5},{5,4},{6,7},{7,6},{8,9},{9,8},{10,11... | collective-permute-start | bytes 2359304 | tf_op jit(solution)/shard_map/ppermute | solution.py:319
  531.3 57.4 %collective-permute-start.31 = (bf16[256,1536]{1,0:T(8,128)(2,1)S(1)}, bf16[256,1536]{1,0:T(8,128)(2,1)}, u32[]{:S(2)}, u32[]{:S(2)}) collective-permute-start(bf16[256,1536]{1,0:T(8,128)(2,1)S(1)} %dynamic-slice_convert_fusion.10), channel_id=1, source_target_pairs={{0,1},{1,0},{2,3},{3,2},{4,5},{5,4},{6,7},{7,6},{8,9},{9,8},{10,11... | collective-permute-start | bytes 2359304 | tf_op jit(solution)/shard_map/ppermute | solution.py:319
  546.3 26.3 %collective-permute-start.36 = (bf16[256,1536]{1,0:T(8,128)(2,1)}, bf16[256,1536]{1,0:T(8,128)(2,1)}, u32[]{:S(2)}, u32[]{:S(2)}) collective-permute-start(bf16[256,1536]{1,0:T(8,128)(2,1)} %dynamic-slice_convert_fusion.9), channel_id=1, source_target_pairs={{0,1},{1,0},{2,3},{3,2},{4,5},{5,4},{6,7},{7,6},{8,9},{9,8},{10,11... | collective-permute-start | bytes 2359304 | tf_op jit(solution)/shard_map/ppermute | solution.py:319
  556.5 237.2 %all-gather.11.cloned.1.call-start = ((), (), s32[]{:S(2)}) async-start(), calls=%async_computation.2 | async-start | bytes 7077888 | tf_op jit(solution)/shard_map/all_gather | solution.py:621
  569.6 18.8 %collective-permute-start.83 = (bf16[384,1024]{0,1:T(8,128)(2,1)S(1)}, bf16[384,1024]{0,1:T(8,128)(2,1)S(1)}, u32[]{:S(2)}, u32[]{:S(2)}) collective-permute-start(bf16[384,1024]{0,1:T(8,128)(2,1)S(1)} %fusion.44), channel_id=1, source_target_pairs={{0,2},{2,4},{4,6},{6,0},{1,3},{3,5},{5,7},{7,1},{8,10},{10,12},{12... | collective-permute-start | bytes 2359304 | tf_op jit(solution)/shard_map/ppermute | solution.py:373
  574.1 18.1 %collective-permute-start.41 = (bf16[128,1536]{1,0:T(8,128)(2,1)S(1)}, bf16[128,1536]{1,0:T(8,128)(2,1)S(1)}, u32[]{:S(2)}, u32[]{:S(2)}) collective-permute-start(bf16[128,1536]{1,0:T(8,128)(2,1)S(1)} %get-tuple-element.205), channel_id=1, source_target_pairs={{0,8},{8,0},{16,24},{24,16},{1,9},{9,1},{17,25},{25,17},{2,10},{10... | collective-permute-start | bytes 1179656 | tf_op jit(solution)/shard_map/ppermute | solution.py:323
  588.7 17.9 %collective-permute-start.84 = (bf16[384,1024]{0,1:T(8,128)(2,1)S(1)}, bf16[384,1024]{0,1:T(8,128)(2,1)S(1)}, u32[]{:S(2)}, u32[]{:S(2)}) collective-permute-start(bf16[384,1024]{0,1:T(8,128)(2,1)S(1)} %fusion.47), channel_id=1, source_target_pairs={{0,2},{2,4},{4,6},{6,0},{1,3},{3,5},{5,7},{7,1},{8,10},{10,12},{12... | collective-permute-start | bytes 2359304 | tf_op jit(solution)/shard_map/ppermute | solution.py:373
  590.1 17.7 %collective-permute-start.37 = (bf16[128,1536]{1,0:T(8,128)(2,1)S(1)}, bf16[128,1536]{1,0:T(8,128)(2,1)S(1)}, u32[]{:S(2)}, u32[]{:S(2)}) collective-permute-start(bf16[128,1536]{1,0:T(8,128)(2,1)S(1)} %get-tuple-element.204), channel_id=1, source_target_pairs={{0,16},{16,0},{8,24},{24,8},{1,17},{17,1},{9,25},{25,9},{2,18},{18... | collective-permute-start | bytes 1179656 | tf_op jit(solution)/shard_map/ppermute | solution.py:327
  630.6 67.6 %collective-permute-start.60 = (bf16[256,1536]{1,0:T(8,128)(2,1)}, bf16[256,1536]{1,0:T(8,128)(2,1)S(1)}, u32[]{:S(2)}, u32[]{:S(2)}) collective-permute-start(bf16[256,1536]{1,0:T(8,128)(2,1)} %dynamic-slice_convert_fusion.3), channel_id=1, source_target_pairs={{0,1},{1,0},{2,3},{3,2},{4,5},{5,4},{6,7},{7,6},{8,9},{9,8},{10,11... | collective-permute-start | bytes 2359304 | tf_op jit(solution)/shard_map/ppermute | solution.py:319
  644.0 17.2 %collective-permute-start.78 = (bf16[192,1536]{1,0:T(8,128)(2,1)S(1)}, bf16[192,1536]{1,0:T(8,128)(2,1)S(1)}, u32[]{:S(2)}, u32[]{:S(2)}) collective-permute-start(bf16[192,1536]{1,0:T(8,128)(2,1)S(1)} %bitcast_convert_fusion), channel_id=1, source_target_pairs={{2,0},{6,4},{8,10},{12,14},{22,20},{18,16},{28,30},{24,26},{3,1},{... | collective-permute-start | bytes 1769480 | tf_op jit(solution)/shard_map/ppermute | solution.py:332
  646.1 19.5 %collective-permute-start.73 = (bf16[128,1536]{1,0:T(8,128)(2,1)S(1)}, bf16[128,1536]{1,0:T(8,128)(2,1)S(1)}, u32[]{:S(2)}, u32[]{:S(2)}) collective-permute-start(bf16[128,1536]{1,0:T(8,128)(2,1)S(1)} %get-tuple-element.201), channel_id=1, source_target_pairs={{0,8},{8,0},{16,24},{24,16},{1,9},{9,1},{17,25},{25,17},{2,10},{10... | collective-permute-start | bytes 1179656 | tf_op jit(solution)/shard_map/ppermute | solution.py:323
  661.3 17.3 %collective-permute-start.79 = (bf16[192,1536]{1,0:T(8,128)(2,1)S(1)}, bf16[192,1536]{1,0:T(8,128)(2,1)S(1)}, u32[]{:S(2)}, u32[]{:S(2)}) collective-permute-start(bf16[192,1536]{1,0:T(8,128)(2,1)S(1)} %fusion.127), channel_id=1, source_target_pairs={{4,0},{14,10},{16,20},{26,30},{5,1},{15,11},{17,21},{27,31}} | collective-permute-start | bytes 1769480 | tf_op jit(solution)/shard_map/ppermute | solution.py:332
  662.6 17.6 %collective-permute-start.69 = (bf16[128,1536]{1,0:T(8,128)(2,1)S(1)}, bf16[128,1536]{1,0:T(8,128)(2,1)S(1)}, u32[]{:S(2)}, u32[]{:S(2)}) collective-permute-start(bf16[128,1536]{1,0:T(8,128)(2,1)S(1)} %get-tuple-element.200), channel_id=1, source_target_pairs={{0,16},{16,0},{8,24},{24,8},{1,17},{17,1},{9,25},{25,9},{2,18},{18... | collective-permute-start | bytes 1179656 | tf_op jit(solution)/shard_map/ppermute | solution.py:327
  666.6 31.6 %collective-permute-start.74 = (bf16[256,1536]{1,0:T(8,128)(2,1)}, bf16[256,1536]{1,0:T(8,128)(2,1)S(1)}, u32[]{:S(2)}, u32[]{:S(2)}) collective-permute-start(bf16[256,1536]{1,0:T(8,128)(2,1)} %pad_maximum_fusion.20), channel_id=1, source_target_pairs={{0,16},{16,0},{8,24},{24,8},{1,17},{17,1},{9,25},{25,9},{2,18},{18... | collective-permute-start | bytes 2359304 | tf_op jit(solution)/shard_map/ppermute | solution.py:327
  681.2 29.6 %collective-permute-start.70 = (bf16[256,1536]{1,0:T(8,128)(2,1)}, bf16[256,1536]{1,0:T(8,128)(2,1)S(1)}, u32[]{:S(2)}, u32[]{:S(2)}) collective-permute-start(bf16[256,1536]{1,0:T(8,128)(2,1)} %pad_maximum_fusion.19), channel_id=1, source_target_pairs={{0,8},{8,0},{16,24},{24,16},{1,9},{9,1},{17,25},{25,17},{2,10},{10... | collective-permute-start | bytes 2359304 | tf_op jit(solution)/shard_map/ppermute | solution.py:323
  694.8 66.1 %collective-permute-start.81 = (bf16[192,1536]{1,0:T(8,128)(2,1)}, bf16[192,1536]{1,0:T(8,128)(2,1)}, u32[]{:S(2)}, u32[]{:S(2)}) collective-permute-start(bf16[192,1536]{1,0:T(8,128)(2,1)} %broadcast_select_fusion.35), channel_id=1, source_target_pairs={{0,16},{8,24},{10,26},{2,18},{20,4},{28,12},{30,14},{22,6},{1,17},... | collective-permute-start | bytes 1769480 | tf_op jit(solution)/shard_map/ppermute | solution.py:332
  698.2 64.7 %collective-permute-start.42 = (bf16[256,1536]{1,0:T(8,128)(2,1)}, bf16[256,1536]{1,0:T(8,128)(2,1)}, u32[]{:S(2)}, u32[]{:S(2)}) collective-permute-start(bf16[256,1536]{1,0:T(8,128)(2,1)} %pad_maximum_fusion.16), channel_id=1, source_target_pairs={{0,16},{16,0},{8,24},{24,8},{1,17},{17,1},{9,25},{25,9},{2,18},{18... | collective-permute-start | bytes 2359304 | tf_op jit(solution)/shard_map/ppermute | solution.py:327
  698.3 64.6 %collective-permute-start.38 = (bf16[256,1536]{1,0:T(8,128)(2,1)}, bf16[256,1536]{1,0:T(8,128)(2,1)}, u32[]{:S(2)}, u32[]{:S(2)}) collective-permute-start(bf16[256,1536]{1,0:T(8,128)(2,1)} %pad_maximum_fusion.15), channel_id=1, source_target_pairs={{0,8},{8,0},{16,24},{24,16},{1,9},{9,1},{17,25},{25,17},{2,10},{10... | collective-permute-start | bytes 2359304 | tf_op jit(solution)/shard_map/ppermute | solution.py:323
  (198 other events, 2495.1 us)
Sparse Core Ops, SparseCore 0:
  431.7 37.8 all-gather.6
  556.6 37.2 all-gather.8
  625.0 50.9 all-gather.10

commit v2 on v1

v2 whole, which is shorter than its diff:
```python
import functools
import jax
import jax.numpy as jnp
from jax import lax
from jax.experimental import pallas as pl
from jax.experimental.pallas import tpu as pltpu

LANES = 128
EDGE = 64
TOP = 16
LIGHT = pl.CostEstimate(flops=1_000_000, bytes_accessed=1_000_000, transcendentals=0)


def taps_kernel(taps_q, taps_k, scaling, kernel_ref, forward_ref, backward_ref):
    half = (taps_k - 1) // 2
    row = lax.broadcasted_iota(jnp.int32, (2 * LANES, LANES), 0)
    col = lax.broadcasted_iota(jnp.int32, (2 * LANES, LANES), 1)
    forth = col - row + EDGE + half
    back = row - col - EDGE + half
    for head in range(2):
        for tap in range(taps_q):
            ahead = jnp.zeros((2 * LANES, LANES), jnp.float32)
            behind = jnp.zeros((2 * LANES, LANES), jnp.float32)
            for tap_k in range(taps_k):
                value = kernel_ref[head, tap, tap_k]
                ahead = jnp.where(forth == tap_k, value, ahead)
                behind = jnp.where(back == tap_k, value, behind)
            ahead = ahead * scaling
            high = ahead.astype(jnp.bfloat16)
            cols = slice(tap * LANES, (tap + 1) * LANES)
            forward_ref[head, : 2 * LANES, cols] = high
            forward_ref[head, 2 * LANES : 4 * LANES, cols] = high
            forward_ref[head, 4 * LANES :, cols] = (ahead - high.astype(jnp.float32)).astype(jnp.bfloat16)
            backward_ref[head, tap * 2 * LANES : (tap + 1) * 2 * LANES, :] = behind.astype(jnp.bfloat16)


def tap_bands(kernels, scaling):
    heads, taps_q, taps_k = kernels.shape
    return pl.pallas_call(
        functools.partial(taps_kernel, taps_q, taps_k, scaling),
        out_shape=(
            jax.ShapeDtypeStruct((heads, 6 * LANES, taps_q * LANES), jnp.bfloat16),
            jax.ShapeDtypeStruct((heads, taps_q * 2 * LANES, LANES), jnp.bfloat16),
        ),
        in_specs=[pl.BlockSpec(memory_space=pltpu.SMEM)],
        out_specs=(pl.BlockSpec(memory_space=pltpu.VMEM),) * 2,
        compiler_params=pltpu.CompilerParams(vmem_limit_bytes=32 * 1024 * 1024),
        cost_estimate=LIGHT,
        name="tap_bands",
    )(kernels)


def place_columns_kernel(sections, chunk, where_ref, *refs):
    ins, out_ref = refs[:-1], refs[-1]
    line, core = where_ref[0], where_ref[1]
    width = 2 * chunk
    chips = len(ins) // 2
    for k in range(chips):
        own = ins[2 * k][...].astype(jnp.float32)
        other = ins[2 * k + 1][...].astype(jnp.float32)
        first = jnp.where(core == 0, own, other)
        second = jnp.where(core == 0, other, own)
        for s in range(sections):
            both = jnp.concatenate([first[:, s * chunk : (s + 1) * chunk], second[:, s * chunk : (s + 1) * chunk]], 1)
            at = pl.multiple_of(s * chips * width + (line ^ k) * width, LANES)
            out_ref[:, pl.ds(at, width)] = both


def place_columns(place, pieces, sections, chunk):
    rows, cols = pieces[0].shape
    cols_out = sections * chunk * len(pieces)
    steps = 4 if rows % 64 == 0 else 1
    spec = pl.BlockSpec((rows // steps, cols), lambda s, place: (s, 0))
    return pl.pallas_call(
        functools.partial(place_columns_kernel, sections, chunk),
        out_shape=jax.ShapeDtypeStruct((rows, cols_out), jnp.float32),
        grid_spec=pltpu.PrefetchScalarGridSpec(
            num_scalar_prefetch=1,
            grid=(steps,),
            in_specs=[spec] * len(pieces),
            out_specs=pl.BlockSpec((rows // steps, cols_out), lambda s, place: (s, 0)),
        ),
        compiler_params=pltpu.CompilerParams(vmem_limit_bytes=40 * 1024 * 1024),
        cost_estimate=LIGHT,
        name="place_columns",
    )(place, *pieces)


def place_feed_kernel(sections, chunk, pieces, where_ref, *refs):
    ins, extras = refs[:pieces], refs[pieces : 2 * pieces]
    gate_ref, down_ref, out_ref = refs[2 * pieces :]
    line, core = where_ref[0], where_ref[1]
    width = 2 * chunk
    chips = pieces // 2
    gate_cols = sections * chunk
    for k in range(chips):
        own = ins[2 * k][...].astype(jnp.float32)
        other = ins[2 * k + 1][...].astype(jnp.float32)
        first = jnp.where(core == 0, own, other)
        second = jnp.where(core == 0, other, own)
        for s in range(sections):
            both = jnp.concatenate([first[:, s * chunk : (s + 1) * chunk], second[:, s * chunk : (s + 1) * chunk]], 1)
            at = pl.multiple_of(s * chips * width + (line ^ k) * width, LANES)
            gate_ref[:, pl.ds(at, width)] = both
        at = pl.multiple_of((line ^ k) * width, width)
        down_ref[pl.ds(at, chunk), :] = first[:, gate_cols:]
        down_ref[pl.ds(at + chunk, chunk), :] = second[:, gate_cols:]

    @pl.when(pl.program_id(0) == 0)
    def _():
        rows = extras[0].shape[0]
        for k in range(chips):
            for e in range(2):
                at = pl.multiple_of(((core ^ e) * chips + (line ^ k)) * rows, rows)
                out_ref[pl.ds(at, rows), :] = extras[2 * k + e][...].astype(jnp.float32)


def place_feed(place, pieces, chunk, blocks):
    rows, cols = pieces[0].shape
    extra = rows - blocks * chunk
    sections = (cols // chunk) * 2 // 3
    hidden = cols - sections * chunk
    gate_cols = sections * chunk * len(pieces)
    last = blocks * chunk // extra
    return pl.pallas_call(
        functools.partial(place_feed_kernel, sections, chunk, len(pieces)),
        out_shape=(
            jax.ShapeDtypeStruct((blocks * chunk, gate_cols), jnp.float32),
            jax.ShapeDtypeStruct((chunk * len(pieces), hidden * blocks), jnp.float32),
            jax.ShapeDtypeStruct((extra * len(pieces), cols), jnp.float32),
        ),
        grid_spec=pltpu.PrefetchScalarGridSpec(
            num_scalar_prefetch=1,
            grid=(blocks,),
            in_specs=[pl.BlockSpec((chunk, cols), lambda s, place: (s, 0))] * len(pieces)
            + [pl.BlockSpec((extra, cols), lambda s, place: (last, 0))] * len(pieces),
            out_specs=(
                pl.BlockSpec((chunk, gate_cols), lambda s, place: (s, 0)),
                pl.BlockSpec((chunk * len(pieces), hidden), lambda s, place: (0, s)),
                pl.BlockSpec((extra * len(pieces), cols), lambda s, place: (0, 0)),
            ),
        ),
        compiler_params=pltpu.CompilerParams(vmem_limit_bytes=48 * 1024 * 1024),
        cost_estimate=LIGHT,
        name="place_feed",
    )(place, *pieces, *pieces)


def masked_scores(q_blk, keys, since, first_row):
    scores = lax.dot_general(q_blk, keys, (((1,), (1,)), ((), ())), preferred_element_type=jnp.float32)
    rows = first_row + lax.broadcasted_iota(jnp.int32, scores.shape, 0)
    back = rows + EDGE - lax.broadcasted_iota(jnp.int32, scores.shape, 1)
    limit = jnp.concatenate([since] * (scores.shape[1] // LANES), 1)
    return jnp.where((back >= 0) & (back <= limit), scores, 0.0)


def head_places(heads, head_size):
    return [((head * head_size) // LANES, (head * head_size) % LANES) for head in range(heads)]


def split_heads(joined, heads, head_size):
    real = lax.broadcasted_iota(jnp.int32, (joined.shape[0], LANES), 1) < head_size
    out = []
    for tile, shift in head_places(heads, head_size):
        if shift:
            both = joined[:, tile * LANES : (tile + 2) * LANES]
            piece = pltpu.roll(both, 2 * LANES - shift, 1)[:, :LANES]
        else:
            piece = joined[:, tile * LANES : (tile + 1) * LANES]
        out.append(jnp.where(real, piece, 0.0))
    return out


def join_heads(pieces, head_size):
    count = pieces[0].shape[0]
    nothing = jnp.zeros((count, LANES), jnp.float32)
    tiles = [nothing] * 5
    for piece, (tile, shift) in zip(pieces, head_places(len(pieces), head_size)):
        if shift:
            both = pltpu.roll(jnp.concatenate([piece, nothing], 1), shift, 1)
            tiles[tile] = tiles[tile] + both[:, :LANES]
            tiles[tile + 1] = tiles[tile + 1] + both[:, LANES:]
        else:
            tiles[tile] = tiles[tile] + piece
    return jnp.concatenate(tiles, 1)


def forward_kernel(
    taps_q, head_size, core_ref, mix_ref, own_ref, other_ref, since_ref, joined_ref, taps_ref, gain_ref,
    proj_ref, att_ref, grouped_ref, weights_ref, keys_pad, s_high, s_low, spread, grouped_row,
):
    seq_len = proj_ref.shape[0]
    half_len = seq_len // 2
    blocks = seq_len // LANES
    own_at = pl.multiple_of(core_ref[0] * half_len, half_len)
    other_at = pl.multiple_of((1 - core_ref[0]) * half_len, half_len)
    keys_pad[...] = jnp.zeros_like(keys_pad)
    s_high[...] = jnp.zeros_like(s_high)
    s_low[...] = jnp.zeros_like(s_low)
    for ref, at in ((own_ref, own_at), (other_ref, other_at)):
        joined = jnp.dot(ref[...], joined_ref[...], preferred_element_type=jnp.float32)
        for head, piece in enumerate(split_heads(joined, 6, head_size)):
            proj_ref[pl.ds(at, half_len), head * LANES : (head + 1) * LANES] = piece.astype(jnp.bfloat16)

    def one_head(head, carry):
        lane = pl.multiple_of(head * LANES, LANES)
        lane_k = pl.multiple_of((head + 2) * LANES, LANES)
        keys_pad[EDGE : EDGE + seq_len, :] = proj_ref[:, pl.ds(lane_k, LANES)]
        for qi in range(blocks):
            first = qi * LANES
            width = (qi + 2) * LANES
            scores = masked_scores(
                proj_ref[first : first + LANES, pl.ds(lane, LANES)],
                keys_pad[:width, :],
                since_ref[first : first + LANES, :],
                first,
            )
            high = scores.astype(jnp.bfloat16)
            s_high[TOP + first : TOP + first + LANES, :width] = high
            s_low[TOP + first : TOP + first + LANES, :width] = (scores - high.astype(jnp.float32)).astype(jnp.bfloat16)
        for m in range(blocks):
            first = m * LANES
            count = seq_len - first
            high = s_high[first:, first : first + 2 * LANES]
            left = jnp.concatenate([high, s_low[first:, first : first + 2 * LANES], high], 1)
            spread[first:, :] = jnp.dot(left, taps_ref[head], preferred_element_type=jnp.float32)
            since = since_ref[first:, :]
            logits = spread[TOP + first :, :LANES]
            for tap in range(1, taps_q):
                moved = spread[TOP + first - tap : TOP + seq_len - tap, tap * LANES : (tap + 1) * LANES]
                logits = logits + jnp.where(since >= tap, moved, 0.0)
            weights_ref[head, first:, first : first + LANES] = logits
        for qi in range(blocks):
            first = qi * LANES
            width = (qi + 1) * LANES
            logits = weights_ref[head, first : first + LANES, :width]
            rows = first + lax.broadcasted_iota(jnp.int32, logits.shape, 0)
            back = rows - lax.broadcasted_iota(jnp.int32, logits.shape, 1)
            limit = jnp.concatenate([since_ref[first : first + LANES, :]] * (qi + 1), 1)
            logits = jnp.where((back >= 0) & (back <= limit), logits, -1e30)
            raised = jnp.exp(logits - jnp.max(logits, axis=1, keepdims=True))
            weights_ref[head, first : first + LANES, :width] = raised / jnp.sum(raised, axis=1, keepdims=True)
        return carry

    lax.fori_loop(0, 2, one_head, 0)
    real = lax.broadcasted_iota(jnp.int32, (LANES, LANES), 1) < head_size
    for qi in range(blocks):
        first = qi * LANES
        width = (qi + 1) * LANES
        low = weights_ref[0, first : first + LANES, :width]
        upp = weights_ref[1, first : first + LANES, :width]
        for head in range(2):
            mixed = (mix_ref[head, 0] * low + mix_ref[head, 1] * upp).astype(jnp.bfloat16)
            cols = slice(head * LANES, (head + 1) * LANES)
            att = jnp.dot(
                mixed, proj_ref[:width, (4 + head) * LANES : (5 + head) * LANES], preferred_element_type=jnp.float32
            )
            att_ref[first : first + LANES, cols] = att
            normal, _ = normalize(att, real, head_size)
            grouped_row[first : first + LANES, cols] = (normal * gain_ref[:, cols]).astype(jnp.bfloat16)
    grouped_ref[:half_len, :] = grouped_row[pl.ds(own_at, half_len), :]
    grouped_ref[half_len:, :] = grouped_row[pl.ds(other_at, half_len), :]


def normalize(att, real, head_size):
    mean = jnp.sum(att, axis=1, keepdims=True) * (1.0 / head_size)
    centered = jnp.where(real, att - mean, 0.0)
    spread = jnp.sum(centered * centered, axis=1, keepdims=True) * (1.0 / head_size)
    scale = lax.rsqrt(spread + 1e-05)
    return centered * scale, scale


def attend_row(core, own, other, since, mix, joined, taps_forward, gain_pad, taps_q, head_size):
    seq_len = 2 * own.shape[0]
    full = seq_len + 2 * EDGE
    vmem = pl.BlockSpec(memory_space=pltpu.VMEM)
    smem = pl.BlockSpec(memory_space=pltpu.SMEM)
    return pl.pallas_call(
        functools.partial(forward_kernel, taps_q, head_size),
        out_shape=(
            jax.ShapeDtypeStruct((seq_len, 6 * LANES), jnp.bfloat16),
            jax.ShapeDtypeStruct((seq_len, 2 * LANES), jnp.float32),
            jax.ShapeDtypeStruct((seq_len, 2 * LANES), jnp.bfloat16),
            jax.ShapeDtypeStruct((2, seq_len, seq_len), jnp.float32),
        ),
        in_specs=[smem, smem] + [vmem] * 6,
        out_specs=(vmem,) * 4,
        scratch_shapes=[
            pltpu.VMEM((full, LANES), jnp.bfloat16),
            pltpu.VMEM((TOP + seq_len, full), jnp.bfloat16),
            pltpu.VMEM((TOP + seq_len, full), jnp.bfloat16),
            pltpu.VMEM((TOP + seq_len, taps_q * LANES), jnp.float32),
            pltpu.VMEM((seq_len, 2 * LANES), jnp.bfloat16),
        ],
        compiler_params=pltpu.CompilerParams(vmem_limit_bytes=40 * 1024 * 1024),
        cost_estimate=LIGHT,
        name="attend_row",
    )(core, mix, own, other, since, joined, taps_forward, gain_pad)


def backward_kernel(
    taps_q, taps_k, head_size, scaling, core_ref, mix_ref, own_ref, other_ref, out_weight_ref, joined_ref,
    proj_ref, since_ref, taps_ref, gain_ref, att_ref, weights_ref,
    joined_grad_ref, mine_ref, theirs_ref, small_ref, tap_ref,
    keys_pad, grad_att, conv_grad, shifted, s_low, s_grad, since_pad, grad_ref, out_ref,
):
    seq_len = proj_ref.shape[0]
    half_len = seq_len // 2
    own_at = pl.multiple_of(core_ref[0] * half_len, half_len)
    other_at = pl.multiple_of((1 - core_ref[0]) * half_len, half_len)
    for ref, at in ((own_ref, own_at), (other_ref, other_at)):
        grad_ref[pl.ds(at, half_len), :] = lax.dot_general(
            ref[...], out_weight_ref[...], (((1,), (1,)), ((), ())), preferred_element_type=jnp.float32
        )
    blocks = seq_len // LANES
    half = (taps_k - 1) // 2
    full = seq_len + 2 * EDGE
    keys_pad[...] = jnp.zeros_like(keys_pad)
    s_low[...] = jnp.zeros_like(s_low)
    s_grad[...] = jnp.zeros_like(s_grad)
    shifted[...] = jnp.zeros_like(shifted)
    conv_grad[...] = jnp.zeros_like(conv_grad)
    since_pad[:seq_len, :] = since_ref[...]
    since_pad[seq_len:, :] = jnp.zeros((8, LANES), jnp.int32)
    small_ref[...] = jnp.zeros_like(small_ref)

    real = lax.broadcasted_iota(jnp.int32, (LANES, LANES), 1) < head_size
    for head in range(2):
        cols = slice(head * LANES, (head + 1) * LANES)
        group_sum = jnp.zeros((1, LANES), jnp.float32)
        for qi in range(blocks):
            rows = slice(qi * LANES, (qi + 1) * LANES)
            normal, scale = normalize(att_ref[rows, cols], real, head_size)
            grad = grad_ref[rows, cols]
            group_sum = group_sum + jnp.sum(grad * normal, axis=0, keepdims=True)
            lift = grad * gain_ref[:, cols]
            mean = jnp.sum(lift, axis=1, keepdims=True) * (1.0 / head_size)
            along = jnp.sum(lift * normal, axis=1, keepdims=True) * (1.0 / head_size)
            grad_att[rows, cols] = jnp.where(real, scale * (lift - mean - normal * along), 0.0).astype(jnp.bfloat16)
        small_ref[head : head + 1, :] = group_sum

    sums = [[jnp.zeros((1, LANES), jnp.float32) for _ in range(2)] for _ in range(2)]
    grad_v = [[], []]
    for qi in range(blocks):
        first = qi * LANES
        width = (qi + 1) * LANES
        rows = slice(first, first + LANES)
        maps = [weights_ref[k, rows, :width] for k in range(2)]
        grad_mixed = []
        for head in range(2):
            cols = slice(head * LANES, (head + 1) * LANES)
            values = proj_ref[:width, (4 + head) * LANES : (5 + head) * LANES]
            gm = lax.dot_general(
                grad_att[rows, cols], values, (((1,), (1,)), ((), ())), preferred_element_type=jnp.float32
            )
            grad_mixed.append(gm)
        for head in range(2):
            for k in range(2):
                part = jnp.sum(grad_mixed[head] * maps[k], axis=0, keepdims=True)
                for b in range(qi + 1):
                    sums[head][k] = sums[head][k] + part[:, b * LANES : (b + 1) * LANES]
        for k in range(2):
            grad_w = mix_ref[0, k] * grad_mixed[0] + mix_ref[1, k] * grad_mixed[1]
            inner = jnp.sum(grad_w * maps[k], axis=1, keepdims=True)
            conv_grad[k, rows, :width] = maps[k] * (grad_w - inner)
    for head in range(2):
        for k in range(2):
            small_ref[2 + 2 * head + k : 3 + 2 * head + k, :] = sums[head][k]
        cols = slice(head * LANES, (head + 1) * LANES)
        for kb in range(blocks):
            first = kb * LANES
            mixed = (
                mix_ref[head, 0] * weights_ref[0, first:, first : first + LANES]
                + mix_ref[head, 1] * weights_ref[1, first:, first : first + LANES]
            ).astype(jnp.bfloat16)
            out_ref[first : first + LANES, (4 + head) * LANES : (5 + head) * LANES] = lax.dot_general(
                mixed, grad_att[first:, cols], (((0,), (0,)), ((), ())), preferred_element_type=jnp.float32
            )

    def one_head(head, carry):
        lane = pl.multiple_of(head * LANES, LANES)
        lane_k = pl.multiple_of((head + 2) * LANES, LANES)
        keys_pad[EDGE : EDGE + seq_len, :] = proj_ref[:, pl.ds(lane_k, LANES)]
        for qi in range(blocks):
            first = qi * LANES
            width = (qi + 2) * LANES
            scores = masked_scores(
                proj_ref[first : first + LANES, pl.ds(lane, LANES)],
                keys_pad[:width, :],
                since_ref[first : first + LANES, :],
                first,
            )
            s_low[TOP + first : TOP + first + LANES, :width] = scores.astype(jnp.bfloat16)
            reach = min(width, seq_len)
            for tap in range(taps_q):
                moved = conv_grad[head, first + tap : first + tap + LANES, :reach]
                if tap > 0:
                    limit = since_pad[first + tap : first + tap + LANES, :]
                    limit = jnp.concatenate([limit] * (reach // LANES), 1)
                    moved = jnp.where(limit >= tap, moved, 0.0)
                shifted[tap, TOP + first : TOP + first + LANES, LANES : LANES + reach] = moved.astype(jnp.bfloat16)
        for m in range(blocks + 1):
            first = max(m - 1, 0) * LANES
            left = jnp.concatenate(
                [shifted[tap, TOP + first :, m * LANES : (m + 2) * LANES] for tap in range(taps_q)], 1
            )
            grad = jnp.dot(left, taps_ref[head], preferred_element_type=jnp.float32)
            rows = first + lax.broadcasted_iota(jnp.int32, grad.shape, 0)
            back = rows + EDGE - m * LANES - lax.broadcasted_iota(jnp.int32, grad.shape, 1)
            keep = (back >= 0) & (back <= since_ref[first:, :])
            s_grad[first:, m * LANES : (m + 1) * LANES] = jnp.where(keep, grad, 0.0).astype(jnp.bfloat16)
        total = jnp.zeros((2 * LANES, taps_q * LANES), jnp.float32)
        for m in range(blocks):
            first = m * LANES
            right = jnp.concatenate(
                [shifted[tap, first:, (m + 1) * LANES : (m + 2) * LANES] for tap in range(taps_q)], 1
            )
            total = total + lax.dot_general(
                s_low[first:, first : first + 2 * LANES], right, (((0,), (0,)), ((), ())),
                preferred_element_type=jnp.float32,
            )
        ridge = lax.broadcasted_iota(jnp.int32, (2 * LANES, LANES), 1) - lax.broadcasted_iota(
            jnp.int32, (2 * LANES, LANES), 0
        )
        for tap_k in range(taps_k):
            on = ridge == tap_k - EDGE - half
            for tap in range(taps_q):
                line = jnp.where(on, total[:, tap * LANES : (tap + 1) * LANES], 0.0)
                tap_ref[head, tap * taps_k + tap_k : tap * taps_k + tap_k + 1, :] = jnp.sum(line, axis=0, keepdims=True)
        for qi in range(blocks):
            first = qi * LANES
            width = (qi + 2) * LANES
            grad_q = jnp.dot(
                s_grad[first : first + LANES, :width], keys_pad[:width, :], preferred_element_type=jnp.float32
            )
            out_ref[first : first + LANES, pl.ds(lane, LANES)] = grad_q * scaling
        for kb in range(blocks):
            first = kb * LANES
            grad_k = lax.dot_general(
                s_grad[first:, first + EDGE : first + EDGE + LANES],
                proj_ref[first:, pl.ds(lane, LANES)],
                (((0,), (0,)), ((), ())),
                preferred_element_type=jnp.float32,
            )
            out_ref[first : first + LANES, pl.ds(lane_k, LANES)] = grad_k * scaling
        return carry

    lax.fori_loop(0, 2, one_head, 0)
    for at, first in ((own_at, 0), (other_at, half_len)):
        pieces = [out_ref[pl.ds(at, half_len), head * LANES : (head + 1) * LANES] for head in range(6)]
        joined = join_heads(pieces, head_size).astype(jnp.bfloat16)
        joined_grad_ref[first : first + half_len, :] = joined
        grad_in = lax.dot_general(
            joined, joined_ref[...], (((1,), (1,)), ((), ())), preferred_element_type=jnp.float32
        )
        if first:
            theirs_ref[...] = grad_in.astype(jnp.bfloat16)
        else:
            mine_ref[...] = grad_in


def attend_row_back(
    core, own, other, out_weight, joined, saved, since, mix, taps_backward, gain_pad, taps_q, taps_k, head_size
):
    projected, att, weights = saved
    seq_len = projected.shape[0]
    width = own.shape[1]
    full = seq_len + 2 * EDGE
    vmem = pl.BlockSpec(memory_space=pltpu.VMEM)
    smem = pl.BlockSpec(memory_space=pltpu.SMEM)
    return pl.pallas_call(
        functools.partial(backward_kernel, taps_q, taps_k, head_size, head_size ** (-0.5)),
        out_shape=(
            jax.ShapeDtypeStruct((seq_len, joined.shape[1]), jnp.bfloat16),
            jax.ShapeDtypeStruct((seq_len // 2, width), jnp.float32),
            jax.ShapeDtypeStruct((seq_len // 2, width), jnp.bfloat16),
            jax.ShapeDtypeStruct((8, LANES), jnp.float32),
            jax.ShapeDtypeStruct((2, taps_q * taps_k, LANES), jnp.float32),
        ),
        in_specs=[smem, smem] + [vmem] * 10,
        out_specs=(vmem,) * 5,
        scratch_shapes=[
            pltpu.VMEM((full, LANES), jnp.bfloat16),
            pltpu.VMEM((seq_len, 2 * LANES), jnp.bfloat16),
            pltpu.VMEM((2, seq_len + 8, seq_len), jnp.float32),
            pltpu.VMEM((taps_q, TOP + seq_len, seq_len + 2 * LANES), jnp.bfloat16),
            pltpu.VMEM((TOP + seq_len, full), jnp.bfloat16),
            pltpu.VMEM((seq_len, full), jnp.bfloat16),
            pltpu.VMEM((seq_len + 8, LANES), jnp.int32),
            pltpu.VMEM((seq_len, 2 * LANES), jnp.float32),
            pltpu.VMEM((seq_len, 6 * LANES), jnp.float32),
        ],
        compiler_params=pltpu.CompilerParams(vmem_limit_bytes=48 * 1024 * 1024),
        cost_estimate=LIGHT,
        name="attend_row_back",
    )(core, mix, own, other, out_weight, joined, projected, since, taps_backward, gain_pad, att, weights)


def feed_kernel(wide, own_ref, other_ref, cot_own_ref, cot_other_ref, gate_ref, cut_ref,
                hidden_ref, grads_ref, ffn_mine_ref, ffn_theirs_ref, back_mine_ref, back_theirs_ref, down_ref):
    half_len = own_ref.shape[0]
    cols = down_ref.shape[0]
    chunk = cols // wide
    blocks = down_ref.shape[1] // cols
    for z in range(wide):
        for b in range(blocks):
            first = (z * blocks + b) * chunk
            down_ref[z * chunk : (z + 1) * chunk, b * cols : (b + 1) * cols] = cut_ref[first : first + chunk, :]
    for first, ref, cot_ref in ((0, own_ref, cot_own_ref), (half_len, other_ref, cot_other_ref)):
        rows = slice(first, first + half_len)
        both = jnp.dot(ref[...], gate_ref[...], preferred_element_type=jnp.float32)
        gating, upward = both[:, :cols], both[:, cols:]
        grad = lax.dot_general(
            cot_ref[...], down_ref[...], (((1,), (1,)), ((), ())), preferred_element_type=jnp.float32
        )
        sig = 1.0 / (1.0 + jnp.exp(-gating))
        silu = gating * sig
        hidden = (silu * upward).astype(jnp.bfloat16)
        hidden_ref[rows, :] = hidden
        grads_ref[rows, :cols] = (grad * upward * (sig * (1.0 + gating * (1.0 - sig)))).astype(jnp.bfloat16)
        grads_ref[rows, cols:] = (grad * silu).astype(jnp.bfloat16)
        back = lax.dot_general(
            grads_ref[rows, :], gate_ref[...], (((1,), (1,)), ((), ())), preferred_element_type=jnp.float32
        )
        ffn = jnp.dot(hidden, down_ref[...], preferred_element_type=jnp.float32)
        if first:
            back_theirs_ref[...] = back.astype(jnp.bfloat16)
            ffn_theirs_ref[...] = ffn.astype(jnp.bfloat16)
        else:
            back_mine_ref[...] = back
            ffn_mine_ref[...] = ffn


def feed_row(own, other, cot_own, cot_other, weights, wide):
    half_len, width = own.shape
    cols = weights[1].shape[1]
    vmem = pl.BlockSpec(memory_space=pltpu.VMEM)
    return pl.pallas_call(
        functools.partial(feed_kernel, wide),
        out_shape=(
            jax.ShapeDtypeStruct((2 * half_len, cols), jnp.bfloat16),
            jax.ShapeDtypeStruct((2 * half_len, 2 * cols), jnp.bfloat16),
            jax.ShapeDtypeStruct((half_len, width), jnp.float32),
            jax.ShapeDtypeStruct((half_len, width), jnp.bfloat16),
            jax.ShapeDtypeStruct((half_len, width), jnp.float32),
            jax.ShapeDtypeStruct((half_len, width), jnp.bfloat16),
        ),
        in_specs=[vmem] * 6,
        out_specs=(vmem,) * 6,
        scratch_shapes=[pltpu.VMEM((cols, width), jnp.bfloat16)],
        compiler_params=pltpu.CompilerParams(vmem_limit_bytes=48 * 1024 * 1024),
        cost_estimate=LIGHT,
        name="feed_row",
    )(own, other, cot_own, cot_other, *weights)


def feed_grad_kernel(counts, *refs):
    lefts, grads, hiddens, cots = (
        jnp.concatenate([ref[...] for ref in refs[sum(counts[:i]) : sum(counts[: i + 1])]], 0) for i in range(4)
    )
    out_ref = refs[-1]
    chunk = hiddens.shape[1]
    cols = out_ref.shape[1] - grads.shape[1]
    out_ref[:, : grads.shape[1]] = lax.dot_general(
        lefts, grads, (((0,), (0,)), ((), ())), preferred_element_type=jnp.float32
    ).astype(jnp.bfloat16)
    down = lax.dot_general(hiddens, cots, (((0,), (0,)), ((), ())), preferred_element_type=jnp.float32)
    for b in range(down.shape[1] // cols):
        out_ref[b * chunk : (b + 1) * chunk, grads.shape[1] :] = down[:, b * cols : (b + 1) * cols].astype(jnp.bfloat16)


def feed_grad(lefts, grads, hiddens, cots, wide):
    width = lefts[0].shape[1]
    cols = hiddens[0].shape[1]
    block, chunk = width // wide, cols // wide
    if block % LANES or chunk % LANES:
        gate = lax.dot_general(
            jnp.concatenate(lefts, 0), jnp.concatenate(grads, 0), (((0,), (0,)), ((), ())),
            preferred_element_type=jnp.float32,
        )
        down = lax.dot_general(
            jnp.concatenate(hiddens, 0), jnp.concatenate(cots, 0), (((0,), (0,)), ((), ())),
            preferred_element_type=jnp.float32,
        )
        down = jnp.swapaxes(down.reshape(wide, chunk, width // cols, cols), 1, 2).reshape(width, cols)
        return jnp.concatenate([gate, down], 1).astype(jnp.bfloat16)
    count = sum(a.shape[0] for a in lefts)
    cols_out = grads[0].shape[1] + cols
    return pl.pallas_call(
        functools.partial(feed_grad_kernel, (len(lefts), len(grads), len(hiddens), len(cots))),
        out_shape=jax.ShapeDtypeStruct((width, cols_out), jnp.bfloat16),
        grid=(wide,),
        in_specs=[pl.BlockSpec((a.shape[0], block), lambda s: (0, s)) for a in lefts]
        + [pl.BlockSpec(a.shape, lambda s: (0, 0)) for a in grads]
        + [pl.BlockSpec((a.shape[0], chunk), lambda s: (0, s)) for a in hiddens]
        + [pl.BlockSpec(a.shape, lambda s: (0, 0)) for a in cots],
        out_specs=pl.BlockSpec((block, cols_out), lambda s: (s, 0)),
        compiler_params=pltpu.CompilerParams(vmem_limit_bytes=56 * 1024 * 1024),
        cost_estimate=LIGHT,
        name="feed_grad",
    )(*lefts, *grads, *hiddens, *cots)


def weight_kernel(lefts, *refs):
    left = jnp.concatenate([ref[...] for ref in refs[:lefts]], 0)
    right = jnp.concatenate([ref[...] for ref in refs[lefts:-1]], 0)
    refs[-1][...] = lax.dot_general(
        left, right, (((0,), (0,)), ((), ())), preferred_element_type=jnp.float32
    ).astype(jnp.bfloat16)


def weight_grad(lefts, rights, block, name):
    rows_out, cols_out = lefts[0].shape[1], rights[0].shape[1]
    count = sum(a.shape[0] for a in lefts)
    return pl.pallas_call(
        functools.partial(weight_kernel, len(lefts)),
        out_shape=jax.ShapeDtypeStruct((rows_out, cols_out), jnp.bfloat16),
        grid=(rows_out // block,),
        in_specs=[pl.BlockSpec((a.shape[0], block), lambda s: (0, s)) for a in lefts]
        + [pl.BlockSpec(a.shape, lambda s: (0, 0)) for a in rights],
        out_specs=pl.BlockSpec((block, cols_out), lambda s: (s, 0)),
        compiler_params=pltpu.CompilerParams(vmem_limit_bytes=48 * 1024 * 1024),
        cost_estimate=LIGHT,
        name=name,
    )(*lefts, *rights)


def halves_kernel(mine_ref, came_ref, low_ref, high_ref):
    cut = low_ref.shape[0]
    low_ref[...] = (mine_ref[:cut, :] + came_ref[:cut, :].astype(jnp.float32)).astype(jnp.bfloat16)
    high_ref[...] = (mine_ref[cut:, :] + came_ref[cut:, :].astype(jnp.float32)).astype(jnp.bfloat16)


def sum_halves(mine, came):
    half = jax.ShapeDtypeStruct((mine.shape[0] // 2, mine.shape[1]), jnp.bfloat16)
    vmem = pl.BlockSpec(memory_space=pltpu.VMEM)
    return pl.pallas_call(
        halves_kernel, out_shape=(half, half), in_specs=[vmem] * 2, out_specs=(vmem,) * 2,
        compiler_params=pltpu.CompilerParams(vmem_limit_bytes=16 * 1024 * 1024), cost_estimate=LIGHT, name="sum_halves",
    )(mine, came)


def sum_kernel(second, mine_ref, came_ref, extra_ref, out_ref):
    cut = extra_ref.shape[0]
    rows, rest = (slice(cut, 2 * cut), slice(0, cut)) if second else (slice(0, cut), slice(cut, 2 * cut))
    total = mine_ref[rows, :] + came_ref[rows, :].astype(jnp.float32) + extra_ref[...].astype(jnp.float32)
    out_ref[rows, :] = total.astype(jnp.bfloat16)
    out_ref[rest, :] = (mine_ref[rest, :] + came_ref[rest, :].astype(jnp.float32)).astype(jnp.bfloat16)


def low_sum(mine, came, extra, second):
    vmem = pl.BlockSpec(memory_space=pltpu.VMEM)
    return pl.pallas_call(
        functools.partial(sum_kernel, second), out_shape=jax.ShapeDtypeStruct(mine.shape, jnp.bfloat16),
        in_specs=[vmem] * 3, out_specs=vmem,
        compiler_params=pltpu.CompilerParams(vmem_limit_bytes=16 * 1024 * 1024), cost_estimate=LIGHT, name="low_sum",
    )(mine, came, extra)


def pair_kernel(mine_ref, came_ref, out_ref):
    out_ref[...] = (mine_ref[...] + came_ref[...].astype(jnp.float32)).astype(jnp.bfloat16)


def pair_sum(mine, came):
    vmem = pl.BlockSpec(memory_space=pltpu.VMEM)
    return pl.pallas_call(
        pair_kernel, out_shape=jax.ShapeDtypeStruct(mine.shape, jnp.bfloat16), in_specs=[vmem] * 2, out_specs=vmem,
        compiler_params=pltpu.CompilerParams(vmem_limit_bytes=16 * 1024 * 1024), cost_estimate=LIGHT, name="pair_sum",
    )(mine, came)


from jax.sharding import PartitionSpec as P

PLANE = ("narrow", "seq")
SWAP = [(0, 1), (1, 0)]


def seq_swap(array):
    return lax.ppermute(array, "seq", SWAP)


def x_swap(array):
    return lax.ppermute(array, "narrow", [(0, 1), (1, 0), (2, 3), (3, 2)])


def y_swap(array):
    return lax.ppermute(array, "narrow", [(0, 2), (2, 0), (1, 3), (3, 1)])


def diagonal_swap(array):
    return lax.ppermute(array, "narrow", [(i, i ^ 3) for i in range(4)])


def gather_plane(own):
    half = own.shape[0] // 2
    from_x = x_swap(own)
    from_y = y_swap(own)
    corner = jnp.concatenate([y_swap(from_x[:half]), x_swap(from_y[half:])], 0)
    return [(a, seq_swap(a)) for a in (own, from_x, from_y, corner)]


def after(array, *others):
    return lax.optimization_barrier((array, *others))[0] if others else array


class Steps:
    def __init__(self):
        self.ended = ()

    def hold(self, array):
        return after(array, *self.ended)

    def end(self, *arrays):
        self.ended = arrays


def half_rows(array, second):
    cut = array.shape[0] // 2
    return array[cut:] if second else array[:cut]


def whole_sum(mine, came, from_x, from_y):
    return mine + came.astype(jnp.float32) + from_x.astype(jnp.float32) + from_y.astype(jnp.float32)


def wide_shift(array, by):
    count = lax.axis_size("wide")
    return lax.ppermute(array, "wide", [(i, (i + by) % count) for i in range(count)])


def wide_block(blocks, step):
    count = lax.axis_size("wide")
    at = (lax.axis_index("wide") - step) % count
    return lax.dynamic_index_in_dim(blocks, at, 0, keepdims=False)


def wide_stack(pieces):
    whole = jnp.zeros((len(pieces),) + pieces[0].shape, pieces[0].dtype)
    for step, piece in enumerate(pieces):
        whole = lax.dynamic_update_index_in_dim(whole, piece, (lax.axis_index("wide") - step) % len(pieces), 0)
    return whole


def gather_wide(piece):
    return lax.all_gather(piece, "wide", axis=0, tiled=True)


def scatter_wide(whole):
    return lax.psum_scatter(whole, "wide", scatter_dimension=0, tiled=True)


def exchange_plane(blocks):
    line = lax.axis_index("narrow")

    def block(k):
        return lax.dynamic_index_in_dim(blocks, line ^ k, 0, keepdims=False)

    came = [block(0), x_swap(block(1)), y_swap(block(2)), diagonal_swap(block(3))]
    whole = jnp.zeros_like(blocks)
    for k in range(4):
        whole = lax.dynamic_update_index_in_dim(whole, came[k], line ^ k, 0)
    return whole


def pad_heads(array, head_size):
    heads = array.shape[1] // head_size
    split = array.reshape(array.shape[0], heads, head_size)
    return jnp.pad(split, ((0, 0), (0, 0), (0, LANES - head_size))).reshape(array.shape[0], heads * LANES)


def times(left, right):
    return jnp.dot(left, right, preferred_element_type=jnp.float32)


def norm_scale(values):
    return lax.rsqrt(jnp.mean(values * values, axis=-1, keepdims=True) + 1e-06)


def norm_back(values, scale, gain, grad):
    lift = grad * gain
    along = jnp.mean(lift * values, axis=-1, keepdims=True)
    return scale * lift - values * (scale * scale * scale * along), jnp.sum(grad * values * scale, axis=0)


def on_device(
    inputs,
    doc_start,
    norm_gain,
    qkv_weight,
    logit_kernel,
    head_mix,
    group_gain,
    out_weight,
    feed_gain,
    gate_up,
    down_weight,
    cotangent,
):
    tokens_dev, width = inputs.shape
    head_count, taps_q, taps_k = logit_kernel.shape
    head_size = width // head_count
    group_cols = 2 * head_size
    cores = lax.axis_size(PLANE)
    wide = lax.axis_size("wide")
    line = lax.axis_index("narrow")
    part = lax.axis_index(PLANE)
    chunk = gate_up.shape[1] // (2 * wide * cores)
    scaling = head_size ** (-0.5)

    core = lax.axis_index("seq").astype(jnp.int32).reshape(1)
    place = jnp.stack([line, lax.axis_index("seq"), lax.axis_index("wide")]).astype(jnp.int32)

    joined_piece = jnp.concatenate(
        [
            lax.dynamic_slice_in_dim(qkv_weight, s * width + part * group_cols, group_cols, 1)
            for s in range(3)
        ]
        + [jnp.zeros((qkv_weight.shape[0], -3 * group_cols % LANES), qkv_weight.dtype)],
        1,
    )
    joined = gather_wide(joined_piece)
    inputs, doc_start, out_weight = lax.optimization_barrier((inputs, doc_start, out_weight, joined_piece))[:3]

    flow = Steps()
    hold = flow.hold
    feed_cols = wide * chunk
    first_pos = lax.axis_index(("narrow", "wide", "seq")) * tokens_dev

    out_rows = group_cols // 4
    ring = wide == 4

    inputs_f = inputs.astype(jnp.float32)
    scale_in = norm_scale(inputs_f)
    normed = (inputs_f * scale_in * norm_gain).astype(jnp.bfloat16)
    since = first_pos + jnp.arange(tokens_dev, dtype=jnp.int32) - doc_start
    since_x, since_y, since_d = x_swap(since), y_swap(since), diagonal_swap(since)
    out_pieces = [lax.dynamic_slice_in_dim(out_weight, (lax.axis_index("seq") * 4 + line) * out_rows, out_rows, 0)]
    if ring:
        out_pieces += [wide_shift(out_pieces[0], 1), wide_shift(out_pieces[0], 2)]
    flow.end(normed, since_x, since_y, since_d, out_pieces[-1])

    normed_x, normed_y, normed_o = x_swap(hold(normed)), y_swap(hold(normed)), seq_swap(hold(normed))
    if ring:
        out_pieces.append(wide_shift(hold(out_pieces[0]), 3))
    kernels = lax.dynamic_slice_in_dim(logit_kernel, 2 * part, 2, 0)
    mix = lax.dynamic_slice_in_dim(head_mix, 2 * part, 2, 0)
    taps_forward, taps_backward = tap_bands(hold(kernels), scaling)
    gain_pad = pad_heads(lax.dynamic_slice_in_dim(group_gain, part * group_cols, group_cols, 0)[None], head_size)
    gate_piece = jnp.concatenate(
        [
            lax.dynamic_slice_in_dim(hold(gate_up), (s * cores + part) * chunk, chunk, 1)
            for s in range(2 * wide)
        ],
        1,
    )
    down_piece = lax.dynamic_slice_in_dim(hold(down_weight), part * chunk, chunk, 0)
    down_piece = jnp.concatenate(
        [down_piece[:, at : at + feed_cols] for at in range(0, width, feed_cols)], 0
    )
    since_same = jnp.stack([since, since_x, since_y, since_d])
    since_other = seq_swap(hold(since_same))
    flow.end(normed_x, normed_y, normed_o, taps_forward, gate_piece, down_piece, out_pieces[-1], since_other)

    corner_low, corner_high = y_swap(hold(half_rows(normed_x, False))), x_swap(hold(half_rows(normed_y, True)))
    normed_xo, normed_yo = seq_swap(hold(normed_x)), seq_swap(hold(normed_y))
    first = lax.axis_index("seq") == 0
    since_all = hold(
        jnp.concatenate([jnp.where(first, since_same, since_other), jnp.where(first, since_other, since_same)], 1)
    )
    since_rows = [jnp.broadcast_to(since_all[k][:, None], (2 * tokens_dev, LANES)) for k in range(4)]
    flow.end(corner_low, corner_high, normed_xo, normed_yo, *since_rows)

    normed_c = jnp.concatenate([corner_low, corner_high], 0)
    normed_co = seq_swap(hold(normed_c))
    if ring:
        out_own = exchange_plane(hold(wide_stack(out_pieces)))
    else:
        out_own = lax.dynamic_slice_in_dim(gather_wide(hold(out_weight)), part * group_cols, group_cols, 0)
    normed_rows = [(normed, normed_o), (normed_x, normed_xo), (normed_y, normed_yo), (normed_c, normed_co)]
    flow.end(normed_co, joined, out_own)

    saved, grouped_rows = [None] * 4, [None] * 4

    def attend(k):
        projected, attended, grouped_rows[k], weights = attend_row(
            hold(core), *normed_rows[k], since_rows[k], mix, joined, taps_forward, gain_pad, taps_q, head_size
        )
        saved[k] = (projected, attended, weights)

    feed_own = [gather_wide(hold(gate_piece)), gather_wide(hold(down_piece))]
    out_own = jnp.pad(
        hold(out_own).reshape(2, head_size, width), ((0, 0), (0, LANES - head_size), (0, 0))
    ).reshape(2 * LANES, width)
    branch_mine, branch_theirs = [None] * 4, [None] * 4

    def branch(k):
        branch_theirs[k] = times(hold(grouped_rows[k])[tokens_dev:], out_own).astype(jnp.bfloat16)
        branch_mine[k] = times(hold(grouped_rows[k])[:tokens_dev], out_own)

    cot_x, cot_y = x_swap(hold(cotangent)), y_swap(hold(cotangent))
    attend(3)
    flow.end(grouped_rows[3], out_own)
    branch(3)
    flow.end(branch_theirs[3], branch_mine[3])
    came_3 = seq_swap(hold(branch_theirs[3]))
    cot_o = seq_swap(hold(cotangent))
    attend(1)
    flow.end(grouped_rows[1], cot_x, cot_y, came_3, cot_o)
    low, high = sum_halves(branch_mine[3], hold(came_3))
    branch(1)
    flow.end(low, high, branch_theirs[1], branch_mine[1])
    to_y, to_x = x_swap(hold(low)), y_swap(hold(high))
    came_1, cot_xo = seq_swap(hold(branch_theirs[1])), seq_swap(hold(cot_x))
    attend(2)
    flow.end(grouped_rows[2], came_1, cot_xo, to_x, to_y)
    branch(2)
    low_x = low_sum(branch_mine[1], hold(came_1), to_x, True)
    flow.end(branch_theirs[2], branch_mine[2], low_x)
    came_2, cot_yo = seq_swap(hold(branch_theirs[2])), seq_swap(hold(cot_y))
    flow.end(came_2, cot_yo)
    low_y = low_sum(branch_mine[2], hold(came_2), to_y, False)
    flow.end(low_x, low_y)
    branch_x, branch_y = x_swap(hold(low_x)), y_swap(hold(low_y))
    attend(0)
    flow.end(grouped_rows[0], branch_x, branch_y)
    branch(0)
    flow.end(branch_theirs[0], branch_mine[0])
    came_0 = seq_swap(hold(branch_theirs[0]))
    flow.end(came_0)
    residual = inputs_f + whole_sum(branch_mine[0], hold(came_0), branch_x, branch_y)
    scale_mid = norm_scale(residual)
    normed_ffn = (residual * scale_mid * feed_gain).astype(jnp.bfloat16)
    flow.end(normed_ffn)

    ffn_x, ffn_y, ffn_o = x_swap(hold(normed_ffn)), y_swap(hold(normed_ffn)), seq_swap(hold(normed_ffn))
    flow.end(ffn_o, ffn_x, ffn_y)
    corner_low, corner_high = y_swap(hold(half_rows(ffn_x, False))), x_swap(hold(half_rows(ffn_y, True)))
    ffn_xo, ffn_yo = seq_swap(hold(ffn_x)), seq_swap(hold(ffn_y))
    flow.end(corner_low, corner_high, ffn_xo, ffn_yo)
    cot_low, cot_high = y_swap(hold(half_rows(cot_x, False))), x_swap(hold(half_rows(cot_y, True)))
    ffn_c = jnp.concatenate([corner_low, corner_high], 0)
    ffn_co = seq_swap(hold(ffn_c))
    hidden_rows, gate_grads, feed_out = [None] * 4, [None] * 4, [None] * 4
    ffn_rows = [(normed_ffn, ffn_o), (ffn_x, ffn_xo), (ffn_y, ffn_yo), (ffn_c, ffn_co)]
    cotangent_rows = [(cotangent, cot_o), (cot_x, cot_xo), (cot_y, cot_yo), None]

    def feed(k):
        hidden_rows[k], gate_grads[k], *feed_out[k] = feed_row(
            hold(ffn_rows[k][0]), ffn_rows[k][1], *cotangent_rows[k], feed_own, wide
        )

    feed(0)
    flow.end(hidden_rows[0], ffn_co, cot_low, cot_high)
    cot_c = jnp.concatenate([cot_low, cot_high], 0)
    cot_co = seq_swap(hold(cot_c))
    cotangent_rows[3] = (cot_c, cot_co)
    back_came = [None] * 4
    back_came[0] = seq_swap(hold(feed_out[0][3]))
    feed(1)
    flow.end(hidden_rows[1], cot_co, back_came[0])
    back_came[1] = seq_swap(hold(feed_out[1][3]))
    feed_came = [seq_swap(hold(feed_out[0][1])), seq_swap(hold(feed_out[1][1]))]
    feed(3)
    flow.end(hidden_rows[3], back_came[1], *feed_came)
    back_came[3] = seq_swap(hold(feed_out[3][3]))
    flow.end(back_came[3])
    low, high = sum_halves(feed_out[3][2], hold(back_came[3]))
    flow.end(low, high)
    to_y, to_x = x_swap(hold(low)), y_swap(hold(high))
    feed(2)
    flow.end(hidden_rows[2], to_x, to_y)
    back_came[2] = seq_swap(hold(feed_out[2][3]))
    feed_came.append(seq_swap(hold(feed_out[2][1])))
    low_x = low_sum(feed_out[1][2], back_came[1], hold(to_x), True)
    flow.end(back_came[2], feed_came[2], low_x)
    low_y = low_sum(feed_out[2][2], hold(back_came[2]), to_y, False)
    flow.end(low_x, low_y)
    back_x, back_y = x_swap(hold(low_x)), y_swap(hold(low_y))
    feed_grad_own = feed_grad(
        [hold(a) for k in ffn_rows for a in k], gate_grads, hidden_rows, [a for k in cotangent_rows for a in k], wide
    )
    flow.end(back_x, back_y, feed_grad_own)
    shard_feed = scatter_wide(hold(feed_grad_own))
    feed_came.append(seq_swap(hold(feed_out[3][1])))
    grad_ffn = whole_sum(feed_out[0][2], hold(back_came[0]), back_x, back_y)
    norm_part, grad_feed = norm_back(residual, scale_mid, feed_gain, grad_ffn)
    grad_residual = norm_part + cotangent.astype(jnp.float32)
    grad_branch = grad_residual.astype(jnp.bfloat16)
    flow.end(grad_branch, feed_came[3])

    gb_x, gb_y, gb_o = x_swap(hold(grad_branch)), y_swap(hold(grad_branch)), seq_swap(hold(grad_branch))
    low, high = sum_halves(feed_out[3][0], hold(feed_came[3]))
    flow.end(gb_o, low, high)
    branch_rows = [(grad_branch, gb_o), None, None, None]
    grad_joined, normed_mine, normed_theirs, smalls, tap_sums = ([None] * 4 for _ in range(5))

    def attend_back(k):
        grad_joined[k], normed_mine[k], normed_theirs[k], smalls[k], tap_sums[k] = attend_row_back(
            hold(core), *branch_rows[k], out_own, joined, saved[k], since_rows[k], mix, taps_backward, gain_pad,
            taps_q, taps_k, head_size,
        )

    attend_back(0)
    flow.end(grad_joined[0], gb_x, gb_y)
    gb_xo, gb_yo = seq_swap(hold(gb_x)), seq_swap(hold(gb_y))
    branch_rows[1], branch_rows[2] = (gb_x, gb_xo), (gb_y, gb_yo)
    flow.end(gb_xo, gb_yo)
    corner_low, corner_high = y_swap(hold(half_rows(gb_x, False))), x_swap(hold(half_rows(gb_y, True)))
    to_y, to_x = x_swap(hold(low)), y_swap(hold(high))
    attend_back(1)
    flow.end(grad_joined[1], corner_low, corner_high, to_x, to_y)
    low_x = low_sum(feed_out[1][0], feed_came[1], hold(to_x), True)
    low_y = low_sum(feed_out[2][0], feed_came[2], hold(to_y), False)
    gb_c = jnp.concatenate([corner_low, corner_high], 0)
    flow.end(low_x, low_y, gb_c)
    feed_x, feed_y = x_swap(hold(low_x)), y_swap(hold(low_y))
    gb_co = seq_swap(hold(gb_c))
    branch_rows[3] = (gb_c, gb_co)
    normed_came = [None] * 4
    normed_came[1] = seq_swap(hold(normed_theirs[1]))
    attend_back(2)
    flow.end(grad_joined[2], gb_co, normed_came[1], feed_x, feed_y)
    block_out = (residual + whole_sum(feed_out[0][0], hold(feed_came[0]), feed_x, feed_y)).astype(jnp.bfloat16)
    normed_came[2] = seq_swap(hold(normed_theirs[2]))
    grad_out_own = weight_grad(grouped_rows, [hold(a) for k in branch_rows for a in k], LANES, "out_grad")
    grad_out_own = grad_out_own.reshape(2, LANES, width)[:, :head_size].reshape(2 * head_size, width)
    low_x = pair_sum(normed_mine[1], hold(normed_came[1]))
    flow.end(normed_came[2], grad_out_own, low_x)
    low_y = pair_sum(normed_mine[2], hold(normed_came[2]))
    flow.end(low_x, low_y)
    grad_x, grad_y = x_swap(hold(low_x)), y_swap(hold(low_y))
    out_terms = hold(grad_out_own)
    if ring:
        out_terms = exchange_plane(out_terms.reshape(4, out_rows, width))
    attend_back(3)
    flow.end(grad_joined[3], grad_x, grad_y, out_terms)

    normed_came[3], normed_came[0] = seq_swap(hold(normed_theirs[3])), seq_swap(hold(normed_theirs[0]))
    flow.end(normed_came[3], normed_came[0])
    low = pair_sum(normed_mine[3], hold(normed_came[3]))
    flow.end(low)
    grad_d = diagonal_swap(hold(low))
    out_came = [out_terms]
    if ring:
        out_came = [wide_shift(hold(wide_block(out_terms, -step)), step) for step in range(1, 4)]
    joined_grad_own = weight_grad(
        [hold(a) for k in normed_rows for a in k], grad_joined, 2 * LANES, "joined_grad"
    )
    flow.end(grad_d, joined_grad_own, *out_came)
    shard_joined = scatter_wide(hold(joined_grad_own))
    if ring:
        out_sum = wide_block(out_terms, 0).astype(jnp.float32)
        for came in out_came:
            out_sum = out_sum + hold(came).astype(jnp.float32)
        shard_feed = jnp.concatenate([shard_feed, out_sum.astype(jnp.bfloat16)], 0)
    flow.end(shard_feed)
    feed_x, feed_y, feed_o = x_swap(hold(shard_feed)), y_swap(hold(shard_feed)), seq_swap(hold(shard_feed))
    grad_normed = whole_sum(normed_mine[0], normed_came[0], grad_x, grad_y) + hold(grad_d).astype(jnp.float32)
    norm_part, grad_norm = norm_back(inputs_f, scale_in, norm_gain, grad_normed)
    grad_input = norm_part + grad_residual
    small = hold(smalls[0] + smalls[1] + smalls[2] + smalls[3])
    taps = jnp.sum(tap_sums[0] + tap_sums[1] + tap_sums[2] + tap_sums[3], axis=2) * scaling

    def placed(array, total):
        array = array.reshape(-1)
        return lax.dynamic_update_slice(jnp.zeros((total,), jnp.float32), array, (part * array.shape[0],))

    pieces = [
        grad_feed,
        placed(small[:2, :head_size], width),
        placed(hold(taps), head_count * taps_q * taps_k),
        placed(jnp.sum(small[2:6], axis=1), 2 * head_count),
    ]
    lengths = [a.shape[0] for a in pieces]
    fill = -(sum(lengths) + width) % (8 * LANES)
    packed = jnp.concatenate(pieces + [jnp.zeros((fill,), jnp.float32)]).reshape(-1, LANES)
    packed = jnp.concatenate([packed, grad_norm.reshape(-1, LANES)], 0)
    flow.end(packed, feed_x, feed_y, feed_o)
    packed = packed + seq_swap(hold(packed))
    feed_low, feed_high = y_swap(hold(half_rows(feed_x, False))), x_swap(hold(half_rows(feed_y, True)))
    feed_xo, feed_yo = seq_swap(hold(feed_x)), seq_swap(hold(feed_y))
    flow.end(feed_low, feed_high, feed_xo, feed_yo, packed, shard_joined)

    def columns(rows_of, sections, size):
        if 2 * size % LANES == 0:
            return place_columns(place, [a for k in rows_of for a in k], sections, size)
        every = lax.all_gather(rows_of[0][0], PLANE, axis=0)[:, :, : sections * size]
        split = every.reshape(cores, rows_of[0][0].shape[0], sections, size)
        return jnp.moveaxis(split, 0, 2).reshape(rows_of[0][0].shape[0], -1).astype(jnp.float32)

    def wide_sums(array, hops):
        if wide & (wide - 1):
            return lax.psum(array, "wide") if 1 in hops else array
        for hop in hops:
            array = array + lax.ppermute(array, "wide", [(i, i ^ hop) for i in range(wide)])
        return array

    joined_x, joined_y, joined_o = x_swap(hold(shard_joined)), y_swap(hold(shard_joined)), seq_swap(hold(shard_joined))
    feed_c = jnp.concatenate([feed_low, feed_high], 0)
    feed_co = seq_swap(hold(feed_c))
    packed = wide_sums(hold(packed), [1])
    flow.end(joined_x, joined_y, joined_o, feed_co, packed)
    joined_low, joined_high = y_swap(hold(half_rows(joined_x, False))), x_swap(hold(half_rows(joined_y, True)))
    joined_xo, joined_yo = seq_swap(hold(joined_x)), seq_swap(hold(joined_y))
    packed = wide_sums(hold(packed), [2 << i for i in range(16) if 2 << i < wide])
    if ring:
        grad_gate, grad_down, grad_out = place_feed(
            place, [hold(shard_feed), feed_o, feed_x, feed_xo, feed_y, feed_yo, feed_c, feed_co], chunk,
            width // feed_cols,
        )
    else:
        every = lax.all_gather(shard_feed, PLANE, axis=0)
        split = every[:, :, : 2 * feed_cols].reshape(cores, shard_feed.shape[0], 2 * wide, chunk)
        grad_gate = jnp.moveaxis(split, 0, 2).reshape(shard_feed.shape[0], -1).astype(jnp.float32)
        split = every[:, :, 2 * feed_cols :].reshape(cores, width // feed_cols, chunk, feed_cols)
        grad_down = jnp.swapaxes(split, 1, 2).reshape(cores * chunk, width).astype(jnp.float32)
        grad_out = scatter_wide(lax.all_gather(out_terms, PLANE, axis=0, tiled=True)).astype(jnp.float32)
    flow.end(joined_low, joined_high, joined_xo, joined_yo, packed, grad_gate)
    joined_c = jnp.concatenate([joined_low, joined_high], 0)
    joined_co = seq_swap(hold(joined_c))
    packed = packed + x_swap(hold(packed))
    packed = packed + y_swap(packed)
    joined_rows = [(shard_joined, joined_o), (joined_x, joined_xo), (joined_y, joined_yo), (joined_c, joined_co)]
    grad_qkv = columns(joined_rows, 3, group_cols)
    packed = packed.reshape(-1)
    grad_norm = packed[-width:]
    parts = []
    for length in lengths:
        parts.append(packed[:length])
        packed = packed[length:]
    grad_feed, grad_group, grad_kernel, grad_mix = parts
    return (
        block_out,
        grad_input,
        grad_norm,
        grad_qkv,
        grad_kernel.reshape(head_count, taps_q, taps_k),
        grad_mix.reshape(head_count, 2),
        grad_group,
        grad_out,
        grad_feed,
        grad_gate,
        grad_down,
    )


def solution(mesh):
    tokens = P(("narrow", "wide", "seq"), None)
    rows = P("wide", None)
    return jax.shard_map(
        on_device,
        mesh=mesh,
        in_specs=(tokens, P(("narrow", "wide", "seq")), P(), rows, P(), P(), P(), rows, P(), rows, rows, tokens),
        out_specs=(tokens, tokens, P(), rows, P(), P(), P(), rows, P(), rows, rows),
        check_vma=False,
    )
```

time: 871 us -> 559 us (0.64)
  Pallas kernels: 65.2 us -> 179 us
  matrix products: 107 us -> 4.96 us
  other arithmetic: 118 us -> 20.3 us
  waiting for transfers between devices: 253 us -> 163 us
  local copies, waits for them, and re-layouts: 168 us -> 92.1 us
  blocking collectives: 53 us -> 0 us
    ppermute x24 -> x12, waiting for transfers between devices: 140 us -> 12.8 us  [the longest x6 8.95 us: wide_shift(): lax.ppermute(array, 'wide', [(i, (i + by) % count) for i in range(count)])]
    pallas_call x0 -> x22, Pallas kernels: none -> 92.1 us  [the longest x4 33.6 us: feed_row(): pl.pallas_call(functools.partial(feed_kernel, wide), out_shape=(jax.Shape...]
    dot_general x25 -> x0, matrix products: 65.2 us -> none  [the longest x20 41.8 us: times_back(): lax.dot_general(left, right, (((1,), (1,)), ((), ())), preferred_element_...]
    psum x1 -> x0, blocking collectives: 45.1 us -> none  [on_device(): lax.psum((grad_norm, grad_feed, placed(small[:2, :head_size], width), pla...]
    dot_general x20 -> x8, matrix products: 42 us -> 4.96 us  [times(): return jnp.dot(left, right, preferred_element_type=jnp.float32)]
    unnamed x387 -> x334, local copies, waits for them, and re-layouts: 92.9 us -> 59 us
    convert_element_type x19 -> x1, other arithmetic: 34.9 us -> 1.24 us  [on_device(): shard_feed = jnp.concatenate([shard_feed, out_sum.astype(jnp.bfloat16)], 0)]
    unnamed x31 -> x0, other arithmetic: 33 us -> none
  transfers between devices with their start and end apart: 92 -> 105, of which waited for: 30 -> 42; matrix products, arithmetic and copies ran while one was open for 37% -> 11% of each run, Pallas kernels for 8% -> 30%
where the time goes in v2:
time: 559 us; the launch traced here: 551 us
  Pallas kernels  179 us (32%)
  waiting for transfers between devices  163 us (29%)
  local copies, waits for them, and re-layouts  92.1 us (16%)
  starting transfers between devices  75.6 us (14%)
  other arithmetic  20.3 us (4%)
  between operations  15.9 us (3%)
    ppermute x23, waiting for transfers between devices, y_swap(): return lax.ppermute(array, 'narrow', [(0, 2), (2, 0), (1, 3), (3, 1)])  76.2 us
    unnamed x334, local copies, waits for them, and re-layouts  59 us
    pallas_call x4, Pallas kernels, attend_row_back(): pl.pallas_call(functools.partial(backward_kernel, taps_q, taps_k, head_si...  55.1 us
    ppermute x23, waiting for transfers between devices, x_swap(): return lax.ppermute(array, 'narrow', [(0, 1), (1, 0), (2, 3), (3, 2)])  47 us
    pallas_call x4, Pallas kernels, feed_row(): pl.pallas_call(functools.partial(feed_kernel, wide), out_shape=(jax.Shape...  33.6 us
    pallas_call x4, Pallas kernels, attend_row(): pl.pallas_call(functools.partial(forward_kernel, taps_q, head_size), out_...  32 us
    ppermute x23, starting transfers between devices, y_swap(): return lax.ppermute(array, 'narrow', [(0, 2), (2, 0), (1, 3), (3, 1)])  25.3 us
    ppermute x23, starting transfers between devices, x_swap(): return lax.ppermute(array, 'narrow', [(0, 1), (1, 0), (2, 3), (3, 2)])  24.8 us
  transfers between devices with their start and end apart: 105, of which 42 were waited for; matrix products, arithmetic and copies ran while one was open for 11% of the time, Pallas kernels for 30%

profile of v2, /device:TPU:0, one launch (start us, length us, event | category | flops | bytes accessed | tf_op | source)
XLA Modules:
  0.0 550.7 jit_solution(10193835457582369813)
XLA Ops:
  9.8 2.9 collective-permute-start
  12.7 1.5 collective-permute-start.1
  15.1 1.6 bitcast_dynamic-update-slice_fusion.9
  16.7 3.1 collective-permute-start.3
  19.8 1.6 collective-permute-start.14
  24.2 5.1 collective-permute-done.3
  29.3 1.6 collective-permute-start.5
  45.4 3.3 tap_bands.1
  50.6 3.8 collective-permute-done.7
  56.0 1.6 bitcast_dynamic-update-slice_fusion.6
  58.7 6.3 %collective-permute-done.9 = bf16[128,1536]{1,0:T(8,128)(2,1)S(1)} collective-permute-done((bf16[128,1536]{1,0:T(8,128)(2,1)S(1)}, bf16[128,1536]{1,0:T(8,128)(2,1)S(1)}, u32[]{:S(2)}, u32[]{:S(2)}) %collective-permute-start.9) | collective-permute-done | bytes 393248 | tf_op jit(solution)/shard_map/ppermute | solution.py:687
  65.0 3.7 collective-permute-done.10
  72.5 1.8 dynamic-slice_bitcast_fusion.6
  80.1 5.6 %collective-permute-done.16 = bf16[48,1536]{1,0:T(8,128)(2,1)S(1)} collective-permute-done((bf16[48,1536]{1,0:T(8,128)(2,1)S(1)}, bf16[48,1536]{1,0:T(8,128)(2,1)S(1)}, u32[]{:S(2)}, u32[]{:S(2)}) %collective-permute-start.16) | collective-permute-done | bytes 147488 | tf_op jit(solution)/shard_map/ppermute | solution.py:687
  89.3 1.5 copy-done.2
  92.0 7.6 %attend_row.4 = (bf16[512,768]{1,0:T(8,128)(2,1)S(1)}, f32[512,256]{1,0:T(8,128)S(1)}, bf16[512,256]{1,0:T(8,128)(2,1)S(1)}, f32[2,512,512]{2,1,0:T(8,128)S(1)}) custom-call(s32[1]{0:T(128)} %bitcast.core_ref, f32[2,2]{1,0:T(2,128)S(1)} %copy.30.mix_ref, bf16[256,1536]{1,0:T(8,128)(2,1)S(1)} %copy-done.25, bf16[256,1536]{1,0:T(8,128)(2,1)S(1)} %copy-done.46, ...), custom_call_target="tpu_custom_call" | custom-call | flops 1000000 | bytes 1000000 | tf_op jit(solution)/shard_map/attend_row/pallas_call | solution.py:278
  105.9 8.0 %attend_row.5 = (bf16[512,768]{1,0:T(8,128)(2,1)S(1)}, f32[512,256]{1,0:T(8,128)S(1)}, bf16[512,256]{1,0:T(8,128)(2,1)S(1)}, f32[2,512,512]{2,1,0:T(8,128)S(1)}) custom-call(s32[1]{0:T(128)} %bitcast.core_ref, f32[2,2]{1,0:T(2,128)S(1)} %copy.30.mix_ref, bf16[256,1536]{1,0:T(8,128)(2,1)} %collective-permute-done.4.own_ref.refs_2_, ...), custom_call_target="tpu_custom_call" | custom-call | flops 1000000 | bytes 1000000 | tf_op jit(solution)/shard_map/attend_row/pallas_call | solution.py:278
  115.6 7.0 %collective-permute-done.18.cot_own_ref.refs_18_ = bf16[256,1536]{1,0:T(8,128)(2,1)} collective-permute-done((bf16[256,1536]{1,0:T(8,128)(2,1)S(1)}, bf16[256,1536]{1,0:T(8,128)(2,1)}, u32[]{:S(2)}, u32[]{:S(2)}) %collective-permute-start.18) | collective-permute-done | bytes 786464 | tf_op jit(solution)/shard_map/ppermute | solution.py:683
  129.7 1.7 copy-done.5
  133.5 8.0 %attend_row.6 = (bf16[512,768]{1,0:T(8,128)(2,1)S(1)}, f32[512,256]{1,0:T(8,128)S(1)}, bf16[512,256]{1,0:T(8,128)(2,1)S(1)}, f32[2,512,512]{2,1,0:T(8,128)S(1)}) custom-call(s32[1]{0:T(128)} %bitcast.core_ref, f32[2,2]{1,0:T(2,128)S(1)} %copy.30.mix_ref, bf16[256,1536]{1,0:T(8,128)(2,1)S(1)} %copy-done.23, bf16[256,1536]{1,0:T(8,128)(2,1)S(1)} %copy-done.41, ...), custom_call_target="tpu_custom_call" | custom-call | flops 1000000 | bytes 1000000 | tf_op jit(solution)/shard_map/attend_row/pallas_call | solution.py:278
  142.3 3.2 low_sum.6
  147.6 1.8 collective-permute-done.27.cot_other_ref.refs_21_
  150.5 2.1 low_sum.7
  154.6 1.7 copy-done.6
  157.2 8.4 %attend_row.7 = (bf16[512,768]{1,0:T(8,128)(2,1)S(1)}, f32[512,256]{1,0:T(8,128)S(1)}, bf16[512,256]{1,0:T(8,128)(2,1)S(1)}, f32[2,512,512]{2,1,0:T(8,128)S(1)}) custom-call(s32[1]{0:T(128)} %bitcast.core_ref, f32[2,2]{1,0:T(2,128)S(1)} %copy.30.mix_ref, bf16[256,1536]{1,0:T(8,128)(2,1)} %fusion.2.own_ref.refs_0_, ...), custom_call_target="tpu_custom_call" | custom-call | flops 1000000 | bytes 1000000 | tf_op jit(solution)/shard_map/attend_row/pallas_call | solution.py:278
  165.7 6.7 %collective-permute-done.28 = bf16[256,1536]{1,0:T(8,128)(2,1)} collective-permute-done((bf16[256,1536]{1,0:T(8,128)(2,1)}, bf16[256,1536]{1,0:T(8,128)(2,1)}, u32[]{:S(2)}, u32[]{:S(2)}) %collective-permute-start.28) | collective-permute-done | bytes 786464 | tf_op jit(solution)/shard_map/ppermute | solution.py:683
  174.0 2.3 collective-permute-done.30
  176.3 2.0 multiply_reduce_fusion.2
  180.6 17.6 %collective-permute-done.31.own_ref.refs_2_ = bf16[256,1536]{1,0:T(8,128)(2,1)S(1)} collective-permute-done((bf16[256,1536]{1,0:T(8,128)(2,1)S(1)}, bf16[256,1536]{1,0:T(8,128)(2,1)S(1)}, u32[]{:S(2)}, u32[]{:S(2)}) %collective-permute-start.31) | collective-permute-done | bytes 786464 | tf_op jit(solution)/shard_map/ppermute | solution.py:683
  203.4 7.9 %collective-permute-done.34 = bf16[128,1536]{1,0:T(8,128)(2,1)S(1)} collective-permute-done((bf16[128,1536]{1,0:T(8,128)(2,1)S(1)}, bf16[128,1536]{1,0:T(8,128)(2,1)S(1)}, u32[]{:S(2)}, u32[]{:S(2)}) %collective-permute-start.34) | collective-permute-done | bytes 393248 | tf_op jit(solution)/shard_map/ppermute | solution.py:687
  217.4 10.6 %all-gather.6.cloned.1.call-done.gate_ref = bf16[1536,1024]{1,0:T(8,128)(2,1)} async-done(((bf16[384,1024]{1,0:T(8,128)(2,1)}), bf16[1536,1024]{1,0:T(8,128)(2,1)}) %all-gather.6.cloned.1.call-update) | async-done | bytes 3145744 | tf_op jit(solution)/shard_map/all_gather | solution.py:745
  230.3 7.7 %feed_row.4 = (bf16[512,512]{1,0:T(8,128)(2,1)S(1)}, bf16[512,1024]{1,0:T(8,128)(2,1)}, f32[256,1536]{1,0:T(8,128)}, bf16[256,1536]{1,0:T(8,128)(2,1)S(1)}, f32[...) custom-call(bf16[256,1536]{1,0:T(8,128)(2,1)S(1)} %multiply_convert_fusion.own_ref.refs_0_, ...), custom_call_target="tpu_custom_call" | custom-call | flops 1000000 | bytes 1000000 | tf_op jit(solution)/shard_map/feed_row/pallas_call | solution.py:538
  240.9 8.6 %feed_row.5 = (bf16[512,512]{1,0:T(8,128)(2,1)S(1)}, bf16[512,1024]{1,0:T(8,128)(2,1)}, f32[256,1536]{1,0:T(8,128)}, bf16[256,1536]{1,0:T(8,128)(2,1)S(1)}, f32[...) custom-call(bf16[256,1536]{1,0:T(8,128)(2,1)S(1)} %copy-done.16, bf16[256,1536]{1,0:T(8,128)(2,1)S(1)} %copy-done.35, ...), custom_call_target="tpu_custom_call" | custom-call | flops 1000000 | bytes 1000000 | tf_op jit(solution)/shard_map/feed_row/pallas_call | solution.py:538
  251.3 9.7 %feed_row.6 = (bf16[512,512]{1,0:T(8,128)(2,1)S(1)}, bf16[512,1024]{1,0:T(8,128)(2,1)}, f32[256,1536]{1,0:T(8,128)}, bf16[256,1536]{1,0:T(8,128)(2,1)}, f32[256,...) custom-call(bf16[256,1536]{1,0:T(8,128)(2,1)} %constant_dynamic-update-slice_fusion.2.own_ref.refs_6_, ...), custom_call_target="tpu_custom_call" | custom-call | flops 1000000 | bytes 1000000 | tf_op jit(solution)/shard_map/feed_row/pallas_call | solution.py:538
  262.4 1.9 collective-permute-done.46.came_ref
  265.8 1.5 collective-permute-start.48
  268.9 7.7 %feed_row.7 = (bf16[512,512]{1,0:T(8,128)(2,1)S(1)}, bf16[512,1024]{1,0:T(8,128)(2,1)}, f32[256,1536]{1,0:T(8,128)}, bf16[256,1536]{1,0:T(8,128)(2,1)S(1)}, f32[...) custom-call(bf16[256,1536]{1,0:T(8,128)(2,1)S(1)} %copy-done.18, bf16[256,1536]{1,0:T(8,128)(2,1)S(1)} %copy-done.33, ...), custom_call_target="tpu_custom_call" | custom-call | flops 1000000 | bytes 1000000 | tf_op jit(solution)/shard_map/feed_row/pallas_call | solution.py:538
  279.2 1.6 collective-permute-done.50.came_ref
  284.2 17.0 %feed_grad.1 = bf16[1536,1536]{1,0:T(8,128)(2,1)} custom-call(bf16[256,1536]{1,0:T(8,128)(2,1)} %copy-done.11, bf16[256,1536]{1,0:T(8,128)(2,1)} %copy-done.30, bf16[256,1536]{1,0:T(8,128)(2,1)} %copy-done.15, bf16[256,1536]{1,0:T(8,128)(2,1)} %copy-done.34, bf16[256,1536]{1,0:T(8,128)(2,1)} %copy-done.17, bf16[256,1536]{1,0:T(8,128)(2,1)} %copy-done.32, ...), custom_call_target="tpu_custom_call" | custom-call | flops 1000000 | bytes 1000000 | tf_op jit(solution)/shard_map/feed_grad/pallas_call | solution.py:589
  303.3 3.2 multiply_reduce_fusion
  307.8 1.5 collective-permute-start.54
  311.0 13.7 %attend_row_back.4 = (bf16[512,640]{1,0:T(8,128)(2,1)S(1)}, f32[256,1536]{1,0:T(8,128)}, bf16[256,1536]{1,0:T(8,128)(2,1)S(1)}, f32[8,128]{1,0:T(8,128)S(1)}, f32[2,66,128]{2,1,0:T(8,128)S(1)}) custom-call(s32[1]{0:T(128)} %bitcast.core_ref, f32[2,2]{1,0:T(2,128)S(1)} %copy.30.mix_ref, bf16[256,1536]{1,0:T(8,128)(2,1)S(1)} %fusion.25.own_ref.refs_4_, ...), custom_call_target="tpu_custom_call" | custom-call | flops 1000000 | bytes 1000000 | tf_op jit(solution)/shard_map/attend_row_back/pallas_call | solution.py:471
  324.7 3.1 collective-permute-done.54.own_ref.refs_6_
  329.5 1.7 collective-permute-done.58.other_ref.refs_9_
  336.4 14.0 %attend_row_back.5 = (bf16[512,640]{1,0:T(8,128)(2,1)S(1)}, f32[256,1536]{1,0:T(8,128)}, bf16[256,1536]{1,0:T(8,128)(2,1)S(1)}, f32[8,128]{1,0:T(8,128)S(1)}, f32[2,66,128]{2,1,0:T(8,128)S(1)}) custom-call(s32[1]{0:T(128)} %bitcast.core_ref, f32[2,2]{1,0:T(2,128)S(1)} %copy.30.mix_ref, bf16[256,1536]{1,0:T(8,128)(2,1)S(1)} %collective-permute-done.54.own_ref.refs_6_, ...), custom_call_target="tpu_custom_call" | custom-call | flops 1000000 | bytes 1000000 | tf_op jit(solution)/shard_map/attend_row_back/pallas_call | solution.py:471
  356.7 1.5 collective-permute-start.66
  359.6 13.7 %attend_row_back.6 = (bf16[512,640]{1,0:T(8,128)(2,1)S(1)}, f32[256,1536]{1,0:T(8,128)}, bf16[256,1536]{1,0:T(8,128)(2,1)S(1)}, f32[8,128]{1,0:T(8,128)S(1)}, f32[2,66,128]{2,1,0:T(8,128)S(1)}) custom-call(s32[1]{0:T(128)} %bitcast.core_ref, f32[2,2]{1,0:T(2,128)S(1)} %copy.30.mix_ref, bf16[256,1536]{1,0:T(8,128)(2,1)S(1)} %collective-permute-done.56.own_ref.refs_8_, ...), custom_call_target="tpu_custom_call" | custom-call | flops 1000000 | bytes 1000000 | tf_op jit(solution)/shard_map/attend_row_back/pallas_call | solution.py:471
  377.7 4.3 out_grad.1
  385.0 2.4 collective-permute-start.72
  388.5 13.7 %attend_row_back.7 = (bf16[512,640]{1,0:T(8,128)(2,1)S(1)}, f32[256,1536]{1,0:T(8,128)}, bf16[256,1536]{1,0:T(8,128)(2,1)S(1)}, f32[8,128]{1,0:T(8,128)S(1)}, f32[2,66,128]{2,1,0:T(8,128)S(1)}) custom-call(s32[1]{0:T(128)} %bitcast.core_ref, f32[2,2]{1,0:T(2,128)S(1)} %copy.30.mix_ref, bf16[256,1536]{1,0:T(8,128)(2,1)S(1)} %copy-done.21, ...), custom_call_target="tpu_custom_call" | custom-call | flops 1000000 | bytes 1000000 | tf_op jit(solution)/shard_map/attend_row_back/pallas_call | solution.py:471
  402.3 7.3 %collective-permute-done.69 = bf16[256,1536]{1,0:T(8,128)(2,1)S(1)} collective-permute-done((bf16[256,1536]{1,0:T(8,128)(2,1)S(1)}, bf16[256,1536]{1,0:T(8,128)(2,1)S(1)}, u32[]{:S(2)}, u32[]{:S(2)}) %collective-permute-start.69) | collective-permute-done | bytes 786464 | tf_op jit(solution)/shard_map/ppermute | solution.py:687
  410.2 1.8 collective-permute-done.73
  416.2 1.8 dynamic-slice_bitcast_fusion.1
  419.6 3.4 collective-permute-start.78
  426.3 9.0 %joined_grad.1 = bf16[1536,640]{1,0:T(8,128)(2,1)} custom-call(bf16[256,1536]{1,0:T(8,128)(2,1)} %fusion.2.own_ref.refs_0_, bf16[256,1536]{1,0:T(8,128)(2,1)} %collective-permute-done.6.other_ref.refs_1_, bf16[256,1536]{1,0:T(8,128)(2,1)} %collective-permute-done.4.own_ref.refs_2_, bf16[256,1536]{1,0:T(8,128)(2,1)S(1)} %copy-done.44, ...), custom_call_target="tpu_custom_call" | custom-call | flops 1000000 | bytes 1000000 | tf_op jit(solution)/shard_map/joined_grad/pallas_call | solution.py:615
  442.1 4.1 fusion.7
  446.2 22.7 %collective-permute-done.80.refs_4_.refs_12_ = bf16[432,1536]{1,0:T(8,128)(2,1)} collective-permute-done((bf16[432,1536]{1,0:T(8,128)(2,1)S(1)}, bf16[432,1536]{1,0:T(8,128)(2,1)}, u32[]{:S(2)}, u32[]{:S(2)}) %collective-permute-start.80) | collective-permute-done | bytes 1327136 | tf_op jit(solution)/shard_map/ppermute | solution.py:687
  476.0 12.6 %collective-permute-done.83 = bf16[216,1536]{1,0:T(8,128)(2,1)S(1)} collective-permute-done((bf16[216,1536]{1,0:T(8,128)(2,1)S(1)}, bf16[216,1536]{1,0:T(8,128)(2,1)S(1)}, u32[]{:S(2)}, u32[]{:S(2)}) %collective-permute-start.83) | collective-permute-done | bytes 663584 | tf_op jit(solution)/shard_map/ppermute | solution.py:687
  493.3 3.8 collective-permute-done.87
  497.1 7.9 %collective-permute-done.89.refs_4_ = bf16[384,640]{1,0:T(8,128)(2,1)S(1)} collective-permute-done((bf16[384,640]{1,0:T(8,128)(2,1)}, bf16[384,640]{1,0:T(8,128)(2,1)S(1)}, u32[]{:S(2)}, u32[]{:S(2)}) %collective-permute-start.89) | collective-permute-done | bytes 491552 | tf_op jit(solution)/shard_map/ppermute | solution.py:687
  511.9 11.7 %place_feed.1 = (f32[384,8192]{1,0:T(8,128)}, f32[1024,1536]{1,0:T(8,128)}, f32[384,1536]{1,0:T(8,128)}) custom-call(s32[3]{0:T(128)S(1)} %pad_add_fusion.2.where_ref, bf16[432,1536]{1,0:T(8,128)(2,1)S(1)} %pad_maximum_fusion.refs_0_.refs_8_, bf16[432,1536]{1,0:T(8,128)(2,1)} %collective-permute-done.81.refs_1_.refs_9_, ...), custom_call_target="tpu_custom_call" | custom-call | flops 1000000 | bytes 1000000 | tf_op jit(solution)/shard_map/place_feed/pallas_call | solution.py:125
  524.6 3.1 collective-permute-done.97
  528.3 4.2 fusion.5
  538.5 5.4 place_columns.1
  (623 shorter events, 166.0 us)
Async XLA Ops:
  7.2 80.8 %all-gather.4.cloned.1.call-start = ((), (), s32[]{:S(2)}) async-start(), calls=%async_computation.2 | async-start | bytes 2457600 | tf_op jit(solution)/shard_map/all_gather | solution.py:745
  9.8 14.4 %collective-permute-start = (s32[256]{0:T(256)S(1)}, s32[256]{0:T(256)S(1)}, u32[]{:S(2)}, u32[]{:S(2)}) collective-permute-start(s32[256]{0:T(256)S(1)} %add_subtract_fusion), channel_id=1, source_target_pairs={{0,8},{8,0},{16,24},{24,16},{1,9},{9,1},{17,25},{25,17},{2,10},{10... | collective-permute-start | bytes 3080 | tf_op jit(solution)/shard_map/ppermute | solution.py:683
  19.8 21.5 %collective-permute-start.14 = (bf16[48,1536]{1,0:T(8,128)(2,1)}, bf16[48,1536]{1,0:T(8,128)(2,1)S(1)}, u32[]{:S(2)}, u32[]{:S(2)}) collective-permute-start(bf16[48,1536]{1,0:T(8,128)(2,1)} %get-tuple-element.241), channel_id=1, source_target_pairs={{0,2},{2,4},{4,6},{6,0},{1,3},{3,5},{5,7},{7,1},{8,10},{10,12},{12... | collective-permute-start | bytes 442376 | tf_op jit(solution)/shard_map/ppermute | solution.py:728
  21.4 196.1 %all-gather.8.cloned.1.call-start = ((), (), s32[]{:S(2)}) async-start(), calls=%async_computation.4 | async-start | bytes 1966080 | tf_op jit(solution)/shard_map/all_gather | solution.py:745
  29.3 25.1 %collective-permute-start.5 = (bf16[256,1536]{1,0:T(8,128)(2,1)}, bf16[256,1536]{1,0:T(8,128)(2,1)S(1)}, u32[]{:S(2)}, u32[]{:S(2)}) collective-permute-start(bf16[256,1536]{1,0:T(8,128)(2,1)} %fusion.2.own_ref.refs_0_), channel_id=1, source_target_pairs={{0,16},{16,0},{8,24},{24,8},{1,17},{17,1},{9,25},{25,9},{2,18},{18... | collective-permute-start | bytes 2359304 | tf_op jit(solution)/shard_map/ppermute | solution.py:687
  30.9 18.4 %collective-permute-start.4 = (bf16[256,1536]{1,0:T(8,128)(2,1)}, bf16[256,1536]{1,0:T(8,128)(2,1)}, u32[]{:S(2)}, u32[]{:S(2)}) collective-permute-start(bf16[256,1536]{1,0:T(8,128)(2,1)} %fusion.2.own_ref.refs_0_), channel_id=1, source_target_pairs={{0,8},{8,0},{16,24},{24,16},{1,9},{9,1},{17,25},{25,17},{2,10},{10... | collective-permute-start | bytes 2359304 | tf_op jit(solution)/shard_map/ppermute | solution.py:683
  32.4 22.0 %collective-permute-start.6 = (bf16[256,1536]{1,0:T(8,128)(2,1)}, bf16[256,1536]{1,0:T(8,128)(2,1)}, u32[]{:S(2)}, u32[]{:S(2)}) collective-permute-start(bf16[256,1536]{1,0:T(8,128)(2,1)} %fusion.2.own_ref.refs_0_), channel_id=1, source_target_pairs={{0,1},{1,0},{2,3},{3,2},{4,5},{5,4},{6,7},{7,6},{8,9},{9,8},{10,11... | collective-permute-start | bytes 2359304 | tf_op jit(solution)/shard_map/ppermute | solution.py:679
  32.4 16.2 %collective-permute-start.8 = (s32[4,256]{1,0:T(4,128)S(1)}, s32[4,256]{1,0:T(4,128)S(1)}, u32[]{:S(2)}, u32[]{:S(2)}) collective-permute-start(s32[4,256]{1,0:T(4,128)S(1)} %pad_add_fusion.1), channel_id=1, source_target_pairs={{0,1},{1,0},{2,3},{3,2},{4,5},{5,4},{6,7},{7,6},{8,9},{9,8},{10,11... | collective-permute-start | bytes 12296 | tf_op jit(solution)/shard_map/ppermute | solution.py:679
  55.5 13.2 %collective-permute-start.12 = (bf16[256,1536]{1,0:T(8,128)(2,1)S(1)}, bf16[256,1536]{1,0:T(8,128)(2,1)S(1)}, u32[]{:S(2)}, u32[]{:S(2)}) collective-permute-start(bf16[256,1536]{1,0:T(8,128)(2,1)S(1)} %collective-permute-done.5.own_ref.refs_4_), channel_id=1, source_target_pairs={{0,1},{1,0},{2,3},{3,2},{4,5},{5,4},{6,7},{7,6},{8,9},{9,8},{10,11... | collective-permute-start | bytes 2359304 | tf_op jit(solution)/shard_map/ppermute | solution.py:679
  55.5 13.2 %collective-permute-start.11 = (bf16[256,1536]{1,0:T(8,128)(2,1)}, bf16[256,1536]{1,0:T(8,128)(2,1)S(1)}, u32[]{:S(2)}, u32[]{:S(2)}) collective-permute-start(bf16[256,1536]{1,0:T(8,128)(2,1)} %collective-permute-done.4.own_ref.refs_2_), channel_id=1, source_target_pairs={{0,1},{1,0},{2,3},{3,2},{4,5},{5,4},{6,7},{7,6},{8,9},{9,8},{10,11... | collective-permute-start | bytes 2359304 | tf_op jit(solution)/shard_map/ppermute | solution.py:679
  103.3 19.3 %collective-permute-start.18 = (bf16[256,1536]{1,0:T(8,128)(2,1)S(1)}, bf16[256,1536]{1,0:T(8,128)(2,1)}, u32[]{:S(2)}, u32[]{:S(2)}) collective-permute-start(bf16[256,1536]{1,0:T(8,128)(2,1)S(1)} %copy-done.8), channel_id=1, source_target_pairs={{0,8},{8,0},{16,24},{24,16},{1,9},{9,1},{17,25},{25,17},{2,10},{10... | collective-permute-start | bytes 2359304 | tf_op jit(solution)/shard_map/ppermute | solution.py:683
  104.3 18.9 %collective-permute-start.19 = (bf16[256,1536]{1,0:T(8,128)(2,1)S(1)}, bf16[256,1536]{1,0:T(8,128)(2,1)S(1)}, u32[]{:S(2)}, u32[]{:S(2)}) collective-permute-start(bf16[256,1536]{1,0:T(8,128)(2,1)S(1)} %copy-done.8), channel_id=1, source_target_pairs={{0,16},{16,0},{8,24},{24,8},{1,17},{17,1},{9,25},{25,9},{2,18},{18... | collective-permute-start | bytes 2359304 | tf_op jit(solution)/shard_map/ppermute | solution.py:687
  105.4 17.9 %collective-permute-start.20 = (bf16[256,1536]{1,0:T(8,128)(2,1)S(1)}, bf16[256,1536]{1,0:T(8,128)(2,1)S(1)}, u32[]{:S(2)}, u32[]{:S(2)}) collective-permute-start(bf16[256,1536]{1,0:T(8,128)(2,1)S(1)} %convolution_convert_fusion.3), channel_id=1, source_target_pairs={{0,1},{1,0},{2,3},{3,2},{4,5},{5,4},{6,7},{7,6},{8,9},{9,8},{10,11... | collective-permute-start | bytes 2359304 | tf_op jit(solution)/shard_map/ppermute | solution.py:679
  127.1 15.2 %collective-permute-start.23 = (bf16[256,1536]{1,0:T(8,128)(2,1)}, bf16[256,1536]{1,0:T(8,128)(2,1)}, u32[]{:S(2)}, u32[]{:S(2)}) collective-permute-start(bf16[256,1536]{1,0:T(8,128)(2,1)} %collective-permute-done.18.cot_own_ref.refs_18_), channel_id=1, source_target_pairs={{0,1},{1,0},{2,3},{3,2},{4,5},{5,4},{6,7},{7,6},{8,9},{9,8},{10,11... | collective-permute-start | bytes 2359304 | tf_op jit(solution)/shard_map/ppermute | solution.py:679
  127.1 15.2 %collective-permute-start.22 = (bf16[256,1536]{1,0:T(8,128)(2,1)}, bf16[256,1536]{1,0:T(8,128)(2,1)}, u32[]{:S(2)}, u32[]{:S(2)}) collective-permute-start(bf16[256,1536]{1,0:T(8,128)(2,1)} %convolution_convert_fusion.2), channel_id=1, source_target_pairs={{0,1},{1,0},{2,3},{3,2},{4,5},{5,4},{6,7},{7,6},{8,9},{9,8},{10,11... | collective-permute-start | bytes 2359304 | tf_op jit(solution)/shard_map/ppermute | solution.py:679
  127.6 14.7 %collective-permute-start.25 = (bf16[128,1536]{1,0:T(8,128)(2,1)}, bf16[128,1536]{1,0:T(8,128)(2,1)}, u32[]{:S(2)}, u32[]{:S(2)}) collective-permute-start(bf16[128,1536]{1,0:T(8,128)(2,1)} %get-tuple-element.268), channel_id=1, source_target_pairs={{0,8},{8,0},{16,24},{24,16},{1,9},{9,1},{17,25},{25,17},{2,10},{10... | collective-permute-start | bytes 1179656 | tf_op jit(solution)/shard_map/ppermute | solution.py:683
  128.6 13.7 %collective-permute-start.24 = (bf16[128,1536]{1,0:T(8,128)(2,1)}, bf16[128,1536]{1,0:T(8,128)(2,1)}, u32[]{:S(2)}, u32[]{:S(2)}) collective-permute-start(bf16[128,1536]{1,0:T(8,128)(2,1)} %get-tuple-element.267), channel_id=1, source_target_pairs={{0,16},{16,0},{8,24},{24,8},{1,17},{17,1},{9,25},{25,9},{2,18},{18... | collective-permute-start | bytes 1179656 | tf_op jit(solution)/shard_map/ppermute | solution.py:687
  129.6 98.4 %all-gather.6.cloned.1.call-start = ((), (), s32[]{:S(2)}) async-start(), calls=%async_computation.3 | async-start | bytes 3932160 | tf_op jit(solution)/shard_map/all_gather | solution.py:745
  152.5 19.9 %collective-permute-start.28 = (bf16[256,1536]{1,0:T(8,128)(2,1)}, bf16[256,1536]{1,0:T(8,128)(2,1)}, u32[]{:S(2)}, u32[]{:S(2)}) collective-permute-start(bf16[256,1536]{1,0:T(8,128)(2,1)} %low_sum.6), channel_id=1, source_target_pairs={{0,8},{8,0},{16,24},{24,16},{1,9},{9,1},{17,25},{25,17},{2,10},{10... | collective-permute-start | bytes 2359304 | tf_op jit(solution)/shard_map/ppermute | solution.py:683
  153.5 19.6 %collective-permute-start.29 = (bf16[256,1536]{1,0:T(8,128)(2,1)}, bf16[256,1536]{1,0:T(8,128)(2,1)}, u32[]{:S(2)}, u32[]{:S(2)}) collective-permute-start(bf16[256,1536]{1,0:T(8,128)(2,1)} %low_sum.7), channel_id=1, source_target_pairs={{0,16},{16,0},{8,24},{24,8},{1,17},{17,1},{9,25},{25,9},{2,18},{18... | collective-permute-start | bytes 2359304 | tf_op jit(solution)/shard_map/ppermute | solution.py:687
  154.6 282.7 %reduce-scatter.3.cloned.1.call-start = ((), (), s32[]{:S(2)}) async-start(), calls=%async_computation.5 | async-start | bytes 5898240 | tf_op jit(solution)/shard_map/reduce_scatter | solution.py:749
  178.5 19.6 %collective-permute-start.31 = (bf16[256,1536]{1,0:T(8,128)(2,1)S(1)}, bf16[256,1536]{1,0:T(8,128)(2,1)S(1)}, u32[]{:S(2)}, u32[]{:S(2)}) collective-permute-start(bf16[256,1536]{1,0:T(8,128)(2,1)S(1)} %multiply_convert_fusion.own_ref.refs_0_), channel_id=1, source_target_pairs={{0,8},{8,0},{16,24},{24,16},{1,9},{9,1},{17,25},{25,17},{2,10},{10... | collective-permute-start | bytes 2359304 | tf_op jit(solution)/shard_map/ppermute | solution.py:683
  179.7 18.5 %collective-permute-start.32 = (bf16[256,1536]{1,0:T(8,128)(2,1)S(1)}, bf16[256,1536]{1,0:T(8,128)(2,1)S(1)}, u32[]{:S(2)}, u32[]{:S(2)}) collective-permute-start(bf16[256,1536]{1,0:T(8,128)(2,1)S(1)} %multiply_convert_fusion.own_ref.refs_0_), channel_id=1, source_target_pairs={{0,1},{1,0},{2,3},{3,2},{4,5},{5,4},{6,7},{7,6},{8,9},{9,8},{10,11... | collective-permute-start | bytes 2359304 | tf_op jit(solution)/shard_map/ppermute | solution.py:679
  179.7 20.0 %collective-permute-start.33 = (bf16[256,1536]{1,0:T(8,128)(2,1)S(1)}, bf16[256,1536]{1,0:T(8,128)(2,1)S(1)}, u32[]{:S(2)}, u32[]{:S(2)}) collective-permute-start(bf16[256,1536]{1,0:T(8,128)(2,1)S(1)} %multiply_convert_fusion.own_ref.refs_0_), channel_id=1, source_target_pairs={{0,16},{16,0},{8,24},{24,8},{1,17},{17,1},{9,25},{25,9},{2,18},{18... | collective-permute-start | bytes 2359304 | tf_op jit(solution)/shard_map/ppermute | solution.py:687
  199.6 13.3 %collective-permute-start.36 = (bf16[256,1536]{1,0:T(8,128)(2,1)S(1)}, bf16[256,1536]{1,0:T(8,128)(2,1)S(1)}, u32[]{:S(2)}, u32[]{:S(2)}) collective-permute-start(bf16[256,1536]{1,0:T(8,128)(2,1)S(1)} %collective-permute-done.31.own_ref.refs_2_), channel_id=1, source_target_pairs={{0,1},{1,0},{2,3},{3,2},{4,5},{5,4},{6,7},{7,6},{8,9},{9,8},{10,11... | collective-permute-start | bytes 2359304 | tf_op jit(solution)/shard_map/ppermute | solution.py:679
  213.9 24.2 %collective-permute-start.39 = (bf16[128,1536]{1,0:T(8,128)(2,1)S(1)}, bf16[128,1536]{1,0:T(8,128)(2,1)}, u32[]{:S(2)}, u32[]{:S(2)}) collective-permute-start(bf16[128,1536]{1,0:T(8,128)(2,1)S(1)} %slice.174), channel_id=1, source_target_pairs={{0,16},{16,0},{8,24},{24,8},{1,17},{17,1},{9,25},{25,9},{2,18},{18... | collective-permute-start | bytes 1179656 | tf_op jit(solution)/shard_map/ppermute | solution.py:687
  215.7 24.6 %collective-permute-start.38 = (bf16[256,1536]{1,0:T(8,128)(2,1)}, bf16[256,1536]{1,0:T(8,128)(2,1)}, u32[]{:S(2)}, u32[]{:S(2)}) collective-permute-start(bf16[256,1536]{1,0:T(8,128)(2,1)} %constant_dynamic-update-slice_fusion.2.own_ref.refs_6_), channel_id=1, source_target_pairs={{0,1},{1,0},{2,3},{3,2},{4,5},{5,4},{6,7},{7,6},{8,9},{9,8},{10,11... | collective-permute-start | bytes 2359304 | tf_op jit(solution)/shard_map/ppermute | solution.py:679
  216.5 22.8 %collective-permute-start.40 = (bf16[128,1536]{1,0:T(8,128)(2,1)}, bf16[128,1536]{1,0:T(8,128)(2,1)}, u32[]{:S(2)}, u32[]{:S(2)}) collective-permute-start(bf16[128,1536]{1,0:T(8,128)(2,1)} %slice.175), channel_id=1, source_target_pairs={{0,8},{8,0},{16,24},{24,16},{1,9},{9,1},{17,25},{25,17},{2,10},{10... | collective-permute-start | bytes 1179656 | tf_op jit(solution)/shard_map/ppermute | solution.py:683
  282.1 19.8 %collective-permute-start.51 = (bf16[256,1536]{1,0:T(8,128)(2,1)S(1)}, bf16[256,1536]{1,0:T(8,128)(2,1)}, u32[]{:S(2)}, u32[]{:S(2)}) collective-permute-start(bf16[256,1536]{1,0:T(8,128)(2,1)S(1)} %low_sum.8), channel_id=1, source_target_pairs={{0,8},{8,0},{16,24},{24,16},{1,9},{9,1},{17,25},{25,17},{2,10},{10... | collective-permute-start | bytes 2359304 | tf_op jit(solution)/shard_map/ppermute | solution.py:683
  282.7 19.4 %collective-permute-start.52 = (bf16[256,1536]{1,0:T(8,128)(2,1)S(1)}, bf16[256,1536]{1,0:T(8,128)(2,1)}, u32[]{:S(2)}, u32[]{:S(2)}) collective-permute-start(bf16[256,1536]{1,0:T(8,128)(2,1)S(1)} %low_sum.9), channel_id=1, source_target_pairs={{0,16},{16,0},{8,24},{24,8},{1,17},{17,1},{9,25},{25,9},{2,18},{18... | collective-permute-start | bytes 2359304 | tf_op jit(solution)/shard_map/ppermute | solution.py:687
  302.1 188.9 %reduce-scatter.5.cloned.1.call-start = ((), (), s32[]{:S(2)}) async-start(), calls=%async_computation.6 | async-start | bytes 2457600 | tf_op jit(solution)/shard_map/reduce_scatter | solution.py:749
  307.8 20.0 %collective-permute-start.54 = (bf16[256,1536]{1,0:T(8,128)(2,1)S(1)}, bf16[256,1536]{1,0:T(8,128)(2,1)S(1)}, u32[]{:S(2)}, u32[]{:S(2)}) collective-permute-start(bf16[256,1536]{1,0:T(8,128)(2,1)S(1)} %fusion.25.own_ref.refs_4_), channel_id=1, source_target_pairs={{0,8},{8,0},{16,24},{24,16},{1,9},{9,1},{17,25},{25,17},{2,10},{10... | collective-permute-start | bytes 2359304 | tf_op jit(solution)/shard_map/ppermute | solution.py:683
  309.3 19.6 %collective-permute-start.56 = (bf16[256,1536]{1,0:T(8,128)(2,1)S(1)}, bf16[256,1536]{1,0:T(8,128)(2,1)S(1)}, u32[]{:S(2)}, u32[]{:S(2)}) collective-permute-start(bf16[256,1536]{1,0:T(8,128)(2,1)S(1)} %fusion.25.own_ref.refs_4_), channel_id=1, source_target_pairs={{0,16},{16,0},{8,24},{24,8},{1,17},{17,1},{9,25},{25,9},{2,18},{18... | collective-permute-start | bytes 2359304 | tf_op jit(solution)/shard_map/ppermute | solution.py:687
  332.4 19.5 %collective-permute-start.61 = (bf16[128,1536]{1,0:T(8,128)(2,1)S(1)}, bf16[128,1536]{1,0:T(8,128)(2,1)S(1)}, u32[]{:S(2)}, u32[]{:S(2)}) collective-permute-start(bf16[128,1536]{1,0:T(8,128)(2,1)S(1)} %slice.177), channel_id=1, source_target_pairs={{0,8},{8,0},{16,24},{24,16},{1,9},{9,1},{17,25},{25,17},{2,10},{10... | collective-permute-start | bytes 1179656 | tf_op jit(solution)/shard_map/ppermute | solution.py:683
  332.9 19.0 %collective-permute-start.60 = (bf16[128,1536]{1,0:T(8,128)(2,1)S(1)}, bf16[128,1536]{1,0:T(8,128)(2,1)S(1)}, u32[]{:S(2)}, u32[]{:S(2)}) collective-permute-start(bf16[128,1536]{1,0:T(8,128)(2,1)S(1)} %slice.176), channel_id=1, source_target_pairs={{0,16},{16,0},{8,24},{24,8},{1,17},{17,1},{9,25},{25,9},{2,18},{18... | collective-permute-start | bytes 1179656 | tf_op jit(solution)/shard_map/ppermute | solution.py:687
  334.4 17.5 %collective-permute-start.62 = (bf16[128,1536]{1,0:T(8,128)(2,1)S(1)}, bf16[128,1536]{1,0:T(8,128)(2,1)S(1)}, u32[]{:S(2)}, u32[]{:S(2)}) collective-permute-start(bf16[128,1536]{1,0:T(8,128)(2,1)S(1)} %get-tuple-element.363), channel_id=1, source_target_pairs={{0,8},{8,0},{16,24},{24,16},{1,9},{9,1},{17,25},{25,17},{2,10},{10... | collective-permute-start | bytes 1179656 | tf_op jit(solution)/shard_map/ppermute | solution.py:683
  335.9 17.1 %collective-permute-start.59 = (bf16[128,1536]{1,0:T(8,128)(2,1)S(1)}, bf16[128,1536]{1,0:T(8,128)(2,1)S(1)}, u32[]{:S(2)}, u32[]{:S(2)}) collective-permute-start(bf16[128,1536]{1,0:T(8,128)(2,1)S(1)} %get-tuple-element.355), channel_id=1, source_target_pairs={{0,16},{16,0},{8,24},{24,8},{1,17},{17,1},{9,25},{25,9},{2,18},{18... | collective-permute-start | bytes 1179656 | tf_op jit(solution)/shard_map/ppermute | solution.py:687
  356.7 18.9 %collective-permute-start.66 = (bf16[256,1536]{1,0:T(8,128)(2,1)S(1)}, bf16[256,1536]{1,0:T(8,128)(2,1)}, u32[]{:S(2)}, u32[]{:S(2)}) collective-permute-start(bf16[256,1536]{1,0:T(8,128)(2,1)S(1)} %low_sum.11), channel_id=1, source_target_pairs={{0,16},{16,0},{8,24},{24,8},{1,17},{17,1},{9,25},{25,9},{2,18},{18... | collective-permute-start | bytes 2359304 | tf_op jit(solution)/shard_map/ppermute | solution.py:687
  358.3 18.5 %collective-permute-start.65 = (bf16[256,1536]{1,0:T(8,128)(2,1)S(1)}, bf16[256,1536]{1,0:T(8,128)(2,1)}, u32[]{:S(2)}, u32[]{:S(2)}) collective-permute-start(bf16[256,1536]{1,0:T(8,128)(2,1)S(1)} %low_sum.10), channel_id=1, source_target_pairs={{0,8},{8,0},{16,24},{24,16},{1,9},{9,1},{17,25},{25,17},{2,10},{10... | collective-permute-start | bytes 2359304 | tf_op jit(solution)/shard_map/ppermute | solution.py:683
  359.0 17.8 %collective-permute-start.63 = (bf16[256,1536]{1,0:T(8,128)(2,1)S(1)}, bf16[256,1536]{1,0:T(8,128)(2,1)S(1)}, u32[]{:S(2)}, u32[]{:S(2)}) collective-permute-start(bf16[256,1536]{1,0:T(8,128)(2,1)S(1)} %constant_dynamic-update-slice_fusion.6.refs_10_.own_ref), channel_id=1, source_target_pairs={{0,1},{1,0},{2,3},{3,2},{4,5},{5,4},{6,7},{7,6},{8,9},{9,8},{10,11... | collective-permute-start | bytes 2359304 | tf_op jit(solution)/shard_map/ppermute | solution.py:679
  359.0 17.8 %collective-permute-start.64 = (bf16[256,1536]{1,0:T(8,128)(2,1)S(1)}, bf16[256,1536]{1,0:T(8,128)(2,1)S(1)}, u32[]{:S(2)}, u32[]{:S(2)}) collective-permute-start(bf16[256,1536]{1,0:T(8,128)(2,1)S(1)} %copy-done.118), channel_id=1, source_target_pairs={{0,1},{1,0},{2,3},{3,2},{4,5},{5,4},{6,7},{7,6},{8,9},{9,8},{10,11... | collective-permute-start | bytes 2359304 | tf_op jit(solution)/shard_map/ppermute | solution.py:679
  383.8 18.4 %collective-permute-start.70 = (bf16[48,1536]{1,0:T(8,128)(2,1)S(1)}, bf16[48,1536]{1,0:T(8,128)(2,1)S(1)}, u32[]{:S(2)}, u32[]{:S(2)}) collective-permute-start(bf16[48,1536]{1,0:T(8,128)(2,1)S(1)} %get-tuple-element.489), channel_id=1, source_target_pairs={{0,8},{8,0},{16,24},{24,16},{1,9},{9,1},{17,25},{25,17},{2,10},{10... | collective-permute-start | bytes 442376 | tf_op jit(solution)/shard_map/ppermute | solution.py:683
  384.4 17.8 %collective-permute-start.71 = (bf16[48,1536]{1,0:T(8,128)(2,1)S(1)}, bf16[48,1536]{1,0:T(8,128)(2,1)S(1)}, u32[]{:S(2)}, u32[]{:S(2)}) collective-permute-start(bf16[48,1536]{1,0:T(8,128)(2,1)S(1)} %get-tuple-element.488), channel_id=1, source_target_pairs={{0,16},{16,0},{8,24},{24,8},{1,17},{17,1},{9,25},{25,9},{2,18},{18... | collective-permute-start | bytes 442376 | tf_op jit(solution)/shard_map/ppermute | solution.py:687
  385.0 17.3 %collective-permute-start.72 = (bf16[48,1536]{1,0:T(8,128)(2,1)S(1)}, bf16[48,1536]{1,0:T(8,128)(2,1)S(1)}, u32[]{:S(2)}, u32[]{:S(2)}) collective-permute-start(bf16[48,1536]{1,0:T(8,128)(2,1)S(1)} %get-tuple-element.487), channel_id=1, source_target_pairs={{0,24},{8,16},{16,8},{24,0},{1,25},{9,17},{17,9},{25,1},{2,26},{10... | collective-permute-start | bytes 442376 | tf_op jit(solution)/shard_map/ppermute | solution.py:691
  387.3 22.3 %collective-permute-start.69 = (bf16[256,1536]{1,0:T(8,128)(2,1)S(1)}, bf16[256,1536]{1,0:T(8,128)(2,1)S(1)}, u32[]{:S(2)}, u32[]{:S(2)}) collective-permute-start(bf16[256,1536]{1,0:T(8,128)(2,1)S(1)} %pair_sum.4), channel_id=1, source_target_pairs={{0,16},{16,0},{8,24},{24,8},{1,17},{17,1},{9,25},{25,9},{2,18},{18... | collective-permute-start | bytes 2359304 | tf_op jit(solution)/shard_map/ppermute | solution.py:687
  387.9 21.7 %collective-permute-start.68 = (bf16[256,1536]{1,0:T(8,128)(2,1)S(1)}, bf16[256,1536]{1,0:T(8,128)(2,1)S(1)}, u32[]{:S(2)}, u32[]{:S(2)}) collective-permute-start(bf16[256,1536]{1,0:T(8,128)(2,1)S(1)} %pair_sum.3), channel_id=1, source_target_pairs={{0,8},{8,0},{16,24},{24,16},{1,9},{9,1},{17,25},{25,17},{2,10},{10... | collective-permute-start | bytes 2359304 | tf_op jit(solution)/shard_map/ppermute | solution.py:683
  414.7 20.7 %collective-permute-start.75 = (bf16[256,1536]{1,0:T(8,128)(2,1)S(1)}, bf16[256,1536]{1,0:T(8,128)(2,1)}, u32[]{:S(2)}, u32[]{:S(2)}) collective-permute-start(bf16[256,1536]{1,0:T(8,128)(2,1)S(1)} %pair_sum.5), channel_id=1, source_target_pairs={{0,24},{8,16},{16,8},{24,0},{1,25},{9,17},{17,9},{25,1},{2,26},{10... | collective-permute-start | bytes 2359304 | tf_op jit(solution)/shard_map/ppermute | solution.py:691
  418.1 17.2 %collective-permute-start.77 = (bf16[48,1536]{1,0:T(8,128)(2,1)}, bf16[48,1536]{1,0:T(8,128)(2,1)S(1)}, u32[]{:S(2)}, u32[]{:S(2)}) collective-permute-start(bf16[48,1536]{1,0:T(8,128)(2,1)} %get-tuple-element.418), channel_id=1, source_target_pairs={{0,4},{2,6},{4,0},{6,2},{1,5},{3,7},{5,1},{7,3},{8,12},{10,14},{12... | collective-permute-start | bytes 442376 | tf_op jit(solution)/shard_map/ppermute | solution.py:728
  419.2 16.1 %collective-permute-start.76 = (bf16[48,1536]{1,0:T(8,128)(2,1)}, bf16[48,1536]{1,0:T(8,128)(2,1)}, u32[]{:S(2)}, u32[]{:S(2)}) collective-permute-start(bf16[48,1536]{1,0:T(8,128)(2,1)} %get-tuple-element.409), channel_id=1, source_target_pairs={{0,2},{2,4},{4,6},{6,0},{1,3},{3,5},{5,7},{7,1},{8,10},{10,12},{12... | collective-permute-start | bytes 442376 | tf_op jit(solution)/shard_map/ppermute | solution.py:728
  419.6 15.7 %collective-permute-start.78 = (bf16[48,1536]{1,0:T(8,128)(2,1)}, bf16[48,1536]{1,0:T(8,128)(2,1)}, u32[]{:S(2)}, u32[]{:S(2)}) collective-permute-start(bf16[48,1536]{1,0:T(8,128)(2,1)} %get-tuple-element.419), channel_id=1, source_target_pairs={{0,6},{2,0},{4,2},{6,4},{1,7},{3,1},{5,3},{7,5},{8,14},{10,8},{12,... | collective-permute-start | bytes 442376 | tf_op jit(solution)/shard_map/ppermute | solution.py:728
  438.7 30.2 %collective-permute-start.80 = (bf16[432,1536]{1,0:T(8,128)(2,1)S(1)}, bf16[432,1536]{1,0:T(8,128)(2,1)}, u32[]{:S(2)}, u32[]{:S(2)}) collective-permute-start(bf16[432,1536]{1,0:T(8,128)(2,1)S(1)} %pad_maximum_fusion.refs_0_.refs_8_), channel_id=1, source_target_pairs={{0,16},{16,0},{8,24},{24,8},{1,17},{17,1},{9,25},{25,9},{2,18},{18... | collective-permute-start | bytes 3981320 | tf_op jit(solution)/shard_map/ppermute | solution.py:687
  440.2 29.9 %collective-permute-start.79 = (bf16[432,1536]{1,0:T(8,128)(2,1)S(1)}, bf16[432,1536]{1,0:T(8,128)(2,1)}, u32[]{:S(2)}, u32[]{:S(2)}) collective-permute-start(bf16[432,1536]{1,0:T(8,128)(2,1)S(1)} %pad_maximum_fusion.refs_0_.refs_8_), channel_id=1, source_target_pairs={{0,8},{8,0},{16,24},{24,16},{1,9},{9,1},{17,25},{25,17},{2,10},{10... | collective-permute-start | bytes 3981320 | tf_op jit(solution)/shard_map/ppermute | solution.py:683
  440.9 29.2 %collective-permute-start.81 = (bf16[432,1536]{1,0:T(8,128)(2,1)S(1)}, bf16[432,1536]{1,0:T(8,128)(2,1)}, u32[]{:S(2)}, u32[]{:S(2)}) collective-permute-start(bf16[432,1536]{1,0:T(8,128)(2,1)S(1)} %pad_maximum_fusion.refs_0_.refs_8_), channel_id=1, source_target_pairs={{0,1},{1,0},{2,3},{3,2},{4,5},{5,4},{6,7},{7,6},{8,9},{9,8},{10,11... | collective-permute-start | bytes 3981320 | tf_op jit(solution)/shard_map/ppermute | solution.py:679
  470.1 21.0 %collective-permute-start.86 = (bf16[432,1536]{1,0:T(8,128)(2,1)}, bf16[432,1536]{1,0:T(8,128)(2,1)}, u32[]{:S(2)}, u32[]{:S(2)}) collective-permute-start(bf16[432,1536]{1,0:T(8,128)(2,1)} %collective-permute-done.80.refs_4_.refs_12_), channel_id=1, source_target_pairs={{0,1},{1,0},{2,3},{3,2},{4,5},{5,4},{6,7},{7,6},{8,9},{9,8},{10,11... | collective-permute-start | bytes 3981320 | tf_op jit(solution)/shard_map/ppermute | solution.py:679
  470.1 21.0 %collective-permute-start.85 = (bf16[432,1536]{1,0:T(8,128)(2,1)}, bf16[432,1536]{1,0:T(8,128)(2,1)}, u32[]{:S(2)}, u32[]{:S(2)}) collective-permute-start(bf16[432,1536]{1,0:T(8,128)(2,1)} %collective-permute-done.79.refs_2_.refs_10_), channel_id=1, source_target_pairs={{0,1},{1,0},{2,3},{3,2},{4,5},{5,4},{6,7},{7,6},{8,9},{9,8},{10,11... | collective-permute-start | bytes 3981320 | tf_op jit(solution)/shard_map/ppermute | solution.py:679
  471.7 16.9 %collective-permute-start.83 = (bf16[216,1536]{1,0:T(8,128)(2,1)S(1)}, bf16[216,1536]{1,0:T(8,128)(2,1)S(1)}, u32[]{:S(2)}, u32[]{:S(2)}) collective-permute-start(bf16[216,1536]{1,0:T(8,128)(2,1)S(1)} %slice.179), channel_id=1, source_target_pairs={{0,16},{16,0},{8,24},{24,8},{1,17},{17,1},{9,25},{25,9},{2,18},{18... | collective-permute-start | bytes 1990664 | tf_op jit(solution)/shard_map/ppermute | solution.py:687
  473.5 16.6 %collective-permute-start.84 = (bf16[216,1536]{1,0:T(8,128)(2,1)S(1)}, bf16[216,1536]{1,0:T(8,128)(2,1)S(1)}, u32[]{:S(2)}, u32[]{:S(2)}) collective-permute-start(bf16[216,1536]{1,0:T(8,128)(2,1)S(1)} %slice.180), channel_id=1, source_target_pairs={{0,8},{8,0},{16,24},{24,16},{1,9},{9,1},{17,25},{25,17},{2,10},{10... | collective-permute-start | bytes 1990664 | tf_op jit(solution)/shard_map/ppermute | solution.py:683
  491.1 15.8 %collective-permute-start.91 = (bf16[432,1536]{1,0:T(8,128)(2,1)}, bf16[432,1536]{1,0:T(8,128)(2,1)S(1)}, u32[]{:S(2)}, u32[]{:S(2)}) collective-permute-start(bf16[432,1536]{1,0:T(8,128)(2,1)} %constant_dynamic-update-slice_fusion.8.refs_6_.refs_14_), channel_id=1, source_target_pairs={{0,1},{1,0},{2,3},{3,2},{4,5},{5,4},{6,7},{7,6},{8,9},{9,8},{10,11... | collective-permute-start | bytes 3981320 | tf_op jit(solution)/shard_map/ppermute | solution.py:679
  491.1 13.8 %collective-permute-start.89 = (bf16[384,640]{1,0:T(8,128)(2,1)}, bf16[384,640]{1,0:T(8,128)(2,1)S(1)}, u32[]{:S(2)}, u32[]{:S(2)}) collective-permute-start(bf16[384,640]{1,0:T(8,128)(2,1)} %reduce-scatter.5.cloned.1.call-done.refs_0_), channel_id=1, source_target_pairs={{0,16},{16,0},{8,24},{24,8},{1,17},{17,1},{9,25},{25,9},{2,18},{18... | collective-permute-start | bytes 1474568 | tf_op jit(solution)/shard_map/ppermute | solution.py:687
  492.6 13.5 %collective-permute-start.88 = (bf16[384,640]{1,0:T(8,128)(2,1)}, bf16[384,640]{1,0:T(8,128)(2,1)S(1)}, u32[]{:S(2)}, u32[]{:S(2)}) collective-permute-start(bf16[384,640]{1,0:T(8,128)(2,1)} %reduce-scatter.5.cloned.1.call-done.refs_0_), channel_id=1, source_target_pairs={{0,8},{8,0},{16,24},{24,16},{1,9},{9,1},{17,25},{25,17},{2,10},{10... | collective-permute-start | bytes 1474568 | tf_op jit(solution)/shard_map/ppermute | solution.py:683
  506.9 16.8 %collective-permute-start.96 = (bf16[384,640]{1,0:T(8,128)(2,1)S(1)}, bf16[384,640]{1,0:T(8,128)(2,1)S(1)}, u32[]{:S(2)}, u32[]{:S(2)}) collective-permute-start(bf16[384,640]{1,0:T(8,128)(2,1)S(1)} %collective-permute-done.89.refs_4_), channel_id=1, source_target_pairs={{0,1},{1,0},{2,3},{3,2},{4,5},{5,4},{6,7},{7,6},{8,9},{9,8},{10,11... | collective-permute-start | bytes 1474568 | tf_op jit(solution)/shard_map/ppermute | solution.py:679
  506.9 16.8 %collective-permute-start.95 = (bf16[384,640]{1,0:T(8,128)(2,1)S(1)}, bf16[384,640]{1,0:T(8,128)(2,1)S(1)}, u32[]{:S(2)}, u32[]{:S(2)}) collective-permute-start(bf16[384,640]{1,0:T(8,128)(2,1)S(1)} %collective-permute-done.88.refs_2_), channel_id=1, source_target_pairs={{0,1},{1,0},{2,3},{3,2},{4,5},{5,4},{6,7},{7,6},{8,9},{9,8},{10,11... | collective-permute-start | bytes 1474568 | tf_op jit(solution)/shard_map/ppermute | solution.py:679
  508.1 15.5 %collective-permute-start.93 = (bf16[192,640]{1,0:T(8,128)(2,1)}, bf16[192,640]{1,0:T(8,128)(2,1)S(1)}, u32[]{:S(2)}, u32[]{:S(2)}) collective-permute-start(bf16[192,640]{1,0:T(8,128)(2,1)} %slice.181), channel_id=1, source_target_pairs={{0,16},{16,0},{8,24},{24,8},{1,17},{17,1},{9,25},{25,9},{2,18},{18... | collective-permute-start | bytes 737288 | tf_op jit(solution)/shard_map/ppermute | solution.py:687
  509.6 14.1 %collective-permute-start.94 = (bf16[192,640]{1,0:T(8,128)(2,1)}, bf16[192,640]{1,0:T(8,128)(2,1)S(1)}, u32[]{:S(2)}, u32[]{:S(2)}) collective-permute-start(bf16[192,640]{1,0:T(8,128)(2,1)} %slice.182), channel_id=1, source_target_pairs={{0,8},{8,0},{16,24},{24,16},{1,9},{9,1},{17,25},{25,17},{2,10},{10... | collective-permute-start | bytes 737288 | tf_op jit(solution)/shard_map/ppermute | solution.py:683
  (200 other events, 1454.2 us)
Sparse Core Ops, SparseCore 0:
  21.5 46.6 all-gather.3
  129.7 34.2 all-gather.7
  165.7 62.3 all-gather.5
  302.3 83.8 reduce-scatter.2
  436.1 39.2 reduce-scatter.4

commit v3 on v2

--- a/solution.py
+++ b/solution.py
@@ -8,7 +8,12 @@
 LANES = 128
 EDGE = 64
 TOP = 16
+ROOM = 60 * 1024 * 1024
 LIGHT = pl.CostEstimate(flops=1_000_000, bytes_accessed=1_000_000, transcendentals=0)
+
+
+def cost(micros):
+    return pl.CostEstimate(flops=0, bytes_accessed=3_600_000 * micros, transcendentals=0)
 
 
 def taps_kernel(taps_q, taps_k, scaling, kernel_ref, forward_ref, backward_ref):
@@ -80,8 +85,8 @@
             in_specs=[spec] * len(pieces),
             out_specs=pl.BlockSpec((rows // steps, cols_out), lambda s, place: (s, 0)),
         ),
-        compiler_params=pltpu.CompilerParams(vmem_limit_bytes=40 * 1024 * 1024),
-        cost_estimate=LIGHT,
+        compiler_params=pltpu.CompilerParams(vmem_limit_bytes=ROOM),
+        cost_estimate=cost(5),
         name="place_columns",
     )(place, *pieces)
 
@@ -140,8 +145,8 @@
                 pl.BlockSpec((extra * len(pieces), cols), lambda s, place: (0, 0)),
             ),
         ),
-        compiler_params=pltpu.CompilerParams(vmem_limit_bytes=48 * 1024 * 1024),
-        cost_estimate=LIGHT,
+        compiler_params=pltpu.CompilerParams(vmem_limit_bytes=ROOM),
+        cost_estimate=cost(11),
         name="place_feed",
     )(place, *pieces, *pieces)
 
@@ -185,24 +190,64 @@
     return jnp.concatenate(tiles, 1)
 
 
-def forward_kernel(
-    taps_q, head_size, core_ref, mix_ref, own_ref, other_ref, since_ref, joined_ref, taps_ref, gain_ref,
-    proj_ref, att_ref, grouped_ref, weights_ref, keys_pad, s_high, s_low, spread, grouped_row,
-):
-    seq_len = proj_ref.shape[0]
+def forward_kernel(taps_q, head_size, rows, core_ref, mix_ref, since_all, joined_ref, taps_ref, gain_ref, *refs):
+    halves, outs = refs[: 2 * rows], refs[2 * rows : 2 * rows + 4]
+    pieces, proj, att, grouped, maps, keys_pad, s_high, s_low, spread, grouped_row, in_sems, out_sems = refs[2 * rows + 4 :]
+    arrivals = [pltpu.make_async_copy(ref, pieces.at[i], in_sems.at[i]) for i, ref in enumerate(halves)]
+    for arrival in arrivals:
+        arrival.start()
+    seq_len = proj.shape[1]
     half_len = seq_len // 2
     blocks = seq_len // LANES
-    own_at = pl.multiple_of(core_ref[0] * half_len, half_len)
-    other_at = pl.multiple_of((1 - core_ref[0]) * half_len, half_len)
+    core = core_ref[0]
     keys_pad[...] = jnp.zeros_like(keys_pad)
     s_high[...] = jnp.zeros_like(s_high)
     s_low[...] = jnp.zeros_like(s_low)
-    for ref, at in ((own_ref, own_at), (other_ref, other_at)):
-        joined = jnp.dot(ref[...], joined_ref[...], preferred_element_type=jnp.float32)
+    for arrival in arrivals:
+        arrival.wait()
+
+    def project(step, carry):
+        row, part = lax.div(step, 2), lax.rem(step, 2)
+        at = pl.multiple_of(jnp.bitwise_xor(core, part) * half_len, half_len)
+        joined = jnp.dot(pieces[step], joined_ref[...], preferred_element_type=jnp.float32)
         for head, piece in enumerate(split_heads(joined, 6, head_size)):
-            proj_ref[pl.ds(at, half_len), head * LANES : (head + 1) * LANES] = piece.astype(jnp.bfloat16)
-
-    def one_head(head, carry):
+            proj[row, pl.ds(at, half_len), head * LANES : (head + 1) * LANES] = piece.astype(jnp.bfloat16)
+        return carry
+
+    lax.fori_loop(0, 2 * rows, project, 0)
+    real = lax.broadcasted_iota(jnp.int32, (LANES, LANES), 1) < head_size
+
+    def mix_row(row):
+        for qi in range(blocks):
+            first = qi * LANES
+            width = (qi + 1) * LANES
+            low = maps[row, 0, first : first + LANES, :width]
+            upp = maps[row, 1, first : first + LANES, :width]
+            for head in range(2):
+                mixed = (mix_ref[head, 0] * low + mix_ref[head, 1] * upp).astype(jnp.bfloat16)
+                cols = slice(head * LANES, (head + 1) * LANES)
+                attended = jnp.dot(
+                    mixed, proj[row, :width, (4 + head) * LANES : (5 + head) * LANES],
+                    preferred_element_type=jnp.float32,
+                )
+                att[row, first : first + LANES, cols] = attended
+                normal, _ = normalize(attended, real, head_size)
+                grouped_row[first : first + LANES, cols] = (normal * gain_ref[:, cols]).astype(jnp.bfloat16)
+        for part in range(2):
+            at = pl.multiple_of(jnp.bitwise_xor(core, part) * half_len, half_len)
+            grouped[row, part * half_len : (part + 1) * half_len, :] = grouped_row[pl.ds(at, half_len), :]
+        for copy in copies_out(row):
+            copy.start()
+
+    def copies_out(row):
+        return [
+            pltpu.make_async_copy(here.at[row], there.at[row], out_sems.at[kind, row])
+            for kind, (here, there) in enumerate(zip((proj, att, grouped, maps), outs))
+        ]
+
+    def one_head(step, carry):
+        row, head = lax.div(step, 2), lax.rem(step, 2)
+        proj_ref, since_ref, weights_ref = proj.at[row], since_all.at[row], maps.at[row]
         lane = pl.multiple_of(head * LANES, LANES)
         lane_k = pl.multiple_of((head + 2) * LANES, LANES)
         keys_pad[EDGE : EDGE + seq_len, :] = proj_ref[:, pl.ds(lane_k, LANES)]
@@ -240,26 +285,17 @@
             logits = jnp.where((back >= 0) & (back <= limit), logits, -1e30)
             raised = jnp.exp(logits - jnp.max(logits, axis=1, keepdims=True))
             weights_ref[head, first : first + LANES, :width] = raised / jnp.sum(raised, axis=1, keepdims=True)
+
+        @pl.when(head == 1)
+        def _():
+            mix_row(row)
+
         return carry
 
-    lax.fori_loop(0, 2, one_head, 0)
-    real = lax.broadcasted_iota(jnp.int32, (LANES, LANES), 1) < head_size
-    for qi in range(blocks):
-        first = qi * LANES
-        width = (qi + 1) * LANES
-        low = weights_ref[0, first : first + LANES, :width]
-        upp = weights_ref[1, first : first + LANES, :width]
-        for head in range(2):
-            mixed = (mix_ref[head, 0] * low + mix_ref[head, 1] * upp).astype(jnp.bfloat16)
-            cols = slice(head * LANES, (head + 1) * LANES)
-            att = jnp.dot(
-                mixed, proj_ref[:width, (4 + head) * LANES : (5 + head) * LANES], preferred_element_type=jnp.float32
-            )
-            att_ref[first : first + LANES, cols] = att
-            normal, _ = normalize(att, real, head_size)
-            grouped_row[first : first + LANES, cols] = (normal * gain_ref[:, cols]).astype(jnp.bfloat16)
-    grouped_ref[:half_len, :] = grouped_row[pl.ds(own_at, half_len), :]
-    grouped_ref[half_len:, :] = grouped_row[pl.ds(other_at, half_len), :]
+    lax.fori_loop(0, 2 * rows, one_head, 0)
+    for row in range(rows):
+        for copy in copies_out(row):
+            copy.wait()
 
 
 def normalize(att, real, head_size):
@@ -270,40 +306,55 @@
     return centered * scale, scale
 
 
-def attend_row(core, own, other, since, mix, joined, taps_forward, gain_pad, taps_q, head_size):
-    seq_len = 2 * own.shape[0]
+def attend_rows(core, halves, since, mix, joined, taps_forward, gain_pad, taps_q, head_size):
+    rows, seq_len = since.shape[:2]
     full = seq_len + 2 * EDGE
     vmem = pl.BlockSpec(memory_space=pltpu.VMEM)
     smem = pl.BlockSpec(memory_space=pltpu.SMEM)
-    return pl.pallas_call(
-        functools.partial(forward_kernel, taps_q, head_size),
-        out_shape=(
-            jax.ShapeDtypeStruct((seq_len, 6 * LANES), jnp.bfloat16),
-            jax.ShapeDtypeStruct((seq_len, 2 * LANES), jnp.float32),
-            jax.ShapeDtypeStruct((seq_len, 2 * LANES), jnp.bfloat16),
-            jax.ShapeDtypeStruct((2, seq_len, seq_len), jnp.float32),
-        ),
-        in_specs=[smem, smem] + [vmem] * 6,
-        out_specs=(vmem,) * 4,
-        scratch_shapes=[
+    anywhere = pl.BlockSpec(memory_space=pl.ANY)
+    shapes = (
+        ((rows, seq_len, 6 * LANES), jnp.bfloat16),
+        ((rows, seq_len, 2 * LANES), jnp.float32),
+        ((rows, seq_len, 2 * LANES), jnp.bfloat16),
+        ((rows, 2, seq_len, seq_len), jnp.float32),
+    )
+    return pl.pallas_call(
+        functools.partial(forward_kernel, taps_q, head_size, rows),
+        out_shape=tuple(jax.ShapeDtypeStruct(*a) for a in shapes),
+        in_specs=[smem, smem] + [vmem] * 4 + [anywhere] * len(halves),
+        out_specs=(anywhere,) * 4,
+        scratch_shapes=[pltpu.VMEM((len(halves),) + halves[0].shape, jnp.bfloat16)]
+        + [pltpu.VMEM(*a) for a in shapes]
+        + [
             pltpu.VMEM((full, LANES), jnp.bfloat16),
             pltpu.VMEM((TOP + seq_len, full), jnp.bfloat16),
             pltpu.VMEM((TOP + seq_len, full), jnp.bfloat16),
             pltpu.VMEM((TOP + seq_len, taps_q * LANES), jnp.float32),
             pltpu.VMEM((seq_len, 2 * LANES), jnp.bfloat16),
+            pltpu.SemaphoreType.DMA((len(halves),)),
+            pltpu.SemaphoreType.DMA((4, rows)),
         ],
-        compiler_params=pltpu.CompilerParams(vmem_limit_bytes=40 * 1024 * 1024),
+        compiler_params=pltpu.CompilerParams(vmem_limit_bytes=52 * 1024 * 1024),
         cost_estimate=LIGHT,
-        name="attend_row",
-    )(core, mix, own, other, since, joined, taps_forward, gain_pad)
+        name="attend_rows",
+    )(core, mix, since, joined, taps_forward, gain_pad, *halves)
 
 
 def backward_kernel(
-    taps_q, taps_k, head_size, scaling, core_ref, mix_ref, own_ref, other_ref, out_weight_ref, joined_ref,
-    proj_ref, since_ref, taps_ref, gain_ref, att_ref, weights_ref,
+    taps_q, taps_k, head_size, scaling, row, core_ref, mix_ref, own_ref, other_ref, out_weight_ref, joined_ref,
+    taps_ref, gain_ref, proj_all, since_all, att_all, weights_all,
     joined_grad_ref, mine_ref, theirs_ref, small_ref, tap_ref,
     keys_pad, grad_att, conv_grad, shifted, s_low, s_grad, since_pad, grad_ref, out_ref,
+    proj_ref, since_ref, att_ref, weights_ref, sems,
 ):
+    arrivals = [
+        pltpu.make_async_copy(source.at[row], here, sems.at[i])
+        for i, (source, here) in enumerate(
+            ((since_all, since_ref), (att_all, att_ref), (proj_all, proj_ref), (weights_all, weights_ref))
+        )
+    ]
+    for arrival in arrivals:
+        arrival.start()
     seq_len = proj_ref.shape[0]
     half_len = seq_len // 2
     own_at = pl.multiple_of(core_ref[0] * half_len, half_len)
@@ -320,6 +371,8 @@
     s_grad[...] = jnp.zeros_like(s_grad)
     shifted[...] = jnp.zeros_like(shifted)
     conv_grad[...] = jnp.zeros_like(conv_grad)
+    for arrival in arrivals:
+        arrival.wait()
     since_pad[:seq_len, :] = since_ref[...]
     since_pad[seq_len:, :] = jnp.zeros((8, LANES), jnp.int32)
     small_ref[...] = jnp.zeros_like(small_ref)
@@ -456,28 +509,29 @@
         if first:
             theirs_ref[...] = grad_in.astype(jnp.bfloat16)
         else:
-            mine_ref[...] = grad_in
+            mine_ref[...] = grad_in.astype(jnp.bfloat16)
 
 
 def attend_row_back(
-    core, own, other, out_weight, joined, saved, since, mix, taps_backward, gain_pad, taps_q, taps_k, head_size
+    row, core, own, other, out_weight, joined, saved, since, mix, taps_backward, gain_pad, taps_q, taps_k, head_size
 ):
     projected, att, weights = saved
-    seq_len = projected.shape[0]
+    seq_len = projected.shape[1]
     width = own.shape[1]
     full = seq_len + 2 * EDGE
     vmem = pl.BlockSpec(memory_space=pltpu.VMEM)
     smem = pl.BlockSpec(memory_space=pltpu.SMEM)
-    return pl.pallas_call(
-        functools.partial(backward_kernel, taps_q, taps_k, head_size, head_size ** (-0.5)),
+    anywhere = pl.BlockSpec(memory_space=pl.ANY)
+    return pl.pallas_call(
+        functools.partial(backward_kernel, taps_q, taps_k, head_size, head_size ** (-0.5), row),
         out_shape=(
             jax.ShapeDtypeStruct((seq_len, joined.shape[1]), jnp.bfloat16),
-            jax.ShapeDtypeStruct((seq_len // 2, width), jnp.float32),
+            jax.ShapeDtypeStruct((seq_len // 2, width), jnp.bfloat16),
             jax.ShapeDtypeStruct((seq_len // 2, width), jnp.bfloat16),
             jax.ShapeDtypeStruct((8, LANES), jnp.float32),
             jax.ShapeDtypeStruct((2, taps_q * taps_k, LANES), jnp.float32),
         ),
-        in_specs=[smem, smem] + [vmem] * 10,
+        in_specs=[smem, smem] + [vmem] * 6 + [anywhere] * 4,
         out_specs=(vmem,) * 5,
         scratch_shapes=[
             pltpu.VMEM((full, LANES), jnp.bfloat16),
@@ -489,23 +543,49 @@
             pltpu.VMEM((seq_len + 8, LANES), jnp.int32),
             pltpu.VMEM((seq_len, 2 * LANES), jnp.float32),
             pltpu.VMEM((seq_len, 6 * LANES), jnp.float32),
+            pltpu.VMEM(projected.shape[1:], jnp.bfloat16),
+            pltpu.VMEM(since.shape[1:], jnp.int32),
+            pltpu.VMEM(att.shape[1:], jnp.float32),
+            pltpu.VMEM(weights.shape[1:], jnp.float32),
+            pltpu.SemaphoreType.DMA((4,)),
         ],
         compiler_params=pltpu.CompilerParams(vmem_limit_bytes=48 * 1024 * 1024),
-        cost_estimate=LIGHT,
+        cost_estimate=cost(14),
         name="attend_row_back",
-    )(core, mix, own, other, out_weight, joined, projected, since, taps_backward, gain_pad, att, weights)
-
-
-def feed_kernel(wide, own_ref, other_ref, cot_own_ref, cot_other_ref, gate_ref, cut_ref,
-                hidden_ref, grads_ref, ffn_mine_ref, ffn_theirs_ref, back_mine_ref, back_theirs_ref, down_ref):
-    half_len = own_ref.shape[0]
+    )(core, mix, own, other, out_weight, joined, taps_backward, gain_pad, projected, since, att, weights)
+
+
+def split_kernel(wide, feed_ref, gate_ref, down_ref):
     cols = down_ref.shape[0]
     chunk = cols // wide
     blocks = down_ref.shape[1] // cols
+    gate_ref[...] = feed_ref[:, : 2 * cols]
     for z in range(wide):
         for b in range(blocks):
             first = (z * blocks + b) * chunk
-            down_ref[z * chunk : (z + 1) * chunk, b * cols : (b + 1) * cols] = cut_ref[first : first + chunk, :]
+            down_ref[z * chunk : (z + 1) * chunk, b * cols : (b + 1) * cols] = feed_ref[first : first + chunk, 2 * cols :]
+
+
+def split_feed(feed, wide):
+    vmem = pl.BlockSpec(memory_space=pltpu.VMEM)
+    rows, cols = feed.shape[0], feed.shape[1] // 3
+    return pl.pallas_call(
+        functools.partial(split_kernel, wide),
+        out_shape=(
+            jax.ShapeDtypeStruct((rows, 2 * cols), jnp.bfloat16), jax.ShapeDtypeStruct((cols, rows), jnp.bfloat16),
+        ),
+        in_specs=[vmem],
+        out_specs=(vmem,) * 2,
+        compiler_params=pltpu.CompilerParams(vmem_limit_bytes=24 * 1024 * 1024),
+        cost_estimate=LIGHT,
+        name="split_feed",
+    )(feed)
+
+
+def feed_kernel(own_ref, other_ref, cot_own_ref, cot_other_ref, gate_ref, down_ref,
+                hidden_ref, grads_ref, ffn_mine_ref, ffn_theirs_ref, back_mine_ref, back_theirs_ref):
+    half_len = own_ref.shape[0]
+    cols = down_ref.shape[0]
     for first, ref, cot_ref in ((0, own_ref, cot_own_ref), (half_len, other_ref, cot_other_ref)):
         rows = slice(first, first + half_len)
         both = jnp.dot(ref[...], gate_ref[...], preferred_element_type=jnp.float32)
@@ -527,31 +607,30 @@
             back_theirs_ref[...] = back.astype(jnp.bfloat16)
             ffn_theirs_ref[...] = ffn.astype(jnp.bfloat16)
         else:
-            back_mine_ref[...] = back
-            ffn_mine_ref[...] = ffn
-
-
-def feed_row(own, other, cot_own, cot_other, weights, wide):
+            back_mine_ref[...] = back.astype(jnp.bfloat16)
+            ffn_mine_ref[...] = ffn.astype(jnp.bfloat16)
+
+
+def feed_row(own, other, cot_own, cot_other, gate, down):
     half_len, width = own.shape
-    cols = weights[1].shape[1]
+    cols = down.shape[0]
     vmem = pl.BlockSpec(memory_space=pltpu.VMEM)
     return pl.pallas_call(
-        functools.partial(feed_kernel, wide),
+        feed_kernel,
         out_shape=(
             jax.ShapeDtypeStruct((2 * half_len, cols), jnp.bfloat16),
             jax.ShapeDtypeStruct((2 * half_len, 2 * cols), jnp.bfloat16),
-            jax.ShapeDtypeStruct((half_len, width), jnp.float32),
             jax.ShapeDtypeStruct((half_len, width), jnp.bfloat16),
-            jax.ShapeDtypeStruct((half_len, width), jnp.float32),
+            jax.ShapeDtypeStruct((half_len, width), jnp.bfloat16),
+            jax.ShapeDtypeStruct((half_len, width), jnp.bfloat16),
             jax.ShapeDtypeStruct((half_len, width), jnp.bfloat16),
         ),
         in_specs=[vmem] * 6,
         out_specs=(vmem,) * 6,
-        scratch_shapes=[pltpu.VMEM((cols, width), jnp.bfloat16)],
         compiler_params=pltpu.CompilerParams(vmem_limit_bytes=48 * 1024 * 1024),
-        cost_estimate=LIGHT,
+        cost_estimate=cost(8),
         name="feed_row",
-    )(own, other, cot_own, cot_other, *weights)
+    )(own, other, cot_own, cot_other, gate, down)
 
 
 def feed_grad_kernel(counts, *refs):
@@ -595,8 +674,8 @@
         + [pl.BlockSpec((a.shape[0], chunk), lambda s: (0, s)) for a in hiddens]
         + [pl.BlockSpec(a.shape, lambda s: (0, 0)) for a in cots],
         out_specs=pl.BlockSpec((block, cols_out), lambda s: (s, 0)),
-        compiler_params=pltpu.CompilerParams(vmem_limit_bytes=56 * 1024 * 1024),
-        cost_estimate=LIGHT,
+        compiler_params=pltpu.CompilerParams(vmem_limit_bytes=ROOM),
+        cost_estimate=cost(17),
         name="feed_grad",
     )(*lefts, *grads, *hiddens, *cots)
 
@@ -609,6 +688,19 @@
     ).astype(jnp.bfloat16)
 
 
+def small_weight_grad(lefts, rights, name):
+    vmem = pl.BlockSpec(memory_space=pltpu.VMEM)
+    return pl.pallas_call(
+        functools.partial(weight_kernel, len(lefts)),
+        out_shape=jax.ShapeDtypeStruct((lefts[0].shape[1], rights[0].shape[1]), jnp.bfloat16),
+        in_specs=[vmem] * (len(lefts) + len(rights)),
+        out_specs=vmem,
+        compiler_params=pltpu.CompilerParams(vmem_limit_bytes=32 * 1024 * 1024),
+        cost_estimate=cost(3),
+        name=name,
+    )(*lefts, *rights)
+
+
 def weight_grad(lefts, rights, block, name):
     rows_out, cols_out = lefts[0].shape[1], rights[0].shape[1]
     count = sum(a.shape[0] for a in lefts)
@@ -619,16 +711,16 @@
         in_specs=[pl.BlockSpec((a.shape[0], block), lambda s: (0, s)) for a in lefts]
         + [pl.BlockSpec(a.shape, lambda s: (0, 0)) for a in rights],
         out_specs=pl.BlockSpec((block, cols_out), lambda s: (s, 0)),
-        compiler_params=pltpu.CompilerParams(vmem_limit_bytes=48 * 1024 * 1024),
-        cost_estimate=LIGHT,
+        compiler_params=pltpu.CompilerParams(vmem_limit_bytes=ROOM),
+        cost_estimate=cost(8),
         name=name,
     )(*lefts, *rights)
 
 
 def halves_kernel(mine_ref, came_ref, low_ref, high_ref):
     cut = low_ref.shape[0]
-    low_ref[...] = (mine_ref[:cut, :] + came_ref[:cut, :].astype(jnp.float32)).astype(jnp.bfloat16)
-    high_ref[...] = (mine_ref[cut:, :] + came_ref[cut:, :].astype(jnp.float32)).astype(jnp.bfloat16)
+    low_ref[...] = (mine_ref[:cut, :].astype(jnp.float32) + came_ref[:cut, :].astype(jnp.float32)).astype(jnp.bfloat16)
+    high_ref[...] = (mine_ref[cut:, :].astype(jnp.float32) + came_ref[cut:, :].astype(jnp.float32)).astype(jnp.bfloat16)
 
 
 def sum_halves(mine, came):
@@ -643,9 +735,9 @@
 def sum_kernel(second, mine_ref, came_ref, extra_ref, out_ref):
     cut = extra_ref.shape[0]
     rows, rest = (slice(cut, 2 * cut), slice(0, cut)) if second else (slice(0, cut), slice(cut, 2 * cut))
-    total = mine_ref[rows, :] + came_ref[rows, :].astype(jnp.float32) + extra_ref[...].astype(jnp.float32)
+    total = mine_ref[rows, :].astype(jnp.float32) + came_ref[rows, :].astype(jnp.float32) + extra_ref[...].astype(jnp.float32)
     out_ref[rows, :] = total.astype(jnp.bfloat16)
-    out_ref[rest, :] = (mine_ref[rest, :] + came_ref[rest, :].astype(jnp.float32)).astype(jnp.bfloat16)
+    out_ref[rest, :] = (mine_ref[rest, :].astype(jnp.float32) + came_ref[rest, :].astype(jnp.float32)).astype(jnp.bfloat16)
 
 
 def low_sum(mine, came, extra, second):
@@ -658,7 +750,7 @@
 
 
 def pair_kernel(mine_ref, came_ref, out_ref):
-    out_ref[...] = (mine_ref[...] + came_ref[...].astype(jnp.float32)).astype(jnp.bfloat16)
+    out_ref[...] = (mine_ref[...].astype(jnp.float32) + came_ref[...].astype(jnp.float32)).astype(jnp.bfloat16)
 
 
 def pair_sum(mine, came):
@@ -667,6 +759,83 @@
         pair_kernel, out_shape=jax.ShapeDtypeStruct(mine.shape, jnp.bfloat16), in_specs=[vmem] * 2, out_specs=vmem,
         compiler_params=pltpu.CompilerParams(vmem_limit_bytes=16 * 1024 * 1024), cost_estimate=LIGHT, name="pair_sum",
     )(mine, came)
+
+
+def place_out_kernel(place_ref, *refs):
+    out_ref = refs[-1]
+    out_ref[...] = jnp.zeros_like(out_ref)
+    for step, ref in enumerate(refs[:-1]):
+        chunk = jnp.bitwise_xor(place_ref[0], step)
+        rows = ref.shape[0]
+        at = pl.multiple_of(lax.div(chunk, 2) * LANES + lax.rem(chunk, 2) * rows, 16)
+        out_ref[pl.ds(at, rows), :] = ref[...]
+
+
+def place_out(place, pieces):
+    vmem = pl.BlockSpec(memory_space=pltpu.VMEM)
+    return pl.pallas_call(
+        place_out_kernel,
+        out_shape=jax.ShapeDtypeStruct((2 * LANES, pieces[0].shape[1]), jnp.bfloat16),
+        in_specs=[pl.BlockSpec(memory_space=pltpu.SMEM)] + [vmem] * len(pieces),
+        out_specs=vmem,
+        compiler_params=pltpu.CompilerParams(vmem_limit_bytes=16 * 1024 * 1024),
+        cost_estimate=LIGHT,
+        name="place_out",
+    )(place, *pieces)
+
+
+def branch_kernel(grouped_ref, out_ref, *refs):
+    weight = out_ref[...]
+    for row in range(grouped_ref.shape[0]):
+        mine_ref, theirs_ref = refs[2 * row : 2 * row + 2]
+        half_len = mine_ref.shape[0]
+        mine_ref[...] = jnp.dot(grouped_ref[row, :half_len, :], weight, preferred_element_type=jnp.float32).astype(
+            jnp.bfloat16
+        )
+        theirs_ref[...] = jnp.dot(grouped_ref[row, half_len:, :], weight, preferred_element_type=jnp.float32).astype(
+            jnp.bfloat16
+        )
+
+
+def branch_rows_of(grouped, out_own):
+    vmem = pl.BlockSpec(memory_space=pltpu.VMEM)
+    rows, half_len, width = grouped.shape[0], grouped.shape[1] // 2, out_own.shape[1]
+    flat = pl.pallas_call(
+        branch_kernel,
+        out_shape=(
+            jax.ShapeDtypeStruct((half_len, width), jnp.bfloat16),
+        ) * (2 * rows),
+        in_specs=[vmem] * 2,
+        out_specs=(vmem,) * (2 * rows),
+        compiler_params=pltpu.CompilerParams(vmem_limit_bytes=32 * 1024 * 1024),
+        cost_estimate=LIGHT,
+        name="branch",
+    )(grouped, out_own)
+    return flat[0::2], flat[1::2]
+
+
+def pick_kernel(place_ref, *refs):
+    ins, outs = refs[:4], refs[4:]
+    for step, out in enumerate(outs):
+        behind = jnp.bitwise_and(place_ref[2] - jnp.bitwise_xor(place_ref[0], step), 3)
+        for k, ref in enumerate(ins):
+
+            @pl.when(behind == k)
+            def _():
+                out[...] = ref[...]
+
+
+def pick_out(place, pieces):
+    vmem = pl.BlockSpec(memory_space=pltpu.VMEM)
+    return pl.pallas_call(
+        pick_kernel,
+        out_shape=(jax.ShapeDtypeStruct(pieces[0].shape, pieces[0].dtype),) * 4,
+        in_specs=[pl.BlockSpec(memory_space=pltpu.SMEM)] + [vmem] * 4,
+        out_specs=(vmem,) * 4,
+        compiler_params=pltpu.CompilerParams(vmem_limit_bytes=16 * 1024 * 1024),
+        cost_estimate=LIGHT,
+        name="pick_out",
+    )(place, *pieces)
 
 
 from jax.sharding import PartitionSpec as P
@@ -720,7 +889,7 @@
 
 
 def whole_sum(mine, came, from_x, from_y):
-    return mine + came.astype(jnp.float32) + from_x.astype(jnp.float32) + from_y.astype(jnp.float32)
+    return mine.astype(jnp.float32) + came.astype(jnp.float32) + from_x.astype(jnp.float32) + from_y.astype(jnp.float32)
 
 
 def wide_shift(array, by):
@@ -755,10 +924,14 @@
     def block(k):
         return lax.dynamic_index_in_dim(blocks, line ^ k, 0, keepdims=False)
 
-    came = [block(0), x_swap(block(1)), y_swap(block(2)), diagonal_swap(block(3))]
-    whole = jnp.zeros_like(blocks)
+    return [block(0), x_swap(block(1)), y_swap(block(2)), diagonal_swap(block(3))]
+
+
+def in_place(pieces):
+    line = lax.axis_index("narrow")
+    whole = jnp.zeros((4,) + pieces[0].shape, pieces[0].dtype)
     for k in range(4):
-        whole = lax.dynamic_update_index_in_dim(whole, came[k], line ^ k, 0)
+        whole = lax.dynamic_update_index_in_dim(whole, pieces[k], line ^ k, 0)
     return whole
 
 
@@ -833,15 +1006,18 @@
     scale_in = norm_scale(inputs_f)
     normed = (inputs_f * scale_in * norm_gain).astype(jnp.bfloat16)
     since = first_pos + jnp.arange(tokens_dev, dtype=jnp.int32) - doc_start
-    since_x, since_y, since_d = x_swap(since), y_swap(since), diagonal_swap(since)
+    since_same = jnp.stack([since, x_swap(since), y_swap(since), diagonal_swap(since)])
     out_pieces = [lax.dynamic_slice_in_dim(out_weight, (lax.axis_index("seq") * 4 + line) * out_rows, out_rows, 0)]
-    if ring:
-        out_pieces += [wide_shift(out_pieces[0], 1), wide_shift(out_pieces[0], 2)]
-    flow.end(normed, since_x, since_y, since_d, out_pieces[-1])
+
+    def out_step():
+        if ring:
+            out_pieces.append(wide_shift(hold(out_pieces[-1]), 1))
+
+    out_step()
+    flow.end(normed, out_pieces[-1])
 
     normed_x, normed_y, normed_o = x_swap(hold(normed)), y_swap(hold(normed)), seq_swap(hold(normed))
-    if ring:
-        out_pieces.append(wide_shift(hold(out_pieces[0]), 3))
+    out_step()
     kernels = lax.dynamic_slice_in_dim(logit_kernel, 2 * part, 2, 0)
     mix = lax.dynamic_slice_in_dim(head_mix, 2 * part, 2, 0)
     taps_forward, taps_backward = tap_bands(hold(kernels), scaling)
@@ -857,136 +1033,127 @@
     down_piece = jnp.concatenate(
         [down_piece[:, at : at + feed_cols] for at in range(0, width, feed_cols)], 0
     )
-    since_same = jnp.stack([since, since_x, since_y, since_d])
+    feed_piece = jnp.concatenate([gate_piece, down_piece], 1)
+    flow.end(normed_x, normed_y, normed_o, taps_forward, since_same, feed_piece, out_pieces[-1])
+
+    low, high = half_rows(normed_x, False), half_rows(normed_y, True)
+    flow.end(low, high, *flow.ended)
+    corner_low, corner_high = y_swap(hold(low)), x_swap(hold(high))
+    cot_x, cot_y = x_swap(hold(cotangent)), y_swap(hold(cotangent))
+    out_step()
     since_other = seq_swap(hold(since_same))
-    flow.end(normed_x, normed_y, normed_o, taps_forward, gate_piece, down_piece, out_pieces[-1], since_other)
-
-    corner_low, corner_high = y_swap(hold(half_rows(normed_x, False))), x_swap(hold(half_rows(normed_y, True)))
-    normed_xo, normed_yo = seq_swap(hold(normed_x)), seq_swap(hold(normed_y))
+    flow.end(corner_low, corner_high, since_other, out_pieces[-1])
+
+    normed_c = jnp.concatenate([corner_low, corner_high], 0)
+    normed_xo, normed_yo, normed_co = seq_swap(normed_x), seq_swap(normed_y), seq_swap(hold(normed_c))
     first = lax.axis_index("seq") == 0
     since_all = hold(
         jnp.concatenate([jnp.where(first, since_same, since_other), jnp.where(first, since_other, since_same)], 1)
     )
-    since_rows = [jnp.broadcast_to(since_all[k][:, None], (2 * tokens_dev, LANES)) for k in range(4)]
-    flow.end(corner_low, corner_high, normed_xo, normed_yo, *since_rows)
-
-    normed_c = jnp.concatenate([corner_low, corner_high], 0)
-    normed_co = seq_swap(hold(normed_c))
+    since_rows = jnp.broadcast_to(since_all[:, :, None], since_all.shape + (LANES,))
+    normed_rows = [(normed, normed_o), (normed_x, normed_xo), (normed_y, normed_yo), (normed_c, normed_co)]
     if ring:
-        out_own = exchange_plane(hold(wide_stack(out_pieces)))
+        out_picked = pick_out(hold(place), out_pieces)
+        flow.end(normed_co, normed_xo, normed_yo, joined, since_rows, *out_picked)
+    else:
+        flow.end(normed_co, normed_xo, normed_yo, joined, since_rows)
+
+    feed_own = gather_wide(hold(feed_piece))
+    if ring:
+        out_picked = [hold(a) for a in out_picked]
+        out_pieces = [
+            out_picked[0], x_swap(out_picked[1]), y_swap(out_picked[2]), diagonal_swap(out_picked[3])
+        ]
+    projected, attended, grouped, weights = attend_rows(
+        hold(core), [a for k in normed_rows for a in k], since_rows, mix, joined, taps_forward, gain_pad, taps_q,
+        head_size,
+    )
+    flow.end(grouped, cot_x, cot_y, *out_pieces)
+    if ring:
+        out_own = place_out(hold(place), out_pieces)
     else:
         out_own = lax.dynamic_slice_in_dim(gather_wide(hold(out_weight)), part * group_cols, group_cols, 0)
-    normed_rows = [(normed, normed_o), (normed_x, normed_xo), (normed_y, normed_yo), (normed_c, normed_co)]
-    flow.end(normed_co, joined, out_own)
-
-    saved, grouped_rows = [None] * 4, [None] * 4
-
-    def attend(k):
-        projected, attended, grouped_rows[k], weights = attend_row(
-            hold(core), *normed_rows[k], since_rows[k], mix, joined, taps_forward, gain_pad, taps_q, head_size
-        )
-        saved[k] = (projected, attended, weights)
-
-    feed_own = [gather_wide(hold(gate_piece)), gather_wide(hold(down_piece))]
-    out_own = jnp.pad(
-        hold(out_own).reshape(2, head_size, width), ((0, 0), (0, LANES - head_size), (0, 0))
-    ).reshape(2 * LANES, width)
-    branch_mine, branch_theirs = [None] * 4, [None] * 4
-
-    def branch(k):
-        branch_theirs[k] = times(hold(grouped_rows[k])[tokens_dev:], out_own).astype(jnp.bfloat16)
-        branch_mine[k] = times(hold(grouped_rows[k])[:tokens_dev], out_own)
-
-    cot_x, cot_y = x_swap(hold(cotangent)), y_swap(hold(cotangent))
-    attend(3)
-    flow.end(grouped_rows[3], out_own)
-    branch(3)
-    flow.end(branch_theirs[3], branch_mine[3])
-    came_3 = seq_swap(hold(branch_theirs[3]))
-    cot_o = seq_swap(hold(cotangent))
-    attend(1)
-    flow.end(grouped_rows[1], cot_x, cot_y, came_3, cot_o)
+        out_own = jnp.pad(
+            out_own.reshape(2, head_size, width), ((0, 0), (0, LANES - head_size), (0, 0))
+        ).reshape(2 * LANES, width)
+    branch_mine, branch_theirs = branch_rows_of(grouped, out_own)
+    flow.end(*branch_mine, *branch_theirs)
+    came_3, came_1, came_2 = (seq_swap(hold(branch_theirs[k])) for k in (3, 1, 2))
+    flow.end(came_3, came_1, came_2)
     low, high = sum_halves(branch_mine[3], hold(came_3))
-    branch(1)
-    flow.end(low, high, branch_theirs[1], branch_mine[1])
+    flow.end(low, high)
     to_y, to_x = x_swap(hold(low)), y_swap(hold(high))
-    came_1, cot_xo = seq_swap(hold(branch_theirs[1])), seq_swap(hold(cot_x))
-    attend(2)
-    flow.end(grouped_rows[2], came_1, cot_xo, to_x, to_y)
-    branch(2)
-    low_x = low_sum(branch_mine[1], hold(came_1), to_x, True)
-    flow.end(branch_theirs[2], branch_mine[2], low_x)
-    came_2, cot_yo = seq_swap(hold(branch_theirs[2])), seq_swap(hold(cot_y))
-    flow.end(came_2, cot_yo)
-    low_y = low_sum(branch_mine[2], hold(came_2), to_y, False)
+    came_0, cot_o = seq_swap(hold(branch_theirs[0])), seq_swap(hold(cotangent))
+    flow.end(came_0, to_x, to_y, cot_o)
+    low_x = low_sum(branch_mine[1], came_1, hold(to_x), True)
+    low_y = low_sum(branch_mine[2], came_2, hold(to_y), False)
     flow.end(low_x, low_y)
+    cot_xo, cot_yo = seq_swap(hold(cot_x)), seq_swap(hold(cot_y))
     branch_x, branch_y = x_swap(hold(low_x)), y_swap(hold(low_y))
-    attend(0)
-    flow.end(grouped_rows[0], branch_x, branch_y)
-    branch(0)
-    flow.end(branch_theirs[0], branch_mine[0])
-    came_0 = seq_swap(hold(branch_theirs[0]))
-    flow.end(came_0)
+    flow.end(branch_x, branch_y, cot_xo, cot_yo, feed_own)
     residual = inputs_f + whole_sum(branch_mine[0], hold(came_0), branch_x, branch_y)
     scale_mid = norm_scale(residual)
     normed_ffn = (residual * scale_mid * feed_gain).astype(jnp.bfloat16)
     flow.end(normed_ffn)
 
     ffn_x, ffn_y, ffn_o = x_swap(hold(normed_ffn)), y_swap(hold(normed_ffn)), seq_swap(hold(normed_ffn))
-    flow.end(ffn_o, ffn_x, ffn_y)
-    corner_low, corner_high = y_swap(hold(half_rows(ffn_x, False))), x_swap(hold(half_rows(ffn_y, True)))
-    ffn_xo, ffn_yo = seq_swap(hold(ffn_x)), seq_swap(hold(ffn_y))
-    flow.end(corner_low, corner_high, ffn_xo, ffn_yo)
-    cot_low, cot_high = y_swap(hold(half_rows(cot_x, False))), x_swap(hold(half_rows(cot_y, True)))
-    ffn_c = jnp.concatenate([corner_low, corner_high], 0)
-    ffn_co = seq_swap(hold(ffn_c))
+    flow.end(ffn_o)
     hidden_rows, gate_grads, feed_out = [None] * 4, [None] * 4, [None] * 4
-    ffn_rows = [(normed_ffn, ffn_o), (ffn_x, ffn_xo), (ffn_y, ffn_yo), (ffn_c, ffn_co)]
+    ffn_rows = [(normed_ffn, ffn_o), None, None, None]
     cotangent_rows = [(cotangent, cot_o), (cot_x, cot_xo), (cot_y, cot_yo), None]
+
+    gate_own, down_own = split_feed(hold(feed_own), wide)
 
     def feed(k):
         hidden_rows[k], gate_grads[k], *feed_out[k] = feed_row(
-            hold(ffn_rows[k][0]), ffn_rows[k][1], *cotangent_rows[k], feed_own, wide
+            hold(ffn_rows[k][0]), ffn_rows[k][1], *cotangent_rows[k], gate_own, down_own
         )
 
     feed(0)
-    flow.end(hidden_rows[0], ffn_co, cot_low, cot_high)
+    flow.end(hidden_rows[0], ffn_x, ffn_y)
+    ffn_xo, ffn_yo = seq_swap(hold(ffn_x)), seq_swap(hold(ffn_y))
+    ffn_rows[1], ffn_rows[2] = (ffn_x, ffn_xo), (ffn_y, ffn_yo)
+    low, high = half_rows(cot_x, False), half_rows(cot_y, True)
+    flow.end(ffn_xo, ffn_yo, low, high)
+    cot_low, cot_high = y_swap(hold(low)), x_swap(hold(high))
+    back_came = [None] * 4
+    feed(1)
+    flow.end(hidden_rows[1], cot_low, cot_high)
+    low, high = half_rows(ffn_x, False), half_rows(ffn_y, True)
     cot_c = jnp.concatenate([cot_low, cot_high], 0)
+    flow.end(low, high, cot_c)
+    corner_low, corner_high = y_swap(hold(low)), x_swap(hold(high))
     cot_co = seq_swap(hold(cot_c))
-    cotangent_rows[3] = (cot_c, cot_co)
-    back_came = [None] * 4
-    back_came[0] = seq_swap(hold(feed_out[0][3]))
-    feed(1)
-    flow.end(hidden_rows[1], cot_co, back_came[0])
     back_came[1] = seq_swap(hold(feed_out[1][3]))
-    feed_came = [seq_swap(hold(feed_out[0][1])), seq_swap(hold(feed_out[1][1]))]
+    feed(2)
+    flow.end(hidden_rows[2], corner_low, corner_high, cot_co, back_came[1])
+    back_came[2] = seq_swap(hold(feed_out[2][3]))
+    ffn_c = jnp.concatenate([corner_low, corner_high], 0)
+    low_x = pair_sum(feed_out[1][2], hold(back_came[1]))
+    flow.end(ffn_c, back_came[2], low_x)
+    ffn_co = seq_swap(hold(ffn_c))
+    low_y = pair_sum(feed_out[2][2], hold(back_came[2]))
+    ffn_rows[3], cotangent_rows[3] = (ffn_c, ffn_co), (cot_c, cot_co)
+    flow.end(ffn_co, low_x, low_y)
+    back_x, back_y = x_swap(hold(low_x)), y_swap(hold(low_y))
     feed(3)
-    flow.end(hidden_rows[3], back_came[1], *feed_came)
-    back_came[3] = seq_swap(hold(feed_out[3][3]))
-    flow.end(back_came[3])
-    low, high = sum_halves(feed_out[3][2], hold(back_came[3]))
-    flow.end(low, high)
-    to_y, to_x = x_swap(hold(low)), y_swap(hold(high))
-    feed(2)
-    flow.end(hidden_rows[2], to_x, to_y)
-    back_came[2] = seq_swap(hold(feed_out[2][3]))
-    feed_came.append(seq_swap(hold(feed_out[2][1])))
-    low_x = low_sum(feed_out[1][2], back_came[1], hold(to_x), True)
-    flow.end(back_came[2], feed_came[2], low_x)
-    low_y = low_sum(feed_out[2][2], hold(back_came[2]), to_y, False)
-    flow.end(low_x, low_y)
-    back_x, back_y = x_swap(hold(low_x)), y_swap(hold(low_y))
+    flow.end(hidden_rows[3], back_x, back_y)
+    back_came[3], back_came[0] = seq_swap(hold(feed_out[3][3])), seq_swap(hold(feed_out[0][3]))
+    flow.end(back_came[3], back_came[0])
+    low = pair_sum(feed_out[3][2], hold(back_came[3]))
+    flow.end(low)
+    back_d = diagonal_swap(hold(low))
     feed_grad_own = feed_grad(
         [hold(a) for k in ffn_rows for a in k], gate_grads, hidden_rows, [a for k in cotangent_rows for a in k], wide
     )
-    flow.end(back_x, back_y, feed_grad_own)
+    flow.end(back_d, feed_grad_own)
     shard_feed = scatter_wide(hold(feed_grad_own))
-    feed_came.append(seq_swap(hold(feed_out[3][1])))
-    grad_ffn = whole_sum(feed_out[0][2], hold(back_came[0]), back_x, back_y)
+    feed_came = [seq_swap(hold(feed_out[k][1])) for k in range(4)]
+    grad_ffn = whole_sum(feed_out[0][2], back_came[0], back_x, back_y) + hold(back_d).astype(jnp.float32)
     norm_part, grad_feed = norm_back(residual, scale_mid, feed_gain, grad_ffn)
     grad_residual = norm_part + cotangent.astype(jnp.float32)
     grad_branch = grad_residual.astype(jnp.bfloat16)
-    flow.end(grad_branch, feed_came[3])
+    flow.end(grad_branch, *feed_came)
 
     gb_x, gb_y, gb_o = x_swap(hold(grad_branch)), y_swap(hold(grad_branch)), seq_swap(hold(grad_branch))
     low, high = sum_halves(feed_out[3][0], hold(feed_came[3]))
@@ -996,8 +1163,8 @@
 
     def attend_back(k):
         grad_joined[k], normed_mine[k], normed_theirs[k], smalls[k], tap_sums[k] = attend_row_back(
-            hold(core), *branch_rows[k], out_own, joined, saved[k], since_rows[k], mix, taps_backward, gain_pad,
-            taps_q, taps_k, head_size,
+            k, hold(core), *branch_rows[k], out_own, joined, (projected, attended, weights), since_rows, mix,
+            taps_backward, gain_pad, taps_q, taps_k, head_size,
         )
 
     attend_back(0)
@@ -1013,25 +1180,25 @@
     low_y = low_sum(feed_out[2][0], feed_came[2], hold(to_y), False)
     gb_c = jnp.concatenate([corner_low, corner_high], 0)
     flow.end(low_x, low_y, gb_c)
-    feed_x, feed_y = x_swap(hold(low_x)), y_swap(hold(low_y))
     gb_co = seq_swap(hold(gb_c))
+    flow.end(low_x, low_y, gb_co)
+    feed_main_x, feed_main_y = x_swap(hold(low_x)), y_swap(hold(low_y))
     branch_rows[3] = (gb_c, gb_co)
     normed_came = [None] * 4
     normed_came[1] = seq_swap(hold(normed_theirs[1]))
     attend_back(2)
-    flow.end(grad_joined[2], gb_co, normed_came[1], feed_x, feed_y)
-    block_out = (residual + whole_sum(feed_out[0][0], hold(feed_came[0]), feed_x, feed_y)).astype(jnp.bfloat16)
+    grad_out_own = small_weight_grad([grouped.reshape(-1, 2 * LANES)], [hold(a) for k in branch_rows for a in k], "out_grad")
+    flow.end(grad_joined[2], normed_came[1], grad_out_own, feed_main_x, feed_main_y)
     normed_came[2] = seq_swap(hold(normed_theirs[2]))
-    grad_out_own = weight_grad(grouped_rows, [hold(a) for k in branch_rows for a in k], LANES, "out_grad")
-    grad_out_own = grad_out_own.reshape(2, LANES, width)[:, :head_size].reshape(2 * head_size, width)
     low_x = pair_sum(normed_mine[1], hold(normed_came[1]))
-    flow.end(normed_came[2], grad_out_own, low_x)
+    grad_out_own = hold(grad_out_own).reshape(2, LANES, width)[:, :head_size].reshape(2 * head_size, width)
+    flow.end(normed_came[2], low_x, grad_out_own)
     low_y = pair_sum(normed_mine[2], hold(normed_came[2]))
     flow.end(low_x, low_y)
     grad_x, grad_y = x_swap(hold(low_x)), y_swap(hold(low_y))
     out_terms = hold(grad_out_own)
     if ring:
-        out_terms = exchange_plane(out_terms.reshape(4, out_rows, width))
+        out_terms = in_place(exchange_plane(out_terms.reshape(4, out_rows, width)))
     attend_back(3)
     flow.end(grad_joined[3], grad_x, grad_y, out_terms)
 
@@ -1075,11 +1242,18 @@
     fill = -(sum(lengths) + width) % (8 * LANES)
     packed = jnp.concatenate(pieces + [jnp.zeros((fill,), jnp.float32)]).reshape(-1, LANES)
     packed = jnp.concatenate([packed, grad_norm.reshape(-1, LANES)], 0)
+    packed = packed + seq_swap(packed)
+    if wide & (wide - 1):
+        packed = lax.psum(packed, "wide")
+    else:
+        for hop in [1 << i for i in range(16) if 1 << i < wide]:
+            packed = packed + lax.ppermute(packed, "wide", [(i, i ^ hop) for i in range(wide)])
     flow.end(packed, feed_x, feed_y, feed_o)
-    packed = packed + seq_swap(hold(packed))
+    packed = packed + x_swap(hold(packed))
     feed_low, feed_high = y_swap(hold(half_rows(feed_x, False))), x_swap(hold(half_rows(feed_y, True)))
     feed_xo, feed_yo = seq_swap(hold(feed_x)), seq_swap(hold(feed_y))
-    flow.end(feed_low, feed_high, feed_xo, feed_yo, packed, shard_joined)
+    block_out = (residual + whole_sum(feed_out[0][0], hold(feed_came[0]), feed_main_x, feed_main_y)).astype(jnp.bfloat16)
+    flow.end(feed_low, feed_high, feed_xo, feed_yo, packed, shard_joined, block_out)
 
     def columns(rows_of, sections, size):
         if 2 * size % LANES == 0:
@@ -1088,21 +1262,9 @@
         split = every.reshape(cores, rows_of[0][0].shape[0], sections, size)
         return jnp.moveaxis(split, 0, 2).reshape(rows_of[0][0].shape[0], -1).astype(jnp.float32)
 
-    def wide_sums(array, hops):
-        if wide & (wide - 1):
-            return lax.psum(array, "wide") if 1 in hops else array
-        for hop in hops:
-            array = array + lax.ppermute(array, "wide", [(i, i ^ hop) for i in range(wide)])
-        return array
-
     joined_x, joined_y, joined_o = x_swap(hold(shard_joined)), y_swap(hold(shard_joined)), seq_swap(hold(shard_joined))
     feed_c = jnp.concatenate([feed_low, feed_high], 0)
     feed_co = seq_swap(hold(feed_c))
-    packed = wide_sums(hold(packed), [1])
-    flow.end(joined_x, joined_y, joined_o, feed_co, packed)
-    joined_low, joined_high = y_swap(hold(half_rows(joined_x, False))), x_swap(hold(half_rows(joined_y, True)))
-    joined_xo, joined_yo = seq_swap(hold(joined_x)), seq_swap(hold(joined_y))
-    packed = wide_sums(hold(packed), [2 << i for i in range(16) if 2 << i < wide])
     if ring:
         grad_gate, grad_down, grad_out = place_feed(
             place, [hold(shard_feed), feed_o, feed_x, feed_xo, feed_y, feed_yo, feed_c, feed_co], chunk,
@@ -1114,12 +1276,14 @@
         grad_gate = jnp.moveaxis(split, 0, 2).reshape(shard_feed.shape[0], -1).astype(jnp.float32)
         split = every[:, :, 2 * feed_cols :].reshape(cores, width // feed_cols, chunk, feed_cols)
         grad_down = jnp.swapaxes(split, 1, 2).reshape(cores * chunk, width).astype(jnp.float32)
-        grad_out = scatter_wide(lax.all_gather(out_terms, PLANE, axis=0, tiled=True)).astype(jnp.float32)
-    flow.end(joined_low, joined_high, joined_xo, joined_yo, packed, grad_gate)
+        grad_out = scatter_wide(lax.all_gather(grad_out_own, PLANE, axis=0, tiled=True)).astype(jnp.float32)
+    flow.end(joined_x, joined_y, joined_o, packed, grad_gate)
+    joined_low, joined_high = y_swap(hold(half_rows(joined_x, False))), x_swap(hold(half_rows(joined_y, True)))
+    joined_xo, joined_yo = seq_swap(hold(joined_x)), seq_swap(hold(joined_y))
+    packed = packed + y_swap(hold(packed))
+    flow.end(joined_low, joined_high, joined_xo, joined_yo, packed)
     joined_c = jnp.concatenate([joined_low, joined_high], 0)
     joined_co = seq_swap(hold(joined_c))
-    packed = packed + x_swap(hold(packed))
-    packed = packed + y_swap(packed)
     joined_rows = [(shard_joined, joined_o), (joined_x, joined_xo), (joined_y, joined_yo), (joined_c, joined_co)]
     grad_qkv = columns(joined_rows, 3, group_cols)
     packed = packed.reshape(-1)

time: 559 us -> 497 us (0.89)
  local copies, waits for them, and re-layouts: 92.1 us -> 53.8 us
  waiting for transfers between devices: 163 us -> 141 us
  Pallas kernels: 179 us -> 187 us
    unnamed x334 -> x221, local copies, waits for them, and re-layouts: 59 us -> 36.5 us
    ppermute x23 -> x22, waiting for transfers between devices: 76.2 us -> 55.5 us  [y_swap(): return lax.ppermute(array, 'narrow', [(0, 2), (2, 0), (1, 3), (3, 1)])]
    pallas_call x8 -> x10, Pallas kernels: 65.6 us -> 76.9 us  [the longest x4 35.9 us: feed_row(): pl.pallas_call(feed_kernel, out_shape=(jax.ShapeDtypeStruct((2 * half_len...]
    ppermute x23 -> x22, waiting for transfers between devices: 47 us -> 35.8 us  [x_swap(): return lax.ppermute(array, 'narrow', [(0, 1), (1, 0), (2, 3), (3, 2)])]
    ppermute x2, waiting for transfers between devices: 3.83 us -> 11.9 us  [on_device(): lax.ppermute(packed, 'wide', [(i, i ^ hop) for i in range(wide)])]
    ppermute x42, waiting for transfers between devices: 15.9 us -> 23.7 us  [seq_swap(): return lax.ppermute(array, 'seq', SWAP)]
    dynamic_update_slice x10 -> x3, local copies, waits for them, and re-layouts: 6.62 us -> 0.05 us  [in_place(): whole = lax.dynamic_update_index_in_dim(whole, pieces[k], line ^ k, 0)]
    ppermute x6, waiting for transfers between devices: 8.95 us -> 2.9 us  [wide_shift(): lax.ppermute(array, 'wide', [(i, (i + by) % count) for i in range(count)])]
  transfers between devices with their start and end apart: 105 -> 103, of which waited for: 42 -> 49; matrix products, arithmetic and copies ran while one was open for 11% -> 9% of each run, Pallas kernels for 30% -> 37%
where the time goes in v3:
time: 497 us; the launch traced here: 488 us
  Pallas kernels  187 us (38%)
  waiting for transfers between devices  141 us (28%)
  starting transfers between devices  71.6 us (14%)
  local copies, waits for them, and re-layouts  53.8 us (11%)
  other arithmetic  18.8 us (4%)
  between operations  15.8 us (3%)
    pallas_call x4, Pallas kernels, attend_row_back(): pl.pallas_call(functools.partial(backward_kernel, taps_q, taps_k, head_si...  57.7 us
    ppermute x22, waiting for transfers between devices, y_swap(): return lax.ppermute(array, 'narrow', [(0, 2), (2, 0), (1, 3), (3, 1)])  55.5 us
    unnamed x221, local copies, waits for them, and re-layouts  36.5 us
    pallas_call x4, Pallas kernels, feed_row(): pl.pallas_call(feed_kernel, out_shape=(jax.ShapeDtypeStruct((2 * half_len...  35.9 us
    ppermute x22, waiting for transfers between devices, x_swap(): return lax.ppermute(array, 'narrow', [(0, 1), (1, 0), (2, 3), (3, 2)])  35.8 us
    pallas_call x1, Pallas kernels, attend_rows(): pl.pallas_call(functools.partial(forward_kernel, taps_q, head_size, rows)...  35 us
    ppermute x22, starting transfers between devices, x_swap(): return lax.ppermute(array, 'narrow', [(0, 1), (1, 0), (2, 3), (3, 2)])  25.5 us
    ppermute x42, waiting for transfers between devices, seq_swap(): return lax.ppermute(array, 'seq', SWAP)  23.7 us
  transfers between devices with their start and end apart: 103, of which 49 were waited for; matrix products, arithmetic and copies ran while one was open for 9% of the time, Pallas kernels for 37%

profile of v3, /device:TPU:0, one launch (start us, length us, event | category | flops | bytes accessed | tf_op | source)
XLA Modules:
  0.0 488.4 jit_solution(9478310874434631085)
XLA Ops:
  9.9 3.0 collective-permute-start.4
  14.5 2.1 collective-permute-start
  18.9 2.9 collective-permute-done.refs_1_
  21.8 1.7 collective-permute-start.1
  25.0 1.5 dynamic-slice_dynamic-update-slice_fusion.8
  26.5 1.5 dynamic-slice_dynamic-update-slice_fusion.7
  28.1 1.5 dynamic-slice_dynamic-update-slice_fusion.6
  29.6 1.5 dynamic-slice_dynamic-update-slice_fusion.5
  31.2 1.5 dynamic-slice_dynamic-update-slice_fusion.4
  32.7 1.5 dynamic-slice_dynamic-update-slice_fusion.3
  34.2 1.5 dynamic-slice_dynamic-update-slice_fusion.2
  36.8 1.5 dynamic-slice_dynamic-update-slice_fusion.1
  38.4 3.3 tap_bands.1
  46.9 1.6 collective-permute-start.11
  48.9 8.6 %collective-permute-done.8 = bf16[128,1536]{1,0:T(8,128)(2,1)S(1)} collective-permute-done((bf16[128,1536]{1,0:T(8,128)(2,1)S(1)}, bf16[128,1536]{1,0:T(8,128)(2,1)S(1)}, u32[]{:S(2)}, u32[]{:S(2)}) %collective-permute-start.8) | collective-permute-done | bytes 393248 | tf_op jit(solution)/shard_map/ppermute | solution.py:856
  61.9 4.2 all-gather.3.cloned.1.call-done.joined_ref
  69.1 1.8 collective-permute-start.16
  72.6 1.8 collective-permute-start.17
  76.6 35.0 %attend_rows.1 = (bf16[4,512,768]{2,1,0:T(8,128)(2,1)}, f32[4,512,256]{2,1,0:T(8,128)}, bf16[4,512,256]{2,1,0:T(8,128)(2,1)}, f32[4,2,512,512]{3,2,1,0:T(8,128)}) custom-call(s32[1]{0:T(128)} %bitcast.core_ref, f32[2,2]{1,0:T(2,128)S(1)} %copy.30.mix_ref, s32[4,512,128]{2,1,0:T(8,128)} %broadcast_in_dim.44.since_all, ...), custom_call_target="tpu_custom_call" | custom-call | flops 1000000 | bytes 1000000 | tf_op jit(solution)/shard_map/attend_rows/pallas_call | solution.py:321
  113.3 1.8 branch.1
  121.6 10.0 %collective-permute-done.24.extra_ref = bf16[128,1536]{1,0:T(8,128)(2,1)S(1)} collective-permute-done((bf16[128,1536]{1,0:T(8,128)(2,1)S(1)}, bf16[128,1536]{1,0:T(8,128)(2,1)S(1)}, u32[]{:S(2)}, u32[]{:S(2)}) %collective-permute-start.24) | collective-permute-done | bytes 393248 | tf_op jit(solution)/shard_map/ppermute | solution.py:856
  136.7 16.6 %collective-permute-done.27 = bf16[256,1536]{1,0:T(8,128)(2,1)S(1)} collective-permute-done((bf16[256,1536]{1,0:T(8,128)(2,1)S(1)}, bf16[256,1536]{1,0:T(8,128)(2,1)S(1)}, u32[]{:S(2)}, u32[]{:S(2)}) %collective-permute-start.27) | collective-permute-done | bytes 786464 | tf_op jit(solution)/shard_map/ppermute | solution.py:852
  154.3 1.9 all-gather.5.cloned.1.call-done.feed_ref
  156.2 2.9 multiply_reduce_fusion.2
  159.4 1.6 collective-permute-start.32
  162.8 1.7 copy-done.2
  165.6 8.8 %feed_row.4 = (bf16[512,512]{1,0:T(8,128)(2,1)S(1)}, bf16[512,1024]{1,0:T(8,128)(2,1)}, bf16[256,1536]{1,0:T(8,128)(2,1)S(1)}, bf16[256,1536]{1,0:T(8,128)(2,1)}...) custom-call(bf16[256,1536]{1,0:T(8,128)(2,1)S(1)} %multiply_convert_fusion.own_ref.refs_0_, ...), custom_call_target="tpu_custom_call" | custom-call | bytes 28800000 | tf_op jit(solution)/shard_map/feed_row/pallas_call | solution.py:618
  174.4 4.9 %collective-permute-done.32.own_ref.refs_2_ = bf16[256,1536]{1,0:T(8,128)(2,1)S(1)} collective-permute-done((bf16[256,1536]{1,0:T(8,128)(2,1)S(1)}, bf16[256,1536]{1,0:T(8,128)(2,1)S(1)}, u32[]{:S(2)}, u32[]{:S(2)}) %collective-permute-start.32) | collective-permute-done | bytes 786464 | tf_op jit(solution)/shard_map/ppermute | solution.py:852
  186.1 9.0 %feed_row.6 = (bf16[512,512]{1,0:T(8,128)(2,1)S(1)}, bf16[512,1024]{1,0:T(8,128)(2,1)}, bf16[256,1536]{1,0:T(8,128)(2,1)S(1)}, bf16[256,1536]{1,0:T(8,128)(2,1)}...) custom-call(bf16[256,1536]{1,0:T(8,128)(2,1)S(1)} %collective-permute-done.32.own_ref.refs_2_, ...), custom_call_target="tpu_custom_call" | custom-call | bytes 28800000 | tf_op jit(solution)/shard_map/feed_row/pallas_call | solution.py:618
  198.0 9.1 %feed_row.5 = (bf16[512,512]{1,0:T(8,128)(2,1)S(1)}, bf16[512,1024]{1,0:T(8,128)(2,1)}, bf16[256,1536]{1,0:T(8,128)(2,1)S(1)}, bf16[256,1536]{1,0:T(8,128)(2,1)}...) custom-call(bf16[256,1536]{1,0:T(8,128)(2,1)S(1)} %collective-permute-done.33.own_ref.refs_4_, ...), custom_call_target="tpu_custom_call" | custom-call | bytes 28800000 | tf_op jit(solution)/shard_map/feed_row/pallas_call | solution.py:618
  211.0 2.0 collective-permute-done.43.other_ref.refs_7_
  215.0 9.0 %feed_row.7 = (bf16[512,512]{1,0:T(8,128)(2,1)S(1)}, bf16[512,1024]{1,0:T(8,128)(2,1)}, bf16[256,1536]{1,0:T(8,128)(2,1)S(1)}, bf16[256,1536]{1,0:T(8,128)(2,1)}...) custom-call(bf16[256,1536]{1,0:T(8,128)(2,1)S(1)} %constant_dynamic-update-slice_fusion.4.own_ref.refs_6_, ...), custom_call_target="tpu_custom_call" | custom-call | bytes 28800000 | tf_op jit(solution)/shard_map/feed_row/pallas_call | solution.py:618
  224.9 7.6 %collective-permute-done.45 = bf16[256,1536]{1,0:T(8,128)(2,1)S(1)} collective-permute-done((bf16[256,1536]{1,0:T(8,128)(2,1)S(1)}, bf16[256,1536]{1,0:T(8,128)(2,1)S(1)}, u32[]{:S(2)}, u32[]{:S(2)}) %collective-permute-start.45) | collective-permute-done | bytes 786464 | tf_op jit(solution)/shard_map/ppermute | solution.py:856
  233.3 1.8 collective-permute-done.47
  236.4 2.5 collective-permute-start.48
  238.9 16.9 %feed_grad.1 = bf16[1536,1536]{1,0:T(8,128)(2,1)} custom-call(bf16[256,1536]{1,0:T(8,128)(2,1)} %copy-done.6, bf16[256,1536]{1,0:T(8,128)(2,1)} %copy-done.17, bf16[256,1536]{1,0:T(8,128)(2,1)} %copy-done.10, bf16[256,1536]{1,0:T(8,128)(2,1)} %copy-done.19, bf16[256,1536]{1,0:T(8,128)(2,1)} %copy-done.11, bf16[256,1536]{1,0:T(8,128)(2,1)} %copy-done.18, ...), custom_call_target="tpu_custom_call" | custom-call | bytes 61200000 | tf_op jit(solution)/shard_map/feed_grad/pallas_call | solution.py:668
  258.2 3.3 multiply_reduce_fusion.1
  266.4 14.2 %attend_row_back.4 = (bf16[512,640]{1,0:T(8,128)(2,1)S(1)}, bf16[256,1536]{1,0:T(8,128)(2,1)S(1)}, bf16[256,1536]{1,0:T(8,128)(2,1)S(1)}, f32[8,128]{1,0:T(8,128)S(1)}, f32[2,66,128]{2,1,0:T(8,128)S(1)}) custom-call(s32[1]{0:T(128)} %bitcast.core_ref, f32[2,2]{1,0:T(2,128)S(1)} %copy.30.mix_ref, bf16[256,1536]{1,0:T(8,128)(2,1)S(1)} %fusion.13.own_ref.refs_1_, ...), custom_call_target="tpu_custom_call" | custom-call | bytes 50400000 | tf_op jit(solution)/shard_map/attend_row_back/pallas_call | solution.py:525
  280.6 2.4 collective-permute-done.54.own_ref.refs_3_
  284.8 1.7 collective-permute-done.57.other_ref.refs_6_
  291.7 14.2 %attend_row_back.5 = (bf16[512,640]{1,0:T(8,128)(2,1)S(1)}, bf16[256,1536]{1,0:T(8,128)(2,1)S(1)}, bf16[256,1536]{1,0:T(8,128)(2,1)S(1)}, f32[8,128]{1,0:T(8,128)S(1)}, f32[2,66,128]{2,1,0:T(8,128)S(1)}) custom-call(s32[1]{0:T(128)} %bitcast.core_ref, f32[2,2]{1,0:T(2,128)S(1)} %copy.30.mix_ref, ...), custom_call_target="tpu_custom_call" | custom-call | bytes 50400000 | tf_op jit(solution)/shard_map/attend_row_back/pallas_call | solution.py:525
  308.6 2.3 collective-permute-done.62.refs_8_.other_ref
  310.8 1.5 collective-permute-start.65
  313.4 1.8 out_grad.1
  316.1 15.3 %attend_row_back.6 = (bf16[512,640]{1,0:T(8,128)(2,1)S(1)}, bf16[256,1536]{1,0:T(8,128)(2,1)S(1)}, bf16[256,1536]{1,0:T(8,128)(2,1)}, f32[8,128]{1,0:T(8,128)S(1)}, f32[2,66,128]{2,1,0:T(8,128)S(1)}) custom-call(s32[1]{0:T(128)} %bitcast.core_ref, f32[2,2]{1,0:T(2,128)S(1)} %copy.30.mix_ref, bf16[256,1536]{1,0:T(8,128)(2,1)S(1)} %collective-permute-done.55.own_ref.refs_5_, ...), custom_call_target="tpu_custom_call" | custom-call | bytes 50400000 | tf_op jit(solution)/shard_map/attend_row_back/pallas_call | solution.py:525
  342.3 1.9 collective-permute-start.69
  345.8 14.0 %attend_row_back.7 = (bf16[512,640]{1,0:T(8,128)(2,1)S(1)}, bf16[256,1536]{1,0:T(8,128)(2,1)S(1)}, bf16[256,1536]{1,0:T(8,128)(2,1)S(1)}, f32[8,128]{1,0:T(8,128)S(1)}, f32[2,66,128]{2,1,0:T(8,128)S(1)}) custom-call(s32[1]{0:T(128)} %bitcast.core_ref, f32[2,2]{1,0:T(2,128)S(1)} %copy.30.mix_ref, ...), custom_call_target="tpu_custom_call" | custom-call | bytes 50400000 | tf_op jit(solution)/shard_map/attend_row_back/pallas_call | solution.py:525
  359.9 7.4 %collective-permute-done.71 = bf16[256,1536]{1,0:T(8,128)(2,1)S(1)} collective-permute-done((bf16[256,1536]{1,0:T(8,128)(2,1)S(1)}, bf16[256,1536]{1,0:T(8,128)(2,1)S(1)}, u32[]{:S(2)}, u32[]{:S(2)}) %collective-permute-start.71) | collective-permute-done | bytes 786464 | tf_op jit(solution)/shard_map/ppermute | solution.py:856
  367.8 1.8 collective-permute-done.73
  372.0 1.8 dynamic-slice_bitcast_fusion.1
  375.2 3.3 collective-permute-start.77
  378.5 10.2 %joined_grad.1 = bf16[1536,640]{1,0:T(8,128)(2,1)} custom-call(bf16[256,1536]{1,0:T(8,128)(2,1)} %copy-done.7, bf16[256,1536]{1,0:T(8,128)(2,1)} %copy-done.23, bf16[256,1536]{1,0:T(8,128)(2,1)} %collective-permute-done.1.refs_2_, bf16[256,1536]{1,0:T(8,128)(2,1)} %collective-permute-done.13.refs_3_, bf16[256,1536]{1,0:T(8,128)(2,1)} %collective-permute-done.2.refs_4_, ...), custom_call_target="tpu_custom_call" | custom-call | bytes 28800000 | tf_op jit(solution)/shard_map/joined_grad/pallas_call | solution.py:707
  388.8 2.7 collective-permute-done.75
  393.8 2.6 pad_maximum_fusion.refs_0_.refs_8_
  398.9 2.8 fusion.5
  403.3 5.6 %collective-permute-done.79 = f32[48,128]{1,0:T(8,128)S(1)} collective-permute-done((f32[48,128]{1,0:T(8,128)S(1)}, f32[48,128]{1,0:T(8,128)S(1)}, u32[]{:S(2)}, u32[]{:S(2)}) %collective-permute-start.79) | collective-permute-done | bytes 24608 | tf_op jit(solution)/shard_map/ppermute | solution.py:1250
  409.0 6.3 %collective-permute-done.80 = f32[48,128]{1,0:T(8,128)S(1)} collective-permute-done((f32[48,128]{1,0:T(8,128)S(1)}, f32[48,128]{1,0:T(8,128)S(1)}, u32[]{:S(2)}, u32[]{:S(2)}) %collective-permute-start.80) | collective-permute-done | bytes 24608 | tf_op jit(solution)/shard_map/ppermute | solution.py:1250
  415.2 11.6 %collective-permute-done.82.refs_4_.refs_12_ = bf16[432,1536]{1,0:T(8,128)(2,1)} collective-permute-done((bf16[432,1536]{1,0:T(8,128)(2,1)}, bf16[432,1536]{1,0:T(8,128)(2,1)}, u32[]{:S(2)}, u32[]{:S(2)}) %collective-permute-start.82) | collective-permute-done | bytes 1327136 | tf_op jit(solution)/shard_map/ppermute | solution.py:856
  432.4 2.5 fusion.7
  434.9 8.7 %collective-permute-done.84 = f32[48,128]{1,0:T(8,128)S(1)} collective-permute-done((f32[48,128]{1,0:T(8,128)S(1)}, f32[48,128]{1,0:T(8,128)S(1)}, u32[]{:S(2)}, u32[]{:S(2)}) %collective-permute-start.84) | collective-permute-done | bytes 24608 | tf_op jit(solution)/shard_map/ppermute | solution.py:852
  443.7 1.6 collective-permute-done.85
  449.7 11.6 %place_feed.1 = (f32[384,8192]{1,0:T(8,128)}, f32[1024,1536]{1,0:T(8,128)}, f32[384,1536]{1,0:T(8,128)}) custom-call(s32[3]{0:T(128)} %copy-done.54, bf16[432,1536]{1,0:T(8,128)(2,1)} %pad_maximum_fusion.refs_0_.refs_8_, bf16[432,1536]{1,0:T(8,128)(2,1)} %collective-permute-done.83.refs_1_.refs_9_, ...), custom_call_target="tpu_custom_call" | custom-call | bytes 39600000 | tf_op jit(solution)/shard_map/place_feed/pallas_call | solution.py:130
  464.9 5.6 %collective-permute-done.93 = f32[48,128]{1,0:T(8,128)S(1)} collective-permute-done((f32[48,128]{1,0:T(8,128)S(1)}, f32[48,128]{1,0:T(8,128)S(1)}, u32[]{:S(2)}, u32[]{:S(2)}) %collective-permute-start.93) | collective-permute-done | bytes 24608 | tf_op jit(solution)/shard_map/ppermute | solution.py:856
  474.6 6.8 %place_columns.1 = f32[384,4608]{1,0:T(8,128)} custom-call(s32[3]{0:T(128)} %copy-done.54, bf16[384,640]{1,0:T(8,128)(2,1)} %reduce-scatter.5.cloned.1.call-done.refs_0_, bf16[384,640]{1,0:T(8,128)(2,1)} %collective-permute-done.91.refs_1_, bf16[384,640]{1,0:T(8,128)(2,1)} %copy-done.75, bf16[384,640]{1,0:T(8,128)(2,1)} %copy-done.93, ...), custom_call_target="tpu_custom_call" | custom-call | bytes 18000000 | tf_op jit(solution)/shard_map/place_columns/pallas_call | solution.py:79
  (483 shorter events, 120.7 us)
Async XLA Ops:
  7.2 58.9 %all-gather.3.cloned.1.call-start = ((), (), s32[]{:S(2)}) async-start(), calls=%async_computation.2 | async-start | bytes 2457600 | tf_op jit(solution)/shard_map/all_gather | solution.py:914
  14.4 141.8 %all-gather.5.cloned.1.call-start = ((), (), s32[]{:S(2)}) async-start(), calls=%async_computation.3 | async-start | bytes 5898240 | tf_op jit(solution)/shard_map/all_gather | solution.py:914
  21.8 22.1 %collective-permute-start.1 = (bf16[256,1536]{1,0:T(8,128)(2,1)S(1)}, bf16[256,1536]{1,0:T(8,128)(2,1)}, u32[]{:S(2)}, u32[]{:S(2)}) collective-permute-start(bf16[256,1536]{1,0:T(8,128)(2,1)S(1)} %fusion.2.refs_0_), channel_id=1, source_target_pairs={{0,8},{8,0},{16,24},{24,16},{1,9},{9,1},{17,25},{25,17},{2,10},{10... | collective-permute-start | bytes 2359304 | tf_op jit(solution)/shard_map/ppermute | solution.py:852
  23.5 21.4 %collective-permute-start.2 = (bf16[256,1536]{1,0:T(8,128)(2,1)S(1)}, bf16[256,1536]{1,0:T(8,128)(2,1)}, u32[]{:S(2)}, u32[]{:S(2)}) collective-permute-start(bf16[256,1536]{1,0:T(8,128)(2,1)S(1)} %fusion.2.refs_0_), channel_id=1, source_target_pairs={{0,16},{16,0},{8,24},{24,8},{1,17},{17,1},{9,25},{25,9},{2,18},{18... | collective-permute-start | bytes 2359304 | tf_op jit(solution)/shard_map/ppermute | solution.py:856
  25.0 20.9 %collective-permute-start.3 = (bf16[256,1536]{1,0:T(8,128)(2,1)S(1)}, bf16[256,1536]{1,0:T(8,128)(2,1)S(1)}, u32[]{:S(2)}, u32[]{:S(2)}) collective-permute-start(bf16[256,1536]{1,0:T(8,128)(2,1)S(1)} %fusion.2.refs_0_), channel_id=1, source_target_pairs={{0,1},{1,0},{2,3},{3,2},{4,5},{5,4},{6,7},{7,6},{8,9},{9,8},{10,11... | collective-permute-start | bytes 2359304 | tf_op jit(solution)/shard_map/ppermute | solution.py:848
  25.0 20.9 %collective-permute-start.7 = (bf16[48,1536]{1,0:T(8,128)(2,1)S(1)}, bf16[48,1536]{1,0:T(8,128)(2,1)S(1)}, u32[]{:S(2)}, u32[]{:S(2)}) collective-permute-start(bf16[48,1536]{1,0:T(8,128)(2,1)S(1)} %collective-permute-done.refs_1_), channel_id=1, source_target_pairs={{0,2},{2,4},{4,6},{6,0},{1,3},{3,5},{5,7},{7,1},{8,10},{10,12},{12... | collective-permute-start | bytes 442376 | tf_op jit(solution)/shard_map/ppermute | solution.py:897
  46.0 11.6 %collective-permute-start.8 = (bf16[128,1536]{1,0:T(8,128)(2,1)S(1)}, bf16[128,1536]{1,0:T(8,128)(2,1)S(1)}, u32[]{:S(2)}, u32[]{:S(2)}) collective-permute-start(bf16[128,1536]{1,0:T(8,128)(2,1)S(1)} %slice.122), channel_id=1, source_target_pairs={{0,16},{16,0},{8,24},{24,8},{1,17},{17,1},{9,25},{25,9},{2,18},{18... | collective-permute-start | bytes 1179656 | tf_op jit(solution)/shard_map/ppermute | solution.py:856
  46.5 11.8 %collective-permute-start.9 = (bf16[128,1536]{1,0:T(8,128)(2,1)S(1)}, bf16[128,1536]{1,0:T(8,128)(2,1)S(1)}, u32[]{:S(2)}, u32[]{:S(2)}) collective-permute-start(bf16[128,1536]{1,0:T(8,128)(2,1)S(1)} %slice.123), channel_id=1, source_target_pairs={{0,8},{8,0},{16,24},{24,16},{1,9},{9,1},{17,25},{25,17},{2,10},{10... | collective-permute-start | bytes 1179656 | tf_op jit(solution)/shard_map/ppermute | solution.py:852
  46.9 12.3 %collective-permute-start.11 = (bf16[48,1536]{1,0:T(8,128)(2,1)S(1)}, bf16[48,1536]{1,0:T(8,128)(2,1)S(1)}, u32[]{:S(2)}, u32[]{:S(2)}) collective-permute-start(bf16[48,1536]{1,0:T(8,128)(2,1)S(1)} %collective-permute-done.7.refs_2_), channel_id=1, source_target_pairs={{0,2},{2,4},{4,6},{6,0},{1,3},{3,5},{5,7},{7,1},{8,10},{10,12},{12... | collective-permute-start | bytes 442376 | tf_op jit(solution)/shard_map/ppermute | solution.py:897
  48.4 10.7 %collective-permute-start.10 = (s32[4,256]{1,0:T(4,128)S(1)}, s32[4,256]{1,0:T(4,128)S(1)}, u32[]{:S(2)}, u32[]{:S(2)}) collective-permute-start(s32[4,256]{1,0:T(4,128)S(1)} %pad_add_fusion.1), channel_id=1, source_target_pairs={{0,1},{1,0},{2,3},{3,2},{4,5},{5,4},{6,7},{7,6},{8,9},{9,8},{10,11... | collective-permute-start | bytes 12296 | tf_op jit(solution)/shard_map/ppermute | solution.py:848
  48.4 12.7 %collective-permute-start.13 = (bf16[256,1536]{1,0:T(8,128)(2,1)}, bf16[256,1536]{1,0:T(8,128)(2,1)}, u32[]{:S(2)}, u32[]{:S(2)}) collective-permute-start(bf16[256,1536]{1,0:T(8,128)(2,1)} %collective-permute-done.1.refs_2_), channel_id=1, source_target_pairs={{0,1},{1,0},{2,3},{3,2},{4,5},{5,4},{6,7},{7,6},{8,9},{9,8},{10,11... | collective-permute-start | bytes 2359304 | tf_op jit(solution)/shard_map/ppermute | solution.py:848
  67.5 326.3 %reduce-scatter.3.cloned.1.call-start = ((), (), s32[]{:S(2)}) async-start(), calls=%async_computation.4 | async-start | bytes 5898240 | tf_op jit(solution)/shard_map/reduce_scatter | solution.py:918
  67.6 44.0 %collective-permute-start.15 = (bf16[256,1536]{1,0:T(8,128)(2,1)S(1)}, bf16[256,1536]{1,0:T(8,128)(2,1)S(1)}, u32[]{:S(2)}, u32[]{:S(2)}) collective-permute-start(bf16[256,1536]{1,0:T(8,128)(2,1)S(1)} %copy-done.4), channel_id=1, source_target_pairs={{0,8},{8,0},{16,24},{24,16},{1,9},{9,1},{17,25},{25,17},{2,10},{10... | collective-permute-start | bytes 2359304 | tf_op jit(solution)/shard_map/ppermute | solution.py:852
  69.1 42.5 %collective-permute-start.16 = (bf16[256,1536]{1,0:T(8,128)(2,1)S(1)}, bf16[256,1536]{1,0:T(8,128)(2,1)}, u32[]{:S(2)}, u32[]{:S(2)}) collective-permute-start(bf16[256,1536]{1,0:T(8,128)(2,1)S(1)} %copy-done.4), channel_id=1, source_target_pairs={{0,16},{16,0},{8,24},{24,8},{1,17},{17,1},{9,25},{25,9},{2,18},{18... | collective-permute-start | bytes 2359304 | tf_op jit(solution)/shard_map/ppermute | solution.py:856
  70.9 40.8 %collective-permute-start.19 = (bf16[48,1536]{1,0:T(8,128)(2,1)}, bf16[48,1536]{1,0:T(8,128)(2,1)S(1)}, u32[]{:S(2)}, u32[]{:S(2)}) collective-permute-start(bf16[48,1536]{1,0:T(8,128)(2,1)} %copy-done.59), channel_id=1, source_target_pairs={{0,24},{8,16},{16,8},{24,0},{1,25},{9,17},{17,9},{25,1},{2,26},{10... | collective-permute-start | bytes 442376 | tf_op jit(solution)/shard_map/ppermute | solution.py:860
  71.1 40.5 %collective-permute-start.18 = (bf16[48,1536]{1,0:T(8,128)(2,1)}, bf16[48,1536]{1,0:T(8,128)(2,1)}, u32[]{:S(2)}, u32[]{:S(2)}) collective-permute-start(bf16[48,1536]{1,0:T(8,128)(2,1)} %copy-done.58), channel_id=1, source_target_pairs={{0,16},{16,0},{8,24},{24,8},{1,17},{17,1},{9,25},{25,9},{2,18},{18... | collective-permute-start | bytes 442376 | tf_op jit(solution)/shard_map/ppermute | solution.py:856
  72.6 39.1 %collective-permute-start.17 = (bf16[48,1536]{1,0:T(8,128)(2,1)}, bf16[48,1536]{1,0:T(8,128)(2,1)}, u32[]{:S(2)}, u32[]{:S(2)}) collective-permute-start(bf16[48,1536]{1,0:T(8,128)(2,1)} %copy-done.57), channel_id=1, source_target_pairs={{0,8},{8,0},{16,24},{24,16},{1,9},{9,1},{17,25},{25,17},{2,10},{10... | collective-permute-start | bytes 442376 | tf_op jit(solution)/shard_map/ppermute | solution.py:852
  119.9 12.0 %collective-permute-start.26 = (bf16[256,1536]{1,0:T(8,128)(2,1)S(1)}, bf16[256,1536]{1,0:T(8,128)(2,1)S(1)}, u32[]{:S(2)}, u32[]{:S(2)}) collective-permute-start(bf16[256,1536]{1,0:T(8,128)(2,1)S(1)} %copy-done.4), channel_id=1, source_target_pairs={{0,1},{1,0},{2,3},{3,2},{4,5},{5,4},{6,7},{7,6},{8,9},{9,8},{10,11... | collective-permute-start | bytes 2359304 | tf_op jit(solution)/shard_map/ppermute | solution.py:848
  120.1 12.7 %collective-permute-start.23 = (bf16[256,1536]{1,0:T(8,128)(2,1)S(1)}, bf16[256,1536]{1,0:T(8,128)(2,1)}, u32[]{:S(2)}, u32[]{:S(2)}) collective-permute-start(bf16[256,1536]{1,0:T(8,128)(2,1)S(1)} %get-tuple-element.271), channel_id=1, source_target_pairs={{0,1},{1,0},{2,3},{3,2},{4,5},{5,4},{6,7},{7,6},{8,9},{9,8},{10,11... | collective-permute-start | bytes 2359304 | tf_op jit(solution)/shard_map/ppermute | solution.py:848
  120.5 11.2 %collective-permute-start.24 = (bf16[128,1536]{1,0:T(8,128)(2,1)S(1)}, bf16[128,1536]{1,0:T(8,128)(2,1)S(1)}, u32[]{:S(2)}, u32[]{:S(2)}) collective-permute-start(bf16[128,1536]{1,0:T(8,128)(2,1)S(1)} %get-tuple-element.272), channel_id=1, source_target_pairs={{0,16},{16,0},{8,24},{24,8},{1,17},{17,1},{9,25},{25,9},{2,18},{18... | collective-permute-start | bytes 1179656 | tf_op jit(solution)/shard_map/ppermute | solution.py:856
  121.0 10.9 %collective-permute-start.25 = (bf16[128,1536]{1,0:T(8,128)(2,1)S(1)}, bf16[128,1536]{1,0:T(8,128)(2,1)S(1)}, u32[]{:S(2)}, u32[]{:S(2)}) collective-permute-start(bf16[128,1536]{1,0:T(8,128)(2,1)S(1)} %get-tuple-element.273), channel_id=1, source_target_pairs={{0,8},{8,0},{16,24},{24,16},{1,9},{9,1},{17,25},{25,17},{2,10},{10... | collective-permute-start | bytes 1179656 | tf_op jit(solution)/shard_map/ppermute | solution.py:852
  133.8 19.5 %collective-permute-start.27 = (bf16[256,1536]{1,0:T(8,128)(2,1)S(1)}, bf16[256,1536]{1,0:T(8,128)(2,1)S(1)}, u32[]{:S(2)}, u32[]{:S(2)}) collective-permute-start(bf16[256,1536]{1,0:T(8,128)(2,1)S(1)} %low_sum.4), channel_id=1, source_target_pairs={{0,8},{8,0},{16,24},{24,16},{1,9},{9,1},{17,25},{25,17},{2,10},{10... | collective-permute-start | bytes 2359304 | tf_op jit(solution)/shard_map/ppermute | solution.py:852
  134.5 19.8 %collective-permute-start.28 = (bf16[256,1536]{1,0:T(8,128)(2,1)S(1)}, bf16[256,1536]{1,0:T(8,128)(2,1)}, u32[]{:S(2)}, u32[]{:S(2)}) collective-permute-start(bf16[256,1536]{1,0:T(8,128)(2,1)S(1)} %low_sum.5), channel_id=1, source_target_pairs={{0,16},{16,0},{8,24},{24,8},{1,17},{17,1},{9,25},{25,9},{2,18},{18... | collective-permute-start | bytes 2359304 | tf_op jit(solution)/shard_map/ppermute | solution.py:856
  159.4 20.0 %collective-permute-start.32 = (bf16[256,1536]{1,0:T(8,128)(2,1)S(1)}, bf16[256,1536]{1,0:T(8,128)(2,1)S(1)}, u32[]{:S(2)}, u32[]{:S(2)}) collective-permute-start(bf16[256,1536]{1,0:T(8,128)(2,1)S(1)} %multiply_convert_fusion.own_ref.refs_0_), channel_id=1, source_target_pairs={{0,8},{8,0},{16,24},{24,16},{1,9},{9,1},{17,25},{25,17},{2,10},{10... | collective-permute-start | bytes 2359304 | tf_op jit(solution)/shard_map/ppermute | solution.py:852
  161.0 19.6 %collective-permute-start.33 = (bf16[256,1536]{1,0:T(8,128)(2,1)S(1)}, bf16[256,1536]{1,0:T(8,128)(2,1)S(1)}, u32[]{:S(2)}, u32[]{:S(2)}) collective-permute-start(bf16[256,1536]{1,0:T(8,128)(2,1)S(1)} %multiply_convert_fusion.own_ref.refs_0_), channel_id=1, source_target_pairs={{0,16},{16,0},{8,24},{24,8},{1,17},{17,1},{9,25},{25,9},{2,18},{18... | collective-permute-start | bytes 2359304 | tf_op jit(solution)/shard_map/ppermute | solution.py:856
  184.0 11.2 %collective-permute-start.36 = (bf16[128,1536]{1,0:T(8,128)(2,1)S(1)}, bf16[128,1536]{1,0:T(8,128)(2,1)S(1)}, u32[]{:S(2)}, u32[]{:S(2)}) collective-permute-start(bf16[128,1536]{1,0:T(8,128)(2,1)S(1)} %slice.126), channel_id=1, source_target_pairs={{0,16},{16,0},{8,24},{24,8},{1,17},{17,1},{9,25},{25,9},{2,18},{18... | collective-permute-start | bytes 1179656 | tf_op jit(solution)/shard_map/ppermute | solution.py:856
  185.5 10.9 %collective-permute-start.37 = (bf16[128,1536]{1,0:T(8,128)(2,1)S(1)}, bf16[128,1536]{1,0:T(8,128)(2,1)S(1)}, u32[]{:S(2)}, u32[]{:S(2)}) collective-permute-start(bf16[128,1536]{1,0:T(8,128)(2,1)S(1)} %slice.127), channel_id=1, source_target_pairs={{0,8},{8,0},{16,24},{24,16},{1,9},{9,1},{17,25},{25,17},{2,10},{10... | collective-permute-start | bytes 1179656 | tf_op jit(solution)/shard_map/ppermute | solution.py:852
  196.4 12.0 %collective-permute-start.41 = (bf16[256,1536]{1,0:T(8,128)(2,1)S(1)}, bf16[256,1536]{1,0:T(8,128)(2,1)S(1)}, u32[]{:S(2)}, u32[]{:S(2)}) collective-permute-start(bf16[256,1536]{1,0:T(8,128)(2,1)S(1)} %get-tuple-element.303), channel_id=1, source_target_pairs={{0,1},{1,0},{2,3},{3,2},{4,5},{5,4},{6,7},{7,6},{8,9},{9,8},{10,11... | collective-permute-start | bytes 2359304 | tf_op jit(solution)/shard_map/ppermute | solution.py:848
  196.5 11.9 %collective-permute-start.40 = (bf16[256,1536]{1,0:T(8,128)(2,1)S(1)}, bf16[256,1536]{1,0:T(8,128)(2,1)S(1)}, u32[]{:S(2)}, u32[]{:S(2)}) collective-permute-start(bf16[256,1536]{1,0:T(8,128)(2,1)S(1)} %constant_dynamic-update-slice_fusion.2.cot_own_ref.refs_22_), channel_id=1, source_target_pairs={{0,1},{1,0},{2,3},{3,2},{4,5},{5,4},{6,7},{7,6},{8,9},{9,8},{10,11... | collective-permute-start | bytes 2359304 | tf_op jit(solution)/shard_map/ppermute | solution.py:848
  197.0 11.1 %collective-permute-start.39 = (bf16[128,1536]{1,0:T(8,128)(2,1)S(1)}, bf16[128,1536]{1,0:T(8,128)(2,1)S(1)}, u32[]{:S(2)}, u32[]{:S(2)}) collective-permute-start(bf16[128,1536]{1,0:T(8,128)(2,1)S(1)} %slice.125), channel_id=1, source_target_pairs={{0,8},{8,0},{16,24},{24,16},{1,9},{9,1},{17,25},{25,17},{2,10},{10... | collective-permute-start | bytes 1179656 | tf_op jit(solution)/shard_map/ppermute | solution.py:852
  197.5 10.8 %collective-permute-start.38 = (bf16[128,1536]{1,0:T(8,128)(2,1)S(1)}, bf16[128,1536]{1,0:T(8,128)(2,1)S(1)}, u32[]{:S(2)}, u32[]{:S(2)}) collective-permute-start(bf16[128,1536]{1,0:T(8,128)(2,1)S(1)} %slice.124), channel_id=1, source_target_pairs={{0,16},{16,0},{8,24},{24,8},{1,17},{17,1},{9,25},{25,9},{2,18},{18... | collective-permute-start | bytes 1179656 | tf_op jit(solution)/shard_map/ppermute | solution.py:856
  213.0 19.6 %collective-permute-start.45 = (bf16[256,1536]{1,0:T(8,128)(2,1)S(1)}, bf16[256,1536]{1,0:T(8,128)(2,1)S(1)}, u32[]{:S(2)}, u32[]{:S(2)}) collective-permute-start(bf16[256,1536]{1,0:T(8,128)(2,1)S(1)} %pair_sum.7), channel_id=1, source_target_pairs={{0,16},{16,0},{8,24},{24,8},{1,17},{17,1},{9,25},{25,9},{2,18},{18... | collective-permute-start | bytes 2359304 | tf_op jit(solution)/shard_map/ppermute | solution.py:856
  213.5 19.3 %collective-permute-start.44 = (bf16[256,1536]{1,0:T(8,128)(2,1)S(1)}, bf16[256,1536]{1,0:T(8,128)(2,1)S(1)}, u32[]{:S(2)}, u32[]{:S(2)}) collective-permute-start(bf16[256,1536]{1,0:T(8,128)(2,1)S(1)} %pair_sum.6), channel_id=1, source_target_pairs={{0,8},{8,0},{16,24},{24,16},{1,9},{9,1},{17,25},{25,17},{2,10},{10... | collective-permute-start | bytes 2359304 | tf_op jit(solution)/shard_map/ppermute | solution.py:852
  236.4 20.7 %collective-permute-start.48 = (bf16[256,1536]{1,0:T(8,128)(2,1)S(1)}, bf16[256,1536]{1,0:T(8,128)(2,1)}, u32[]{:S(2)}, u32[]{:S(2)}) collective-permute-start(bf16[256,1536]{1,0:T(8,128)(2,1)S(1)} %pair_sum.8), channel_id=1, source_target_pairs={{0,24},{8,16},{16,8},{24,0},{1,25},{9,17},{17,9},{25,1},{2,26},{10... | collective-permute-start | bytes 2359304 | tf_op jit(solution)/shard_map/ppermute | solution.py:860
  257.1 188.3 %reduce-scatter.5.cloned.1.call-start = ((), (), s32[]{:S(2)}) async-start(), calls=%async_computation.5 | async-start | bytes 2457600 | tf_op jit(solution)/shard_map/reduce_scatter | solution.py:918
  263.2 19.8 %collective-permute-start.54 = (bf16[256,1536]{1,0:T(8,128)(2,1)S(1)}, bf16[256,1536]{1,0:T(8,128)(2,1)S(1)}, u32[]{:S(2)}, u32[]{:S(2)}) collective-permute-start(bf16[256,1536]{1,0:T(8,128)(2,1)S(1)} %fusion.13.own_ref.refs_1_), channel_id=1, source_target_pairs={{0,8},{8,0},{16,24},{24,16},{1,9},{9,1},{17,25},{25,17},{2,10},{10... | collective-permute-start | bytes 2359304 | tf_op jit(solution)/shard_map/ppermute | solution.py:852
  264.7 19.5 %collective-permute-start.55 = (bf16[256,1536]{1,0:T(8,128)(2,1)S(1)}, bf16[256,1536]{1,0:T(8,128)(2,1)S(1)}, u32[]{:S(2)}, u32[]{:S(2)}) collective-permute-start(bf16[256,1536]{1,0:T(8,128)(2,1)S(1)} %fusion.13.own_ref.refs_1_), channel_id=1, source_target_pairs={{0,16},{16,0},{8,24},{24,8},{1,17},{17,1},{9,25},{25,9},{2,18},{18... | collective-permute-start | bytes 2359304 | tf_op jit(solution)/shard_map/ppermute | solution.py:856
  287.7 19.1 %collective-permute-start.60 = (bf16[128,1536]{1,0:T(8,128)(2,1)S(1)}, bf16[128,1536]{1,0:T(8,128)(2,1)S(1)}, u32[]{:S(2)}, u32[]{:S(2)}) collective-permute-start(bf16[128,1536]{1,0:T(8,128)(2,1)S(1)} %slice.129), channel_id=1, source_target_pairs={{0,8},{8,0},{16,24},{24,16},{1,9},{9,1},{17,25},{25,17},{2,10},{10... | collective-permute-start | bytes 1179656 | tf_op jit(solution)/shard_map/ppermute | solution.py:852
  288.2 18.6 %collective-permute-start.59 = (bf16[128,1536]{1,0:T(8,128)(2,1)S(1)}, bf16[128,1536]{1,0:T(8,128)(2,1)S(1)}, u32[]{:S(2)}, u32[]{:S(2)}) collective-permute-start(bf16[128,1536]{1,0:T(8,128)(2,1)S(1)} %slice.128), channel_id=1, source_target_pairs={{0,16},{16,0},{8,24},{24,8},{1,17},{17,1},{9,25},{25,9},{2,18},{18... | collective-permute-start | bytes 1179656 | tf_op jit(solution)/shard_map/ppermute | solution.py:856
  289.7 17.6 %collective-permute-start.61 = (bf16[128,1536]{1,0:T(8,128)(2,1)S(1)}, bf16[128,1536]{1,0:T(8,128)(2,1)S(1)}, u32[]{:S(2)}, u32[]{:S(2)}) collective-permute-start(bf16[128,1536]{1,0:T(8,128)(2,1)S(1)} %get-tuple-element.364), channel_id=1, source_target_pairs={{0,8},{8,0},{16,24},{24,16},{1,9},{9,1},{17,25},{25,17},{2,10},{10... | collective-permute-start | bytes 1179656 | tf_op jit(solution)/shard_map/ppermute | solution.py:852
  291.2 16.3 %collective-permute-start.58 = (bf16[128,1536]{1,0:T(8,128)(2,1)S(1)}, bf16[128,1536]{1,0:T(8,128)(2,1)S(1)}, u32[]{:S(2)}, u32[]{:S(2)}) collective-permute-start(bf16[128,1536]{1,0:T(8,128)(2,1)S(1)} %get-tuple-element.360), channel_id=1, source_target_pairs={{0,16},{16,0},{8,24},{24,8},{1,17},{17,1},{9,25},{25,9},{2,18},{18... | collective-permute-start | bytes 1179656 | tf_op jit(solution)/shard_map/ppermute | solution.py:856
  310.8 22.4 %collective-permute-start.65 = (bf16[256,1536]{1,0:T(8,128)(2,1)S(1)}, bf16[256,1536]{1,0:T(8,128)(2,1)S(1)}, u32[]{:S(2)}, u32[]{:S(2)}) collective-permute-start(bf16[256,1536]{1,0:T(8,128)(2,1)S(1)} %low_sum.7), channel_id=1, source_target_pairs={{0,16},{16,0},{8,24},{24,8},{1,17},{17,1},{9,25},{25,9},{2,18},{18... | collective-permute-start | bytes 2359304 | tf_op jit(solution)/shard_map/ppermute | solution.py:856
  312.4 20.8 %collective-permute-start.64 = (bf16[256,1536]{1,0:T(8,128)(2,1)S(1)}, bf16[256,1536]{1,0:T(8,128)(2,1)S(1)}, u32[]{:S(2)}, u32[]{:S(2)}) collective-permute-start(bf16[256,1536]{1,0:T(8,128)(2,1)S(1)} %low_sum.6), channel_id=1, source_target_pairs={{0,8},{8,0},{16,24},{24,16},{1,9},{9,1},{17,25},{25,17},{2,10},{10... | collective-permute-start | bytes 2359304 | tf_op jit(solution)/shard_map/ppermute | solution.py:852
  313.4 19.8 %collective-permute-start.63 = (bf16[256,1536]{1,0:T(8,128)(2,1)S(1)}, bf16[256,1536]{1,0:T(8,128)(2,1)S(1)}, u32[]{:S(2)}, u32[]{:S(2)}) collective-permute-start(bf16[256,1536]{1,0:T(8,128)(2,1)S(1)} %get-tuple-element.373), channel_id=1, source_target_pairs={{0,1},{1,0},{2,3},{3,2},{4,5},{5,4},{6,7},{7,6},{8,9},{9,8},{10,11... | collective-permute-start | bytes 2359304 | tf_op jit(solution)/shard_map/ppermute | solution.py:848
  340.7 19.1 %collective-permute-start.67 = (bf16[48,1536]{1,0:T(8,128)(2,1)S(1)}, bf16[48,1536]{1,0:T(8,128)(2,1)S(1)}, u32[]{:S(2)}, u32[]{:S(2)}) collective-permute-start(bf16[48,1536]{1,0:T(8,128)(2,1)S(1)} %get-tuple-element.479), channel_id=1, source_target_pairs={{0,8},{8,0},{16,24},{24,16},{1,9},{9,1},{17,25},{25,17},{2,10},{10... | collective-permute-start | bytes 442376 | tf_op jit(solution)/shard_map/ppermute | solution.py:852
  341.7 18.0 %collective-permute-start.68 = (bf16[48,1536]{1,0:T(8,128)(2,1)S(1)}, bf16[48,1536]{1,0:T(8,128)(2,1)S(1)}, u32[]{:S(2)}, u32[]{:S(2)}) collective-permute-start(bf16[48,1536]{1,0:T(8,128)(2,1)S(1)} %get-tuple-element.478), channel_id=1, source_target_pairs={{0,16},{16,0},{8,24},{24,8},{1,17},{17,1},{9,25},{25,9},{2,18},{18... | collective-permute-start | bytes 442376 | tf_op jit(solution)/shard_map/ppermute | solution.py:856
  342.3 17.5 %collective-permute-start.69 = (bf16[48,1536]{1,0:T(8,128)(2,1)S(1)}, bf16[48,1536]{1,0:T(8,128)(2,1)S(1)}, u32[]{:S(2)}, u32[]{:S(2)}) collective-permute-start(bf16[48,1536]{1,0:T(8,128)(2,1)S(1)} %get-tuple-element.477), channel_id=1, source_target_pairs={{0,24},{8,16},{16,8},{24,0},{1,25},{9,17},{17,9},{25,1},{2,26},{10... | collective-permute-start | bytes 442376 | tf_op jit(solution)/shard_map/ppermute | solution.py:860
  344.2 23.0 %collective-permute-start.71 = (bf16[256,1536]{1,0:T(8,128)(2,1)S(1)}, bf16[256,1536]{1,0:T(8,128)(2,1)S(1)}, u32[]{:S(2)}, u32[]{:S(2)}) collective-permute-start(bf16[256,1536]{1,0:T(8,128)(2,1)S(1)} %pair_sum.10), channel_id=1, source_target_pairs={{0,16},{16,0},{8,24},{24,8},{1,17},{17,1},{9,25},{25,9},{2,18},{18... | collective-permute-start | bytes 2359304 | tf_op jit(solution)/shard_map/ppermute | solution.py:856
  344.8 22.5 %collective-permute-start.70 = (bf16[256,1536]{1,0:T(8,128)(2,1)S(1)}, bf16[256,1536]{1,0:T(8,128)(2,1)S(1)}, u32[]{:S(2)}, u32[]{:S(2)}) collective-permute-start(bf16[256,1536]{1,0:T(8,128)(2,1)S(1)} %pair_sum.9), channel_id=1, source_target_pairs={{0,8},{8,0},{16,24},{24,16},{1,9},{9,1},{17,25},{25,17},{2,10},{10... | collective-permute-start | bytes 2359304 | tf_op jit(solution)/shard_map/ppermute | solution.py:852
  371.0 20.5 %collective-permute-start.75 = (bf16[256,1536]{1,0:T(8,128)(2,1)S(1)}, bf16[256,1536]{1,0:T(8,128)(2,1)S(1)}, u32[]{:S(2)}, u32[]{:S(2)}) collective-permute-start(bf16[256,1536]{1,0:T(8,128)(2,1)S(1)} %pair_sum.11), channel_id=1, source_target_pairs={{0,24},{8,16},{16,8},{24,0},{1,25},{9,17},{17,9},{25,1},{2,26},{10... | collective-permute-start | bytes 2359304 | tf_op jit(solution)/shard_map/ppermute | solution.py:860
  373.9 14.9 %collective-permute-start.76 = (bf16[48,1536]{1,0:T(8,128)(2,1)}, bf16[48,1536]{1,0:T(8,128)(2,1)S(1)}, u32[]{:S(2)}, u32[]{:S(2)}) collective-permute-start(bf16[48,1536]{1,0:T(8,128)(2,1)} %get-tuple-element.414), channel_id=1, source_target_pairs={{0,4},{2,6},{4,0},{6,2},{1,5},{3,7},{5,1},{7,3},{8,12},{10,14},{12... | collective-permute-start | bytes 442376 | tf_op jit(solution)/shard_map/ppermute | solution.py:897
  374.7 14.1 %collective-permute-start.74 = (bf16[48,1536]{1,0:T(8,128)(2,1)}, bf16[48,1536]{1,0:T(8,128)(2,1)S(1)}, u32[]{:S(2)}, u32[]{:S(2)}) collective-permute-start(bf16[48,1536]{1,0:T(8,128)(2,1)} %get-tuple-element.404), channel_id=1, source_target_pairs={{0,2},{2,4},{4,6},{6,0},{1,3},{3,5},{5,7},{7,1},{8,10},{10,12},{12... | collective-permute-start | bytes 442376 | tf_op jit(solution)/shard_map/ppermute | solution.py:897
  375.2 13.6 %collective-permute-start.77 = (bf16[48,1536]{1,0:T(8,128)(2,1)}, bf16[48,1536]{1,0:T(8,128)(2,1)S(1)}, u32[]{:S(2)}, u32[]{:S(2)}) collective-permute-start(bf16[48,1536]{1,0:T(8,128)(2,1)} %get-tuple-element.415), channel_id=1, source_target_pairs={{0,6},{2,0},{4,2},{6,4},{1,7},{3,1},{5,3},{7,5},{8,14},{10,8},{12,... | collective-permute-start | bytes 442376 | tf_op jit(solution)/shard_map/ppermute | solution.py:897
  396.4 30.5 %collective-permute-start.82 = (bf16[432,1536]{1,0:T(8,128)(2,1)}, bf16[432,1536]{1,0:T(8,128)(2,1)}, u32[]{:S(2)}, u32[]{:S(2)}) collective-permute-start(bf16[432,1536]{1,0:T(8,128)(2,1)} %pad_maximum_fusion.refs_0_.refs_8_), channel_id=1, source_target_pairs={{0,16},{16,0},{8,24},{24,8},{1,17},{17,1},{9,25},{25,9},{2,18},{18... | collective-permute-start | bytes 3981320 | tf_op jit(solution)/shard_map/ppermute | solution.py:856
  396.7 31.3 %collective-permute-start.81 = (bf16[432,1536]{1,0:T(8,128)(2,1)}, bf16[432,1536]{1,0:T(8,128)(2,1)}, u32[]{:S(2)}, u32[]{:S(2)}) collective-permute-start(bf16[432,1536]{1,0:T(8,128)(2,1)} %pad_maximum_fusion.refs_0_.refs_8_), channel_id=1, source_target_pairs={{0,8},{8,0},{16,24},{24,16},{1,9},{9,1},{17,25},{25,17},{2,10},{10... | collective-permute-start | bytes 3981320 | tf_op jit(solution)/shard_map/ppermute | solution.py:852
  397.8 30.2 %collective-permute-start.83 = (bf16[432,1536]{1,0:T(8,128)(2,1)}, bf16[432,1536]{1,0:T(8,128)(2,1)}, u32[]{:S(2)}, u32[]{:S(2)}) collective-permute-start(bf16[432,1536]{1,0:T(8,128)(2,1)} %pad_maximum_fusion.refs_0_.refs_8_), channel_id=1, source_target_pairs={{0,1},{1,0},{2,3},{3,2},{4,5},{5,4},{6,7},{7,6},{8,9},{9,8},{10,11... | collective-permute-start | bytes 3981320 | tf_op jit(solution)/shard_map/ppermute | solution.py:848
  428.0 17.3 %collective-permute-start.86 = (bf16[216,1536]{1,0:T(8,128)(2,1)S(1)}, bf16[216,1536]{1,0:T(8,128)(2,1)S(1)}, u32[]{:S(2)}, u32[]{:S(2)}) collective-permute-start(bf16[216,1536]{1,0:T(8,128)(2,1)S(1)} %slice.132), channel_id=1, source_target_pairs={{0,8},{8,0},{16,24},{24,16},{1,9},{9,1},{17,25},{25,17},{2,10},{10... | collective-permute-start | bytes 1990664 | tf_op jit(solution)/shard_map/ppermute | solution.py:852
  430.3 15.0 %collective-permute-start.85 = (bf16[216,1536]{1,0:T(8,128)(2,1)S(1)}, bf16[216,1536]{1,0:T(8,128)(2,1)S(1)}, u32[]{:S(2)}, u32[]{:S(2)}) collective-permute-start(bf16[216,1536]{1,0:T(8,128)(2,1)S(1)} %slice.131), channel_id=1, source_target_pairs={{0,16},{16,0},{8,24},{24,8},{1,17},{17,1},{9,25},{25,9},{2,18},{18... | collective-permute-start | bytes 1990664 | tf_op jit(solution)/shard_map/ppermute | solution.py:856
  430.9 14.5 %collective-permute-start.88 = (bf16[432,1536]{1,0:T(8,128)(2,1)}, bf16[432,1536]{1,0:T(8,128)(2,1)}, u32[]{:S(2)}, u32[]{:S(2)}) collective-permute-start(bf16[432,1536]{1,0:T(8,128)(2,1)} %collective-permute-done.82.refs_4_.refs_12_), channel_id=1, source_target_pairs={{0,1},{1,0},{2,3},{3,2},{4,5},{5,4},{6,7},{7,6},{8,9},{9,8},{10,11... | collective-permute-start | bytes 3981320 | tf_op jit(solution)/shard_map/ppermute | solution.py:848
  430.9 14.5 %collective-permute-start.87 = (bf16[432,1536]{1,0:T(8,128)(2,1)}, bf16[432,1536]{1,0:T(8,128)(2,1)}, u32[]{:S(2)}, u32[]{:S(2)}) collective-permute-start(bf16[432,1536]{1,0:T(8,128)(2,1)} %collective-permute-done.81.refs_2_.refs_10_), channel_id=1, source_target_pairs={{0,1},{1,0},{2,3},{3,2},{4,5},{5,4},{6,7},{7,6},{8,9},{9,8},{10,11... | collective-permute-start | bytes 3981320 | tf_op jit(solution)/shard_map/ppermute | solution.py:848
  431.4 12.2 %collective-permute-start.84 = (f32[48,128]{1,0:T(8,128)S(1)}, f32[48,128]{1,0:T(8,128)S(1)}, u32[]{:S(2)}, u32[]{:S(2)}) collective-permute-start(f32[48,128]{1,0:T(8,128)S(1)} %add.323), channel_id=1, source_target_pairs={{0,8},{8,0},{16,24},{24,16},{1,9},{9,1},{17,25},{25,17},{2,10},{10... | collective-permute-start | bytes 73736 | tf_op jit(solution)/shard_map/ppermute | solution.py:852
  445.5 15.8 %collective-permute-start.90 = (bf16[384,640]{1,0:T(8,128)(2,1)}, bf16[384,640]{1,0:T(8,128)(2,1)S(1)}, u32[]{:S(2)}, u32[]{:S(2)}) collective-permute-start(bf16[384,640]{1,0:T(8,128)(2,1)} %reduce-scatter.5.cloned.1.call-done.refs_0_), channel_id=1, source_target_pairs={{0,16},{16,0},{8,24},{24,8},{1,17},{17,1},{9,25},{25,9},{2,18},{18... | collective-permute-start | bytes 1474568 | tf_op jit(solution)/shard_map/ppermute | solution.py:856
  446.1 15.2 %collective-permute-start.89 = (bf16[384,640]{1,0:T(8,128)(2,1)}, bf16[384,640]{1,0:T(8,128)(2,1)S(1)}, u32[]{:S(2)}, u32[]{:S(2)}) collective-permute-start(bf16[384,640]{1,0:T(8,128)(2,1)} %reduce-scatter.5.cloned.1.call-done.refs_0_), channel_id=1, source_target_pairs={{0,8},{8,0},{16,24},{24,16},{1,9},{9,1},{17,25},{25,17},{2,10},{10... | collective-permute-start | bytes 1474568 | tf_op jit(solution)/shard_map/ppermute | solution.py:852
  447.1 14.2 %collective-permute-start.91 = (bf16[384,640]{1,0:T(8,128)(2,1)}, bf16[384,640]{1,0:T(8,128)(2,1)}, u32[]{:S(2)}, u32[]{:S(2)}) collective-permute-start(bf16[384,640]{1,0:T(8,128)(2,1)} %reduce-scatter.5.cloned.1.call-done.refs_0_), channel_id=1, source_target_pairs={{0,1},{1,0},{2,3},{3,2},{4,5},{5,4},{6,7},{7,6},{8,9},{9,8},{10,11... | collective-permute-start | bytes 1474568 | tf_op jit(solution)/shard_map/ppermute | solution.py:848
  (141 other events, 1113.1 us)
Sparse Core Ops, SparseCore 0:
  14.6 51.5 all-gather.2
  68.3 87.8 all-gather.4
  257.2 83.6 reduce-scatter.2
  391.7 39.5 reduce-scatter.4

commit v4 on v3

--- a/solution.py
+++ b/solution.py
@@ -55,29 +55,29 @@
     )(kernels)
 
 
-def place_columns_kernel(sections, chunk, where_ref, *refs):
+def columns_pair(own_ref, other_ref, core, chunk, s):
+    own = own_ref[:, s * chunk : (s + 1) * chunk].astype(jnp.float32)
+    other = other_ref[:, s * chunk : (s + 1) * chunk].astype(jnp.float32)
+    return jnp.concatenate([jnp.where(core == 0, own, other), jnp.where(core == 0, other, own)], 1)
+
+
+def place_columns_kernel(sections, chunk, chips, where_ref, *refs):
     ins, out_ref = refs[:-1], refs[-1]
     line, core = where_ref[0], where_ref[1]
     width = 2 * chunk
-    chips = len(ins) // 2
-    for k in range(chips):
-        own = ins[2 * k][...].astype(jnp.float32)
-        other = ins[2 * k + 1][...].astype(jnp.float32)
-        first = jnp.where(core == 0, own, other)
-        second = jnp.where(core == 0, other, own)
+    for k in range(len(ins) // 2):
         for s in range(sections):
-            both = jnp.concatenate([first[:, s * chunk : (s + 1) * chunk], second[:, s * chunk : (s + 1) * chunk]], 1)
             at = pl.multiple_of(s * chips * width + (line ^ k) * width, LANES)
-            out_ref[:, pl.ds(at, width)] = both
-
-
-def place_columns(place, pieces, sections, chunk):
+            out_ref[:, pl.ds(at, width)] = columns_pair(ins[2 * k], ins[2 * k + 1], core, chunk, s)
+
+
+def place_columns(place, pieces, sections, chunk, chips):
     rows, cols = pieces[0].shape
-    cols_out = sections * chunk * len(pieces)
+    cols_out = 2 * sections * chunk * chips
     steps = 4 if rows % 64 == 0 else 1
     spec = pl.BlockSpec((rows // steps, cols), lambda s, place: (s, 0))
     return pl.pallas_call(
-        functools.partial(place_columns_kernel, sections, chunk),
+        functools.partial(place_columns_kernel, sections, chunk, chips),
         out_shape=jax.ShapeDtypeStruct((rows, cols_out), jnp.float32),
         grid_spec=pltpu.PrefetchScalarGridSpec(
             num_scalar_prefetch=1,
@@ -85,15 +85,47 @@
             in_specs=[spec] * len(pieces),
             out_specs=pl.BlockSpec((rows // steps, cols_out), lambda s, place: (s, 0)),
         ),
-        compiler_params=pltpu.CompilerParams(vmem_limit_bytes=ROOM),
+        compiler_params=pltpu.CompilerParams(vmem_limit_bytes=24 * 1024 * 1024),
         cost_estimate=cost(5),
         name="place_columns",
     )(place, *pieces)
 
 
+def add_columns_kernel(sections, chunk, chips, chip, place_ref, own_ref, other_ref, base_ref, out_ref, blocks, sems):
+    del base_ref
+    line, core = place_ref[0], place_ref[1]
+    width = 2 * chunk
+    copies = []
+    for s in range(sections):
+        blocks[s] = columns_pair(own_ref, other_ref, core, chunk, s)
+        at = pl.multiple_of(s * chips * width + (line ^ chip) * width, LANES)
+        copy = pltpu.make_async_copy(blocks.at[s], out_ref.at[:, pl.ds(at, width)], sems.at[s])
+        copy.start()
+        copies.append(copy)
+    for copy in copies:
+        copy.wait()
+
+
+def add_columns(place, own, other, base, sections, chunk, chips, chip):
+    vmem = pl.BlockSpec(memory_space=pltpu.VMEM)
+    anywhere = pl.BlockSpec(memory_space=pl.ANY)
+    return pl.pallas_call(
+        functools.partial(add_columns_kernel, sections, chunk, chips, chip),
+        out_shape=jax.ShapeDtypeStruct(base.shape, base.dtype),
+        in_specs=[pl.BlockSpec(memory_space=pltpu.SMEM), vmem, vmem, anywhere],
+        out_specs=anywhere,
+        scratch_shapes=[
+            pltpu.VMEM((sections, own.shape[0], 2 * chunk), jnp.float32), pltpu.SemaphoreType.DMA((sections,)),
+        ],
+        input_output_aliases={3: 0},
+        compiler_params=pltpu.CompilerParams(vmem_limit_bytes=12 * 1024 * 1024),
+        cost_estimate=cost(2),
+        name="add_columns",
+    )(place, own, other, base)
+
+
 def place_feed_kernel(sections, chunk, pieces, where_ref, *refs):
-    ins, extras = refs[:pieces], refs[pieces : 2 * pieces]
-    gate_ref, down_ref, out_ref = refs[2 * pieces :]
+    ins, gate_ref, down_ref = refs[:pieces], refs[pieces], refs[pieces + 1]
     line, core = where_ref[0], where_ref[1]
     width = 2 * chunk
     chips = pieces // 2
@@ -111,44 +143,33 @@
         down_ref[pl.ds(at, chunk), :] = first[:, gate_cols:]
         down_ref[pl.ds(at + chunk, chunk), :] = second[:, gate_cols:]
 
-    @pl.when(pl.program_id(0) == 0)
-    def _():
-        rows = extras[0].shape[0]
-        for k in range(chips):
-            for e in range(2):
-                at = pl.multiple_of(((core ^ e) * chips + (line ^ k)) * rows, rows)
-                out_ref[pl.ds(at, rows), :] = extras[2 * k + e][...].astype(jnp.float32)
-
-
-def place_feed(place, pieces, chunk, blocks):
+
+def place_feed(place, pieces, chunk):
     rows, cols = pieces[0].shape
-    extra = rows - blocks * chunk
+    blocks = rows // chunk
     sections = (cols // chunk) * 2 // 3
     hidden = cols - sections * chunk
+    spec = pl.BlockSpec((chunk, cols), lambda s, place: (s, 0))
     gate_cols = sections * chunk * len(pieces)
-    last = blocks * chunk // extra
     return pl.pallas_call(
         functools.partial(place_feed_kernel, sections, chunk, len(pieces)),
         out_shape=(
-            jax.ShapeDtypeStruct((blocks * chunk, gate_cols), jnp.float32),
+            jax.ShapeDtypeStruct((rows, gate_cols), jnp.float32),
             jax.ShapeDtypeStruct((chunk * len(pieces), hidden * blocks), jnp.float32),
-            jax.ShapeDtypeStruct((extra * len(pieces), cols), jnp.float32),
         ),
         grid_spec=pltpu.PrefetchScalarGridSpec(
             num_scalar_prefetch=1,
             grid=(blocks,),
-            in_specs=[pl.BlockSpec((chunk, cols), lambda s, place: (s, 0))] * len(pieces)
-            + [pl.BlockSpec((extra, cols), lambda s, place: (last, 0))] * len(pieces),
+            in_specs=[spec] * len(pieces),
             out_specs=(
                 pl.BlockSpec((chunk, gate_cols), lambda s, place: (s, 0)),
                 pl.BlockSpec((chunk * len(pieces), hidden), lambda s, place: (0, s)),
-                pl.BlockSpec((extra * len(pieces), cols), lambda s, place: (0, 0)),
             ),
         ),
         compiler_params=pltpu.CompilerParams(vmem_limit_bytes=ROOM),
         cost_estimate=cost(11),
         name="place_feed",
-    )(place, *pieces, *pieces)
+    )(place, *pieces)
 
 
 def masked_scores(q_blk, keys, since, first_row):
@@ -203,10 +224,9 @@
     keys_pad[...] = jnp.zeros_like(keys_pad)
     s_high[...] = jnp.zeros_like(s_high)
     s_low[...] = jnp.zeros_like(s_low)
-    for arrival in arrivals:
-        arrival.wait()
 
     def project(step, carry):
+        pltpu.make_async_copy(halves[0], pieces.at[step], in_sems.at[step]).wait()
         row, part = lax.div(step, 2), lax.rem(step, 2)
         at = pl.multiple_of(jnp.bitwise_xor(core, part) * half_len, half_len)
         joined = jnp.dot(pieces[step], joined_ref[...], preferred_element_type=jnp.float32)
@@ -728,7 +748,7 @@
     vmem = pl.BlockSpec(memory_space=pltpu.VMEM)
     return pl.pallas_call(
         halves_kernel, out_shape=(half, half), in_specs=[vmem] * 2, out_specs=(vmem,) * 2,
-        compiler_params=pltpu.CompilerParams(vmem_limit_bytes=16 * 1024 * 1024), cost_estimate=LIGHT, name="sum_halves",
+        compiler_params=pltpu.CompilerParams(vmem_limit_bytes=4 * 1024 * 1024), cost_estimate=LIGHT, name="sum_halves",
     )(mine, came)
 
 
@@ -745,7 +765,7 @@
     return pl.pallas_call(
         functools.partial(sum_kernel, second), out_shape=jax.ShapeDtypeStruct(mine.shape, jnp.bfloat16),
         in_specs=[vmem] * 3, out_specs=vmem,
-        compiler_params=pltpu.CompilerParams(vmem_limit_bytes=16 * 1024 * 1024), cost_estimate=LIGHT, name="low_sum",
+        compiler_params=pltpu.CompilerParams(vmem_limit_bytes=4 * 1024 * 1024), cost_estimate=LIGHT, name="low_sum",
     )(mine, came, extra)
 
 
@@ -757,7 +777,7 @@
     vmem = pl.BlockSpec(memory_space=pltpu.VMEM)
     return pl.pallas_call(
         pair_kernel, out_shape=jax.ShapeDtypeStruct(mine.shape, jnp.bfloat16), in_specs=[vmem] * 2, out_specs=vmem,
-        compiler_params=pltpu.CompilerParams(vmem_limit_bytes=16 * 1024 * 1024), cost_estimate=LIGHT, name="pair_sum",
+        compiler_params=pltpu.CompilerParams(vmem_limit_bytes=4 * 1024 * 1024), cost_estimate=LIGHT, name="pair_sum",
     )(mine, came)
 
 
@@ -836,6 +856,29 @@
         cost_estimate=LIGHT,
         name="pick_out",
     )(place, *pieces)
+
+
+def place_quarters_kernel(place_ref, own_ref, other_ref, out_ref):
+    chips, rows = own_ref.shape[:2]
+    for k in range(chips):
+        for e, ref in enumerate((own_ref, other_ref)):
+            core = jnp.bitwise_xor(place_ref[1], e)
+            at = pl.multiple_of((core * chips + jnp.bitwise_xor(place_ref[0], k)) * rows, rows)
+            out_ref[pl.ds(at, rows), :] = ref[k].astype(jnp.float32)
+
+
+def place_quarters(place, own, other):
+    vmem = pl.BlockSpec(memory_space=pltpu.VMEM)
+    chips, rows, cols = own.shape
+    return pl.pallas_call(
+        place_quarters_kernel,
+        out_shape=jax.ShapeDtypeStruct((2 * chips * rows, cols), jnp.float32),
+        in_specs=[pl.BlockSpec(memory_space=pltpu.SMEM)] + [vmem] * 2,
+        out_specs=vmem,
+        compiler_params=pltpu.CompilerParams(vmem_limit_bytes=16 * 1024 * 1024),
+        cost_estimate=LIGHT,
+        name="place_quarters",
+    )(place, own, other)
 
 
 from jax.sharding import PartitionSpec as P
@@ -1090,7 +1133,8 @@
     flow.end(low_x, low_y)
     cot_xo, cot_yo = seq_swap(hold(cot_x)), seq_swap(hold(cot_y))
     branch_x, branch_y = x_swap(hold(low_x)), y_swap(hold(low_y))
-    flow.end(branch_x, branch_y, cot_xo, cot_yo, feed_own)
+    cot_halves = half_rows(hold(cot_x), False), half_rows(hold(cot_y), True)
+    flow.end(branch_x, branch_y, cot_xo, cot_yo, feed_own, *cot_halves)
     residual = inputs_f + whole_sum(branch_mine[0], hold(came_0), branch_x, branch_y)
     scale_mid = norm_scale(residual)
     normed_ffn = (residual * scale_mid * feed_gain).astype(jnp.bfloat16)
@@ -1113,13 +1157,12 @@
     flow.end(hidden_rows[0], ffn_x, ffn_y)
     ffn_xo, ffn_yo = seq_swap(hold(ffn_x)), seq_swap(hold(ffn_y))
     ffn_rows[1], ffn_rows[2] = (ffn_x, ffn_xo), (ffn_y, ffn_yo)
-    low, high = half_rows(cot_x, False), half_rows(cot_y, True)
-    flow.end(ffn_xo, ffn_yo, low, high)
-    cot_low, cot_high = y_swap(hold(low)), x_swap(hold(high))
+    flow.end(ffn_xo, ffn_yo)
+    cot_low, cot_high = y_swap(hold(cot_halves[0])), x_swap(hold(cot_halves[1]))
+    low, high = half_rows(hold(ffn_x), False), half_rows(hold(ffn_y), True)
     back_came = [None] * 4
     feed(1)
-    flow.end(hidden_rows[1], cot_low, cot_high)
-    low, high = half_rows(ffn_x, False), half_rows(ffn_y, True)
+    flow.end(hidden_rows[1], cot_low, cot_high, low, high)
     cot_c = jnp.concatenate([cot_low, cot_high], 0)
     flow.end(low, high, cot_c)
     corner_low, corner_high = y_swap(hold(low)), x_swap(hold(high))
@@ -1129,10 +1172,9 @@
     flow.end(hidden_rows[2], corner_low, corner_high, cot_co, back_came[1])
     back_came[2] = seq_swap(hold(feed_out[2][3]))
     ffn_c = jnp.concatenate([corner_low, corner_high], 0)
+    ffn_co = seq_swap(ffn_c)
     low_x = pair_sum(feed_out[1][2], hold(back_came[1]))
-    flow.end(ffn_c, back_came[2], low_x)
-    ffn_co = seq_swap(hold(ffn_c))
-    low_y = pair_sum(feed_out[2][2], hold(back_came[2]))
+    low_y = pair_sum(feed_out[2][2], back_came[2])
     ffn_rows[3], cotangent_rows[3] = (ffn_c, ffn_co), (cot_c, cot_co)
     flow.end(ffn_co, low_x, low_y)
     back_x, back_y = x_swap(hold(low_x)), y_swap(hold(low_y))
@@ -1207,7 +1249,7 @@
     low = pair_sum(normed_mine[3], hold(normed_came[3]))
     flow.end(low)
     grad_d = diagonal_swap(hold(low))
-    out_came = [out_terms]
+    out_came = []
     if ring:
         out_came = [wide_shift(hold(wide_block(out_terms, -step)), step) for step in range(1, 4)]
     joined_grad_own = weight_grad(
@@ -1215,12 +1257,6 @@
     )
     flow.end(grad_d, joined_grad_own, *out_came)
     shard_joined = scatter_wide(hold(joined_grad_own))
-    if ring:
-        out_sum = wide_block(out_terms, 0).astype(jnp.float32)
-        for came in out_came:
-            out_sum = out_sum + hold(came).astype(jnp.float32)
-        shard_feed = jnp.concatenate([shard_feed, out_sum.astype(jnp.bfloat16)], 0)
-    flow.end(shard_feed)
     feed_x, feed_y, feed_o = x_swap(hold(shard_feed)), y_swap(hold(shard_feed)), seq_swap(hold(shard_feed))
     grad_normed = whole_sum(normed_mine[0], normed_came[0], grad_x, grad_y) + hold(grad_d).astype(jnp.float32)
     norm_part, grad_norm = norm_back(inputs_f, scale_in, norm_gain, grad_normed)
@@ -1248,27 +1284,25 @@
     else:
         for hop in [1 << i for i in range(16) if 1 << i < wide]:
             packed = packed + lax.ppermute(packed, "wide", [(i, i ^ hop) for i in range(wide)])
+    packed = packed + x_swap(packed)
     flow.end(packed, feed_x, feed_y, feed_o)
-    packed = packed + x_swap(hold(packed))
+    shard_out = out_x = out_y = grad_out_own
+    if ring:
+        out_sum = wide_block(out_terms, 0).astype(jnp.float32) + sum(hold(a).astype(jnp.float32) for a in out_came)
+        shard_out = out_sum.astype(jnp.bfloat16)
+    packed = packed + y_swap(hold(packed))
     feed_low, feed_high = y_swap(hold(half_rows(feed_x, False))), x_swap(hold(half_rows(feed_y, True)))
     feed_xo, feed_yo = seq_swap(hold(feed_x)), seq_swap(hold(feed_y))
     block_out = (residual + whole_sum(feed_out[0][0], hold(feed_came[0]), feed_main_x, feed_main_y)).astype(jnp.bfloat16)
-    flow.end(feed_low, feed_high, feed_xo, feed_yo, packed, shard_joined, block_out)
-
-    def columns(rows_of, sections, size):
-        if 2 * size % LANES == 0:
-            return place_columns(place, [a for k in rows_of for a in k], sections, size)
-        every = lax.all_gather(rows_of[0][0], PLANE, axis=0)[:, :, : sections * size]
-        split = every.reshape(cores, rows_of[0][0].shape[0], sections, size)
-        return jnp.moveaxis(split, 0, 2).reshape(rows_of[0][0].shape[0], -1).astype(jnp.float32)
+    flow.end(feed_low, feed_high, feed_xo, feed_yo, packed, shard_joined, block_out, shard_out)
 
     joined_x, joined_y, joined_o = x_swap(hold(shard_joined)), y_swap(hold(shard_joined)), seq_swap(hold(shard_joined))
     feed_c = jnp.concatenate([feed_low, feed_high], 0)
     feed_co = seq_swap(hold(feed_c))
     if ring:
-        grad_gate, grad_down, grad_out = place_feed(
-            place, [hold(shard_feed), feed_o, feed_x, feed_xo, feed_y, feed_yo, feed_c, feed_co], chunk,
-            width // feed_cols,
+        out_x, out_y = x_swap(hold(shard_out)), y_swap(hold(shard_out))
+        grad_gate, grad_down = place_feed(
+            place, [hold(shard_feed), feed_o, feed_x, feed_xo, feed_y, feed_yo, feed_c, feed_co], chunk
         )
     else:
         every = lax.all_gather(shard_feed, PLANE, axis=0)
@@ -1277,15 +1311,29 @@
         split = every[:, :, 2 * feed_cols :].reshape(cores, width // feed_cols, chunk, feed_cols)
         grad_down = jnp.swapaxes(split, 1, 2).reshape(cores * chunk, width).astype(jnp.float32)
         grad_out = scatter_wide(lax.all_gather(grad_out_own, PLANE, axis=0, tiled=True)).astype(jnp.float32)
-    flow.end(joined_x, joined_y, joined_o, packed, grad_gate)
+    flow.end(joined_x, joined_y, joined_o, packed, grad_gate, out_x, out_y)
     joined_low, joined_high = y_swap(hold(half_rows(joined_x, False))), x_swap(hold(half_rows(joined_y, True)))
+    if ring:
+        out_c = y_swap(hold(out_x))
     joined_xo, joined_yo = seq_swap(hold(joined_x)), seq_swap(hold(joined_y))
-    packed = packed + y_swap(hold(packed))
-    flow.end(joined_low, joined_high, joined_xo, joined_yo, packed)
+    joined_rows = [(shard_joined, joined_o), (joined_x, joined_xo), (joined_y, joined_yo)]
+    whole_columns = 2 * group_cols % LANES == 0
+    if whole_columns:
+        grad_qkv = place_columns(hold(place), [a for k in joined_rows for a in k], 3, group_cols, 4)
+        flow.end(joined_low, joined_high, grad_qkv, *([out_c] if ring else []))
+    else:
+        flow.end(joined_low, joined_high)
     joined_c = jnp.concatenate([joined_low, joined_high], 0)
     joined_co = seq_swap(hold(joined_c))
-    joined_rows = [(shard_joined, joined_o), (joined_x, joined_xo), (joined_y, joined_yo), (joined_c, joined_co)]
-    grad_qkv = columns(joined_rows, 3, group_cols)
+    if ring:
+        quarters = jnp.stack([shard_out, out_x, out_y, out_c])
+        grad_out = place_quarters(place, quarters, seq_swap(hold(quarters)))
+    if whole_columns:
+        grad_qkv = add_columns(place, joined_c, joined_co, grad_qkv, 3, group_cols, 4, 3)
+    else:
+        every = lax.all_gather(shard_joined, PLANE, axis=0)[:, :, : 3 * group_cols]
+        split = every.reshape(cores, shard_joined.shape[0], 3, group_cols)
+        grad_qkv = jnp.moveaxis(split, 0, 2).reshape(shard_joined.shape[0], -1).astype(jnp.float32)
     packed = packed.reshape(-1)
     grad_norm = packed[-width:]
     parts = []

time: 497 us -> 493 us (level)
    ppermute x22 -> x24, waiting for transfers between devices: 55.5 us -> 47.8 us  [y_swap(): return lax.ppermute(array, 'narrow', [(0, 2), (2, 0), (1, 3), (3, 1)])]
    ppermute x22 -> x24, starting transfers between devices: 22.5 us -> 28 us  [y_swap(): return lax.ppermute(array, 'narrow', [(0, 2), (2, 0), (1, 3), (3, 1)])]
    unnamed x221 -> x203, local copies, waits for them, and re-layouts: 36.5 us -> 33.8 us
    ppermute x22 -> x23, waiting for transfers between devices: 35.8 us -> 37.5 us  [x_swap(): return lax.ppermute(array, 'narrow', [(0, 1), (1, 0), (2, 3), (3, 2)])]
    ppermute x22 -> x23, starting transfers between devices: 25.5 us -> 24.3 us  [x_swap(): return lax.ppermute(array, 'narrow', [(0, 1), (1, 0), (2, 3), (3, 2)])]
    ppermute x42 -> x43, waiting for transfers between devices: 23.7 us -> 22.8 us  [seq_swap(): return lax.ppermute(array, 'seq', SWAP)]
    ppermute x42 -> x43, starting transfers between devices: 9.37 us -> 10.1 us  [seq_swap(): return lax.ppermute(array, 'seq', SWAP)]
  transfers between devices with their start and end apart: 103 -> 107, of which waited for: 49 -> 48; matrix products, arithmetic and copies ran while one was open for 9% -> 10% of each run, Pallas kernels for 37% -> 38%
where the time goes in v4:
time: 493 us; the launch traced here: 485 us
  Pallas kernels  185 us (38%)
  waiting for transfers between devices  138 us (28%)
  starting transfers between devices  72.5 us (15%)
  local copies, waits for them, and re-layouts  52.5 us (11%)
  other arithmetic  21 us (4%)
  between operations  15.6 us (3%)
    pallas_call x4, Pallas kernels, attend_row_back(): pl.pallas_call(functools.partial(backward_kernel, taps_q, taps_k, head_si...  57.6 us
    ppermute x24, waiting for transfers between devices, y_swap(): return lax.ppermute(array, 'narrow', [(0, 2), (2, 0), (1, 3), (3, 1)])  47.8 us
    ppermute x23, waiting for transfers between devices, x_swap(): return lax.ppermute(array, 'narrow', [(0, 1), (1, 0), (2, 3), (3, 2)])  37.5 us
    pallas_call x4, Pallas kernels, feed_row(): pl.pallas_call(feed_kernel, out_shape=(jax.ShapeDtypeStruct((2 * half_len...  35.9 us
    unnamed x203, local copies, waits for them, and re-layouts  33.8 us
    pallas_call x1, Pallas kernels, attend_rows(): pl.pallas_call(functools.partial(forward_kernel, taps_q, head_size, rows)...  32.9 us
    ppermute x24, starting transfers between devices, y_swap(): return lax.ppermute(array, 'narrow', [(0, 2), (2, 0), (1, 3), (3, 1)])  28 us
    ppermute x23, starting transfers between devices, x_swap(): return lax.ppermute(array, 'narrow', [(0, 1), (1, 0), (2, 3), (3, 2)])  24.3 us
  transfers between devices with their start and end apart: 107, of which 48 were waited for; matrix products, arithmetic and copies ran while one was open for 10% of the time, Pallas kernels for 38%

profile of v4, /device:TPU:0, one launch (start us, length us, event | category | flops | bytes accessed | tf_op | source)
XLA Modules:
  0.0 484.6 jit_solution(12907210129799362472)
XLA Ops:
  9.9 3.0 collective-permute-start.4
  14.5 2.1 collective-permute-start
  18.9 2.9 collective-permute-done.refs_1_
  21.8 1.7 collective-permute-start.1
  38.4 3.3 tap_bands.1
  46.9 1.6 collective-permute-start.11
  48.9 8.6 %collective-permute-done.8 = bf16[128,1536]{1,0:T(8,128)(2,1)S(1)} collective-permute-done((bf16[128,1536]{1,0:T(8,128)(2,1)S(1)}, bf16[128,1536]{1,0:T(8,128)(2,1)S(1)}, u32[]{:S(2)}, u32[]{:S(2)}) %collective-permute-start.8) | collective-permute-done | bytes 393248 | tf_op jit(solution)/shard_map/ppermute | solution.py:899
  62.0 4.2 all-gather.3.cloned.1.call-done.joined_ref
  69.1 1.8 collective-permute-start.16
  72.6 1.8 collective-permute-start.17
  76.6 32.9 %attend_rows.1 = (bf16[4,512,768]{2,1,0:T(8,128)(2,1)}, f32[4,512,256]{2,1,0:T(8,128)}, bf16[4,512,256]{2,1,0:T(8,128)(2,1)}, f32[4,2,512,512]{3,2,1,0:T(8,128)}) custom-call(s32[1]{0:T(128)} %bitcast.core_ref, f32[2,2]{1,0:T(2,128)S(1)} %copy.31.mix_ref, s32[4,512,128]{2,1,0:T(8,128)} %broadcast_in_dim.44.since_all, ...), custom_call_target="tpu_custom_call" | custom-call | flops 1000000 | bytes 1000000 | tf_op jit(solution)/shard_map/attend_rows/pallas_call | solution.py:341
  111.1 1.8 branch.1
  119.4 10.0 %collective-permute-done.24.extra_ref = bf16[128,1536]{1,0:T(8,128)(2,1)S(1)} collective-permute-done((bf16[128,1536]{1,0:T(8,128)(2,1)S(1)}, bf16[128,1536]{1,0:T(8,128)(2,1)S(1)}, u32[]{:S(2)}, u32[]{:S(2)}) %collective-permute-start.24) | collective-permute-done | bytes 393248 | tf_op jit(solution)/shard_map/ppermute | solution.py:899
  133.7 1.8 slice.99
  136.2 14.9 %collective-permute-done.27 = bf16[256,1536]{1,0:T(8,128)(2,1)S(1)} collective-permute-done((bf16[256,1536]{1,0:T(8,128)(2,1)S(1)}, bf16[256,1536]{1,0:T(8,128)(2,1)S(1)}, u32[]{:S(2)}, u32[]{:S(2)}) %collective-permute-start.27) | collective-permute-done | bytes 786464 | tf_op jit(solution)/shard_map/ppermute | solution.py:895
  152.0 4.2 all-gather.5.cloned.1.call-done.feed_ref
  156.2 2.9 multiply_reduce_fusion.2
  162.8 1.7 copy-done.2
  165.6 8.8 %feed_row.4 = (bf16[512,512]{1,0:T(8,128)(2,1)S(1)}, bf16[512,1024]{1,0:T(8,128)(2,1)}, bf16[256,1536]{1,0:T(8,128)(2,1)S(1)}, bf16[256,1536]{1,0:T(8,128)(2,1)}...) custom-call(bf16[256,1536]{1,0:T(8,128)(2,1)S(1)} %multiply_convert_fusion.own_ref.refs_0_, ...), custom_call_target="tpu_custom_call" | custom-call | bytes 28800000 | tf_op jit(solution)/shard_map/feed_row/pallas_call | solution.py:638
  175.2 4.1 collective-permute-done.32.own_ref.refs_2_
  181.1 1.8 collective-permute-done.35.other_ref.refs_5_
  186.1 9.0 %feed_row.5 = (bf16[512,512]{1,0:T(8,128)(2,1)S(1)}, bf16[512,1024]{1,0:T(8,128)(2,1)}, bf16[256,1536]{1,0:T(8,128)(2,1)S(1)}, bf16[256,1536]{1,0:T(8,128)(2,1)}...) custom-call(bf16[256,1536]{1,0:T(8,128)(2,1)S(1)} %collective-permute-done.32.own_ref.refs_2_, ...), custom_call_target="tpu_custom_call" | custom-call | bytes 28800000 | tf_op jit(solution)/shard_map/feed_row/pallas_call | solution.py:638
  198.1 9.1 %feed_row.6 = (bf16[512,512]{1,0:T(8,128)(2,1)S(1)}, bf16[512,1024]{1,0:T(8,128)(2,1)}, bf16[256,1536]{1,0:T(8,128)(2,1)S(1)}, bf16[256,1536]{1,0:T(8,128)(2,1)}...) custom-call(bf16[256,1536]{1,0:T(8,128)(2,1)S(1)} %collective-permute-done.33.own_ref.refs_4_, ...), custom_call_target="tpu_custom_call" | custom-call | bytes 28800000 | tf_op jit(solution)/shard_map/feed_row/pallas_call | solution.py:638
  213.9 9.0 %feed_row.7 = (bf16[512,512]{1,0:T(8,128)(2,1)S(1)}, bf16[512,1024]{1,0:T(8,128)(2,1)}, bf16[256,1536]{1,0:T(8,128)(2,1)S(1)}, bf16[256,1536]{1,0:T(8,128)(2,1)}...) custom-call(bf16[256,1536]{1,0:T(8,128)(2,1)S(1)} %constant_dynamic-update-slice_fusion.4.own_ref.refs_6_, ...), custom_call_target="tpu_custom_call" | custom-call | bytes 28800000 | tf_op jit(solution)/shard_map/feed_row/pallas_call | solution.py:638
  223.7 7.7 %collective-permute-done.45 = bf16[256,1536]{1,0:T(8,128)(2,1)S(1)} collective-permute-done((bf16[256,1536]{1,0:T(8,128)(2,1)S(1)}, bf16[256,1536]{1,0:T(8,128)(2,1)S(1)}, u32[]{:S(2)}, u32[]{:S(2)}) %collective-permute-start.45) | collective-permute-done | bytes 786464 | tf_op jit(solution)/shard_map/ppermute | solution.py:899
  233.1 1.8 collective-permute-done.47
  236.8 16.9 %feed_grad.1 = bf16[1536,1536]{1,0:T(8,128)(2,1)} custom-call(bf16[256,1536]{1,0:T(8,128)(2,1)} %copy-done.6, bf16[256,1536]{1,0:T(8,128)(2,1)} %copy-done.17, bf16[256,1536]{1,0:T(8,128)(2,1)} %copy-done.10, bf16[256,1536]{1,0:T(8,128)(2,1)} %copy-done.19, bf16[256,1536]{1,0:T(8,128)(2,1)} %copy-done.11, bf16[256,1536]{1,0:T(8,128)(2,1)} %copy-done.18, ...), custom_call_target="tpu_custom_call" | custom-call | bytes 61200000 | tf_op jit(solution)/shard_map/feed_grad/pallas_call | solution.py:688
  253.7 3.2 collective-permute-done.48
  258.0 4.2 multiply_reduce_fusion.1
  265.8 14.2 %attend_row_back.4 = (bf16[512,640]{1,0:T(8,128)(2,1)S(1)}, bf16[256,1536]{1,0:T(8,128)(2,1)S(1)}, bf16[256,1536]{1,0:T(8,128)(2,1)S(1)}, f32[8,128]{1,0:T(8,128)S(1)}, f32[2,66,128]{2,1,0:T(8,128)S(1)}) custom-call(s32[1]{0:T(128)} %bitcast.core_ref, f32[2,2]{1,0:T(2,128)S(1)} %copy.31.mix_ref, bf16[256,1536]{1,0:T(8,128)(2,1)S(1)} %fusion.11.own_ref.refs_1_, ...), custom_call_target="tpu_custom_call" | custom-call | bytes 50400000 | tf_op jit(solution)/shard_map/attend_row_back/pallas_call | solution.py:545
  280.0 3.5 collective-permute-done.54.own_ref.refs_3_
  284.1 1.7 collective-permute-done.57.other_ref.refs_6_
  286.9 1.7 collective-permute-start.60
  289.2 1.8 collective-permute-start.58
  290.9 14.1 %attend_row_back.5 = (bf16[512,640]{1,0:T(8,128)(2,1)S(1)}, bf16[256,1536]{1,0:T(8,128)(2,1)S(1)}, bf16[256,1536]{1,0:T(8,128)(2,1)S(1)}, f32[8,128]{1,0:T(8,128)S(1)}, f32[2,66,128]{2,1,0:T(8,128)S(1)}) custom-call(s32[1]{0:T(128)} %bitcast.core_ref, f32[2,2]{1,0:T(2,128)S(1)} %copy.31.mix_ref, ...), custom_call_target="tpu_custom_call" | custom-call | bytes 50400000 | tf_op jit(solution)/shard_map/attend_row_back/pallas_call | solution.py:545
  308.6 2.3 collective-permute-done.62.refs_8_.other_ref
  312.1 1.8 out_grad.1
  314.8 15.3 %attend_row_back.6 = (bf16[512,640]{1,0:T(8,128)(2,1)S(1)}, bf16[256,1536]{1,0:T(8,128)(2,1)S(1)}, bf16[256,1536]{1,0:T(8,128)(2,1)}, f32[8,128]{1,0:T(8,128)S(1)}, f32[2,66,128]{2,1,0:T(8,128)S(1)}) custom-call(s32[1]{0:T(128)} %bitcast.core_ref, f32[2,2]{1,0:T(2,128)S(1)} %copy.31.mix_ref, bf16[256,1536]{1,0:T(8,128)(2,1)S(1)} %collective-permute-done.55.own_ref.refs_5_, ...), custom_call_target="tpu_custom_call" | custom-call | bytes 50400000 | tf_op jit(solution)/shard_map/attend_row_back/pallas_call | solution.py:545
  340.5 1.8 collective-permute-start.70
  342.9 1.7 collective-permute-start.68
  345.7 13.9 %attend_row_back.7 = (bf16[512,640]{1,0:T(8,128)(2,1)S(1)}, bf16[256,1536]{1,0:T(8,128)(2,1)S(1)}, bf16[256,1536]{1,0:T(8,128)(2,1)S(1)}, f32[8,128]{1,0:T(8,128)S(1)}, f32[2,66,128]{2,1,0:T(8,128)S(1)}) custom-call(s32[1]{0:T(128)} %bitcast.core_ref, f32[2,2]{1,0:T(2,128)S(1)} %copy.31.mix_ref, ...), custom_call_target="tpu_custom_call" | custom-call | bytes 50400000 | tf_op jit(solution)/shard_map/attend_row_back/pallas_call | solution.py:545
  359.8 6.2 %collective-permute-done.68 = bf16[256,1536]{1,0:T(8,128)(2,1)S(1)} collective-permute-done((bf16[256,1536]{1,0:T(8,128)(2,1)S(1)}, bf16[256,1536]{1,0:T(8,128)(2,1)S(1)}, u32[]{:S(2)}, u32[]{:S(2)}) %collective-permute-start.68) | collective-permute-done | bytes 786464 | tf_op jit(solution)/shard_map/ppermute | solution.py:899
  366.6 1.8 collective-permute-done.73
  369.7 2.2 collective-permute-start.74
  371.9 1.9 dynamic-slice_bitcast_fusion
  374.1 2.0 collective-permute-start.75
  376.0 10.2 %joined_grad.1 = bf16[1536,640]{1,0:T(8,128)(2,1)} custom-call(bf16[256,1536]{1,0:T(8,128)(2,1)} %copy-done.7, bf16[256,1536]{1,0:T(8,128)(2,1)} %copy-done.23, bf16[256,1536]{1,0:T(8,128)(2,1)} %collective-permute-done.1.refs_2_, bf16[256,1536]{1,0:T(8,128)(2,1)} %collective-permute-done.13.refs_3_, bf16[256,1536]{1,0:T(8,128)(2,1)} %collective-permute-done.2.refs_4_, ...), custom_call_target="tpu_custom_call" | custom-call | bytes 28800000 | tf_op jit(solution)/shard_map/joined_grad/pallas_call | solution.py:727
  387.7 2.7 collective-permute-done.74
  390.6 1.8 collective-permute-start.83
  394.4 3.5 fusion.5
  399.4 4.4 collective-permute-done.79
  404.0 5.6 %collective-permute-done.80 = f32[48,128]{1,0:T(8,128)S(1)} collective-permute-done((f32[48,128]{1,0:T(8,128)S(1)}, f32[48,128]{1,0:T(8,128)S(1)}, u32[]{:S(2)}, u32[]{:S(2)}) %collective-permute-start.80) | collective-permute-done | bytes 24608 | tf_op jit(solution)/shard_map/ppermute | solution.py:1286
  411.1 8.9 %collective-permute-done.81 = f32[48,128]{1,0:T(8,128)S(1)} collective-permute-done((f32[48,128]{1,0:T(8,128)S(1)}, f32[48,128]{1,0:T(8,128)S(1)}, u32[]{:S(2)}, u32[]{:S(2)}) %collective-permute-start.81) | collective-permute-done | bytes 24608 | tf_op jit(solution)/shard_map/ppermute | solution.py:895
  424.2 1.7 collective-permute-start.85
  425.9 5.0 %fusion.7 = (f32[256,1536]{1,0:T(8,128)}, bf16[256,1536]{1,0:T(8,128)(2,1)}) fusion(bf16[256,1536]{1,0:T(8,128)(2,1)S(1)} %copy-done.65, f32[256,1536]{1,0:T(8,128)} %get-tuple-element.464, f32[256]{0:T(256)S(1)} %fusion.10, f32[1536]{0:T(1024)S(1)} %copy-done.89, f32[256]{0:T(256)S(1)} %add_rsqrt_fusion.1, bf16[256,1536]{1,0:T(8,128)(2,1)S(1)} %copy-done.5, ...), kind=kLoop, calls=%fused_computation.13 | loop fusion | flops 8257536 | bytes 11812864 | tf_op jit(solution)/shard_map/add | solution.py:1263
  432.1 4.9 %collective-permute-done.85 = f32[48,128]{1,0:T(8,128)S(1)} collective-permute-done((f32[48,128]{1,0:T(8,128)S(1)}, f32[48,128]{1,0:T(8,128)S(1)}, u32[]{:S(2)}, u32[]{:S(2)}) %collective-permute-start.85) | collective-permute-done | bytes 24608 | tf_op jit(solution)/shard_map/ppermute | solution.py:899
  441.4 10.3 %place_feed.1 = (f32[384,8192]{1,0:T(8,128)}, f32[1024,1536]{1,0:T(8,128)}) custom-call(s32[3]{0:T(128)} %copy-done.55, bf16[384,1536]{1,0:T(8,128)(2,1)} %reduce-scatter.3.cloned.1.call-done.refs_0_, bf16[384,1536]{1,0:T(8,128)(2,1)} %collective-permute-done.84.refs_1_, bf16[384,1536]{1,0:T(8,128)(2,1)} %collective-permute-done.82.refs_2_, ...), custom_call_target="tpu_custom_call" | custom-call | bytes 39600000 | tf_op jit(solution)/shard_map/place_feed/pallas_call | solution.py:154
  451.8 2.6 collective-permute-done.94
  456.3 1.6 collective-permute-start.96
  458.9 3.4 collective-permute-done.100
  463.3 2.5 collective-permute-done.96
  465.9 4.1 place_columns.1.base_ref
  473.5 1.9 add_columns.1
  475.5 2.1 place_quarters.1
  (475 shorter events, 127.5 us)
Async XLA Ops:
  7.2 58.9 %all-gather.3.cloned.1.call-start = ((), (), s32[]{:S(2)}) async-start(), calls=%async_computation.2 | async-start | bytes 2457600 | tf_op jit(solution)/shard_map/all_gather | solution.py:957
  14.4 141.8 %all-gather.5.cloned.1.call-start = ((), (), s32[]{:S(2)}) async-start(), calls=%async_computation.3 | async-start | bytes 5898240 | tf_op jit(solution)/shard_map/all_gather | solution.py:957
  21.8 22.1 %collective-permute-start.1 = (bf16[256,1536]{1,0:T(8,128)(2,1)S(1)}, bf16[256,1536]{1,0:T(8,128)(2,1)}, u32[]{:S(2)}, u32[]{:S(2)}) collective-permute-start(bf16[256,1536]{1,0:T(8,128)(2,1)S(1)} %fusion.2.refs_0_), channel_id=1, source_target_pairs={{0,8},{8,0},{16,24},{24,16},{1,9},{9,1},{17,25},{25,17},{2,10},{10... | collective-permute-start | bytes 2359304 | tf_op jit(solution)/shard_map/ppermute | solution.py:895
  23.5 21.4 %collective-permute-start.2 = (bf16[256,1536]{1,0:T(8,128)(2,1)S(1)}, bf16[256,1536]{1,0:T(8,128)(2,1)}, u32[]{:S(2)}, u32[]{:S(2)}) collective-permute-start(bf16[256,1536]{1,0:T(8,128)(2,1)S(1)} %fusion.2.refs_0_), channel_id=1, source_target_pairs={{0,16},{16,0},{8,24},{24,8},{1,17},{17,1},{9,25},{25,9},{2,18},{18... | collective-permute-start | bytes 2359304 | tf_op jit(solution)/shard_map/ppermute | solution.py:899
  25.0 20.9 %collective-permute-start.3 = (bf16[256,1536]{1,0:T(8,128)(2,1)S(1)}, bf16[256,1536]{1,0:T(8,128)(2,1)S(1)}, u32[]{:S(2)}, u32[]{:S(2)}) collective-permute-start(bf16[256,1536]{1,0:T(8,128)(2,1)S(1)} %fusion.2.refs_0_), channel_id=1, source_target_pairs={{0,1},{1,0},{2,3},{3,2},{4,5},{5,4},{6,7},{7,6},{8,9},{9,8},{10,11... | collective-permute-start | bytes 2359304 | tf_op jit(solution)/shard_map/ppermute | solution.py:891
  25.0 20.9 %collective-permute-start.7 = (bf16[48,1536]{1,0:T(8,128)(2,1)S(1)}, bf16[48,1536]{1,0:T(8,128)(2,1)S(1)}, u32[]{:S(2)}, u32[]{:S(2)}) collective-permute-start(bf16[48,1536]{1,0:T(8,128)(2,1)S(1)} %collective-permute-done.refs_1_), channel_id=1, source_target_pairs={{0,2},{2,4},{4,6},{6,0},{1,3},{3,5},{5,7},{7,1},{8,10},{10,12},{12... | collective-permute-start | bytes 442376 | tf_op jit(solution)/shard_map/ppermute | solution.py:940
  46.0 11.6 %collective-permute-start.8 = (bf16[128,1536]{1,0:T(8,128)(2,1)S(1)}, bf16[128,1536]{1,0:T(8,128)(2,1)S(1)}, u32[]{:S(2)}, u32[]{:S(2)}) collective-permute-start(bf16[128,1536]{1,0:T(8,128)(2,1)S(1)} %slice.122), channel_id=1, source_target_pairs={{0,16},{16,0},{8,24},{24,8},{1,17},{17,1},{9,25},{25,9},{2,18},{18... | collective-permute-start | bytes 1179656 | tf_op jit(solution)/shard_map/ppermute | solution.py:899
  46.5 11.8 %collective-permute-start.9 = (bf16[128,1536]{1,0:T(8,128)(2,1)S(1)}, bf16[128,1536]{1,0:T(8,128)(2,1)S(1)}, u32[]{:S(2)}, u32[]{:S(2)}) collective-permute-start(bf16[128,1536]{1,0:T(8,128)(2,1)S(1)} %slice.123), channel_id=1, source_target_pairs={{0,8},{8,0},{16,24},{24,16},{1,9},{9,1},{17,25},{25,17},{2,10},{10... | collective-permute-start | bytes 1179656 | tf_op jit(solution)/shard_map/ppermute | solution.py:895
  46.9 12.3 %collective-permute-start.11 = (bf16[48,1536]{1,0:T(8,128)(2,1)S(1)}, bf16[48,1536]{1,0:T(8,128)(2,1)S(1)}, u32[]{:S(2)}, u32[]{:S(2)}) collective-permute-start(bf16[48,1536]{1,0:T(8,128)(2,1)S(1)} %collective-permute-done.7.refs_2_), channel_id=1, source_target_pairs={{0,2},{2,4},{4,6},{6,0},{1,3},{3,5},{5,7},{7,1},{8,10},{10,12},{12... | collective-permute-start | bytes 442376 | tf_op jit(solution)/shard_map/ppermute | solution.py:940
  48.4 12.7 %collective-permute-start.13 = (bf16[256,1536]{1,0:T(8,128)(2,1)}, bf16[256,1536]{1,0:T(8,128)(2,1)}, u32[]{:S(2)}, u32[]{:S(2)}) collective-permute-start(bf16[256,1536]{1,0:T(8,128)(2,1)} %collective-permute-done.1.refs_2_), channel_id=1, source_target_pairs={{0,1},{1,0},{2,3},{3,2},{4,5},{5,4},{6,7},{7,6},{8,9},{9,8},{10,11... | collective-permute-start | bytes 2359304 | tf_op jit(solution)/shard_map/ppermute | solution.py:891
  67.5 323.0 %reduce-scatter.3.cloned.1.call-start = ((), (), s32[]{:S(2)}) async-start(), calls=%async_computation.4 | async-start | bytes 5898240 | tf_op jit(solution)/shard_map/reduce_scatter | solution.py:961
  67.6 41.9 %collective-permute-start.15 = (bf16[256,1536]{1,0:T(8,128)(2,1)S(1)}, bf16[256,1536]{1,0:T(8,128)(2,1)S(1)}, u32[]{:S(2)}, u32[]{:S(2)}) collective-permute-start(bf16[256,1536]{1,0:T(8,128)(2,1)S(1)} %copy-done.4), channel_id=1, source_target_pairs={{0,8},{8,0},{16,24},{24,16},{1,9},{9,1},{17,25},{25,17},{2,10},{10... | collective-permute-start | bytes 2359304 | tf_op jit(solution)/shard_map/ppermute | solution.py:895
  69.1 40.3 %collective-permute-start.16 = (bf16[256,1536]{1,0:T(8,128)(2,1)S(1)}, bf16[256,1536]{1,0:T(8,128)(2,1)}, u32[]{:S(2)}, u32[]{:S(2)}) collective-permute-start(bf16[256,1536]{1,0:T(8,128)(2,1)S(1)} %copy-done.4), channel_id=1, source_target_pairs={{0,16},{16,0},{8,24},{24,8},{1,17},{17,1},{9,25},{25,9},{2,18},{18... | collective-permute-start | bytes 2359304 | tf_op jit(solution)/shard_map/ppermute | solution.py:899
  70.9 38.6 %collective-permute-start.19 = (bf16[48,1536]{1,0:T(8,128)(2,1)}, bf16[48,1536]{1,0:T(8,128)(2,1)S(1)}, u32[]{:S(2)}, u32[]{:S(2)}) collective-permute-start(bf16[48,1536]{1,0:T(8,128)(2,1)} %copy-done.61), channel_id=1, source_target_pairs={{0,24},{8,16},{16,8},{24,0},{1,25},{9,17},{17,9},{25,1},{2,26},{10... | collective-permute-start | bytes 442376 | tf_op jit(solution)/shard_map/ppermute | solution.py:903
  71.1 38.3 %collective-permute-start.18 = (bf16[48,1536]{1,0:T(8,128)(2,1)}, bf16[48,1536]{1,0:T(8,128)(2,1)}, u32[]{:S(2)}, u32[]{:S(2)}) collective-permute-start(bf16[48,1536]{1,0:T(8,128)(2,1)} %copy-done.60), channel_id=1, source_target_pairs={{0,16},{16,0},{8,24},{24,8},{1,17},{17,1},{9,25},{25,9},{2,18},{18... | collective-permute-start | bytes 442376 | tf_op jit(solution)/shard_map/ppermute | solution.py:899
  72.6 36.9 %collective-permute-start.17 = (bf16[48,1536]{1,0:T(8,128)(2,1)}, bf16[48,1536]{1,0:T(8,128)(2,1)}, u32[]{:S(2)}, u32[]{:S(2)}) collective-permute-start(bf16[48,1536]{1,0:T(8,128)(2,1)} %copy-done.59), channel_id=1, source_target_pairs={{0,8},{8,0},{16,24},{24,16},{1,9},{9,1},{17,25},{25,17},{2,10},{10... | collective-permute-start | bytes 442376 | tf_op jit(solution)/shard_map/ppermute | solution.py:895
  117.7 12.0 %collective-permute-start.26 = (bf16[256,1536]{1,0:T(8,128)(2,1)S(1)}, bf16[256,1536]{1,0:T(8,128)(2,1)S(1)}, u32[]{:S(2)}, u32[]{:S(2)}) collective-permute-start(bf16[256,1536]{1,0:T(8,128)(2,1)S(1)} %copy-done.4), channel_id=1, source_target_pairs={{0,1},{1,0},{2,3},{3,2},{4,5},{5,4},{6,7},{7,6},{8,9},{9,8},{10,11... | collective-permute-start | bytes 2359304 | tf_op jit(solution)/shard_map/ppermute | solution.py:891
  117.9 12.7 %collective-permute-start.23 = (bf16[256,1536]{1,0:T(8,128)(2,1)S(1)}, bf16[256,1536]{1,0:T(8,128)(2,1)}, u32[]{:S(2)}, u32[]{:S(2)}) collective-permute-start(bf16[256,1536]{1,0:T(8,128)(2,1)S(1)} %get-tuple-element.272), channel_id=1, source_target_pairs={{0,1},{1,0},{2,3},{3,2},{4,5},{5,4},{6,7},{7,6},{8,9},{9,8},{10,11... | collective-permute-start | bytes 2359304 | tf_op jit(solution)/shard_map/ppermute | solution.py:891
  118.3 11.2 %collective-permute-start.24 = (bf16[128,1536]{1,0:T(8,128)(2,1)S(1)}, bf16[128,1536]{1,0:T(8,128)(2,1)S(1)}, u32[]{:S(2)}, u32[]{:S(2)}) collective-permute-start(bf16[128,1536]{1,0:T(8,128)(2,1)S(1)} %get-tuple-element.273), channel_id=1, source_target_pairs={{0,16},{16,0},{8,24},{24,8},{1,17},{17,1},{9,25},{25,9},{2,18},{18... | collective-permute-start | bytes 1179656 | tf_op jit(solution)/shard_map/ppermute | solution.py:899
  118.8 10.9 %collective-permute-start.25 = (bf16[128,1536]{1,0:T(8,128)(2,1)S(1)}, bf16[128,1536]{1,0:T(8,128)(2,1)S(1)}, u32[]{:S(2)}, u32[]{:S(2)}) collective-permute-start(bf16[128,1536]{1,0:T(8,128)(2,1)S(1)} %get-tuple-element.274), channel_id=1, source_target_pairs={{0,8},{8,0},{16,24},{24,16},{1,9},{9,1},{17,25},{25,17},{2,10},{10... | collective-permute-start | bytes 1179656 | tf_op jit(solution)/shard_map/ppermute | solution.py:895
  131.6 19.5 %collective-permute-start.27 = (bf16[256,1536]{1,0:T(8,128)(2,1)S(1)}, bf16[256,1536]{1,0:T(8,128)(2,1)S(1)}, u32[]{:S(2)}, u32[]{:S(2)}) collective-permute-start(bf16[256,1536]{1,0:T(8,128)(2,1)S(1)} %low_sum.4), channel_id=1, source_target_pairs={{0,8},{8,0},{16,24},{24,16},{1,9},{9,1},{17,25},{25,17},{2,10},{10... | collective-permute-start | bytes 2359304 | tf_op jit(solution)/shard_map/ppermute | solution.py:895
  132.2 19.8 %collective-permute-start.28 = (bf16[256,1536]{1,0:T(8,128)(2,1)S(1)}, bf16[256,1536]{1,0:T(8,128)(2,1)}, u32[]{:S(2)}, u32[]{:S(2)}) collective-permute-start(bf16[256,1536]{1,0:T(8,128)(2,1)S(1)} %low_sum.5), channel_id=1, source_target_pairs={{0,16},{16,0},{8,24},{24,8},{1,17},{17,1},{9,25},{25,9},{2,18},{18... | collective-permute-start | bytes 2359304 | tf_op jit(solution)/shard_map/ppermute | solution.py:899
  159.4 20.0 %collective-permute-start.32 = (bf16[256,1536]{1,0:T(8,128)(2,1)S(1)}, bf16[256,1536]{1,0:T(8,128)(2,1)S(1)}, u32[]{:S(2)}, u32[]{:S(2)}) collective-permute-start(bf16[256,1536]{1,0:T(8,128)(2,1)S(1)} %multiply_convert_fusion.own_ref.refs_0_), channel_id=1, source_target_pairs={{0,8},{8,0},{16,24},{24,16},{1,9},{9,1},{17,25},{25,17},{2,10},{10... | collective-permute-start | bytes 2359304 | tf_op jit(solution)/shard_map/ppermute | solution.py:895
  161.0 19.6 %collective-permute-start.33 = (bf16[256,1536]{1,0:T(8,128)(2,1)S(1)}, bf16[256,1536]{1,0:T(8,128)(2,1)S(1)}, u32[]{:S(2)}, u32[]{:S(2)}) collective-permute-start(bf16[256,1536]{1,0:T(8,128)(2,1)S(1)} %multiply_convert_fusion.own_ref.refs_0_), channel_id=1, source_target_pairs={{0,16},{16,0},{8,24},{24,8},{1,17},{17,1},{9,25},{25,9},{2,18},{18... | collective-permute-start | bytes 2359304 | tf_op jit(solution)/shard_map/ppermute | solution.py:899
  184.0 11.2 %collective-permute-start.36 = (bf16[128,1536]{1,0:T(8,128)(2,1)S(1)}, bf16[128,1536]{1,0:T(8,128)(2,1)S(1)}, u32[]{:S(2)}, u32[]{:S(2)}) collective-permute-start(bf16[128,1536]{1,0:T(8,128)(2,1)S(1)} %copy-done.87), channel_id=1, source_target_pairs={{0,16},{16,0},{8,24},{24,8},{1,17},{17,1},{9,25},{25,9},{2,18},{18... | collective-permute-start | bytes 1179656 | tf_op jit(solution)/shard_map/ppermute | solution.py:899
  196.4 12.0 %collective-permute-start.42 = (bf16[256,1536]{1,0:T(8,128)(2,1)S(1)}, bf16[256,1536]{1,0:T(8,128)(2,1)S(1)}, u32[]{:S(2)}, u32[]{:S(2)}) collective-permute-start(bf16[256,1536]{1,0:T(8,128)(2,1)S(1)} %constant_dynamic-update-slice_fusion.2.cot_own_ref.refs_22_), channel_id=1, source_target_pairs={{0,1},{1,0},{2,3},{3,2},{4,5},{5,4},{6,7},{7,6},{8,9},{9,8},{10,11... | collective-permute-start | bytes 2359304 | tf_op jit(solution)/shard_map/ppermute | solution.py:891
  196.5 11.9 %collective-permute-start.41 = (bf16[256,1536]{1,0:T(8,128)(2,1)S(1)}, bf16[256,1536]{1,0:T(8,128)(2,1)S(1)}, u32[]{:S(2)}, u32[]{:S(2)}) collective-permute-start(bf16[256,1536]{1,0:T(8,128)(2,1)S(1)} %get-tuple-element.302), channel_id=1, source_target_pairs={{0,1},{1,0},{2,3},{3,2},{4,5},{5,4},{6,7},{7,6},{8,9},{9,8},{10,11... | collective-permute-start | bytes 2359304 | tf_op jit(solution)/shard_map/ppermute | solution.py:891
  197.0 11.1 %collective-permute-start.38 = (bf16[128,1536]{1,0:T(8,128)(2,1)S(1)}, bf16[128,1536]{1,0:T(8,128)(2,1)S(1)}, u32[]{:S(2)}, u32[]{:S(2)}) collective-permute-start(bf16[128,1536]{1,0:T(8,128)(2,1)S(1)} %slice.100), channel_id=1, source_target_pairs={{0,16},{16,0},{8,24},{24,8},{1,17},{17,1},{9,25},{25,9},{2,18},{18... | collective-permute-start | bytes 1179656 | tf_op jit(solution)/shard_map/ppermute | solution.py:899
  211.8 19.6 %collective-permute-start.45 = (bf16[256,1536]{1,0:T(8,128)(2,1)S(1)}, bf16[256,1536]{1,0:T(8,128)(2,1)S(1)}, u32[]{:S(2)}, u32[]{:S(2)}) collective-permute-start(bf16[256,1536]{1,0:T(8,128)(2,1)S(1)} %pair_sum.7), channel_id=1, source_target_pairs={{0,16},{16,0},{8,24},{24,8},{1,17},{17,1},{9,25},{25,9},{2,18},{18... | collective-permute-start | bytes 2359304 | tf_op jit(solution)/shard_map/ppermute | solution.py:899
  213.3 19.3 %collective-permute-start.44 = (bf16[256,1536]{1,0:T(8,128)(2,1)S(1)}, bf16[256,1536]{1,0:T(8,128)(2,1)S(1)}, u32[]{:S(2)}, u32[]{:S(2)}) collective-permute-start(bf16[256,1536]{1,0:T(8,128)(2,1)S(1)} %pair_sum.6), channel_id=1, source_target_pairs={{0,8},{8,0},{16,24},{24,16},{1,9},{9,1},{17,25},{25,17},{2,10},{10... | collective-permute-start | bytes 2359304 | tf_op jit(solution)/shard_map/ppermute | solution.py:895
  236.2 20.7 %collective-permute-start.48 = (bf16[256,1536]{1,0:T(8,128)(2,1)S(1)}, bf16[256,1536]{1,0:T(8,128)(2,1)}, u32[]{:S(2)}, u32[]{:S(2)}) collective-permute-start(bf16[256,1536]{1,0:T(8,128)(2,1)S(1)} %pair_sum.8), channel_id=1, source_target_pairs={{0,24},{8,16},{16,8},{24,0},{1,25},{9,17},{17,9},{25,1},{2,26},{10... | collective-permute-start | bytes 2359304 | tf_op jit(solution)/shard_map/ppermute | solution.py:903
  256.9 180.3 %reduce-scatter.5.cloned.1.call-start = ((), (), s32[]{:S(2)}) async-start(), calls=%async_computation.5 | async-start | bytes 2457600 | tf_op jit(solution)/shard_map/reduce_scatter | solution.py:961
  263.5 20.0 %collective-permute-start.54 = (bf16[256,1536]{1,0:T(8,128)(2,1)S(1)}, bf16[256,1536]{1,0:T(8,128)(2,1)S(1)}, u32[]{:S(2)}, u32[]{:S(2)}) collective-permute-start(bf16[256,1536]{1,0:T(8,128)(2,1)S(1)} %fusion.11.own_ref.refs_1_), channel_id=1, source_target_pairs={{0,8},{8,0},{16,24},{24,16},{1,9},{9,1},{17,25},{25,17},{2,10},{10... | collective-permute-start | bytes 2359304 | tf_op jit(solution)/shard_map/ppermute | solution.py:895
  263.6 19.9 %collective-permute-start.55 = (bf16[256,1536]{1,0:T(8,128)(2,1)S(1)}, bf16[256,1536]{1,0:T(8,128)(2,1)S(1)}, u32[]{:S(2)}, u32[]{:S(2)}) collective-permute-start(bf16[256,1536]{1,0:T(8,128)(2,1)S(1)} %fusion.11.own_ref.refs_1_), channel_id=1, source_target_pairs={{0,16},{16,0},{8,24},{24,8},{1,17},{17,1},{9,25},{25,9},{2,18},{18... | collective-permute-start | bytes 2359304 | tf_op jit(solution)/shard_map/ppermute | solution.py:899
  286.9 19.1 %collective-permute-start.60 = (bf16[128,1536]{1,0:T(8,128)(2,1)S(1)}, bf16[128,1536]{1,0:T(8,128)(2,1)S(1)}, u32[]{:S(2)}, u32[]{:S(2)}) collective-permute-start(bf16[128,1536]{1,0:T(8,128)(2,1)S(1)} %slice.125), channel_id=1, source_target_pairs={{0,8},{8,0},{16,24},{24,16},{1,9},{9,1},{17,25},{25,17},{2,10},{10... | collective-permute-start | bytes 1179656 | tf_op jit(solution)/shard_map/ppermute | solution.py:895
  288.6 17.4 %collective-permute-start.59 = (bf16[128,1536]{1,0:T(8,128)(2,1)S(1)}, bf16[128,1536]{1,0:T(8,128)(2,1)S(1)}, u32[]{:S(2)}, u32[]{:S(2)}) collective-permute-start(bf16[128,1536]{1,0:T(8,128)(2,1)S(1)} %slice.124), channel_id=1, source_target_pairs={{0,16},{16,0},{8,24},{24,8},{1,17},{17,1},{9,25},{25,9},{2,18},{18... | collective-permute-start | bytes 1179656 | tf_op jit(solution)/shard_map/ppermute | solution.py:899
  288.9 17.6 %collective-permute-start.61 = (bf16[128,1536]{1,0:T(8,128)(2,1)S(1)}, bf16[128,1536]{1,0:T(8,128)(2,1)S(1)}, u32[]{:S(2)}, u32[]{:S(2)}) collective-permute-start(bf16[128,1536]{1,0:T(8,128)(2,1)S(1)} %get-tuple-element.364), channel_id=1, source_target_pairs={{0,8},{8,0},{16,24},{24,16},{1,9},{9,1},{17,25},{25,17},{2,10},{10... | collective-permute-start | bytes 1179656 | tf_op jit(solution)/shard_map/ppermute | solution.py:895
  289.2 18.7 %collective-permute-start.58 = (bf16[128,1536]{1,0:T(8,128)(2,1)S(1)}, bf16[128,1536]{1,0:T(8,128)(2,1)S(1)}, u32[]{:S(2)}, u32[]{:S(2)}) collective-permute-start(bf16[128,1536]{1,0:T(8,128)(2,1)S(1)} %get-tuple-element.360), channel_id=1, source_target_pairs={{0,16},{16,0},{8,24},{24,8},{1,17},{17,1},{9,25},{25,9},{2,18},{18... | collective-permute-start | bytes 1179656 | tf_op jit(solution)/shard_map/ppermute | solution.py:899
  310.9 21.1 %collective-permute-start.65 = (bf16[256,1536]{1,0:T(8,128)(2,1)S(1)}, bf16[256,1536]{1,0:T(8,128)(2,1)S(1)}, u32[]{:S(2)}, u32[]{:S(2)}) collective-permute-start(bf16[256,1536]{1,0:T(8,128)(2,1)S(1)} %low_sum.7), channel_id=1, source_target_pairs={{0,16},{16,0},{8,24},{24,8},{1,17},{17,1},{9,25},{25,9},{2,18},{18... | collective-permute-start | bytes 2359304 | tf_op jit(solution)/shard_map/ppermute | solution.py:899
  311.1 20.8 %collective-permute-start.64 = (bf16[256,1536]{1,0:T(8,128)(2,1)S(1)}, bf16[256,1536]{1,0:T(8,128)(2,1)S(1)}, u32[]{:S(2)}, u32[]{:S(2)}) collective-permute-start(bf16[256,1536]{1,0:T(8,128)(2,1)S(1)} %low_sum.6), channel_id=1, source_target_pairs={{0,8},{8,0},{16,24},{24,16},{1,9},{9,1},{17,25},{25,17},{2,10},{10... | collective-permute-start | bytes 2359304 | tf_op jit(solution)/shard_map/ppermute | solution.py:895
  312.1 19.9 %collective-permute-start.63 = (bf16[256,1536]{1,0:T(8,128)(2,1)S(1)}, bf16[256,1536]{1,0:T(8,128)(2,1)S(1)}, u32[]{:S(2)}, u32[]{:S(2)}) collective-permute-start(bf16[256,1536]{1,0:T(8,128)(2,1)S(1)} %get-tuple-element.373), channel_id=1, source_target_pairs={{0,1},{1,0},{2,3},{3,2},{4,5},{5,4},{6,7},{7,6},{8,9},{9,8},{10,11... | collective-permute-start | bytes 2359304 | tf_op jit(solution)/shard_map/ppermute | solution.py:891
  339.4 20.3 %collective-permute-start.69 = (bf16[48,1536]{1,0:T(8,128)(2,1)S(1)}, bf16[48,1536]{1,0:T(8,128)(2,1)S(1)}, u32[]{:S(2)}, u32[]{:S(2)}) collective-permute-start(bf16[48,1536]{1,0:T(8,128)(2,1)S(1)} %get-tuple-element.481), channel_id=1, source_target_pairs={{0,8},{8,0},{16,24},{24,16},{1,9},{9,1},{17,25},{25,17},{2,10},{10... | collective-permute-start | bytes 442376 | tf_op jit(solution)/shard_map/ppermute | solution.py:895
  340.5 19.3 %collective-permute-start.70 = (bf16[48,1536]{1,0:T(8,128)(2,1)S(1)}, bf16[48,1536]{1,0:T(8,128)(2,1)S(1)}, u32[]{:S(2)}, u32[]{:S(2)}) collective-permute-start(bf16[48,1536]{1,0:T(8,128)(2,1)S(1)} %get-tuple-element.480), channel_id=1, source_target_pairs={{0,16},{16,0},{8,24},{24,8},{1,17},{17,1},{9,25},{25,9},{2,18},{18... | collective-permute-start | bytes 442376 | tf_op jit(solution)/shard_map/ppermute | solution.py:899
  342.2 17.5 %collective-permute-start.71 = (bf16[48,1536]{1,0:T(8,128)(2,1)S(1)}, bf16[48,1536]{1,0:T(8,128)(2,1)S(1)}, u32[]{:S(2)}, u32[]{:S(2)}) collective-permute-start(bf16[48,1536]{1,0:T(8,128)(2,1)S(1)} %get-tuple-element.479), channel_id=1, source_target_pairs={{0,24},{8,16},{16,8},{24,0},{1,25},{9,17},{17,9},{25,1},{2,26},{10... | collective-permute-start | bytes 442376 | tf_op jit(solution)/shard_map/ppermute | solution.py:903
  342.9 23.1 %collective-permute-start.68 = (bf16[256,1536]{1,0:T(8,128)(2,1)S(1)}, bf16[256,1536]{1,0:T(8,128)(2,1)S(1)}, u32[]{:S(2)}, u32[]{:S(2)}) collective-permute-start(bf16[256,1536]{1,0:T(8,128)(2,1)S(1)} %pair_sum.10), channel_id=1, source_target_pairs={{0,16},{16,0},{8,24},{24,8},{1,17},{17,1},{9,25},{25,9},{2,18},{18... | collective-permute-start | bytes 2359304 | tf_op jit(solution)/shard_map/ppermute | solution.py:899
  344.6 21.4 %collective-permute-start.67 = (bf16[256,1536]{1,0:T(8,128)(2,1)S(1)}, bf16[256,1536]{1,0:T(8,128)(2,1)S(1)}, u32[]{:S(2)}, u32[]{:S(2)}) collective-permute-start(bf16[256,1536]{1,0:T(8,128)(2,1)S(1)} %pair_sum.9), channel_id=1, source_target_pairs={{0,8},{8,0},{16,24},{24,16},{1,9},{9,1},{17,25},{25,17},{2,10},{10... | collective-permute-start | bytes 2359304 | tf_op jit(solution)/shard_map/ppermute | solution.py:895
  369.7 20.7 %collective-permute-start.74 = (bf16[256,1536]{1,0:T(8,128)(2,1)S(1)}, bf16[256,1536]{1,0:T(8,128)(2,1)}, u32[]{:S(2)}, u32[]{:S(2)}) collective-permute-start(bf16[256,1536]{1,0:T(8,128)(2,1)S(1)} %pair_sum.11), channel_id=1, source_target_pairs={{0,24},{8,16},{16,8},{24,0},{1,25},{9,17},{17,9},{25,1},{2,26},{10... | collective-permute-start | bytes 2359304 | tf_op jit(solution)/shard_map/ppermute | solution.py:903
  373.7 12.5 %collective-permute-start.77 = (bf16[48,1536]{1,0:T(8,128)(2,1)}, bf16[48,1536]{1,0:T(8,128)(2,1)}, u32[]{:S(2)}, u32[]{:S(2)}) collective-permute-start(bf16[48,1536]{1,0:T(8,128)(2,1)} %get-tuple-element.414), channel_id=1, source_target_pairs={{0,6},{2,0},{4,2},{6,4},{1,7},{3,1},{5,3},{7,5},{8,14},{10,8},{12,... | collective-permute-start | bytes 442376 | tf_op jit(solution)/shard_map/ppermute | solution.py:940
  373.8 13.9 %collective-permute-start.76 = (bf16[48,1536]{1,0:T(8,128)(2,1)}, bf16[48,1536]{1,0:T(8,128)(2,1)}, u32[]{:S(2)}, u32[]{:S(2)}) collective-permute-start(bf16[48,1536]{1,0:T(8,128)(2,1)} %get-tuple-element.413), channel_id=1, source_target_pairs={{0,4},{2,6},{4,0},{6,2},{1,5},{3,7},{5,1},{7,3},{8,12},{10,14},{12... | collective-permute-start | bytes 442376 | tf_op jit(solution)/shard_map/ppermute | solution.py:940
  374.1 13.6 %collective-permute-start.75 = (bf16[48,1536]{1,0:T(8,128)(2,1)}, bf16[48,1536]{1,0:T(8,128)(2,1)}, u32[]{:S(2)}, u32[]{:S(2)}) collective-permute-start(bf16[48,1536]{1,0:T(8,128)(2,1)} %get-tuple-element.412), channel_id=1, source_target_pairs={{0,2},{2,4},{4,6},{6,0},{1,3},{3,5},{5,7},{7,1},{8,10},{10,12},{12... | collective-permute-start | bytes 442376 | tf_op jit(solution)/shard_map/ppermute | solution.py:940
  390.6 29.5 %collective-permute-start.83 = (bf16[384,1536]{1,0:T(8,128)(2,1)}, bf16[384,1536]{1,0:T(8,128)(2,1)}, u32[]{:S(2)}, u32[]{:S(2)}) collective-permute-start(bf16[384,1536]{1,0:T(8,128)(2,1)} %reduce-scatter.3.cloned.1.call-done.refs_0_), channel_id=1, source_target_pairs={{0,16},{16,0},{8,24},{24,8},{1,17},{17,1},{9,25},{25,9},{2,18},{18... | collective-permute-start | bytes 3538952 | tf_op jit(solution)/shard_map/ppermute | solution.py:899
  392.4 28.8 %collective-permute-start.82 = (bf16[384,1536]{1,0:T(8,128)(2,1)}, bf16[384,1536]{1,0:T(8,128)(2,1)}, u32[]{:S(2)}, u32[]{:S(2)}) collective-permute-start(bf16[384,1536]{1,0:T(8,128)(2,1)} %reduce-scatter.3.cloned.1.call-done.refs_0_), channel_id=1, source_target_pairs={{0,8},{8,0},{16,24},{24,16},{1,9},{9,1},{17,25},{25,17},{2,10},{10... | collective-permute-start | bytes 3538952 | tf_op jit(solution)/shard_map/ppermute | solution.py:895
  393.3 27.9 %collective-permute-start.84 = (bf16[384,1536]{1,0:T(8,128)(2,1)}, bf16[384,1536]{1,0:T(8,128)(2,1)}, u32[]{:S(2)}, u32[]{:S(2)}) collective-permute-start(bf16[384,1536]{1,0:T(8,128)(2,1)} %reduce-scatter.3.cloned.1.call-done.refs_0_), channel_id=1, source_target_pairs={{0,1},{1,0},{2,3},{3,2},{4,5},{5,4},{6,7},{7,6},{8,9},{9,8},{10,11... | collective-permute-start | bytes 3538952 | tf_op jit(solution)/shard_map/ppermute | solution.py:891
  421.2 15.9 %collective-permute-start.87 = (bf16[192,1536]{1,0:T(8,128)(2,1)S(1)}, bf16[192,1536]{1,0:T(8,128)(2,1)S(1)}, u32[]{:S(2)}, u32[]{:S(2)}) collective-permute-start(bf16[192,1536]{1,0:T(8,128)(2,1)S(1)} %slice.129), channel_id=1, source_target_pairs={{0,8},{8,0},{16,24},{24,16},{1,9},{9,1},{17,25},{25,17},{2,10},{10... | collective-permute-start | bytes 1769480 | tf_op jit(solution)/shard_map/ppermute | solution.py:895
  423.2 13.8 %collective-permute-start.86 = (bf16[192,1536]{1,0:T(8,128)(2,1)S(1)}, bf16[192,1536]{1,0:T(8,128)(2,1)S(1)}, u32[]{:S(2)}, u32[]{:S(2)}) collective-permute-start(bf16[192,1536]{1,0:T(8,128)(2,1)S(1)} %slice.128), channel_id=1, source_target_pairs={{0,16},{16,0},{8,24},{24,8},{1,17},{17,1},{9,25},{25,9},{2,18},{18... | collective-permute-start | bytes 1769480 | tf_op jit(solution)/shard_map/ppermute | solution.py:899
  423.7 13.5 %collective-permute-start.89 = (bf16[384,1536]{1,0:T(8,128)(2,1)}, bf16[384,1536]{1,0:T(8,128)(2,1)}, u32[]{:S(2)}, u32[]{:S(2)}) collective-permute-start(bf16[384,1536]{1,0:T(8,128)(2,1)} %collective-permute-done.83.refs_4_), channel_id=1, source_target_pairs={{0,1},{1,0},{2,3},{3,2},{4,5},{5,4},{6,7},{7,6},{8,9},{9,8},{10,11... | collective-permute-start | bytes 3538952 | tf_op jit(solution)/shard_map/ppermute | solution.py:891
  423.7 13.5 %collective-permute-start.88 = (bf16[384,1536]{1,0:T(8,128)(2,1)}, bf16[384,1536]{1,0:T(8,128)(2,1)}, u32[]{:S(2)}, u32[]{:S(2)}) collective-permute-start(bf16[384,1536]{1,0:T(8,128)(2,1)} %collective-permute-done.82.refs_2_), channel_id=1, source_target_pairs={{0,1},{1,0},{2,3},{3,2},{4,5},{5,4},{6,7},{7,6},{8,9},{9,8},{10,11... | collective-permute-start | bytes 3538952 | tf_op jit(solution)/shard_map/ppermute | solution.py:891
  424.2 12.8 %collective-permute-start.85 = (f32[48,128]{1,0:T(8,128)S(1)}, f32[48,128]{1,0:T(8,128)S(1)}, u32[]{:S(2)}, u32[]{:S(2)}) collective-permute-start(f32[48,128]{1,0:T(8,128)S(1)} %add.319), channel_id=1, source_target_pairs={{0,16},{16,0},{8,24},{24,8},{1,17},{17,1},{9,25},{25,9},{2,18},{18... | collective-permute-start | bytes 73736 | tf_op jit(solution)/shard_map/ppermute | solution.py:899
  437.3 17.9 %collective-permute-start.90 = (bf16[384,640]{1,0:T(8,128)(2,1)}, bf16[384,640]{1,0:T(8,128)(2,1)S(1)}, u32[]{:S(2)}, u32[]{:S(2)}) collective-permute-start(bf16[384,640]{1,0:T(8,128)(2,1)} %reduce-scatter.5.cloned.1.call-done.refs_0_), channel_id=1, source_target_pairs={{0,8},{8,0},{16,24},{24,16},{1,9},{9,1},{17,25},{25,17},{2,10},{10... | collective-permute-start | bytes 1474568 | tf_op jit(solution)/shard_map/ppermute | solution.py:895
  438.4 16.8 %collective-permute-start.91 = (bf16[384,640]{1,0:T(8,128)(2,1)}, bf16[384,640]{1,0:T(8,128)(2,1)S(1)}, u32[]{:S(2)}, u32[]{:S(2)}) collective-permute-start(bf16[384,640]{1,0:T(8,128)(2,1)} %reduce-scatter.5.cloned.1.call-done.refs_0_), channel_id=1, source_target_pairs={{0,16},{16,0},{8,24},{24,8},{1,17},{17,1},{9,25},{25,9},{2,18},{18... | collective-permute-start | bytes 1474568 | tf_op jit(solution)/shard_map/ppermute | solution.py:899
  438.9 16.3 %collective-permute-start.92 = (bf16[384,640]{1,0:T(8,128)(2,1)}, bf16[384,640]{1,0:T(8,128)(2,1)S(1)}, u32[]{:S(2)}, u32[]{:S(2)}) collective-permute-start(bf16[384,640]{1,0:T(8,128)(2,1)} %reduce-scatter.5.cloned.1.call-done.refs_0_), channel_id=1, source_target_pairs={{0,1},{1,0},{2,3},{3,2},{4,5},{5,4},{6,7},{7,6},{8,9},{9,8},{10,11... | collective-permute-start | bytes 1474568 | tf_op jit(solution)/shard_map/ppermute | solution.py:891
  438.9 15.5 %collective-permute-start.94 = (bf16[48,1536]{1,0:T(8,128)(2,1)S(1)}, bf16[48,1536]{1,0:T(8,128)(2,1)}, u32[]{:S(2)}, u32[]{:S(2)}) collective-permute-start(bf16[48,1536]{1,0:T(8,128)(2,1)S(1)} %fusion.8), channel_id=1, source_target_pairs={{0,8},{8,0},{16,24},{24,16},{1,9},{9,1},{17,25},{25,17},{2,10},{10... | collective-permute-start | bytes 442376 | tf_op jit(solution)/shard_map/ppermute | solution.py:895
  440.1 15.1 %collective-permute-start.95 = (bf16[48,1536]{1,0:T(8,128)(2,1)S(1)}, bf16[48,1536]{1,0:T(8,128)(2,1)}, u32[]{:S(2)}, u32[]{:S(2)}) collective-permute-start(bf16[48,1536]{1,0:T(8,128)(2,1)S(1)} %fusion.8), channel_id=1, source_target_pairs={{0,16},{16,0},{8,24},{24,8},{1,17},{17,1},{9,25},{25,9},{2,18},{18... | collective-permute-start | bytes 442376 | tf_op jit(solution)/shard_map/ppermute | solution.py:899
  457.9 12.1 %collective-permute-start.97 = (bf16[192,640]{1,0:T(8,128)(2,1)S(1)}, bf16[192,640]{1,0:T(8,128)(2,1)S(1)}, u32[]{:S(2)}, u32[]{:S(2)}) collective-permute-start(bf16[192,640]{1,0:T(8,128)(2,1)S(1)} %slice.131), channel_id=1, source_target_pairs={{0,8},{8,0},{16,24},{24,16},{1,9},{9,1},{17,25},{25,17},{2,10},{10... | collective-permute-start | bytes 737288 | tf_op jit(solution)/shard_map/ppermute | solution.py:895
  (136 other events, 1029.0 us)
Sparse Core Ops, SparseCore 0:
  14.6 51.5 all-gather.2
  68.3 87.8 all-gather.4
  257.0 81.8 reduce-scatter.2
  390.5 40.4 reduce-scatter.4

commit v5 on v4

--- a/solution.py
+++ b/solution.py
@@ -211,9 +211,12 @@
     return jnp.concatenate(tiles, 1)
 
 
-def forward_kernel(taps_q, head_size, rows, core_ref, mix_ref, since_all, joined_ref, taps_ref, gain_ref, *refs):
-    halves, outs = refs[: 2 * rows], refs[2 * rows : 2 * rows + 4]
-    pieces, proj, att, grouped, maps, keys_pad, s_high, s_low, spread, grouped_row, in_sems, out_sems = refs[2 * rows + 4 :]
+def forward_kernel(taps_q, head_size, rows, core_ref, mix_ref, joined_ref, taps_ref, gain_ref, *refs):
+    halves, outs = refs[: 2 * rows], refs[2 * rows : 2 * rows + 5]
+    (
+        pieces, proj, att, grouped, maps, since_all, keys_pad, s_high, s_low, spread, grouped_row, in_sems, out_sems
+    ) = refs[2 * rows + 5 :]
+    width = joined_ref.shape[0]
     arrivals = [pltpu.make_async_copy(ref, pieces.at[i], in_sems.at[i]) for i, ref in enumerate(halves)]
     for arrival in arrivals:
         arrival.start()
@@ -229,7 +232,10 @@
         pltpu.make_async_copy(halves[0], pieces.at[step], in_sems.at[step]).wait()
         row, part = lax.div(step, 2), lax.rem(step, 2)
         at = pl.multiple_of(jnp.bitwise_xor(core, part) * half_len, half_len)
-        joined = jnp.dot(pieces[step], joined_ref[...], preferred_element_type=jnp.float32)
+        joined = jnp.dot(pieces[step, :, :width], joined_ref[...], preferred_element_type=jnp.float32)
+        extra = pieces[step, :, width:].astype(jnp.float32)
+        since = (extra[:, 0:1] * 256.0 + extra[:, 1:2]).astype(jnp.int32)
+        since_all[row, pl.ds(at, half_len), :] = jnp.broadcast_to(since, (half_len, LANES))
         for head, piece in enumerate(split_heads(joined, 6, head_size)):
             proj[row, pl.ds(at, half_len), head * LANES : (head + 1) * LANES] = piece.astype(jnp.bfloat16)
         return carry
@@ -262,7 +268,7 @@
     def copies_out(row):
         return [
             pltpu.make_async_copy(here.at[row], there.at[row], out_sems.at[kind, row])
-            for kind, (here, there) in enumerate(zip((proj, att, grouped, maps), outs))
+            for kind, (here, there) in enumerate(zip((proj, att, grouped, maps, since_all), outs))
         ]
 
     def one_head(step, carry):
@@ -326,8 +332,8 @@
     return centered * scale, scale
 
 
-def attend_rows(core, halves, since, mix, joined, taps_forward, gain_pad, taps_q, head_size):
-    rows, seq_len = since.shape[:2]
+def attend_rows(core, halves, mix, joined, taps_forward, gain_pad, taps_q, head_size):
+    rows, seq_len = len(halves) // 2, 2 * halves[0].shape[0]
     full = seq_len + 2 * EDGE
     vmem = pl.BlockSpec(memory_space=pltpu.VMEM)
     smem = pl.BlockSpec(memory_space=pltpu.SMEM)
@@ -337,12 +343,13 @@
         ((rows, seq_len, 2 * LANES), jnp.float32),
         ((rows, seq_len, 2 * LANES), jnp.bfloat16),
         ((rows, 2, seq_len, seq_len), jnp.float32),
+        ((rows, seq_len, LANES), jnp.int32),
     )
     return pl.pallas_call(
         functools.partial(forward_kernel, taps_q, head_size, rows),
         out_shape=tuple(jax.ShapeDtypeStruct(*a) for a in shapes),
-        in_specs=[smem, smem] + [vmem] * 4 + [anywhere] * len(halves),
-        out_specs=(anywhere,) * 4,
+        in_specs=[smem, smem] + [vmem] * 3 + [anywhere] * len(halves),
+        out_specs=(anywhere,) * 5,
         scratch_shapes=[pltpu.VMEM((len(halves),) + halves[0].shape, jnp.bfloat16)]
         + [pltpu.VMEM(*a) for a in shapes]
         + [
@@ -352,12 +359,12 @@
             pltpu.VMEM((TOP + seq_len, taps_q * LANES), jnp.float32),
             pltpu.VMEM((seq_len, 2 * LANES), jnp.bfloat16),
             pltpu.SemaphoreType.DMA((len(halves),)),
-            pltpu.SemaphoreType.DMA((4, rows)),
+            pltpu.SemaphoreType.DMA((5, rows)),
         ],
         compiler_params=pltpu.CompilerParams(vmem_limit_bytes=52 * 1024 * 1024),
         cost_estimate=LIGHT,
         name="attend_rows",
-    )(core, mix, since, joined, taps_forward, gain_pad, *halves)
+    )(core, mix, joined, taps_forward, gain_pad, *halves)
 
 
 def backward_kernel(
@@ -722,7 +729,7 @@
 
 
 def weight_grad(lefts, rights, block, name):
-    rows_out, cols_out = lefts[0].shape[1], rights[0].shape[1]
+    rows_out, cols_out = lefts[0].shape[1] // block * block, rights[0].shape[1]
     count = sum(a.shape[0] for a in lefts)
     return pl.pallas_call(
         functools.partial(weight_kernel, len(lefts)),
@@ -1047,9 +1054,13 @@
 
     inputs_f = inputs.astype(jnp.float32)
     scale_in = norm_scale(inputs_f)
-    normed = (inputs_f * scale_in * norm_gain).astype(jnp.bfloat16)
     since = first_pos + jnp.arange(tokens_dev, dtype=jnp.int32) - doc_start
-    since_same = jnp.stack([since, x_swap(since), y_swap(since), diagonal_swap(since)])
+    high = since // 256
+    lane = jnp.arange(LANES, dtype=jnp.int32)[None, :]
+    extra = jnp.where(lane == 0, high[:, None], jnp.where(lane == 1, (since - 256 * high)[:, None], 0))
+    normed = jnp.concatenate(
+        [(inputs_f * scale_in * norm_gain).astype(jnp.bfloat16), extra.astype(jnp.bfloat16)], 1
+    )
     out_pieces = [lax.dynamic_slice_in_dim(out_weight, (lax.axis_index("seq") * 4 + line) * out_rows, out_rows, 0)]
 
     def out_step():
@@ -1077,29 +1088,23 @@
         [down_piece[:, at : at + feed_cols] for at in range(0, width, feed_cols)], 0
     )
     feed_piece = jnp.concatenate([gate_piece, down_piece], 1)
-    flow.end(normed_x, normed_y, normed_o, taps_forward, since_same, feed_piece, out_pieces[-1])
+    flow.end(normed_x, normed_y, normed_o, taps_forward, feed_piece, out_pieces[-1])
 
     low, high = half_rows(normed_x, False), half_rows(normed_y, True)
     flow.end(low, high, *flow.ended)
     corner_low, corner_high = y_swap(hold(low)), x_swap(hold(high))
     cot_x, cot_y = x_swap(hold(cotangent)), y_swap(hold(cotangent))
     out_step()
-    since_other = seq_swap(hold(since_same))
-    flow.end(corner_low, corner_high, since_other, out_pieces[-1])
+    flow.end(corner_low, corner_high, out_pieces[-1])
 
     normed_c = jnp.concatenate([corner_low, corner_high], 0)
     normed_xo, normed_yo, normed_co = seq_swap(normed_x), seq_swap(normed_y), seq_swap(hold(normed_c))
-    first = lax.axis_index("seq") == 0
-    since_all = hold(
-        jnp.concatenate([jnp.where(first, since_same, since_other), jnp.where(first, since_other, since_same)], 1)
-    )
-    since_rows = jnp.broadcast_to(since_all[:, :, None], since_all.shape + (LANES,))
     normed_rows = [(normed, normed_o), (normed_x, normed_xo), (normed_y, normed_yo), (normed_c, normed_co)]
     if ring:
         out_picked = pick_out(hold(place), out_pieces)
-        flow.end(normed_co, normed_xo, normed_yo, joined, since_rows, *out_picked)
+        flow.end(normed_co, normed_xo, normed_yo, joined, *out_picked)
     else:
-        flow.end(normed_co, normed_xo, normed_yo, joined, since_rows)
+        flow.end(normed_co, normed_xo, normed_yo, joined)
 
     feed_own = gather_wide(hold(feed_piece))
     if ring:
@@ -1107,8 +1112,8 @@
         out_pieces = [
             out_picked[0], x_swap(out_picked[1]), y_swap(out_picked[2]), diagonal_swap(out_picked[3])
         ]
-    projected, attended, grouped, weights = attend_rows(
-        hold(core), [a for k in normed_rows for a in k], since_rows, mix, joined, taps_forward, gain_pad, taps_q,
+    projected, attended, grouped, weights, since_rows = attend_rows(
+        hold(core), [a for k in normed_rows for a in k], mix, joined, taps_forward, gain_pad, taps_q,
         head_size,
     )
     flow.end(grouped, cot_x, cot_y, *out_pieces)

time: 493 us -> 490 us (level)
  starting transfers between devices: 72.5 us -> 67.1 us
    ppermute x23 -> x22, starting transfers between devices: 24.3 us -> 20.8 us  [x_swap(): return lax.ppermute(array, 'narrow', [(0, 1), (1, 0), (2, 3), (3, 2)])]
    ppermute x24 -> x23, starting transfers between devices: 28 us -> 26.2 us  [y_swap(): return lax.ppermute(array, 'narrow', [(0, 2), (2, 0), (1, 3), (3, 1)])]
    unnamed x203 -> x205, local copies, waits for them, and re-layouts: 33.8 us -> 35.3 us
    ppermute x24 -> x23, waiting for transfers between devices: 47.8 us -> 49.3 us  [y_swap(): return lax.ppermute(array, 'narrow', [(0, 2), (2, 0), (1, 3), (3, 1)])]
    ppermute x43 -> x42, starting transfers between devices: 10.1 us -> 9.21 us  [seq_swap(): return lax.ppermute(array, 'seq', SWAP)]
    ppermute x23 -> x22, waiting for transfers between devices: 37.5 us -> 37.8 us  [x_swap(): return lax.ppermute(array, 'narrow', [(0, 1), (1, 0), (2, 3), (3, 2)])]
    ppermute x43 -> x42, waiting for transfers between devices: 22.8 us -> 22.7 us  [seq_swap(): return lax.ppermute(array, 'seq', SWAP)]
  transfers between devices with their start and end apart: 107 -> 103, of which waited for: 48 -> 47; matrix products, arithmetic and copies ran while one was open for 10% -> 10% of each run, Pallas kernels for 38% -> 38%
where the time goes in v5:
time: 490 us; the launch traced here: 481 us
  Pallas kernels  184 us (38%)
  waiting for transfers between devices  141 us (29%)
  starting transfers between devices  67.1 us (14%)
  local copies, waits for them, and re-layouts  52 us (11%)
  other arithmetic  21 us (4%)
  between operations  15.7 us (3%)
    pallas_call x4, Pallas kernels, attend_row_back(): pl.pallas_call(functools.partial(backward_kernel, taps_q, taps_k, head_si...  57.6 us
    ppermute x23, waiting for transfers between devices, y_swap(): return lax.ppermute(array, 'narrow', [(0, 2), (2, 0), (1, 3), (3, 1)])  49.3 us
    ppermute x22, waiting for transfers between devices, x_swap(): return lax.ppermute(array, 'narrow', [(0, 1), (1, 0), (2, 3), (3, 2)])  37.8 us
    pallas_call x4, Pallas kernels, feed_row(): pl.pallas_call(feed_kernel, out_shape=(jax.ShapeDtypeStruct((2 * half_len...  35.8 us
    unnamed x205, local copies, waits for them, and re-layouts  35.3 us
    pallas_call x1, Pallas kernels, attend_rows(): pl.pallas_call(functools.partial(forward_kernel, taps_q, head_size, rows)...  32.8 us
    ppermute x23, starting transfers between devices, y_swap(): return lax.ppermute(array, 'narrow', [(0, 2), (2, 0), (1, 3), (3, 1)])  26.2 us
    ppermute x42, waiting for transfers between devices, seq_swap(): return lax.ppermute(array, 'seq', SWAP)  22.7 us
  transfers between devices with their start and end apart: 103, of which 47 were waited for; matrix products, arithmetic and copies ran while one was open for 10% of the time, Pallas kernels for 38%

profile of v5, /device:TPU:0, one launch (start us, length us, event | category | flops | bytes accessed | tf_op | source)
XLA Modules:
  0.0 481.3 jit_solution(9879257522374057113)
XLA Ops:
  10.0 3.1 collective-permute-start
  14.3 4.6 collective-permute-done.refs_1_
  35.3 3.3 tap_bands.1
  45.9 9.4 %collective-permute-done.5 = bf16[128,1664]{1,0:T(8,128)(2,1)S(1)} collective-permute-done((bf16[128,1664]{1,0:T(8,128)(2,1)S(1)}, bf16[128,1664]{1,0:T(8,128)(2,1)S(1)}, u32[]{:S(2)}, u32[]{:S(2)}) %collective-permute-start.5) | collective-permute-done | bytes 426016 | tf_op jit(solution)/shard_map/ppermute | solution.py:906
  59.5 3.3 all-gather.3.cloned.1.call-done.joined_ref
  64.5 1.8 collective-permute-start.12
  68.0 1.8 collective-permute-start.13
  70.8 32.8 %attend_rows.1 = (bf16[4,512,768]{2,1,0:T(8,128)(2,1)}, f32[4,512,256]{2,1,0:T(8,128)}, bf16[4,512,256]{2,1,0:T(8,128)(2,1)}, f32[4,2,512,512]{3,2,1,0:T(8,128)}, s32[4,512,128]{2,1,0:T(8,128)}) custom-call(s32[1]{0:T(128)} %bitcast.core_ref, f32[2,2]{1,0:T(2,128)S(1)} %copy.31.mix_ref, bf16[1536,640]{1,0:T(8,128)(2,1)} %all-gather.3.cloned.1.call-done.joined_ref, ...), custom_call_target="tpu_custom_call" | custom-call | flops 1000000 | bytes 1000000 | tf_op jit(solution)/shard_map/attend_rows/pallas_call | solution.py:348
  105.6 1.8 branch.1
  108.1 1.7 collective-permute-done.17.came_ref
  113.2 10.8 %collective-permute-done.20.extra_ref = bf16[128,1536]{1,0:T(8,128)(2,1)S(1)} collective-permute-done((bf16[128,1536]{1,0:T(8,128)(2,1)S(1)}, bf16[128,1536]{1,0:T(8,128)(2,1)S(1)}, u32[]{:S(2)}, u32[]{:S(2)}) %collective-permute-start.20) | collective-permute-done | bytes 393248 | tf_op jit(solution)/shard_map/ppermute | solution.py:906
  126.5 1.7 collective-permute-start.24
  128.2 1.8 slice.99
  130.8 15.3 %collective-permute-done.23 = bf16[256,1536]{1,0:T(8,128)(2,1)S(1)} collective-permute-done((bf16[256,1536]{1,0:T(8,128)(2,1)S(1)}, bf16[256,1536]{1,0:T(8,128)(2,1)S(1)}, u32[]{:S(2)}, u32[]{:S(2)}) %collective-permute-start.23) | collective-permute-done | bytes 786464 | tf_op jit(solution)/shard_map/ppermute | solution.py:902
  147.0 6.3 %all-gather.5.cloned.1.call-done.feed_ref = bf16[1536,1536]{1,0:T(8,128)(2,1)} async-done(((bf16[384,1536]{1,0:T(8,128)(2,1)}), bf16[1536,1536]{1,0:T(8,128)(2,1)}) %all-gather.5.cloned.1.call-update) | async-done | bytes 4718608 | tf_op jit(solution)/shard_map/all_gather | solution.py:964
  153.4 2.6 multiply_reduce_fusion.2
  156.3 1.6 collective-permute-start.28
  159.7 1.7 copy-done.2
  162.5 8.9 %feed_row.4 = (bf16[512,512]{1,0:T(8,128)(2,1)S(1)}, bf16[512,1024]{1,0:T(8,128)(2,1)}, bf16[256,1536]{1,0:T(8,128)(2,1)S(1)}, bf16[256,1536]{1,0:T(8,128)(2,1)}...) custom-call(bf16[256,1536]{1,0:T(8,128)(2,1)S(1)} %multiply_convert_fusion.own_ref.refs_0_, ...), custom_call_target="tpu_custom_call" | custom-call | bytes 28800000 | tf_op jit(solution)/shard_map/feed_row/pallas_call | solution.py:645
  172.2 4.1 collective-permute-done.28.own_ref.refs_2_
  178.0 1.8 collective-permute-done.31.other_ref.refs_5_
  183.1 8.9 %feed_row.5 = (bf16[512,512]{1,0:T(8,128)(2,1)S(1)}, bf16[512,1024]{1,0:T(8,128)(2,1)}, bf16[256,1536]{1,0:T(8,128)(2,1)S(1)}, bf16[256,1536]{1,0:T(8,128)(2,1)}...) custom-call(bf16[256,1536]{1,0:T(8,128)(2,1)S(1)} %collective-permute-done.28.own_ref.refs_2_, ...), custom_call_target="tpu_custom_call" | custom-call | bytes 28800000 | tf_op jit(solution)/shard_map/feed_row/pallas_call | solution.py:645
  195.0 9.0 %feed_row.6 = (bf16[512,512]{1,0:T(8,128)(2,1)S(1)}, bf16[512,1024]{1,0:T(8,128)(2,1)}, bf16[256,1536]{1,0:T(8,128)(2,1)S(1)}, bf16[256,1536]{1,0:T(8,128)(2,1)}...) custom-call(bf16[256,1536]{1,0:T(8,128)(2,1)S(1)} %collective-permute-done.29.own_ref.refs_4_, ...), custom_call_target="tpu_custom_call" | custom-call | bytes 28800000 | tf_op jit(solution)/shard_map/feed_row/pallas_call | solution.py:645
  210.8 9.0 %feed_row.7 = (bf16[512,512]{1,0:T(8,128)(2,1)S(1)}, bf16[512,1024]{1,0:T(8,128)(2,1)}, bf16[256,1536]{1,0:T(8,128)(2,1)S(1)}, bf16[256,1536]{1,0:T(8,128)(2,1)}...) custom-call(bf16[256,1536]{1,0:T(8,128)(2,1)S(1)} %constant_dynamic-update-slice_fusion.4.own_ref.refs_6_, ...), custom_call_target="tpu_custom_call" | custom-call | bytes 28800000 | tf_op jit(solution)/shard_map/feed_row/pallas_call | solution.py:645
  220.7 7.6 %collective-permute-done.41 = bf16[256,1536]{1,0:T(8,128)(2,1)S(1)} collective-permute-done((bf16[256,1536]{1,0:T(8,128)(2,1)S(1)}, bf16[256,1536]{1,0:T(8,128)(2,1)S(1)}, u32[]{:S(2)}, u32[]{:S(2)}) %collective-permute-start.41) | collective-permute-done | bytes 786464 | tf_op jit(solution)/shard_map/ppermute | solution.py:906
  230.1 1.8 collective-permute-done.43
  233.7 16.9 %feed_grad.1 = bf16[1536,1536]{1,0:T(8,128)(2,1)} custom-call(bf16[256,1536]{1,0:T(8,128)(2,1)} %copy-done.7, bf16[256,1536]{1,0:T(8,128)(2,1)} %copy-done.18, bf16[256,1536]{1,0:T(8,128)(2,1)} %copy-done.11, bf16[256,1536]{1,0:T(8,128)(2,1)} %copy-done.20, bf16[256,1536]{1,0:T(8,128)(2,1)} %copy-done.12, bf16[256,1536]{1,0:T(8,128)(2,1)} %copy-done.19, ...), custom_call_target="tpu_custom_call" | custom-call | bytes 61200000 | tf_op jit(solution)/shard_map/feed_grad/pallas_call | solution.py:695
  250.6 3.2 collective-permute-done.44
  255.0 4.2 multiply_reduce_fusion.1
  262.7 14.2 %attend_row_back.4 = (bf16[512,640]{1,0:T(8,128)(2,1)S(1)}, bf16[256,1536]{1,0:T(8,128)(2,1)S(1)}, bf16[256,1536]{1,0:T(8,128)(2,1)S(1)}, f32[8,128]{1,0:T(8,128)S(1)}, f32[2,66,128]{2,1,0:T(8,128)S(1)}) custom-call(s32[1]{0:T(128)} %bitcast.core_ref, f32[2,2]{1,0:T(2,128)S(1)} %copy.31.mix_ref, bf16[256,1536]{1,0:T(8,128)(2,1)S(1)} %fusion.11.own_ref.refs_1_, ...), custom_call_target="tpu_custom_call" | custom-call | bytes 50400000 | tf_op jit(solution)/shard_map/attend_row_back/pallas_call | solution.py:552
  276.9 3.5 collective-permute-done.50.own_ref.refs_3_
  280.9 1.7 collective-permute-done.53.other_ref.refs_6_
  283.8 1.7 collective-permute-start.56
  286.1 1.8 collective-permute-start.54
  287.8 14.1 %attend_row_back.5 = (bf16[512,640]{1,0:T(8,128)(2,1)S(1)}, bf16[256,1536]{1,0:T(8,128)(2,1)S(1)}, bf16[256,1536]{1,0:T(8,128)(2,1)S(1)}, f32[8,128]{1,0:T(8,128)S(1)}, f32[2,66,128]{2,1,0:T(8,128)S(1)}) custom-call(s32[1]{0:T(128)} %bitcast.core_ref, f32[2,2]{1,0:T(2,128)S(1)} %copy.31.mix_ref, ...), custom_call_target="tpu_custom_call" | custom-call | bytes 50400000 | tf_op jit(solution)/shard_map/attend_row_back/pallas_call | solution.py:552
  305.5 2.3 collective-permute-done.58.refs_8_.other_ref
  309.0 1.8 out_grad.1
  311.7 15.3 %attend_row_back.6 = (bf16[512,640]{1,0:T(8,128)(2,1)S(1)}, bf16[256,1536]{1,0:T(8,128)(2,1)S(1)}, bf16[256,1536]{1,0:T(8,128)(2,1)}, f32[8,128]{1,0:T(8,128)S(1)}, f32[2,66,128]{2,1,0:T(8,128)S(1)}) custom-call(s32[1]{0:T(128)} %bitcast.core_ref, f32[2,2]{1,0:T(2,128)S(1)} %copy.31.mix_ref, bf16[256,1536]{1,0:T(8,128)(2,1)S(1)} %collective-permute-done.51.own_ref.refs_5_, ...), custom_call_target="tpu_custom_call" | custom-call | bytes 50400000 | tf_op jit(solution)/shard_map/attend_row_back/pallas_call | solution.py:552
  337.3 1.7 collective-permute-start.66
  339.7 1.7 collective-permute-start.64
  342.5 14.0 %attend_row_back.7 = (bf16[512,640]{1,0:T(8,128)(2,1)S(1)}, bf16[256,1536]{1,0:T(8,128)(2,1)S(1)}, bf16[256,1536]{1,0:T(8,128)(2,1)S(1)}, f32[8,128]{1,0:T(8,128)S(1)}, f32[2,66,128]{2,1,0:T(8,128)S(1)}) custom-call(s32[1]{0:T(128)} %bitcast.core_ref, f32[2,2]{1,0:T(2,128)S(1)} %copy.31.mix_ref, ...), custom_call_target="tpu_custom_call" | custom-call | bytes 50400000 | tf_op jit(solution)/shard_map/attend_row_back/pallas_call | solution.py:552
  356.6 6.1 %collective-permute-done.64 = bf16[256,1536]{1,0:T(8,128)(2,1)S(1)} collective-permute-done((bf16[256,1536]{1,0:T(8,128)(2,1)S(1)}, bf16[256,1536]{1,0:T(8,128)(2,1)S(1)}, u32[]{:S(2)}, u32[]{:S(2)}) %collective-permute-start.64) | collective-permute-done | bytes 786464 | tf_op jit(solution)/shard_map/ppermute | solution.py:906
  363.3 1.8 collective-permute-done.69
  366.5 2.2 collective-permute-start.70
  368.7 1.9 dynamic-slice_bitcast_fusion
  370.9 2.0 collective-permute-start.71
  372.9 10.1 %joined_grad.1 = bf16[1536,640]{1,0:T(8,128)(2,1)} custom-call(bf16[256,1664]{1,0:T(8,128)(2,1)} %copy-done.6, bf16[256,1664]{1,0:T(8,128)(2,1)} %collective-permute-done.3.refs_1_, bf16[256,1664]{1,0:T(8,128)(2,1)} %collective-permute-done.1.refs_2_, bf16[256,1664]{1,0:T(8,128)(2,1)} %copy-done.68, bf16[256,1664]{1,0:T(8,128)(2,1)} %collective-permute-done.2.refs_4_, ...), custom_call_target="tpu_custom_call" | custom-call | bytes 28800000 | tf_op jit(solution)/shard_map/joined_grad/pallas_call | solution.py:734
  384.5 2.6 collective-permute-done.70
  387.3 1.8 collective-permute-start.79
  391.2 3.5 fusion.5
  396.2 4.4 collective-permute-done.75
  400.8 5.6 %collective-permute-done.76 = f32[48,128]{1,0:T(8,128)S(1)} collective-permute-done((f32[48,128]{1,0:T(8,128)S(1)}, f32[48,128]{1,0:T(8,128)S(1)}, u32[]{:S(2)}, u32[]{:S(2)}) %collective-permute-start.76) | collective-permute-done | bytes 24608 | tf_op jit(solution)/shard_map/ppermute | solution.py:1291
  407.9 8.9 %collective-permute-done.77 = f32[48,128]{1,0:T(8,128)S(1)} collective-permute-done((f32[48,128]{1,0:T(8,128)S(1)}, f32[48,128]{1,0:T(8,128)S(1)}, u32[]{:S(2)}, u32[]{:S(2)}) %collective-permute-start.77) | collective-permute-done | bytes 24608 | tf_op jit(solution)/shard_map/ppermute | solution.py:902
  420.9 1.7 collective-permute-start.81
  422.6 5.0 %fusion.7 = (f32[256,1536]{1,0:T(8,128)}, bf16[256,1536]{1,0:T(8,128)(2,1)}) fusion(bf16[256,1536]{1,0:T(8,128)(2,1)S(1)} %copy-done.63, f32[256,1536]{1,0:T(8,128)} %get-tuple-element.462, f32[256]{0:T(256)S(1)} %fusion.10, f32[1536]{0:T(1024)S(1)} %copy-done.90, f32[256]{0:T(256)S(1)} %add_rsqrt_fusion.1, bf16[256,1536]{1,0:T(8,128)(2,1)S(1)} %copy-done.5, ...), kind=kLoop, calls=%fused_computation.13 | loop fusion | flops 8257536 | bytes 11812864 | tf_op jit(solution)/shard_map/add | solution.py:1268
  428.8 4.9 %collective-permute-done.81 = f32[48,128]{1,0:T(8,128)S(1)} collective-permute-done((f32[48,128]{1,0:T(8,128)S(1)}, f32[48,128]{1,0:T(8,128)S(1)}, u32[]{:S(2)}, u32[]{:S(2)}) %collective-permute-start.81) | collective-permute-done | bytes 24608 | tf_op jit(solution)/shard_map/ppermute | solution.py:906
  438.2 10.3 %place_feed.1 = (f32[384,8192]{1,0:T(8,128)}, f32[1024,1536]{1,0:T(8,128)}) custom-call(s32[3]{0:T(128)} %copy-done.53, bf16[384,1536]{1,0:T(8,128)(2,1)} %reduce-scatter.3.cloned.1.call-done.refs_0_, bf16[384,1536]{1,0:T(8,128)(2,1)} %collective-permute-done.80.refs_1_, bf16[384,1536]{1,0:T(8,128)(2,1)} %collective-permute-done.78.refs_2_, ...), custom_call_target="tpu_custom_call" | custom-call | bytes 39600000 | tf_op jit(solution)/shard_map/place_feed/pallas_call | solution.py:154
  448.5 2.6 collective-permute-done.90
  453.0 1.6 collective-permute-start.92
  455.7 3.4 collective-permute-done.96
  460.1 2.5 collective-permute-done.92
  462.7 4.1 place_columns.1.base_ref
  470.3 1.9 add_columns.1
  472.3 2.1 place_quarters.1
  (468 shorter events, 120.3 us)
Async XLA Ops:
  7.2 55.6 %all-gather.3.cloned.1.call-start = ((), (), s32[]{:S(2)}) async-start(), calls=%async_computation.2 | async-start | bytes 2457600 | tf_op jit(solution)/shard_map/all_gather | solution.py:964
  9.9 143.5 %all-gather.5.cloned.1.call-start = ((), (), s32[]{:S(2)}) async-start(), calls=%async_computation.3 | async-start | bytes 5898240 | tf_op jit(solution)/shard_map/all_gather | solution.py:964
  18.9 21.9 %collective-permute-start.1 = (bf16[256,1664]{1,0:T(8,128)(2,1)S(1)}, bf16[256,1664]{1,0:T(8,128)(2,1)}, u32[]{:S(2)}, u32[]{:S(2)}) collective-permute-start(bf16[256,1664]{1,0:T(8,128)(2,1)S(1)} %pad_maximum_fusion.refs_0_), channel_id=1, source_target_pairs={{0,8},{8,0},{16,24},{24,16},{1,9},{9,1},{17,25},{25,17},{2,10},{10... | collective-permute-start | bytes 2555912 | tf_op jit(solution)/shard_map/ppermute | solution.py:902
  20.4 21.4 %collective-permute-start.2 = (bf16[256,1664]{1,0:T(8,128)(2,1)S(1)}, bf16[256,1664]{1,0:T(8,128)(2,1)}, u32[]{:S(2)}, u32[]{:S(2)}) collective-permute-start(bf16[256,1664]{1,0:T(8,128)(2,1)S(1)} %pad_maximum_fusion.refs_0_), channel_id=1, source_target_pairs={{0,16},{16,0},{8,24},{24,8},{1,17},{17,1},{9,25},{25,9},{2,18},{18... | collective-permute-start | bytes 2555912 | tf_op jit(solution)/shard_map/ppermute | solution.py:906
  21.9 21.0 %collective-permute-start.3 = (bf16[256,1664]{1,0:T(8,128)(2,1)S(1)}, bf16[256,1664]{1,0:T(8,128)(2,1)}, u32[]{:S(2)}, u32[]{:S(2)}) collective-permute-start(bf16[256,1664]{1,0:T(8,128)(2,1)S(1)} %pad_maximum_fusion.refs_0_), channel_id=1, source_target_pairs={{0,1},{1,0},{2,3},{3,2},{4,5},{5,4},{6,7},{7,6},{8,9},{9,8},{10,11... | collective-permute-start | bytes 2555912 | tf_op jit(solution)/shard_map/ppermute | solution.py:898
  21.9 21.0 %collective-permute-start.4 = (bf16[48,1536]{1,0:T(8,128)(2,1)S(1)}, bf16[48,1536]{1,0:T(8,128)(2,1)S(1)}, u32[]{:S(2)}, u32[]{:S(2)}) collective-permute-start(bf16[48,1536]{1,0:T(8,128)(2,1)S(1)} %collective-permute-done.refs_1_), channel_id=1, source_target_pairs={{0,2},{2,4},{4,6},{6,0},{1,3},{3,5},{5,7},{7,1},{8,10},{10,12},{12... | collective-permute-start | bytes 442376 | tf_op jit(solution)/shard_map/ppermute | solution.py:947
  42.9 12.3 %collective-permute-start.5 = (bf16[128,1664]{1,0:T(8,128)(2,1)S(1)}, bf16[128,1664]{1,0:T(8,128)(2,1)S(1)}, u32[]{:S(2)}, u32[]{:S(2)}) collective-permute-start(bf16[128,1664]{1,0:T(8,128)(2,1)S(1)} %slice.122), channel_id=1, source_target_pairs={{0,16},{16,0},{8,24},{24,8},{1,17},{17,1},{9,25},{25,9},{2,18},{18... | collective-permute-start | bytes 1277960 | tf_op jit(solution)/shard_map/ppermute | solution.py:906
  43.5 12.0 %collective-permute-start.6 = (bf16[128,1664]{1,0:T(8,128)(2,1)S(1)}, bf16[128,1664]{1,0:T(8,128)(2,1)S(1)}, u32[]{:S(2)}, u32[]{:S(2)}) collective-permute-start(bf16[128,1664]{1,0:T(8,128)(2,1)S(1)} %slice.123), channel_id=1, source_target_pairs={{0,8},{8,0},{16,24},{24,16},{1,9},{9,1},{17,25},{25,17},{2,10},{10... | collective-permute-start | bytes 1277960 | tf_op jit(solution)/shard_map/ppermute | solution.py:902
  44.2 11.4 %collective-permute-start.7 = (bf16[48,1536]{1,0:T(8,128)(2,1)S(1)}, bf16[48,1536]{1,0:T(8,128)(2,1)S(1)}, u32[]{:S(2)}, u32[]{:S(2)}) collective-permute-start(bf16[48,1536]{1,0:T(8,128)(2,1)S(1)} %collective-permute-done.4.refs_2_), channel_id=1, source_target_pairs={{0,2},{2,4},{4,6},{6,0},{1,3},{3,5},{5,7},{7,1},{8,10},{10,12},{12... | collective-permute-start | bytes 442376 | tf_op jit(solution)/shard_map/ppermute | solution.py:947
  45.4 11.7 %collective-permute-start.10 = (bf16[256,1664]{1,0:T(8,128)(2,1)}, bf16[256,1664]{1,0:T(8,128)(2,1)S(1)}, u32[]{:S(2)}, u32[]{:S(2)}) collective-permute-start(bf16[256,1664]{1,0:T(8,128)(2,1)} %collective-permute-done.2.refs_4_), channel_id=1, source_target_pairs={{0,1},{1,0},{2,3},{3,2},{4,5},{5,4},{6,7},{7,6},{8,9},{9,8},{10,11... | collective-permute-start | bytes 2555912 | tf_op jit(solution)/shard_map/ppermute | solution.py:898
  45.4 12.3 %collective-permute-start.9 = (bf16[256,1664]{1,0:T(8,128)(2,1)}, bf16[256,1664]{1,0:T(8,128)(2,1)S(1)}, u32[]{:S(2)}, u32[]{:S(2)}) collective-permute-start(bf16[256,1664]{1,0:T(8,128)(2,1)} %collective-permute-done.1.refs_2_), channel_id=1, source_target_pairs={{0,1},{1,0},{2,3},{3,2},{4,5},{5,4},{6,7},{7,6},{8,9},{9,8},{10,11... | collective-permute-start | bytes 2555912 | tf_op jit(solution)/shard_map/ppermute | solution.py:898
  62.9 324.4 %reduce-scatter.3.cloned.1.call-start = ((), (), s32[]{:S(2)}) async-start(), calls=%async_computation.4 | async-start | bytes 5898240 | tf_op jit(solution)/shard_map/reduce_scatter | solution.py:968
  62.9 40.6 %collective-permute-start.11 = (bf16[256,1536]{1,0:T(8,128)(2,1)S(1)}, bf16[256,1536]{1,0:T(8,128)(2,1)S(1)}, u32[]{:S(2)}, u32[]{:S(2)}) collective-permute-start(bf16[256,1536]{1,0:T(8,128)(2,1)S(1)} %copy-done.4), channel_id=1, source_target_pairs={{0,8},{8,0},{16,24},{24,16},{1,9},{9,1},{17,25},{25,17},{2,10},{10... | collective-permute-start | bytes 2359304 | tf_op jit(solution)/shard_map/ppermute | solution.py:902
  64.5 39.1 %collective-permute-start.12 = (bf16[256,1536]{1,0:T(8,128)(2,1)S(1)}, bf16[256,1536]{1,0:T(8,128)(2,1)}, u32[]{:S(2)}, u32[]{:S(2)}) collective-permute-start(bf16[256,1536]{1,0:T(8,128)(2,1)S(1)} %copy-done.4), channel_id=1, source_target_pairs={{0,16},{16,0},{8,24},{24,8},{1,17},{17,1},{9,25},{25,9},{2,18},{18... | collective-permute-start | bytes 2359304 | tf_op jit(solution)/shard_map/ppermute | solution.py:906
  66.3 37.3 %collective-permute-start.15 = (bf16[48,1536]{1,0:T(8,128)(2,1)}, bf16[48,1536]{1,0:T(8,128)(2,1)S(1)}, u32[]{:S(2)}, u32[]{:S(2)}) collective-permute-start(bf16[48,1536]{1,0:T(8,128)(2,1)} %copy-done.59), channel_id=1, source_target_pairs={{0,24},{8,16},{16,8},{24,0},{1,25},{9,17},{17,9},{25,1},{2,26},{10... | collective-permute-start | bytes 442376 | tf_op jit(solution)/shard_map/ppermute | solution.py:910
  66.5 37.1 %collective-permute-start.14 = (bf16[48,1536]{1,0:T(8,128)(2,1)}, bf16[48,1536]{1,0:T(8,128)(2,1)}, u32[]{:S(2)}, u32[]{:S(2)}) collective-permute-start(bf16[48,1536]{1,0:T(8,128)(2,1)} %copy-done.58), channel_id=1, source_target_pairs={{0,16},{16,0},{8,24},{24,8},{1,17},{17,1},{9,25},{25,9},{2,18},{18... | collective-permute-start | bytes 442376 | tf_op jit(solution)/shard_map/ppermute | solution.py:906
  68.0 35.6 %collective-permute-start.13 = (bf16[48,1536]{1,0:T(8,128)(2,1)}, bf16[48,1536]{1,0:T(8,128)(2,1)}, u32[]{:S(2)}, u32[]{:S(2)}) collective-permute-start(bf16[48,1536]{1,0:T(8,128)(2,1)} %copy-done.57), channel_id=1, source_target_pairs={{0,8},{8,0},{16,24},{24,16},{1,9},{9,1},{17,25},{25,17},{2,10},{10... | collective-permute-start | bytes 442376 | tf_op jit(solution)/shard_map/ppermute | solution.py:902
  112.2 11.7 %collective-permute-start.22 = (bf16[256,1536]{1,0:T(8,128)(2,1)S(1)}, bf16[256,1536]{1,0:T(8,128)(2,1)S(1)}, u32[]{:S(2)}, u32[]{:S(2)}) collective-permute-start(bf16[256,1536]{1,0:T(8,128)(2,1)S(1)} %copy-done.4), channel_id=1, source_target_pairs={{0,1},{1,0},{2,3},{3,2},{4,5},{5,4},{6,7},{7,6},{8,9},{9,8},{10,11... | collective-permute-start | bytes 2359304 | tf_op jit(solution)/shard_map/ppermute | solution.py:898
  112.4 12.4 %collective-permute-start.19 = (bf16[256,1536]{1,0:T(8,128)(2,1)S(1)}, bf16[256,1536]{1,0:T(8,128)(2,1)}, u32[]{:S(2)}, u32[]{:S(2)}) collective-permute-start(bf16[256,1536]{1,0:T(8,128)(2,1)S(1)} %get-tuple-element.269), channel_id=1, source_target_pairs={{0,1},{1,0},{2,3},{3,2},{4,5},{5,4},{6,7},{7,6},{8,9},{9,8},{10,11... | collective-permute-start | bytes 2359304 | tf_op jit(solution)/shard_map/ppermute | solution.py:898
  112.8 11.2 %collective-permute-start.20 = (bf16[128,1536]{1,0:T(8,128)(2,1)S(1)}, bf16[128,1536]{1,0:T(8,128)(2,1)S(1)}, u32[]{:S(2)}, u32[]{:S(2)}) collective-permute-start(bf16[128,1536]{1,0:T(8,128)(2,1)S(1)} %get-tuple-element.270), channel_id=1, source_target_pairs={{0,16},{16,0},{8,24},{24,8},{1,17},{17,1},{9,25},{25,9},{2,18},{18... | collective-permute-start | bytes 1179656 | tf_op jit(solution)/shard_map/ppermute | solution.py:906
  126.2 20.0 %collective-permute-start.23 = (bf16[256,1536]{1,0:T(8,128)(2,1)S(1)}, bf16[256,1536]{1,0:T(8,128)(2,1)S(1)}, u32[]{:S(2)}, u32[]{:S(2)}) collective-permute-start(bf16[256,1536]{1,0:T(8,128)(2,1)S(1)} %low_sum.4), channel_id=1, source_target_pairs={{0,8},{8,0},{16,24},{24,16},{1,9},{9,1},{17,25},{25,17},{2,10},{10... | collective-permute-start | bytes 2359304 | tf_op jit(solution)/shard_map/ppermute | solution.py:902
  126.5 20.6 %collective-permute-start.24 = (bf16[256,1536]{1,0:T(8,128)(2,1)S(1)}, bf16[256,1536]{1,0:T(8,128)(2,1)}, u32[]{:S(2)}, u32[]{:S(2)}) collective-permute-start(bf16[256,1536]{1,0:T(8,128)(2,1)S(1)} %low_sum.5), channel_id=1, source_target_pairs={{0,16},{16,0},{8,24},{24,8},{1,17},{17,1},{9,25},{25,9},{2,18},{18... | collective-permute-start | bytes 2359304 | tf_op jit(solution)/shard_map/ppermute | solution.py:906
  156.3 20.0 %collective-permute-start.28 = (bf16[256,1536]{1,0:T(8,128)(2,1)S(1)}, bf16[256,1536]{1,0:T(8,128)(2,1)S(1)}, u32[]{:S(2)}, u32[]{:S(2)}) collective-permute-start(bf16[256,1536]{1,0:T(8,128)(2,1)S(1)} %multiply_convert_fusion.own_ref.refs_0_), channel_id=1, source_target_pairs={{0,8},{8,0},{16,24},{24,16},{1,9},{9,1},{17,25},{25,17},{2,10},{10... | collective-permute-start | bytes 2359304 | tf_op jit(solution)/shard_map/ppermute | solution.py:902
  157.9 19.6 %collective-permute-start.29 = (bf16[256,1536]{1,0:T(8,128)(2,1)S(1)}, bf16[256,1536]{1,0:T(8,128)(2,1)S(1)}, u32[]{:S(2)}, u32[]{:S(2)}) collective-permute-start(bf16[256,1536]{1,0:T(8,128)(2,1)S(1)} %multiply_convert_fusion.own_ref.refs_0_), channel_id=1, source_target_pairs={{0,16},{16,0},{8,24},{24,8},{1,17},{17,1},{9,25},{25,9},{2,18},{18... | collective-permute-start | bytes 2359304 | tf_op jit(solution)/shard_map/ppermute | solution.py:906
  180.9 11.2 %collective-permute-start.32 = (bf16[128,1536]{1,0:T(8,128)(2,1)S(1)}, bf16[128,1536]{1,0:T(8,128)(2,1)S(1)}, u32[]{:S(2)}, u32[]{:S(2)}) collective-permute-start(bf16[128,1536]{1,0:T(8,128)(2,1)S(1)} %copy-done.88), channel_id=1, source_target_pairs={{0,16},{16,0},{8,24},{24,8},{1,17},{17,1},{9,25},{25,9},{2,18},{18... | collective-permute-start | bytes 1179656 | tf_op jit(solution)/shard_map/ppermute | solution.py:906
  193.3 12.0 %collective-permute-start.38 = (bf16[256,1536]{1,0:T(8,128)(2,1)S(1)}, bf16[256,1536]{1,0:T(8,128)(2,1)S(1)}, u32[]{:S(2)}, u32[]{:S(2)}) collective-permute-start(bf16[256,1536]{1,0:T(8,128)(2,1)S(1)} %constant_dynamic-update-slice_fusion.2.cot_own_ref.refs_22_), channel_id=1, source_target_pairs={{0,1},{1,0},{2,3},{3,2},{4,5},{5,4},{6,7},{7,6},{8,9},{9,8},{10,11... | collective-permute-start | bytes 2359304 | tf_op jit(solution)/shard_map/ppermute | solution.py:898
  193.4 11.9 %collective-permute-start.37 = (bf16[256,1536]{1,0:T(8,128)(2,1)S(1)}, bf16[256,1536]{1,0:T(8,128)(2,1)S(1)}, u32[]{:S(2)}, u32[]{:S(2)}) collective-permute-start(bf16[256,1536]{1,0:T(8,128)(2,1)S(1)} %get-tuple-element.299), channel_id=1, source_target_pairs={{0,1},{1,0},{2,3},{3,2},{4,5},{5,4},{6,7},{7,6},{8,9},{9,8},{10,11... | collective-permute-start | bytes 2359304 | tf_op jit(solution)/shard_map/ppermute | solution.py:898
  193.9 11.1 %collective-permute-start.34 = (bf16[128,1536]{1,0:T(8,128)(2,1)S(1)}, bf16[128,1536]{1,0:T(8,128)(2,1)S(1)}, u32[]{:S(2)}, u32[]{:S(2)}) collective-permute-start(bf16[128,1536]{1,0:T(8,128)(2,1)S(1)} %slice.100), channel_id=1, source_target_pairs={{0,16},{16,0},{8,24},{24,8},{1,17},{17,1},{9,25},{25,9},{2,18},{18... | collective-permute-start | bytes 1179656 | tf_op jit(solution)/shard_map/ppermute | solution.py:906
  208.8 19.6 %collective-permute-start.41 = (bf16[256,1536]{1,0:T(8,128)(2,1)S(1)}, bf16[256,1536]{1,0:T(8,128)(2,1)S(1)}, u32[]{:S(2)}, u32[]{:S(2)}) collective-permute-start(bf16[256,1536]{1,0:T(8,128)(2,1)S(1)} %pair_sum.7), channel_id=1, source_target_pairs={{0,16},{16,0},{8,24},{24,8},{1,17},{17,1},{9,25},{25,9},{2,18},{18... | collective-permute-start | bytes 2359304 | tf_op jit(solution)/shard_map/ppermute | solution.py:906
  210.2 19.3 %collective-permute-start.40 = (bf16[256,1536]{1,0:T(8,128)(2,1)S(1)}, bf16[256,1536]{1,0:T(8,128)(2,1)S(1)}, u32[]{:S(2)}, u32[]{:S(2)}) collective-permute-start(bf16[256,1536]{1,0:T(8,128)(2,1)S(1)} %pair_sum.6), channel_id=1, source_target_pairs={{0,8},{8,0},{16,24},{24,16},{1,9},{9,1},{17,25},{25,17},{2,10},{10... | collective-permute-start | bytes 2359304 | tf_op jit(solution)/shard_map/ppermute | solution.py:902
  233.1 20.7 %collective-permute-start.44 = (bf16[256,1536]{1,0:T(8,128)(2,1)S(1)}, bf16[256,1536]{1,0:T(8,128)(2,1)}, u32[]{:S(2)}, u32[]{:S(2)}) collective-permute-start(bf16[256,1536]{1,0:T(8,128)(2,1)S(1)} %pair_sum.8), channel_id=1, source_target_pairs={{0,24},{8,16},{16,8},{24,0},{1,25},{9,17},{17,9},{25,1},{2,26},{10... | collective-permute-start | bytes 2359304 | tf_op jit(solution)/shard_map/ppermute | solution.py:910
  253.8 180.1 %reduce-scatter.5.cloned.1.call-start = ((), (), s32[]{:S(2)}) async-start(), calls=%async_computation.5 | async-start | bytes 2457600 | tf_op jit(solution)/shard_map/reduce_scatter | solution.py:968
  260.4 20.0 %collective-permute-start.50 = (bf16[256,1536]{1,0:T(8,128)(2,1)S(1)}, bf16[256,1536]{1,0:T(8,128)(2,1)S(1)}, u32[]{:S(2)}, u32[]{:S(2)}) collective-permute-start(bf16[256,1536]{1,0:T(8,128)(2,1)S(1)} %fusion.11.own_ref.refs_1_), channel_id=1, source_target_pairs={{0,8},{8,0},{16,24},{24,16},{1,9},{9,1},{17,25},{25,17},{2,10},{10... | collective-permute-start | bytes 2359304 | tf_op jit(solution)/shard_map/ppermute | solution.py:902
  260.5 19.8 %collective-permute-start.51 = (bf16[256,1536]{1,0:T(8,128)(2,1)S(1)}, bf16[256,1536]{1,0:T(8,128)(2,1)S(1)}, u32[]{:S(2)}, u32[]{:S(2)}) collective-permute-start(bf16[256,1536]{1,0:T(8,128)(2,1)S(1)} %fusion.11.own_ref.refs_1_), channel_id=1, source_target_pairs={{0,16},{16,0},{8,24},{24,8},{1,17},{17,1},{9,25},{25,9},{2,18},{18... | collective-permute-start | bytes 2359304 | tf_op jit(solution)/shard_map/ppermute | solution.py:906
  283.8 19.1 %collective-permute-start.56 = (bf16[128,1536]{1,0:T(8,128)(2,1)S(1)}, bf16[128,1536]{1,0:T(8,128)(2,1)S(1)}, u32[]{:S(2)}, u32[]{:S(2)}) collective-permute-start(bf16[128,1536]{1,0:T(8,128)(2,1)S(1)} %slice.125), channel_id=1, source_target_pairs={{0,8},{8,0},{16,24},{24,16},{1,9},{9,1},{17,25},{25,17},{2,10},{10... | collective-permute-start | bytes 1179656 | tf_op jit(solution)/shard_map/ppermute | solution.py:902
  285.5 17.4 %collective-permute-start.55 = (bf16[128,1536]{1,0:T(8,128)(2,1)S(1)}, bf16[128,1536]{1,0:T(8,128)(2,1)S(1)}, u32[]{:S(2)}, u32[]{:S(2)}) collective-permute-start(bf16[128,1536]{1,0:T(8,128)(2,1)S(1)} %slice.124), channel_id=1, source_target_pairs={{0,16},{16,0},{8,24},{24,8},{1,17},{17,1},{9,25},{25,9},{2,18},{18... | collective-permute-start | bytes 1179656 | tf_op jit(solution)/shard_map/ppermute | solution.py:906
  285.8 17.6 %collective-permute-start.57 = (bf16[128,1536]{1,0:T(8,128)(2,1)S(1)}, bf16[128,1536]{1,0:T(8,128)(2,1)S(1)}, u32[]{:S(2)}, u32[]{:S(2)}) collective-permute-start(bf16[128,1536]{1,0:T(8,128)(2,1)S(1)} %get-tuple-element.362), channel_id=1, source_target_pairs={{0,8},{8,0},{16,24},{24,16},{1,9},{9,1},{17,25},{25,17},{2,10},{10... | collective-permute-start | bytes 1179656 | tf_op jit(solution)/shard_map/ppermute | solution.py:902
  286.1 18.7 %collective-permute-start.54 = (bf16[128,1536]{1,0:T(8,128)(2,1)S(1)}, bf16[128,1536]{1,0:T(8,128)(2,1)S(1)}, u32[]{:S(2)}, u32[]{:S(2)}) collective-permute-start(bf16[128,1536]{1,0:T(8,128)(2,1)S(1)} %get-tuple-element.358), channel_id=1, source_target_pairs={{0,16},{16,0},{8,24},{24,8},{1,17},{17,1},{9,25},{25,9},{2,18},{18... | collective-permute-start | bytes 1179656 | tf_op jit(solution)/shard_map/ppermute | solution.py:906
  307.7 21.0 %collective-permute-start.61 = (bf16[256,1536]{1,0:T(8,128)(2,1)S(1)}, bf16[256,1536]{1,0:T(8,128)(2,1)S(1)}, u32[]{:S(2)}, u32[]{:S(2)}) collective-permute-start(bf16[256,1536]{1,0:T(8,128)(2,1)S(1)} %low_sum.7), channel_id=1, source_target_pairs={{0,16},{16,0},{8,24},{24,8},{1,17},{17,1},{9,25},{25,9},{2,18},{18... | collective-permute-start | bytes 2359304 | tf_op jit(solution)/shard_map/ppermute | solution.py:906
  308.0 20.7 %collective-permute-start.60 = (bf16[256,1536]{1,0:T(8,128)(2,1)S(1)}, bf16[256,1536]{1,0:T(8,128)(2,1)S(1)}, u32[]{:S(2)}, u32[]{:S(2)}) collective-permute-start(bf16[256,1536]{1,0:T(8,128)(2,1)S(1)} %low_sum.6), channel_id=1, source_target_pairs={{0,8},{8,0},{16,24},{24,16},{1,9},{9,1},{17,25},{25,17},{2,10},{10... | collective-permute-start | bytes 2359304 | tf_op jit(solution)/shard_map/ppermute | solution.py:902
  309.0 19.8 %collective-permute-start.59 = (bf16[256,1536]{1,0:T(8,128)(2,1)S(1)}, bf16[256,1536]{1,0:T(8,128)(2,1)S(1)}, u32[]{:S(2)}, u32[]{:S(2)}) collective-permute-start(bf16[256,1536]{1,0:T(8,128)(2,1)S(1)} %get-tuple-element.371), channel_id=1, source_target_pairs={{0,1},{1,0},{2,3},{3,2},{4,5},{5,4},{6,7},{7,6},{8,9},{9,8},{10,11... | collective-permute-start | bytes 2359304 | tf_op jit(solution)/shard_map/ppermute | solution.py:898
  336.1 20.4 %collective-permute-start.65 = (bf16[48,1536]{1,0:T(8,128)(2,1)S(1)}, bf16[48,1536]{1,0:T(8,128)(2,1)S(1)}, u32[]{:S(2)}, u32[]{:S(2)}) collective-permute-start(bf16[48,1536]{1,0:T(8,128)(2,1)S(1)} %get-tuple-element.481), channel_id=1, source_target_pairs={{0,8},{8,0},{16,24},{24,16},{1,9},{9,1},{17,25},{25,17},{2,10},{10... | collective-permute-start | bytes 442376 | tf_op jit(solution)/shard_map/ppermute | solution.py:902
  337.3 19.3 %collective-permute-start.66 = (bf16[48,1536]{1,0:T(8,128)(2,1)S(1)}, bf16[48,1536]{1,0:T(8,128)(2,1)S(1)}, u32[]{:S(2)}, u32[]{:S(2)}) collective-permute-start(bf16[48,1536]{1,0:T(8,128)(2,1)S(1)} %get-tuple-element.480), channel_id=1, source_target_pairs={{0,16},{16,0},{8,24},{24,8},{1,17},{17,1},{9,25},{25,9},{2,18},{18... | collective-permute-start | bytes 442376 | tf_op jit(solution)/shard_map/ppermute | solution.py:906
  339.0 17.6 %collective-permute-start.67 = (bf16[48,1536]{1,0:T(8,128)(2,1)S(1)}, bf16[48,1536]{1,0:T(8,128)(2,1)S(1)}, u32[]{:S(2)}, u32[]{:S(2)}) collective-permute-start(bf16[48,1536]{1,0:T(8,128)(2,1)S(1)} %get-tuple-element.479), channel_id=1, source_target_pairs={{0,24},{8,16},{16,8},{24,0},{1,25},{9,17},{17,9},{25,1},{2,26},{10... | collective-permute-start | bytes 442376 | tf_op jit(solution)/shard_map/ppermute | solution.py:910
  339.7 23.1 %collective-permute-start.64 = (bf16[256,1536]{1,0:T(8,128)(2,1)S(1)}, bf16[256,1536]{1,0:T(8,128)(2,1)S(1)}, u32[]{:S(2)}, u32[]{:S(2)}) collective-permute-start(bf16[256,1536]{1,0:T(8,128)(2,1)S(1)} %pair_sum.10), channel_id=1, source_target_pairs={{0,16},{16,0},{8,24},{24,8},{1,17},{17,1},{9,25},{25,9},{2,18},{18... | collective-permute-start | bytes 2359304 | tf_op jit(solution)/shard_map/ppermute | solution.py:906
  341.4 21.4 %collective-permute-start.63 = (bf16[256,1536]{1,0:T(8,128)(2,1)S(1)}, bf16[256,1536]{1,0:T(8,128)(2,1)S(1)}, u32[]{:S(2)}, u32[]{:S(2)}) collective-permute-start(bf16[256,1536]{1,0:T(8,128)(2,1)S(1)} %pair_sum.9), channel_id=1, source_target_pairs={{0,8},{8,0},{16,24},{24,16},{1,9},{9,1},{17,25},{25,17},{2,10},{10... | collective-permute-start | bytes 2359304 | tf_op jit(solution)/shard_map/ppermute | solution.py:902
  366.5 20.7 %collective-permute-start.70 = (bf16[256,1536]{1,0:T(8,128)(2,1)S(1)}, bf16[256,1536]{1,0:T(8,128)(2,1)}, u32[]{:S(2)}, u32[]{:S(2)}) collective-permute-start(bf16[256,1536]{1,0:T(8,128)(2,1)S(1)} %pair_sum.11), channel_id=1, source_target_pairs={{0,24},{8,16},{16,8},{24,0},{1,25},{9,17},{17,9},{25,1},{2,26},{10... | collective-permute-start | bytes 2359304 | tf_op jit(solution)/shard_map/ppermute | solution.py:910
  370.5 12.5 %collective-permute-start.73 = (bf16[48,1536]{1,0:T(8,128)(2,1)}, bf16[48,1536]{1,0:T(8,128)(2,1)}, u32[]{:S(2)}, u32[]{:S(2)}) collective-permute-start(bf16[48,1536]{1,0:T(8,128)(2,1)} %get-tuple-element.412), channel_id=1, source_target_pairs={{0,6},{2,0},{4,2},{6,4},{1,7},{3,1},{5,3},{7,5},{8,14},{10,8},{12,... | collective-permute-start | bytes 442376 | tf_op jit(solution)/shard_map/ppermute | solution.py:947
  370.7 13.9 %collective-permute-start.72 = (bf16[48,1536]{1,0:T(8,128)(2,1)}, bf16[48,1536]{1,0:T(8,128)(2,1)}, u32[]{:S(2)}, u32[]{:S(2)}) collective-permute-start(bf16[48,1536]{1,0:T(8,128)(2,1)} %get-tuple-element.411), channel_id=1, source_target_pairs={{0,4},{2,6},{4,0},{6,2},{1,5},{3,7},{5,1},{7,3},{8,12},{10,14},{12... | collective-permute-start | bytes 442376 | tf_op jit(solution)/shard_map/ppermute | solution.py:947
  370.9 13.6 %collective-permute-start.71 = (bf16[48,1536]{1,0:T(8,128)(2,1)}, bf16[48,1536]{1,0:T(8,128)(2,1)}, u32[]{:S(2)}, u32[]{:S(2)}) collective-permute-start(bf16[48,1536]{1,0:T(8,128)(2,1)} %get-tuple-element.410), channel_id=1, source_target_pairs={{0,2},{2,4},{4,6},{6,0},{1,3},{3,5},{5,7},{7,1},{8,10},{10,12},{12... | collective-permute-start | bytes 442376 | tf_op jit(solution)/shard_map/ppermute | solution.py:947
  387.3 29.5 %collective-permute-start.79 = (bf16[384,1536]{1,0:T(8,128)(2,1)}, bf16[384,1536]{1,0:T(8,128)(2,1)}, u32[]{:S(2)}, u32[]{:S(2)}) collective-permute-start(bf16[384,1536]{1,0:T(8,128)(2,1)} %reduce-scatter.3.cloned.1.call-done.refs_0_), channel_id=1, source_target_pairs={{0,16},{16,0},{8,24},{24,8},{1,17},{17,1},{9,25},{25,9},{2,18},{18... | collective-permute-start | bytes 3538952 | tf_op jit(solution)/shard_map/ppermute | solution.py:906
  389.1 28.8 %collective-permute-start.78 = (bf16[384,1536]{1,0:T(8,128)(2,1)}, bf16[384,1536]{1,0:T(8,128)(2,1)}, u32[]{:S(2)}, u32[]{:S(2)}) collective-permute-start(bf16[384,1536]{1,0:T(8,128)(2,1)} %reduce-scatter.3.cloned.1.call-done.refs_0_), channel_id=1, source_target_pairs={{0,8},{8,0},{16,24},{24,16},{1,9},{9,1},{17,25},{25,17},{2,10},{10... | collective-permute-start | bytes 3538952 | tf_op jit(solution)/shard_map/ppermute | solution.py:902
  390.1 27.9 %collective-permute-start.80 = (bf16[384,1536]{1,0:T(8,128)(2,1)}, bf16[384,1536]{1,0:T(8,128)(2,1)}, u32[]{:S(2)}, u32[]{:S(2)}) collective-permute-start(bf16[384,1536]{1,0:T(8,128)(2,1)} %reduce-scatter.3.cloned.1.call-done.refs_0_), channel_id=1, source_target_pairs={{0,1},{1,0},{2,3},{3,2},{4,5},{5,4},{6,7},{7,6},{8,9},{9,8},{10,11... | collective-permute-start | bytes 3538952 | tf_op jit(solution)/shard_map/ppermute | solution.py:898
  417.9 15.9 %collective-permute-start.83 = (bf16[192,1536]{1,0:T(8,128)(2,1)S(1)}, bf16[192,1536]{1,0:T(8,128)(2,1)S(1)}, u32[]{:S(2)}, u32[]{:S(2)}) collective-permute-start(bf16[192,1536]{1,0:T(8,128)(2,1)S(1)} %slice.129), channel_id=1, source_target_pairs={{0,8},{8,0},{16,24},{24,16},{1,9},{9,1},{17,25},{25,17},{2,10},{10... | collective-permute-start | bytes 1769480 | tf_op jit(solution)/shard_map/ppermute | solution.py:902
  420.0 13.8 %collective-permute-start.82 = (bf16[192,1536]{1,0:T(8,128)(2,1)S(1)}, bf16[192,1536]{1,0:T(8,128)(2,1)S(1)}, u32[]{:S(2)}, u32[]{:S(2)}) collective-permute-start(bf16[192,1536]{1,0:T(8,128)(2,1)S(1)} %slice.128), channel_id=1, source_target_pairs={{0,16},{16,0},{8,24},{24,8},{1,17},{17,1},{9,25},{25,9},{2,18},{18... | collective-permute-start | bytes 1769480 | tf_op jit(solution)/shard_map/ppermute | solution.py:906
  420.4 13.5 %collective-permute-start.85 = (bf16[384,1536]{1,0:T(8,128)(2,1)}, bf16[384,1536]{1,0:T(8,128)(2,1)}, u32[]{:S(2)}, u32[]{:S(2)}) collective-permute-start(bf16[384,1536]{1,0:T(8,128)(2,1)} %collective-permute-done.79.refs_4_), channel_id=1, source_target_pairs={{0,1},{1,0},{2,3},{3,2},{4,5},{5,4},{6,7},{7,6},{8,9},{9,8},{10,11... | collective-permute-start | bytes 3538952 | tf_op jit(solution)/shard_map/ppermute | solution.py:898
  420.4 13.5 %collective-permute-start.84 = (bf16[384,1536]{1,0:T(8,128)(2,1)}, bf16[384,1536]{1,0:T(8,128)(2,1)}, u32[]{:S(2)}, u32[]{:S(2)}) collective-permute-start(bf16[384,1536]{1,0:T(8,128)(2,1)} %collective-permute-done.78.refs_2_), channel_id=1, source_target_pairs={{0,1},{1,0},{2,3},{3,2},{4,5},{5,4},{6,7},{7,6},{8,9},{9,8},{10,11... | collective-permute-start | bytes 3538952 | tf_op jit(solution)/shard_map/ppermute | solution.py:898
  420.9 12.8 %collective-permute-start.81 = (f32[48,128]{1,0:T(8,128)S(1)}, f32[48,128]{1,0:T(8,128)S(1)}, u32[]{:S(2)}, u32[]{:S(2)}) collective-permute-start(f32[48,128]{1,0:T(8,128)S(1)} %add.320), channel_id=1, source_target_pairs={{0,16},{16,0},{8,24},{24,8},{1,17},{17,1},{9,25},{25,9},{2,18},{18... | collective-permute-start | bytes 73736 | tf_op jit(solution)/shard_map/ppermute | solution.py:906
  434.0 17.9 %collective-permute-start.86 = (bf16[384,640]{1,0:T(8,128)(2,1)}, bf16[384,640]{1,0:T(8,128)(2,1)S(1)}, u32[]{:S(2)}, u32[]{:S(2)}) collective-permute-start(bf16[384,640]{1,0:T(8,128)(2,1)} %reduce-scatter.5.cloned.1.call-done.refs_0_), channel_id=1, source_target_pairs={{0,8},{8,0},{16,24},{24,16},{1,9},{9,1},{17,25},{25,17},{2,10},{10... | collective-permute-start | bytes 1474568 | tf_op jit(solution)/shard_map/ppermute | solution.py:902
  435.2 16.8 %collective-permute-start.87 = (bf16[384,640]{1,0:T(8,128)(2,1)}, bf16[384,640]{1,0:T(8,128)(2,1)S(1)}, u32[]{:S(2)}, u32[]{:S(2)}) collective-permute-start(bf16[384,640]{1,0:T(8,128)(2,1)} %reduce-scatter.5.cloned.1.call-done.refs_0_), channel_id=1, source_target_pairs={{0,16},{16,0},{8,24},{24,8},{1,17},{17,1},{9,25},{25,9},{2,18},{18... | collective-permute-start | bytes 1474568 | tf_op jit(solution)/shard_map/ppermute | solution.py:906
  435.6 16.3 %collective-permute-start.88 = (bf16[384,640]{1,0:T(8,128)(2,1)}, bf16[384,640]{1,0:T(8,128)(2,1)S(1)}, u32[]{:S(2)}, u32[]{:S(2)}) collective-permute-start(bf16[384,640]{1,0:T(8,128)(2,1)} %reduce-scatter.5.cloned.1.call-done.refs_0_), channel_id=1, source_target_pairs={{0,1},{1,0},{2,3},{3,2},{4,5},{5,4},{6,7},{7,6},{8,9},{9,8},{10,11... | collective-permute-start | bytes 1474568 | tf_op jit(solution)/shard_map/ppermute | solution.py:898
  435.6 15.5 %collective-permute-start.90 = (bf16[48,1536]{1,0:T(8,128)(2,1)S(1)}, bf16[48,1536]{1,0:T(8,128)(2,1)}, u32[]{:S(2)}, u32[]{:S(2)}) collective-permute-start(bf16[48,1536]{1,0:T(8,128)(2,1)S(1)} %fusion.8), channel_id=1, source_target_pairs={{0,8},{8,0},{16,24},{24,16},{1,9},{9,1},{17,25},{25,17},{2,10},{10... | collective-permute-start | bytes 442376 | tf_op jit(solution)/shard_map/ppermute | solution.py:902
  436.9 15.1 %collective-permute-start.91 = (bf16[48,1536]{1,0:T(8,128)(2,1)S(1)}, bf16[48,1536]{1,0:T(8,128)(2,1)}, u32[]{:S(2)}, u32[]{:S(2)}) collective-permute-start(bf16[48,1536]{1,0:T(8,128)(2,1)S(1)} %fusion.8), channel_id=1, source_target_pairs={{0,16},{16,0},{8,24},{24,8},{1,17},{17,1},{9,25},{25,9},{2,18},{18... | collective-permute-start | bytes 442376 | tf_op jit(solution)/shard_map/ppermute | solution.py:906
  454.7 12.1 %collective-permute-start.93 = (bf16[192,640]{1,0:T(8,128)(2,1)S(1)}, bf16[192,640]{1,0:T(8,128)(2,1)S(1)}, u32[]{:S(2)}, u32[]{:S(2)}) collective-permute-start(bf16[192,640]{1,0:T(8,128)(2,1)S(1)} %slice.131), channel_id=1, source_target_pairs={{0,8},{8,0},{16,24},{24,16},{1,9},{9,1},{17,25},{25,17},{2,10},{10... | collective-permute-start | bytes 737288 | tf_op jit(solution)/shard_map/ppermute | solution.py:902
  (133 other events, 977.5 us)
Sparse Core Ops, SparseCore 0:
  10.2 52.6 all-gather.2
  65.0 88.3 all-gather.4
  253.9 81.8 reduce-scatter.2
  387.3 40.4 reduce-scatter.4

commit v6 on v5

--- a/solution.py
+++ b/solution.py
@@ -1140,10 +1140,10 @@
     branch_x, branch_y = x_swap(hold(low_x)), y_swap(hold(low_y))
     cot_halves = half_rows(hold(cot_x), False), half_rows(hold(cot_y), True)
     flow.end(branch_x, branch_y, cot_xo, cot_yo, feed_own, *cot_halves)
-    residual = inputs_f + whole_sum(branch_mine[0], hold(came_0), branch_x, branch_y)
+    residual = inputs_f + whole_sum(branch_mine[0], came_0, branch_x, branch_y)
     scale_mid = norm_scale(residual)
     normed_ffn = (residual * scale_mid * feed_gain).astype(jnp.bfloat16)
-    flow.end(normed_ffn)
+    flow.end(normed_ffn, *flow.ended)
 
     ffn_x, ffn_y, ffn_o = x_swap(hold(normed_ffn)), y_swap(hold(normed_ffn)), seq_swap(hold(normed_ffn))
     flow.end(ffn_o)

time: 490 us -> 487 us (level)
    unnamed x205 -> x201, local copies, waits for them, and re-layouts: 35.3 us -> 36.6 us
  transfers between devices with their start and end apart: 103 -> 103, of which waited for: 47 -> 46; matrix products, arithmetic and copies ran while one was open for 10% -> 10% of each run, Pallas kernels for 38% -> 38%
where the time goes in v6:
time: 487 us; the launch traced here: 478 us
  Pallas kernels  184 us (38%)
  waiting for transfers between devices  139 us (29%)
  starting transfers between devices  67.4 us (14%)
  local copies, waits for them, and re-layouts  53.3 us (11%)
  other arithmetic  19.1 us (4%)
  between operations  15.6 us (3%)
    pallas_call x4, Pallas kernels, attend_row_back(): pl.pallas_call(functools.partial(backward_kernel, taps_q, taps_k, head_si...  57.6 us
    ppermute x23, waiting for transfers between devices, y_swap(): return lax.ppermute(array, 'narrow', [(0, 2), (2, 0), (1, 3), (3, 1)])  49.2 us
    unnamed x201, local copies, waits for them, and re-layouts  36.6 us
    pallas_call x4, Pallas kernels, feed_row(): pl.pallas_call(feed_kernel, out_shape=(jax.ShapeDtypeStruct((2 * half_len...  35.9 us
    ppermute x22, waiting for transfers between devices, x_swap(): return lax.ppermute(array, 'narrow', [(0, 1), (1, 0), (2, 3), (3, 2)])  33.9 us
    pallas_call x1, Pallas kernels, attend_rows(): pl.pallas_call(functools.partial(forward_kernel, taps_q, head_size, rows)...  32.7 us
    ppermute x23, starting transfers between devices, y_swap(): return lax.ppermute(array, 'narrow', [(0, 2), (2, 0), (1, 3), (3, 1)])  26.3 us
    ppermute x42, waiting for transfers between devices, seq_swap(): return lax.ppermute(array, 'seq', SWAP)  22.7 us
  transfers between devices with their start and end apart: 103, of which 46 were waited for; matrix products, arithmetic and copies ran while one was open for 10% of the time, Pallas kernels for 38%

profile of v6, /device:TPU:0, one launch (start us, length us, event | category | flops | bytes accessed | tf_op | source)
XLA Modules:
  0.0 478.4 jit_solution(16625659371201965025)
XLA Ops:
  10.0 3.1 collective-permute-start
  14.3 4.6 collective-permute-done.refs_1_
  33.8 1.5 dynamic-slice_dynamic-update-slice_fusion.1
  35.3 3.3 tap_bands.1
  45.9 9.4 %collective-permute-done.5 = bf16[128,1664]{1,0:T(8,128)(2,1)S(1)} collective-permute-done((bf16[128,1664]{1,0:T(8,128)(2,1)S(1)}, bf16[128,1664]{1,0:T(8,128)(2,1)S(1)}, u32[]{:S(2)}, u32[]{:S(2)}) %collective-permute-start.5) | collective-permute-done | bytes 426016 | tf_op jit(solution)/shard_map/ppermute | solution.py:906
  59.5 3.3 all-gather.3.cloned.1.call-done.joined_ref
  64.5 1.8 collective-permute-start.12
  68.0 1.8 collective-permute-start.13
  70.8 32.7 %attend_rows.1 = (bf16[4,512,768]{2,1,0:T(8,128)(2,1)}, f32[4,512,256]{2,1,0:T(8,128)}, bf16[4,512,256]{2,1,0:T(8,128)(2,1)}, f32[4,2,512,512]{3,2,1,0:T(8,128)}, s32[4,512,128]{2,1,0:T(8,128)}) custom-call(s32[1]{0:T(128)} %bitcast.core_ref, f32[2,2]{1,0:T(2,128)S(1)} %copy.31.mix_ref, bf16[1536,640]{1,0:T(8,128)(2,1)} %all-gather.3.cloned.1.call-done.joined_ref, ...), custom_call_target="tpu_custom_call" | custom-call | flops 1000000 | bytes 1000000 | tf_op jit(solution)/shard_map/attend_rows/pallas_call | solution.py:348
  105.5 1.8 branch.1
  108.0 1.7 collective-permute-done.17.came_ref
  113.1 10.8 %collective-permute-done.20.extra_ref = bf16[128,1536]{1,0:T(8,128)(2,1)S(1)} collective-permute-done((bf16[128,1536]{1,0:T(8,128)(2,1)S(1)}, bf16[128,1536]{1,0:T(8,128)(2,1)S(1)}, u32[]{:S(2)}, u32[]{:S(2)}) %collective-permute-start.20) | collective-permute-done | bytes 393248 | tf_op jit(solution)/shard_map/ppermute | solution.py:906
  125.0 1.7 collective-permute-start.24
  126.8 1.8 slice.99
  129.8 13.8 %collective-permute-done.23 = bf16[256,1536]{1,0:T(8,128)(2,1)S(1)} collective-permute-done((bf16[256,1536]{1,0:T(8,128)(2,1)S(1)}, bf16[256,1536]{1,0:T(8,128)(2,1)S(1)}, u32[]{:S(2)}, u32[]{:S(2)}) %collective-permute-start.23) | collective-permute-done | bytes 786464 | tf_op jit(solution)/shard_map/ppermute | solution.py:902
  145.7 7.7 %all-gather.5.cloned.1.call-done.feed_ref = bf16[1536,1536]{1,0:T(8,128)(2,1)} async-done(((bf16[384,1536]{1,0:T(8,128)(2,1)}), bf16[1536,1536]{1,0:T(8,128)(2,1)}) %all-gather.5.cloned.1.call-update) | async-done | bytes 4718608 | tf_op jit(solution)/shard_map/all_gather | solution.py:964
  156.4 2.3 copy-done.15
  159.0 1.7 copy-done.2
  161.8 8.9 %feed_row.4 = (bf16[512,512]{1,0:T(8,128)(2,1)S(1)}, bf16[512,1024]{1,0:T(8,128)(2,1)}, bf16[256,1536]{1,0:T(8,128)(2,1)S(1)}, bf16[256,1536]{1,0:T(8,128)(2,1)}...) custom-call(bf16[256,1536]{1,0:T(8,128)(2,1)S(1)} %multiply_convert_fusion.own_ref.refs_0_, ...), custom_call_target="tpu_custom_call" | custom-call | bytes 28800000 | tf_op jit(solution)/shard_map/feed_row/pallas_call | solution.py:645
  171.5 1.8 collective-permute-done.28.own_ref.refs_2_
  175.1 1.8 collective-permute-done.31.other_ref.refs_5_
  180.1 9.0 %feed_row.5 = (bf16[512,512]{1,0:T(8,128)(2,1)S(1)}, bf16[512,1024]{1,0:T(8,128)(2,1)}, bf16[256,1536]{1,0:T(8,128)(2,1)S(1)}, bf16[256,1536]{1,0:T(8,128)(2,1)}...) custom-call(bf16[256,1536]{1,0:T(8,128)(2,1)S(1)} %collective-permute-done.28.own_ref.refs_2_, ...), custom_call_target="tpu_custom_call" | custom-call | bytes 28800000 | tf_op jit(solution)/shard_map/feed_row/pallas_call | solution.py:645
  192.0 9.0 %feed_row.6 = (bf16[512,512]{1,0:T(8,128)(2,1)S(1)}, bf16[512,1024]{1,0:T(8,128)(2,1)}, bf16[256,1536]{1,0:T(8,128)(2,1)S(1)}, bf16[256,1536]{1,0:T(8,128)(2,1)}...) custom-call(bf16[256,1536]{1,0:T(8,128)(2,1)S(1)} %collective-permute-done.29.own_ref.refs_4_, ...), custom_call_target="tpu_custom_call" | custom-call | bytes 28800000 | tf_op jit(solution)/shard_map/feed_row/pallas_call | solution.py:645
  207.8 9.0 %feed_row.7 = (bf16[512,512]{1,0:T(8,128)(2,1)S(1)}, bf16[512,1024]{1,0:T(8,128)(2,1)}, bf16[256,1536]{1,0:T(8,128)(2,1)S(1)}, bf16[256,1536]{1,0:T(8,128)(2,1)}...) custom-call(bf16[256,1536]{1,0:T(8,128)(2,1)S(1)} %constant_dynamic-update-slice_fusion.4.own_ref.refs_6_, ...), custom_call_target="tpu_custom_call" | custom-call | bytes 28800000 | tf_op jit(solution)/shard_map/feed_row/pallas_call | solution.py:645
  217.8 7.6 %collective-permute-done.41 = bf16[256,1536]{1,0:T(8,128)(2,1)S(1)} collective-permute-done((bf16[256,1536]{1,0:T(8,128)(2,1)S(1)}, bf16[256,1536]{1,0:T(8,128)(2,1)S(1)}, u32[]{:S(2)}, u32[]{:S(2)}) %collective-permute-start.41) | collective-permute-done | bytes 786464 | tf_op jit(solution)/shard_map/ppermute | solution.py:906
  227.1 1.8 collective-permute-done.43
  230.8 16.9 %feed_grad.1 = bf16[1536,1536]{1,0:T(8,128)(2,1)} custom-call(bf16[256,1536]{1,0:T(8,128)(2,1)} %copy-done.7, bf16[256,1536]{1,0:T(8,128)(2,1)} %copy-done.18, bf16[256,1536]{1,0:T(8,128)(2,1)} %copy-done.11, bf16[256,1536]{1,0:T(8,128)(2,1)} %copy-done.20, bf16[256,1536]{1,0:T(8,128)(2,1)} %copy-done.12, bf16[256,1536]{1,0:T(8,128)(2,1)} %copy-done.19, ...), custom_call_target="tpu_custom_call" | custom-call | bytes 61200000 | tf_op jit(solution)/shard_map/feed_grad/pallas_call | solution.py:695
  247.7 3.2 collective-permute-done.44
  252.0 4.2 multiply_reduce_fusion.1
  259.7 14.2 %attend_row_back.4 = (bf16[512,640]{1,0:T(8,128)(2,1)S(1)}, bf16[256,1536]{1,0:T(8,128)(2,1)S(1)}, bf16[256,1536]{1,0:T(8,128)(2,1)S(1)}, f32[8,128]{1,0:T(8,128)S(1)}, f32[2,66,128]{2,1,0:T(8,128)S(1)}) custom-call(s32[1]{0:T(128)} %bitcast.core_ref, f32[2,2]{1,0:T(2,128)S(1)} %copy.31.mix_ref, bf16[256,1536]{1,0:T(8,128)(2,1)S(1)} %fusion.11.own_ref.refs_1_, ...), custom_call_target="tpu_custom_call" | custom-call | bytes 50400000 | tf_op jit(solution)/shard_map/attend_row_back/pallas_call | solution.py:552
  273.9 3.5 collective-permute-done.50.own_ref.refs_3_
  278.0 1.7 collective-permute-done.53.other_ref.refs_6_
  280.8 1.7 collective-permute-start.56
  283.1 1.8 collective-permute-start.54
  284.9 14.2 %attend_row_back.5 = (bf16[512,640]{1,0:T(8,128)(2,1)S(1)}, bf16[256,1536]{1,0:T(8,128)(2,1)S(1)}, bf16[256,1536]{1,0:T(8,128)(2,1)S(1)}, f32[8,128]{1,0:T(8,128)S(1)}, f32[2,66,128]{2,1,0:T(8,128)S(1)}) custom-call(s32[1]{0:T(128)} %bitcast.core_ref, f32[2,2]{1,0:T(2,128)S(1)} %copy.31.mix_ref, ...), custom_call_target="tpu_custom_call" | custom-call | bytes 50400000 | tf_op jit(solution)/shard_map/attend_row_back/pallas_call | solution.py:552
  302.5 2.3 collective-permute-done.58.refs_8_.other_ref
  306.1 1.8 out_grad.1
  308.8 15.3 %attend_row_back.6 = (bf16[512,640]{1,0:T(8,128)(2,1)S(1)}, bf16[256,1536]{1,0:T(8,128)(2,1)S(1)}, bf16[256,1536]{1,0:T(8,128)(2,1)}, f32[8,128]{1,0:T(8,128)S(1)}, f32[2,66,128]{2,1,0:T(8,128)S(1)}) custom-call(s32[1]{0:T(128)} %bitcast.core_ref, f32[2,2]{1,0:T(2,128)S(1)} %copy.31.mix_ref, bf16[256,1536]{1,0:T(8,128)(2,1)S(1)} %collective-permute-done.51.own_ref.refs_5_, ...), custom_call_target="tpu_custom_call" | custom-call | bytes 50400000 | tf_op jit(solution)/shard_map/attend_row_back/pallas_call | solution.py:552
  334.3 1.7 collective-permute-start.66
  336.8 1.7 collective-permute-start.64
  339.6 14.0 %attend_row_back.7 = (bf16[512,640]{1,0:T(8,128)(2,1)S(1)}, bf16[256,1536]{1,0:T(8,128)(2,1)S(1)}, bf16[256,1536]{1,0:T(8,128)(2,1)S(1)}, f32[8,128]{1,0:T(8,128)S(1)}, f32[2,66,128]{2,1,0:T(8,128)S(1)}) custom-call(s32[1]{0:T(128)} %bitcast.core_ref, f32[2,2]{1,0:T(2,128)S(1)} %copy.31.mix_ref, ...), custom_call_target="tpu_custom_call" | custom-call | bytes 50400000 | tf_op jit(solution)/shard_map/attend_row_back/pallas_call | solution.py:552
  353.7 6.2 %collective-permute-done.64 = bf16[256,1536]{1,0:T(8,128)(2,1)S(1)} collective-permute-done((bf16[256,1536]{1,0:T(8,128)(2,1)S(1)}, bf16[256,1536]{1,0:T(8,128)(2,1)S(1)}, u32[]{:S(2)}, u32[]{:S(2)}) %collective-permute-start.64) | collective-permute-done | bytes 786464 | tf_op jit(solution)/shard_map/ppermute | solution.py:906
  360.4 1.8 collective-permute-done.69
  363.6 2.2 collective-permute-start.70
  365.7 1.8 dynamic-slice_bitcast_fusion
  367.9 2.0 collective-permute-start.71
  369.9 10.1 %joined_grad.1 = bf16[1536,640]{1,0:T(8,128)(2,1)} custom-call(bf16[256,1664]{1,0:T(8,128)(2,1)} %copy-done.6, bf16[256,1664]{1,0:T(8,128)(2,1)} %collective-permute-done.3.refs_1_, bf16[256,1664]{1,0:T(8,128)(2,1)} %collective-permute-done.1.refs_2_, bf16[256,1664]{1,0:T(8,128)(2,1)} %copy-done.69, bf16[256,1664]{1,0:T(8,128)(2,1)} %collective-permute-done.2.refs_4_, ...), custom_call_target="tpu_custom_call" | custom-call | bytes 28800000 | tf_op jit(solution)/shard_map/joined_grad/pallas_call | solution.py:734
  381.6 2.7 collective-permute-done.70
  384.4 1.8 collective-permute-start.79
  388.2 3.5 fusion.5
  393.2 4.4 collective-permute-done.75
  397.9 5.6 %collective-permute-done.76 = f32[48,128]{1,0:T(8,128)S(1)} collective-permute-done((f32[48,128]{1,0:T(8,128)S(1)}, f32[48,128]{1,0:T(8,128)S(1)}, u32[]{:S(2)}, u32[]{:S(2)}) %collective-permute-start.76) | collective-permute-done | bytes 24608 | tf_op jit(solution)/shard_map/ppermute | solution.py:1291
  404.9 8.9 %collective-permute-done.77 = f32[48,128]{1,0:T(8,128)S(1)} collective-permute-done((f32[48,128]{1,0:T(8,128)S(1)}, f32[48,128]{1,0:T(8,128)S(1)}, u32[]{:S(2)}, u32[]{:S(2)}) %collective-permute-start.77) | collective-permute-done | bytes 24608 | tf_op jit(solution)/shard_map/ppermute | solution.py:902
  418.0 1.7 collective-permute-start.81
  419.7 5.0 %fusion.7 = (f32[256,1536]{1,0:T(8,128)}, bf16[256,1536]{1,0:T(8,128)(2,1)}) fusion(bf16[256,1536]{1,0:T(8,128)(2,1)S(1)} %copy-done.64, f32[256,1536]{1,0:T(8,128)} %get-tuple-element.460, f32[256]{0:T(256)S(1)} %fusion.10, f32[1536]{0:T(1024)S(1)} %copy-done.88, f32[256]{0:T(256)S(1)} %add_rsqrt_fusion.1, bf16[256,1536]{1,0:T(8,128)(2,1)S(1)} %copy-done.5, ...), kind=kLoop, calls=%fused_computation.13 | loop fusion | flops 8257536 | bytes 11812864 | tf_op jit(solution)/shard_map/add | solution.py:1268
  425.9 4.9 %collective-permute-done.81 = f32[48,128]{1,0:T(8,128)S(1)} collective-permute-done((f32[48,128]{1,0:T(8,128)S(1)}, f32[48,128]{1,0:T(8,128)S(1)}, u32[]{:S(2)}, u32[]{:S(2)}) %collective-permute-start.81) | collective-permute-done | bytes 24608 | tf_op jit(solution)/shard_map/ppermute | solution.py:906
  435.2 10.3 %place_feed.1 = (f32[384,8192]{1,0:T(8,128)}, f32[1024,1536]{1,0:T(8,128)}) custom-call(s32[3]{0:T(128)} %copy-done.53, bf16[384,1536]{1,0:T(8,128)(2,1)} %reduce-scatter.3.cloned.1.call-done.refs_0_, bf16[384,1536]{1,0:T(8,128)(2,1)} %collective-permute-done.80.refs_1_, bf16[384,1536]{1,0:T(8,128)(2,1)} %collective-permute-done.78.refs_2_, ...), custom_call_target="tpu_custom_call" | custom-call | bytes 39600000 | tf_op jit(solution)/shard_map/place_feed/pallas_call | solution.py:154
  445.6 2.6 collective-permute-done.90
  450.1 1.6 collective-permute-start.92
  452.8 3.4 collective-permute-done.96
  457.2 2.5 collective-permute-done.92
  459.8 4.1 place_columns.1.base_ref
  467.4 1.9 add_columns.1
  469.3 2.1 place_quarters.1
  (464 shorter events, 120.0 us)
Async XLA Ops:
  7.2 55.6 %all-gather.3.cloned.1.call-start = ((), (), s32[]{:S(2)}) async-start(), calls=%async_computation.2 | async-start | bytes 2457600 | tf_op jit(solution)/shard_map/all_gather | solution.py:964
  9.9 143.5 %all-gather.5.cloned.1.call-start = ((), (), s32[]{:S(2)}) async-start(), calls=%async_computation.3 | async-start | bytes 5898240 | tf_op jit(solution)/shard_map/all_gather | solution.py:964
  18.9 21.9 %collective-permute-start.1 = (bf16[256,1664]{1,0:T(8,128)(2,1)S(1)}, bf16[256,1664]{1,0:T(8,128)(2,1)}, u32[]{:S(2)}, u32[]{:S(2)}) collective-permute-start(bf16[256,1664]{1,0:T(8,128)(2,1)S(1)} %pad_maximum_fusion.refs_0_), channel_id=1, source_target_pairs={{0,8},{8,0},{16,24},{24,16},{1,9},{9,1},{17,25},{25,17},{2,10},{10... | collective-permute-start | bytes 2555912 | tf_op jit(solution)/shard_map/ppermute | solution.py:902
  20.4 21.4 %collective-permute-start.2 = (bf16[256,1664]{1,0:T(8,128)(2,1)S(1)}, bf16[256,1664]{1,0:T(8,128)(2,1)}, u32[]{:S(2)}, u32[]{:S(2)}) collective-permute-start(bf16[256,1664]{1,0:T(8,128)(2,1)S(1)} %pad_maximum_fusion.refs_0_), channel_id=1, source_target_pairs={{0,16},{16,0},{8,24},{24,8},{1,17},{17,1},{9,25},{25,9},{2,18},{18... | collective-permute-start | bytes 2555912 | tf_op jit(solution)/shard_map/ppermute | solution.py:906
  21.9 21.0 %collective-permute-start.3 = (bf16[256,1664]{1,0:T(8,128)(2,1)S(1)}, bf16[256,1664]{1,0:T(8,128)(2,1)}, u32[]{:S(2)}, u32[]{:S(2)}) collective-permute-start(bf16[256,1664]{1,0:T(8,128)(2,1)S(1)} %pad_maximum_fusion.refs_0_), channel_id=1, source_target_pairs={{0,1},{1,0},{2,3},{3,2},{4,5},{5,4},{6,7},{7,6},{8,9},{9,8},{10,11... | collective-permute-start | bytes 2555912 | tf_op jit(solution)/shard_map/ppermute | solution.py:898
  21.9 21.0 %collective-permute-start.4 = (bf16[48,1536]{1,0:T(8,128)(2,1)S(1)}, bf16[48,1536]{1,0:T(8,128)(2,1)S(1)}, u32[]{:S(2)}, u32[]{:S(2)}) collective-permute-start(bf16[48,1536]{1,0:T(8,128)(2,1)S(1)} %collective-permute-done.refs_1_), channel_id=1, source_target_pairs={{0,2},{2,4},{4,6},{6,0},{1,3},{3,5},{5,7},{7,1},{8,10},{10,12},{12... | collective-permute-start | bytes 442376 | tf_op jit(solution)/shard_map/ppermute | solution.py:947
  42.9 12.3 %collective-permute-start.5 = (bf16[128,1664]{1,0:T(8,128)(2,1)S(1)}, bf16[128,1664]{1,0:T(8,128)(2,1)S(1)}, u32[]{:S(2)}, u32[]{:S(2)}) collective-permute-start(bf16[128,1664]{1,0:T(8,128)(2,1)S(1)} %slice.122), channel_id=1, source_target_pairs={{0,16},{16,0},{8,24},{24,8},{1,17},{17,1},{9,25},{25,9},{2,18},{18... | collective-permute-start | bytes 1277960 | tf_op jit(solution)/shard_map/ppermute | solution.py:906
  43.5 12.0 %collective-permute-start.6 = (bf16[128,1664]{1,0:T(8,128)(2,1)S(1)}, bf16[128,1664]{1,0:T(8,128)(2,1)S(1)}, u32[]{:S(2)}, u32[]{:S(2)}) collective-permute-start(bf16[128,1664]{1,0:T(8,128)(2,1)S(1)} %slice.123), channel_id=1, source_target_pairs={{0,8},{8,0},{16,24},{24,16},{1,9},{9,1},{17,25},{25,17},{2,10},{10... | collective-permute-start | bytes 1277960 | tf_op jit(solution)/shard_map/ppermute | solution.py:902
  44.2 11.4 %collective-permute-start.7 = (bf16[48,1536]{1,0:T(8,128)(2,1)S(1)}, bf16[48,1536]{1,0:T(8,128)(2,1)S(1)}, u32[]{:S(2)}, u32[]{:S(2)}) collective-permute-start(bf16[48,1536]{1,0:T(8,128)(2,1)S(1)} %collective-permute-done.4.refs_2_), channel_id=1, source_target_pairs={{0,2},{2,4},{4,6},{6,0},{1,3},{3,5},{5,7},{7,1},{8,10},{10,12},{12... | collective-permute-start | bytes 442376 | tf_op jit(solution)/shard_map/ppermute | solution.py:947
  45.4 11.7 %collective-permute-start.10 = (bf16[256,1664]{1,0:T(8,128)(2,1)}, bf16[256,1664]{1,0:T(8,128)(2,1)S(1)}, u32[]{:S(2)}, u32[]{:S(2)}) collective-permute-start(bf16[256,1664]{1,0:T(8,128)(2,1)} %collective-permute-done.2.refs_4_), channel_id=1, source_target_pairs={{0,1},{1,0},{2,3},{3,2},{4,5},{5,4},{6,7},{7,6},{8,9},{9,8},{10,11... | collective-permute-start | bytes 2555912 | tf_op jit(solution)/shard_map/ppermute | solution.py:898
  45.4 12.3 %collective-permute-start.9 = (bf16[256,1664]{1,0:T(8,128)(2,1)}, bf16[256,1664]{1,0:T(8,128)(2,1)S(1)}, u32[]{:S(2)}, u32[]{:S(2)}) collective-permute-start(bf16[256,1664]{1,0:T(8,128)(2,1)} %collective-permute-done.1.refs_2_), channel_id=1, source_target_pairs={{0,1},{1,0},{2,3},{3,2},{4,5},{5,4},{6,7},{7,6},{8,9},{9,8},{10,11... | collective-permute-start | bytes 2555912 | tf_op jit(solution)/shard_map/ppermute | solution.py:898
  62.9 321.5 %reduce-scatter.3.cloned.1.call-start = ((), (), s32[]{:S(2)}) async-start(), calls=%async_computation.4 | async-start | bytes 5898240 | tf_op jit(solution)/shard_map/reduce_scatter | solution.py:968
  62.9 40.6 %collective-permute-start.11 = (bf16[256,1536]{1,0:T(8,128)(2,1)S(1)}, bf16[256,1536]{1,0:T(8,128)(2,1)S(1)}, u32[]{:S(2)}, u32[]{:S(2)}) collective-permute-start(bf16[256,1536]{1,0:T(8,128)(2,1)S(1)} %copy-done.4), channel_id=1, source_target_pairs={{0,8},{8,0},{16,24},{24,16},{1,9},{9,1},{17,25},{25,17},{2,10},{10... | collective-permute-start | bytes 2359304 | tf_op jit(solution)/shard_map/ppermute | solution.py:902
  64.5 39.1 %collective-permute-start.12 = (bf16[256,1536]{1,0:T(8,128)(2,1)S(1)}, bf16[256,1536]{1,0:T(8,128)(2,1)}, u32[]{:S(2)}, u32[]{:S(2)}) collective-permute-start(bf16[256,1536]{1,0:T(8,128)(2,1)S(1)} %copy-done.4), channel_id=1, source_target_pairs={{0,16},{16,0},{8,24},{24,8},{1,17},{17,1},{9,25},{25,9},{2,18},{18... | collective-permute-start | bytes 2359304 | tf_op jit(solution)/shard_map/ppermute | solution.py:906
  66.3 37.3 %collective-permute-start.15 = (bf16[48,1536]{1,0:T(8,128)(2,1)}, bf16[48,1536]{1,0:T(8,128)(2,1)S(1)}, u32[]{:S(2)}, u32[]{:S(2)}) collective-permute-start(bf16[48,1536]{1,0:T(8,128)(2,1)} %copy-done.59), channel_id=1, source_target_pairs={{0,24},{8,16},{16,8},{24,0},{1,25},{9,17},{17,9},{25,1},{2,26},{10... | collective-permute-start | bytes 442376 | tf_op jit(solution)/shard_map/ppermute | solution.py:910
  66.5 37.1 %collective-permute-start.14 = (bf16[48,1536]{1,0:T(8,128)(2,1)}, bf16[48,1536]{1,0:T(8,128)(2,1)}, u32[]{:S(2)}, u32[]{:S(2)}) collective-permute-start(bf16[48,1536]{1,0:T(8,128)(2,1)} %copy-done.58), channel_id=1, source_target_pairs={{0,16},{16,0},{8,24},{24,8},{1,17},{17,1},{9,25},{25,9},{2,18},{18... | collective-permute-start | bytes 442376 | tf_op jit(solution)/shard_map/ppermute | solution.py:906
  68.0 35.6 %collective-permute-start.13 = (bf16[48,1536]{1,0:T(8,128)(2,1)}, bf16[48,1536]{1,0:T(8,128)(2,1)}, u32[]{:S(2)}, u32[]{:S(2)}) collective-permute-start(bf16[48,1536]{1,0:T(8,128)(2,1)} %copy-done.57), channel_id=1, source_target_pairs={{0,8},{8,0},{16,24},{24,16},{1,9},{9,1},{17,25},{25,17},{2,10},{10... | collective-permute-start | bytes 442376 | tf_op jit(solution)/shard_map/ppermute | solution.py:902
  112.1 11.7 %collective-permute-start.22 = (bf16[256,1536]{1,0:T(8,128)(2,1)S(1)}, bf16[256,1536]{1,0:T(8,128)(2,1)S(1)}, u32[]{:S(2)}, u32[]{:S(2)}) collective-permute-start(bf16[256,1536]{1,0:T(8,128)(2,1)S(1)} %copy-done.4), channel_id=1, source_target_pairs={{0,1},{1,0},{2,3},{3,2},{4,5},{5,4},{6,7},{7,6},{8,9},{9,8},{10,11... | collective-permute-start | bytes 2359304 | tf_op jit(solution)/shard_map/ppermute | solution.py:898
  112.3 11.5 %collective-permute-start.19 = (bf16[256,1536]{1,0:T(8,128)(2,1)S(1)}, bf16[256,1536]{1,0:T(8,128)(2,1)S(1)}, u32[]{:S(2)}, u32[]{:S(2)}) collective-permute-start(bf16[256,1536]{1,0:T(8,128)(2,1)S(1)} %get-tuple-element.268), channel_id=1, source_target_pairs={{0,1},{1,0},{2,3},{3,2},{4,5},{5,4},{6,7},{7,6},{8,9},{9,8},{10,11... | collective-permute-start | bytes 2359304 | tf_op jit(solution)/shard_map/ppermute | solution.py:898
  124.7 18.9 %collective-permute-start.23 = (bf16[256,1536]{1,0:T(8,128)(2,1)S(1)}, bf16[256,1536]{1,0:T(8,128)(2,1)S(1)}, u32[]{:S(2)}, u32[]{:S(2)}) collective-permute-start(bf16[256,1536]{1,0:T(8,128)(2,1)S(1)} %low_sum.4), channel_id=1, source_target_pairs={{0,8},{8,0},{16,24},{24,16},{1,9},{9,1},{17,25},{25,17},{2,10},{10... | collective-permute-start | bytes 2359304 | tf_op jit(solution)/shard_map/ppermute | solution.py:902
  125.0 18.6 %collective-permute-start.24 = (bf16[256,1536]{1,0:T(8,128)(2,1)S(1)}, bf16[256,1536]{1,0:T(8,128)(2,1)S(1)}, u32[]{:S(2)}, u32[]{:S(2)}) collective-permute-start(bf16[256,1536]{1,0:T(8,128)(2,1)S(1)} %low_sum.5), channel_id=1, source_target_pairs={{0,16},{16,0},{8,24},{24,8},{1,17},{17,1},{9,25},{25,9},{2,18},{18... | collective-permute-start | bytes 2359304 | tf_op jit(solution)/shard_map/ppermute | solution.py:906
  126.8 18.9 %collective-permute-start.26 = (bf16[256,1536]{1,0:T(8,128)(2,1)}, bf16[256,1536]{1,0:T(8,128)(2,1)}, u32[]{:S(2)}, u32[]{:S(2)}) collective-permute-start(bf16[256,1536]{1,0:T(8,128)(2,1)} %collective-permute-done.12.cot_own_ref.refs_20_), channel_id=1, source_target_pairs={{0,1},{1,0},{2,3},{3,2},{4,5},{5,4},{6,7},{7,6},{8,9},{9,8},{10,11... | collective-permute-start | bytes 2359304 | tf_op jit(solution)/shard_map/ppermute | solution.py:898
  128.5 17.1 %collective-permute-start.25 = (bf16[256,1536]{1,0:T(8,128)(2,1)S(1)}, bf16[256,1536]{1,0:T(8,128)(2,1)}, u32[]{:S(2)}, u32[]{:S(2)}) collective-permute-start(bf16[256,1536]{1,0:T(8,128)(2,1)S(1)} %copy-done.9), channel_id=1, source_target_pairs={{0,1},{1,0},{2,3},{3,2},{4,5},{5,4},{6,7},{7,6},{8,9},{9,8},{10,11... | collective-permute-start | bytes 2359304 | tf_op jit(solution)/shard_map/ppermute | solution.py:898
  153.4 20.0 %collective-permute-start.28 = (bf16[256,1536]{1,0:T(8,128)(2,1)S(1)}, bf16[256,1536]{1,0:T(8,128)(2,1)S(1)}, u32[]{:S(2)}, u32[]{:S(2)}) collective-permute-start(bf16[256,1536]{1,0:T(8,128)(2,1)S(1)} %multiply_convert_fusion.own_ref.refs_0_), channel_id=1, source_target_pairs={{0,8},{8,0},{16,24},{24,16},{1,9},{9,1},{17,25},{25,17},{2,10},{10... | collective-permute-start | bytes 2359304 | tf_op jit(solution)/shard_map/ppermute | solution.py:902
  154.9 19.7 %collective-permute-start.29 = (bf16[256,1536]{1,0:T(8,128)(2,1)S(1)}, bf16[256,1536]{1,0:T(8,128)(2,1)S(1)}, u32[]{:S(2)}, u32[]{:S(2)}) collective-permute-start(bf16[256,1536]{1,0:T(8,128)(2,1)S(1)} %multiply_convert_fusion.own_ref.refs_0_), channel_id=1, source_target_pairs={{0,16},{16,0},{8,24},{24,8},{1,17},{17,1},{9,25},{25,9},{2,18},{18... | collective-permute-start | bytes 2359304 | tf_op jit(solution)/shard_map/ppermute | solution.py:906
  178.0 11.2 %collective-permute-start.32 = (bf16[128,1536]{1,0:T(8,128)(2,1)S(1)}, bf16[128,1536]{1,0:T(8,128)(2,1)S(1)}, u32[]{:S(2)}, u32[]{:S(2)}) collective-permute-start(bf16[128,1536]{1,0:T(8,128)(2,1)S(1)} %copy-done.86), channel_id=1, source_target_pairs={{0,16},{16,0},{8,24},{24,8},{1,17},{17,1},{9,25},{25,9},{2,18},{18... | collective-permute-start | bytes 1179656 | tf_op jit(solution)/shard_map/ppermute | solution.py:906
  190.4 12.0 %collective-permute-start.38 = (bf16[256,1536]{1,0:T(8,128)(2,1)S(1)}, bf16[256,1536]{1,0:T(8,128)(2,1)S(1)}, u32[]{:S(2)}, u32[]{:S(2)}) collective-permute-start(bf16[256,1536]{1,0:T(8,128)(2,1)S(1)} %constant_dynamic-update-slice_fusion.2.cot_own_ref.refs_22_), channel_id=1, source_target_pairs={{0,1},{1,0},{2,3},{3,2},{4,5},{5,4},{6,7},{7,6},{8,9},{9,8},{10,11... | collective-permute-start | bytes 2359304 | tf_op jit(solution)/shard_map/ppermute | solution.py:898
  190.4 11.9 %collective-permute-start.37 = (bf16[256,1536]{1,0:T(8,128)(2,1)S(1)}, bf16[256,1536]{1,0:T(8,128)(2,1)S(1)}, u32[]{:S(2)}, u32[]{:S(2)}) collective-permute-start(bf16[256,1536]{1,0:T(8,128)(2,1)S(1)} %get-tuple-element.297), channel_id=1, source_target_pairs={{0,1},{1,0},{2,3},{3,2},{4,5},{5,4},{6,7},{7,6},{8,9},{9,8},{10,11... | collective-permute-start | bytes 2359304 | tf_op jit(solution)/shard_map/ppermute | solution.py:898
  205.8 19.6 %collective-permute-start.41 = (bf16[256,1536]{1,0:T(8,128)(2,1)S(1)}, bf16[256,1536]{1,0:T(8,128)(2,1)S(1)}, u32[]{:S(2)}, u32[]{:S(2)}) collective-permute-start(bf16[256,1536]{1,0:T(8,128)(2,1)S(1)} %pair_sum.7), channel_id=1, source_target_pairs={{0,16},{16,0},{8,24},{24,8},{1,17},{17,1},{9,25},{25,9},{2,18},{18... | collective-permute-start | bytes 2359304 | tf_op jit(solution)/shard_map/ppermute | solution.py:906
  207.3 19.3 %collective-permute-start.40 = (bf16[256,1536]{1,0:T(8,128)(2,1)S(1)}, bf16[256,1536]{1,0:T(8,128)(2,1)S(1)}, u32[]{:S(2)}, u32[]{:S(2)}) collective-permute-start(bf16[256,1536]{1,0:T(8,128)(2,1)S(1)} %pair_sum.6), channel_id=1, source_target_pairs={{0,8},{8,0},{16,24},{24,16},{1,9},{9,1},{17,25},{25,17},{2,10},{10... | collective-permute-start | bytes 2359304 | tf_op jit(solution)/shard_map/ppermute | solution.py:902
  230.2 20.7 %collective-permute-start.44 = (bf16[256,1536]{1,0:T(8,128)(2,1)S(1)}, bf16[256,1536]{1,0:T(8,128)(2,1)}, u32[]{:S(2)}, u32[]{:S(2)}) collective-permute-start(bf16[256,1536]{1,0:T(8,128)(2,1)S(1)} %pair_sum.8), channel_id=1, source_target_pairs={{0,24},{8,16},{16,8},{24,0},{1,25},{9,17},{17,9},{25,1},{2,26},{10... | collective-permute-start | bytes 2359304 | tf_op jit(solution)/shard_map/ppermute | solution.py:910
  250.9 180.1 %reduce-scatter.5.cloned.1.call-start = ((), (), s32[]{:S(2)}) async-start(), calls=%async_computation.5 | async-start | bytes 2457600 | tf_op jit(solution)/shard_map/reduce_scatter | solution.py:968
  257.5 20.0 %collective-permute-start.50 = (bf16[256,1536]{1,0:T(8,128)(2,1)S(1)}, bf16[256,1536]{1,0:T(8,128)(2,1)S(1)}, u32[]{:S(2)}, u32[]{:S(2)}) collective-permute-start(bf16[256,1536]{1,0:T(8,128)(2,1)S(1)} %fusion.11.own_ref.refs_1_), channel_id=1, source_target_pairs={{0,8},{8,0},{16,24},{24,16},{1,9},{9,1},{17,25},{25,17},{2,10},{10... | collective-permute-start | bytes 2359304 | tf_op jit(solution)/shard_map/ppermute | solution.py:902
  257.6 19.9 %collective-permute-start.51 = (bf16[256,1536]{1,0:T(8,128)(2,1)S(1)}, bf16[256,1536]{1,0:T(8,128)(2,1)S(1)}, u32[]{:S(2)}, u32[]{:S(2)}) collective-permute-start(bf16[256,1536]{1,0:T(8,128)(2,1)S(1)} %fusion.11.own_ref.refs_1_), channel_id=1, source_target_pairs={{0,16},{16,0},{8,24},{24,8},{1,17},{17,1},{9,25},{25,9},{2,18},{18... | collective-permute-start | bytes 2359304 | tf_op jit(solution)/shard_map/ppermute | solution.py:906
  280.8 19.1 %collective-permute-start.56 = (bf16[128,1536]{1,0:T(8,128)(2,1)S(1)}, bf16[128,1536]{1,0:T(8,128)(2,1)S(1)}, u32[]{:S(2)}, u32[]{:S(2)}) collective-permute-start(bf16[128,1536]{1,0:T(8,128)(2,1)S(1)} %slice.125), channel_id=1, source_target_pairs={{0,8},{8,0},{16,24},{24,16},{1,9},{9,1},{17,25},{25,17},{2,10},{10... | collective-permute-start | bytes 1179656 | tf_op jit(solution)/shard_map/ppermute | solution.py:902
  282.6 17.4 %collective-permute-start.55 = (bf16[128,1536]{1,0:T(8,128)(2,1)S(1)}, bf16[128,1536]{1,0:T(8,128)(2,1)S(1)}, u32[]{:S(2)}, u32[]{:S(2)}) collective-permute-start(bf16[128,1536]{1,0:T(8,128)(2,1)S(1)} %slice.124), channel_id=1, source_target_pairs={{0,16},{16,0},{8,24},{24,8},{1,17},{17,1},{9,25},{25,9},{2,18},{18... | collective-permute-start | bytes 1179656 | tf_op jit(solution)/shard_map/ppermute | solution.py:906
  282.9 17.6 %collective-permute-start.57 = (bf16[128,1536]{1,0:T(8,128)(2,1)S(1)}, bf16[128,1536]{1,0:T(8,128)(2,1)S(1)}, u32[]{:S(2)}, u32[]{:S(2)}) collective-permute-start(bf16[128,1536]{1,0:T(8,128)(2,1)S(1)} %get-tuple-element.360), channel_id=1, source_target_pairs={{0,8},{8,0},{16,24},{24,16},{1,9},{9,1},{17,25},{25,17},{2,10},{10... | collective-permute-start | bytes 1179656 | tf_op jit(solution)/shard_map/ppermute | solution.py:902
  283.1 18.7 %collective-permute-start.54 = (bf16[128,1536]{1,0:T(8,128)(2,1)S(1)}, bf16[128,1536]{1,0:T(8,128)(2,1)S(1)}, u32[]{:S(2)}, u32[]{:S(2)}) collective-permute-start(bf16[128,1536]{1,0:T(8,128)(2,1)S(1)} %get-tuple-element.356), channel_id=1, source_target_pairs={{0,16},{16,0},{8,24},{24,8},{1,17},{17,1},{9,25},{25,9},{2,18},{18... | collective-permute-start | bytes 1179656 | tf_op jit(solution)/shard_map/ppermute | solution.py:906
  304.8 21.0 %collective-permute-start.61 = (bf16[256,1536]{1,0:T(8,128)(2,1)S(1)}, bf16[256,1536]{1,0:T(8,128)(2,1)S(1)}, u32[]{:S(2)}, u32[]{:S(2)}) collective-permute-start(bf16[256,1536]{1,0:T(8,128)(2,1)S(1)} %low_sum.7), channel_id=1, source_target_pairs={{0,16},{16,0},{8,24},{24,8},{1,17},{17,1},{9,25},{25,9},{2,18},{18... | collective-permute-start | bytes 2359304 | tf_op jit(solution)/shard_map/ppermute | solution.py:906
  305.1 20.7 %collective-permute-start.60 = (bf16[256,1536]{1,0:T(8,128)(2,1)S(1)}, bf16[256,1536]{1,0:T(8,128)(2,1)S(1)}, u32[]{:S(2)}, u32[]{:S(2)}) collective-permute-start(bf16[256,1536]{1,0:T(8,128)(2,1)S(1)} %low_sum.6), channel_id=1, source_target_pairs={{0,8},{8,0},{16,24},{24,16},{1,9},{9,1},{17,25},{25,17},{2,10},{10... | collective-permute-start | bytes 2359304 | tf_op jit(solution)/shard_map/ppermute | solution.py:902
  306.1 19.8 %collective-permute-start.59 = (bf16[256,1536]{1,0:T(8,128)(2,1)S(1)}, bf16[256,1536]{1,0:T(8,128)(2,1)S(1)}, u32[]{:S(2)}, u32[]{:S(2)}) collective-permute-start(bf16[256,1536]{1,0:T(8,128)(2,1)S(1)} %get-tuple-element.369), channel_id=1, source_target_pairs={{0,1},{1,0},{2,3},{3,2},{4,5},{5,4},{6,7},{7,6},{8,9},{9,8},{10,11... | collective-permute-start | bytes 2359304 | tf_op jit(solution)/shard_map/ppermute | solution.py:898
  333.2 20.3 %collective-permute-start.65 = (bf16[48,1536]{1,0:T(8,128)(2,1)S(1)}, bf16[48,1536]{1,0:T(8,128)(2,1)S(1)}, u32[]{:S(2)}, u32[]{:S(2)}) collective-permute-start(bf16[48,1536]{1,0:T(8,128)(2,1)S(1)} %get-tuple-element.479), channel_id=1, source_target_pairs={{0,8},{8,0},{16,24},{24,16},{1,9},{9,1},{17,25},{25,17},{2,10},{10... | collective-permute-start | bytes 442376 | tf_op jit(solution)/shard_map/ppermute | solution.py:902
  334.3 19.3 %collective-permute-start.66 = (bf16[48,1536]{1,0:T(8,128)(2,1)S(1)}, bf16[48,1536]{1,0:T(8,128)(2,1)S(1)}, u32[]{:S(2)}, u32[]{:S(2)}) collective-permute-start(bf16[48,1536]{1,0:T(8,128)(2,1)S(1)} %get-tuple-element.478), channel_id=1, source_target_pairs={{0,16},{16,0},{8,24},{24,8},{1,17},{17,1},{9,25},{25,9},{2,18},{18... | collective-permute-start | bytes 442376 | tf_op jit(solution)/shard_map/ppermute | solution.py:906
  336.1 17.5 %collective-permute-start.67 = (bf16[48,1536]{1,0:T(8,128)(2,1)S(1)}, bf16[48,1536]{1,0:T(8,128)(2,1)S(1)}, u32[]{:S(2)}, u32[]{:S(2)}) collective-permute-start(bf16[48,1536]{1,0:T(8,128)(2,1)S(1)} %get-tuple-element.477), channel_id=1, source_target_pairs={{0,24},{8,16},{16,8},{24,0},{1,25},{9,17},{17,9},{25,1},{2,26},{10... | collective-permute-start | bytes 442376 | tf_op jit(solution)/shard_map/ppermute | solution.py:910
  336.8 23.1 %collective-permute-start.64 = (bf16[256,1536]{1,0:T(8,128)(2,1)S(1)}, bf16[256,1536]{1,0:T(8,128)(2,1)S(1)}, u32[]{:S(2)}, u32[]{:S(2)}) collective-permute-start(bf16[256,1536]{1,0:T(8,128)(2,1)S(1)} %pair_sum.10), channel_id=1, source_target_pairs={{0,16},{16,0},{8,24},{24,8},{1,17},{17,1},{9,25},{25,9},{2,18},{18... | collective-permute-start | bytes 2359304 | tf_op jit(solution)/shard_map/ppermute | solution.py:906
  338.5 21.4 %collective-permute-start.63 = (bf16[256,1536]{1,0:T(8,128)(2,1)S(1)}, bf16[256,1536]{1,0:T(8,128)(2,1)S(1)}, u32[]{:S(2)}, u32[]{:S(2)}) collective-permute-start(bf16[256,1536]{1,0:T(8,128)(2,1)S(1)} %pair_sum.9), channel_id=1, source_target_pairs={{0,8},{8,0},{16,24},{24,16},{1,9},{9,1},{17,25},{25,17},{2,10},{10... | collective-permute-start | bytes 2359304 | tf_op jit(solution)/shard_map/ppermute | solution.py:902
  363.6 20.7 %collective-permute-start.70 = (bf16[256,1536]{1,0:T(8,128)(2,1)S(1)}, bf16[256,1536]{1,0:T(8,128)(2,1)}, u32[]{:S(2)}, u32[]{:S(2)}) collective-permute-start(bf16[256,1536]{1,0:T(8,128)(2,1)S(1)} %pair_sum.11), channel_id=1, source_target_pairs={{0,24},{8,16},{16,8},{24,0},{1,25},{9,17},{17,9},{25,1},{2,26},{10... | collective-permute-start | bytes 2359304 | tf_op jit(solution)/shard_map/ppermute | solution.py:910
  367.6 12.5 %collective-permute-start.73 = (bf16[48,1536]{1,0:T(8,128)(2,1)}, bf16[48,1536]{1,0:T(8,128)(2,1)}, u32[]{:S(2)}, u32[]{:S(2)}) collective-permute-start(bf16[48,1536]{1,0:T(8,128)(2,1)} %get-tuple-element.410), channel_id=1, source_target_pairs={{0,6},{2,0},{4,2},{6,4},{1,7},{3,1},{5,3},{7,5},{8,14},{10,8},{12,... | collective-permute-start | bytes 442376 | tf_op jit(solution)/shard_map/ppermute | solution.py:947
  367.7 13.9 %collective-permute-start.72 = (bf16[48,1536]{1,0:T(8,128)(2,1)}, bf16[48,1536]{1,0:T(8,128)(2,1)}, u32[]{:S(2)}, u32[]{:S(2)}) collective-permute-start(bf16[48,1536]{1,0:T(8,128)(2,1)} %get-tuple-element.409), channel_id=1, source_target_pairs={{0,4},{2,6},{4,0},{6,2},{1,5},{3,7},{5,1},{7,3},{8,12},{10,14},{12... | collective-permute-start | bytes 442376 | tf_op jit(solution)/shard_map/ppermute | solution.py:947
  367.9 13.6 %collective-permute-start.71 = (bf16[48,1536]{1,0:T(8,128)(2,1)}, bf16[48,1536]{1,0:T(8,128)(2,1)}, u32[]{:S(2)}, u32[]{:S(2)}) collective-permute-start(bf16[48,1536]{1,0:T(8,128)(2,1)} %get-tuple-element.408), channel_id=1, source_target_pairs={{0,2},{2,4},{4,6},{6,0},{1,3},{3,5},{5,7},{7,1},{8,10},{10,12},{12... | collective-permute-start | bytes 442376 | tf_op jit(solution)/shard_map/ppermute | solution.py:947
  384.4 29.5 %collective-permute-start.79 = (bf16[384,1536]{1,0:T(8,128)(2,1)}, bf16[384,1536]{1,0:T(8,128)(2,1)}, u32[]{:S(2)}, u32[]{:S(2)}) collective-permute-start(bf16[384,1536]{1,0:T(8,128)(2,1)} %reduce-scatter.3.cloned.1.call-done.refs_0_), channel_id=1, source_target_pairs={{0,16},{16,0},{8,24},{24,8},{1,17},{17,1},{9,25},{25,9},{2,18},{18... | collective-permute-start | bytes 3538952 | tf_op jit(solution)/shard_map/ppermute | solution.py:906
  386.2 28.8 %collective-permute-start.78 = (bf16[384,1536]{1,0:T(8,128)(2,1)}, bf16[384,1536]{1,0:T(8,128)(2,1)}, u32[]{:S(2)}, u32[]{:S(2)}) collective-permute-start(bf16[384,1536]{1,0:T(8,128)(2,1)} %reduce-scatter.3.cloned.1.call-done.refs_0_), channel_id=1, source_target_pairs={{0,8},{8,0},{16,24},{24,16},{1,9},{9,1},{17,25},{25,17},{2,10},{10... | collective-permute-start | bytes 3538952 | tf_op jit(solution)/shard_map/ppermute | solution.py:902
  387.1 27.9 %collective-permute-start.80 = (bf16[384,1536]{1,0:T(8,128)(2,1)}, bf16[384,1536]{1,0:T(8,128)(2,1)}, u32[]{:S(2)}, u32[]{:S(2)}) collective-permute-start(bf16[384,1536]{1,0:T(8,128)(2,1)} %reduce-scatter.3.cloned.1.call-done.refs_0_), channel_id=1, source_target_pairs={{0,1},{1,0},{2,3},{3,2},{4,5},{5,4},{6,7},{7,6},{8,9},{9,8},{10,11... | collective-permute-start | bytes 3538952 | tf_op jit(solution)/shard_map/ppermute | solution.py:898
  415.0 15.9 %collective-permute-start.83 = (bf16[192,1536]{1,0:T(8,128)(2,1)S(1)}, bf16[192,1536]{1,0:T(8,128)(2,1)S(1)}, u32[]{:S(2)}, u32[]{:S(2)}) collective-permute-start(bf16[192,1536]{1,0:T(8,128)(2,1)S(1)} %slice.129), channel_id=1, source_target_pairs={{0,8},{8,0},{16,24},{24,16},{1,9},{9,1},{17,25},{25,17},{2,10},{10... | collective-permute-start | bytes 1769480 | tf_op jit(solution)/shard_map/ppermute | solution.py:902
  417.1 13.8 %collective-permute-start.82 = (bf16[192,1536]{1,0:T(8,128)(2,1)S(1)}, bf16[192,1536]{1,0:T(8,128)(2,1)S(1)}, u32[]{:S(2)}, u32[]{:S(2)}) collective-permute-start(bf16[192,1536]{1,0:T(8,128)(2,1)S(1)} %slice.128), channel_id=1, source_target_pairs={{0,16},{16,0},{8,24},{24,8},{1,17},{17,1},{9,25},{25,9},{2,18},{18... | collective-permute-start | bytes 1769480 | tf_op jit(solution)/shard_map/ppermute | solution.py:906
  417.5 13.5 %collective-permute-start.85 = (bf16[384,1536]{1,0:T(8,128)(2,1)}, bf16[384,1536]{1,0:T(8,128)(2,1)}, u32[]{:S(2)}, u32[]{:S(2)}) collective-permute-start(bf16[384,1536]{1,0:T(8,128)(2,1)} %collective-permute-done.79.refs_4_), channel_id=1, source_target_pairs={{0,1},{1,0},{2,3},{3,2},{4,5},{5,4},{6,7},{7,6},{8,9},{9,8},{10,11... | collective-permute-start | bytes 3538952 | tf_op jit(solution)/shard_map/ppermute | solution.py:898
  417.5 13.5 %collective-permute-start.84 = (bf16[384,1536]{1,0:T(8,128)(2,1)}, bf16[384,1536]{1,0:T(8,128)(2,1)}, u32[]{:S(2)}, u32[]{:S(2)}) collective-permute-start(bf16[384,1536]{1,0:T(8,128)(2,1)} %collective-permute-done.78.refs_2_), channel_id=1, source_target_pairs={{0,1},{1,0},{2,3},{3,2},{4,5},{5,4},{6,7},{7,6},{8,9},{9,8},{10,11... | collective-permute-start | bytes 3538952 | tf_op jit(solution)/shard_map/ppermute | solution.py:898
  418.0 12.8 %collective-permute-start.81 = (f32[48,128]{1,0:T(8,128)S(1)}, f32[48,128]{1,0:T(8,128)S(1)}, u32[]{:S(2)}, u32[]{:S(2)}) collective-permute-start(f32[48,128]{1,0:T(8,128)S(1)} %add.320), channel_id=1, source_target_pairs={{0,16},{16,0},{8,24},{24,8},{1,17},{17,1},{9,25},{25,9},{2,18},{18... | collective-permute-start | bytes 73736 | tf_op jit(solution)/shard_map/ppermute | solution.py:906
  431.1 17.9 %collective-permute-start.86 = (bf16[384,640]{1,0:T(8,128)(2,1)}, bf16[384,640]{1,0:T(8,128)(2,1)S(1)}, u32[]{:S(2)}, u32[]{:S(2)}) collective-permute-start(bf16[384,640]{1,0:T(8,128)(2,1)} %reduce-scatter.5.cloned.1.call-done.refs_0_), channel_id=1, source_target_pairs={{0,8},{8,0},{16,24},{24,16},{1,9},{9,1},{17,25},{25,17},{2,10},{10... | collective-permute-start | bytes 1474568 | tf_op jit(solution)/shard_map/ppermute | solution.py:902
  432.3 16.8 %collective-permute-start.87 = (bf16[384,640]{1,0:T(8,128)(2,1)}, bf16[384,640]{1,0:T(8,128)(2,1)S(1)}, u32[]{:S(2)}, u32[]{:S(2)}) collective-permute-start(bf16[384,640]{1,0:T(8,128)(2,1)} %reduce-scatter.5.cloned.1.call-done.refs_0_), channel_id=1, source_target_pairs={{0,16},{16,0},{8,24},{24,8},{1,17},{17,1},{9,25},{25,9},{2,18},{18... | collective-permute-start | bytes 1474568 | tf_op jit(solution)/shard_map/ppermute | solution.py:906
  432.7 16.3 %collective-permute-start.88 = (bf16[384,640]{1,0:T(8,128)(2,1)}, bf16[384,640]{1,0:T(8,128)(2,1)S(1)}, u32[]{:S(2)}, u32[]{:S(2)}) collective-permute-start(bf16[384,640]{1,0:T(8,128)(2,1)} %reduce-scatter.5.cloned.1.call-done.refs_0_), channel_id=1, source_target_pairs={{0,1},{1,0},{2,3},{3,2},{4,5},{5,4},{6,7},{7,6},{8,9},{9,8},{10,11... | collective-permute-start | bytes 1474568 | tf_op jit(solution)/shard_map/ppermute | solution.py:898
  432.7 15.5 %collective-permute-start.90 = (bf16[48,1536]{1,0:T(8,128)(2,1)S(1)}, bf16[48,1536]{1,0:T(8,128)(2,1)}, u32[]{:S(2)}, u32[]{:S(2)}) collective-permute-start(bf16[48,1536]{1,0:T(8,128)(2,1)S(1)} %fusion.8), channel_id=1, source_target_pairs={{0,8},{8,0},{16,24},{24,16},{1,9},{9,1},{17,25},{25,17},{2,10},{10... | collective-permute-start | bytes 442376 | tf_op jit(solution)/shard_map/ppermute | solution.py:902
  433.9 15.1 %collective-permute-start.91 = (bf16[48,1536]{1,0:T(8,128)(2,1)S(1)}, bf16[48,1536]{1,0:T(8,128)(2,1)}, u32[]{:S(2)}, u32[]{:S(2)}) collective-permute-start(bf16[48,1536]{1,0:T(8,128)(2,1)S(1)} %fusion.8), channel_id=1, source_target_pairs={{0,16},{16,0},{8,24},{24,8},{1,17},{17,1},{9,25},{25,9},{2,18},{18... | collective-permute-start | bytes 442376 | tf_op jit(solution)/shard_map/ppermute | solution.py:906
  451.8 12.1 %collective-permute-start.93 = (bf16[192,640]{1,0:T(8,128)(2,1)S(1)}, bf16[192,640]{1,0:T(8,128)(2,1)S(1)}, u32[]{:S(2)}, u32[]{:S(2)}) collective-permute-start(bf16[192,640]{1,0:T(8,128)(2,1)S(1)} %slice.131), channel_id=1, source_target_pairs={{0,8},{8,0},{16,24},{24,16},{1,9},{9,1},{17,25},{25,17},{2,10},{10... | collective-permute-start | bytes 737288 | tf_op jit(solution)/shard_map/ppermute | solution.py:902
  (131 other events, 963.9 us)
Sparse Core Ops, SparseCore 0:
  10.2 52.6 all-gather.2
  65.0 88.3 all-gather.4
  251.0 81.8 reduce-scatter.2
  384.4 40.4 reduce-scatter.4
